TPU v7x, 32 devices: a whole 2x2x4 slice. The times are simulated.
32 devices in a mesh: blk: 4 (over y, x), elem: 8 (over z, core).
Axes of the slice: x: 2, y: 2, z: 4, core: 2. Of those that a mesh axis runs over, the one named last changes fastest.
Arguments:
- state: float32 [256, 125, 16, 128], P('blk', None, 'elem'), may hold values from -18 to 18
- rhs: float32 [256, 125, 16, 128], P('blk', None, 'elem'), may hold values from -6 to 6
- to_modal: float32 [125, 125], replicated, may hold values from -1 to 2
- viscous_op: float32 [125, 125], replicated, may hold values from -0.5 to 0.5
- sweep_gain: float32 [256, 125, 125], P('blk'), may hold values from -1 to 1.2
- inv_blocks: float32 [256, 125, 125], P('blk'), may hold values from -0.125 to 0.125
Outputs:
- line_solution: float32 [256, 125, 16, 128], P(('blk', 'elem'))
All inputs are finite; a program needn't handle non-finite values.
Results may differ from a plain program's by a relative error of at most 0.0003.
Values sent between devices are 32-bit elements; how exact they have to be, the bound alone decides.
No kernel may reach another device: no remote copies, remote signals or barrier semaphores. Data moves between devices by JAX's collectives and lax.ppermute only.
A program may use at most 128 MiB of HBM per device.

v0:
```python
import jax
import jax.numpy as jnp
from jax import lax
from jax.sharding import PartitionSpec as P

ORDER = 4
NODES = 125


def padded(cells, sides, width, closed):
    for axis, dim in sides:
        count = lax.axis_size(axis)
        ends = count if closed else count - 1
        head = lax.slice_in_dim(cells, 0, width, axis=dim)
        tail = lax.slice_in_dim(cells, cells.shape[dim] - width, cells.shape[dim], axis=dim)
        cells = jnp.concatenate(
            [
                lax.ppermute(tail, axis, [(i, (i + 1) % count) for i in range(ends)]),
                cells,
                lax.ppermute(head, axis, [((i + 1) % count, i) for i in range(ends)]),
            ],
            axis=dim,
        )
    return cells


def shifted(array, axis, by):
    length = lax.axis_size(axis)
    return lax.ppermute(array, axis, [(i, (i + by) % length) for i in range(length)])


def apply_block(matrix, field):
    return jnp.einsum("mn,nja->mja", matrix, field, precision=lax.Precision.HIGHEST)


def body(state, rhs, to_modal, viscous_op, sweep_gain, inv_blocks):
    highest = lax.Precision.HIGHEST
    modal = jnp.einsum("mn,knja->kmja", to_modal, state, precision=highest)
    squares = modal * modal
    upper = jnp.sum(squares[:, ORDER**3 :], axis=1) / NODES
    energy = jnp.mean(squares, axis=1) + 1e-06
    sensor = upper / energy
    beside_all = padded(sensor, (("blk", 0),), 1, True)
    outward = padded(sensor, (("elem", 1),), 1, False)
    smooth = (
        4.0 * sensor + beside_all[2:] + beside_all[:-2] + outward[:, 2:] + outward[:, :-2]
    ) / 8.0
    viscous = jnp.einsum("mn,knja->kmja", viscous_op, state, precision=highest)
    force = rhs + smooth[:, None] * viscous
    coupled = jnp.einsum("kmn,knja->kmja", inv_blocks, force, precision=highest)
    nodes_count = sweep_gain.shape[1]
    identity = jnp.eye(nodes_count, dtype=jnp.float32)
    zero_field = jnp.zeros(coupled.shape[1:], jnp.float32)

    def local_step(carry, inputs):
        product, partial_value = carry
        matrix, source = inputs
        product = jnp.dot(matrix, product, precision=highest)
        partial_value = apply_block(matrix, partial_value) + source
        return ((product, partial_value), (product, partial_value))

    (group_map, group_shift), (prefix_maps, partials) = lax.scan(
        local_step, (identity, zero_field), (sweep_gain, coupled)
    )
    group = lax.axis_index("blk")
    groups = lax.axis_size("blk")

    def cycle_step(turn, carry):
        outgoing, incoming = carry
        received = shifted(outgoing, "blk", 1)
        first_turn = turn == group
        second_turn = turn == groups + group
        pushed = apply_block(group_map, received) + group_shift
        incoming = jnp.where(second_turn, received, incoming)
        outgoing = jnp.where(first_turn | second_turn, pushed, outgoing)
        return (outgoing, incoming)

    _, incoming = lax.fori_loop(0, 2 * groups, cycle_step, (zero_field, zero_field))
    moved = lax.all_to_all(partials, "elem", split_axis=0, concat_axis=2, tiled=True)
    incoming_all = lax.all_gather(incoming, "elem", axis=1, tiled=True)
    share = moved.shape[0]
    offset = lax.axis_index("elem") * share
    my_maps = lax.dynamic_slice_in_dim(prefix_maps, offset, share, 0)
    return jnp.einsum("kmn,nja->kmja", my_maps, incoming_all, precision=highest) + moved


def solution(mesh):
    in_specs = (
        P("blk", None, "elem", None),
        P("blk", None, "elem", None),
        P(),
        P(),
        P("blk", None, None),
        P("blk", None, None),
    )
    out_specs = P(("blk", "elem"), None, None, None)
    return jax.shard_map(body, mesh=mesh, in_specs=in_specs, out_specs=out_specs, check_vma=False)
```

profile of v0, /device:TPU:9, one launch (start us, length us, event | category | flops | bytes accessed | tf_op | source)
XLA Modules:
  0.0 539.0 jit_solution(8537781872704107675)
XLA Ops:
  0.8 13.6 %fusion.39 = (f32[64,2,128]{2,1,0:T(2,128)S(1)}, f32[64,125,2,128]{3,1,2,0:T(8,128)S(1)}) fusion(f32[125,125]{1,0:T(8,128)S(1)} %copy-done, f32[64,125,2,128]{3,2,1,0:T(2,128)} %param.10), kind=kOutput, calls=%fused_computation.52 | convolution fusion | flops 3076079616 | bytes 16512036 | tf_op jit(solution)/shard_map/mn,knja->kmja/dot_general | solution.py:38
  15.3 2.6 collective-permute-start.3
  17.9 3.1 collective-permute-start.4
  21.0 2.2 collective-permute-start.1
  23.3 10.1 %fusion.13 = f32[64,2,128,125]{2,3,1,0:T(8,128)} fusion(f32[64,125,2,128]{3,2,1,0:T(2,128)S(1)} %copy-done.2, f32[125,125]{1,0:T(8,128)S(1)} %copy-done.4), kind=kOutput, calls=%fused_computation.24 | convolution fusion | flops 3072000000 | bytes 16446500 | tf_op jit(solution)/shard_map/mn,knja->kmja/dot_general | solution.py:48
  33.6 14.6 %bitcast_add_fusion = f32[64,125,2,128]{3,2,1,0:T(2,128)S(1)} fusion(f32[64,125,2,128]{3,2,1,0:T(2,128)} %param.11, f32[64,2,128,125]{2,3,1,0:T(8,128)} %fusion.13, f32[64,2,128]{2,1,0:T(2,128)S(1)} %fusion.29), kind=kLoop, calls=%fused_computation.22 | loop fusion | flops 4096000 | bytes 24641536 | tf_op jit(solution)/shard_map/add | solution.py:49
  48.3 19.4 %fusion.18 = f32[64,125,2,128]{1,3,2,0:T(8,128)} fusion(f32[64,125,125,1]{2,0,1,3:T(8,128)S(1)} %bitcast.67, f32[64,125,2,128]{3,2,1,0:T(2,128)S(1)} %bitcast_add_fusion), kind=kOutput, calls=%fused_computation.30 | convolution fusion | flops 3072000000 | bytes 20384000 | tf_op jit(solution)/shard_map/kmn,knja->kmja/dot_general | solution.py:50
  67.6 256.5 %while.34 = (s32[]{:T(128)}, f32[125,125]{1,0:T(8,128)S(1)}, f32[125,2,128]{2,0,1:T(8,128)S(1)}, f32[64,125,125]{2,1,0:T(8,128)}, f32[64,125,2,128]{3,2,1,0:T(2,...) while((s32[]{:T(128)}, f32[125,125]{1,0:T(8,128)S(1)}, ...), condition=%wide.region_3.4_spmd.clone, body=%wide.region_2.3_spmd.clone.sunk | while | flops 71501504 | bytes 1974671 | solution.py:62
  67.6 1.1 constant_dynamic-slice_fusion.4
  71.7 1.1 constant_dynamic-slice_fusion.4
  75.7 1.1 constant_dynamic-slice_fusion.4
  79.7 1.1 constant_dynamic-slice_fusion.4
  83.7 1.1 constant_dynamic-slice_fusion.4
  87.7 1.1 constant_dynamic-slice_fusion.4
  91.7 1.1 constant_dynamic-slice_fusion.4
  95.7 1.1 constant_dynamic-slice_fusion.4
  99.7 1.1 constant_dynamic-slice_fusion.4
  103.7 1.1 constant_dynamic-slice_fusion.4
  107.7 1.1 constant_dynamic-slice_fusion.4
  111.8 1.1 constant_dynamic-slice_fusion.4
  119.8 1.1 constant_dynamic-slice_fusion.4
  123.8 1.1 constant_dynamic-slice_fusion.4
  127.8 1.1 constant_dynamic-slice_fusion.4
  131.8 1.1 constant_dynamic-slice_fusion.4
  135.8 1.1 constant_dynamic-slice_fusion.4
  139.8 1.1 constant_dynamic-slice_fusion.4
  143.8 1.1 constant_dynamic-slice_fusion.4
  147.8 1.1 constant_dynamic-slice_fusion.4
  151.8 1.1 constant_dynamic-slice_fusion.4
  155.8 1.1 constant_dynamic-slice_fusion.4
  159.8 1.1 constant_dynamic-slice_fusion.4
  163.8 1.1 constant_dynamic-slice_fusion.4
  167.8 1.1 constant_dynamic-slice_fusion.4
  175.9 1.1 constant_dynamic-slice_fusion.4
  183.9 1.1 constant_dynamic-slice_fusion.4
  191.9 1.1 constant_dynamic-slice_fusion.4
  195.9 1.1 constant_dynamic-slice_fusion.4
  199.9 1.1 constant_dynamic-slice_fusion.4
  203.9 1.1 constant_dynamic-slice_fusion.4
  207.9 1.1 constant_dynamic-slice_fusion.4
  211.9 1.1 constant_dynamic-slice_fusion.4
  215.9 1.1 constant_dynamic-slice_fusion.4
  219.9 1.1 constant_dynamic-slice_fusion.4
  223.9 1.1 constant_dynamic-slice_fusion.4
  231.9 1.1 constant_dynamic-slice_fusion.4
  235.9 1.1 constant_dynamic-slice_fusion.4
  239.9 1.1 constant_dynamic-slice_fusion.4
  247.9 1.1 constant_dynamic-slice_fusion.4
  252.0 1.1 constant_dynamic-slice_fusion.4
  324.1 4.9 all-to-all-start
  329.0 45.8 %while.35 = (s32[]{:T(128)}, f32[125,2,128]{2,0,1:T(8,128)S(1)}, f32[125,2,128]{2,0,1:T(8,128)S(1)}, s32[]{:T(128)}, s32[]{:T(128)}, /*index=5*/f32[125,125]{1,0...) while((s32[]{:T(128)}, f32[125,2,128]{2,0,1:T(8,128)S(1)}, ...), condition=%wide.region_5.6_spmd.clone, body=%wide.region_4.5_spmd.clone.sunk | while | flops 48160004 | bytes 1726667 | solution.py:78
  329.1 1.4 collective-permute-start
  330.5 4.8 collective-permute-done
  335.9 5.2 collective-permute-done
  341.5 5.1 collective-permute-done
  347.0 5.1 collective-permute-done
  352.5 4.7 collective-permute-done
  357.7 4.7 collective-permute-done
  362.8 5.5 %collective-permute-done = f32[125,2,128]{2,0,1:T(8,128)S(1)} collective-permute-done((f32[125,2,128]{2,0,1:T(8,128)S(1)}, f32[125,2,128]{2,0,1:T(8,128)S(1)}, u32[]{:S(2)}, u32[]{:S(2)}) %collective-permute-start) | collective-permute-done | bytes 128032 | tf_op jit(solution)/shard_map/while/body/eval_jaxpr/ppermute | solution.py:29
  368.7 5.8 %collective-permute-done = f32[125,2,128]{2,0,1:T(8,128)S(1)} collective-permute-done((f32[125,2,128]{2,0,1:T(8,128)S(1)}, f32[125,2,128]{2,0,1:T(8,128)S(1)}, u32[]{:S(2)}, u32[]{:S(2)}) %collective-permute-start) | collective-permute-done | bytes 128032 | tf_op jit(solution)/shard_map/while/body/eval_jaxpr/ppermute | solution.py:29
  374.8 143.5 %all_gather.3 = f32[125,16,128]{2,0,1:T(8,128)S(1)} all-gather(f32[125,2,128]{2,0,1:T(8,128)S(1)} %get-tuple-element.186), channel_id=1, replica_groups=mesh['blk'=4,'elem'=8] {'elem'}, dimensions={1}, use_global_device_ids=true | all-gather | bytes 1152000 | tf_op jit(solution)/shard_map/all_gather | solution.py:80
  518.4 4.6 copy.20
  523.0 8.1 %convolution_add_fusion.2 = f32[8,125,16,128]{3,1,2,0:T(8,128)S(1)} fusion(f32[8,125,16,128]{3,1,2,0:T(8,128)S(1)} %bitcast.65, f32[125,16,128]{2,0,1:T(8,128)S(1)} %all_gather.3, f32[64,125,125]{2,1,0:T(8,128)} %get-tuple-element.183, s32[]{:T(128)S(6)} %select_n.37), kind=kOutput, calls=%fused_computation.31 | convolution fusion | flops 3074048000 | bytes 17932292 | tf_op jit(solution)/shard_map/kmn,nja->kmja/dot_general | solution.py:84
  531.1 8.0 %copy.21 = f32[8,125,16,128]{3,2,1,0:T(8,128)} copy(f32[8,125,16,128]{3,1,2,0:T(8,128)S(1)} %convolution_add_fusion.2) | data formatting | bytes 16384000 | tf_op jit(solution)/shard_map/add | solution.py:84
  (529 shorter events, 215.5 us)
Async XLA Ops:
  0.0 0.8 copy-start
  0.0 23.2 %copy-start.2 = (f32[64,125,2,128]{3,2,1,0:T(2,128)S(1)}, f32[64,125,2,128]{3,2,1,0:T(2,128)}, u32[]{:S(2)}) copy-start(f32[64,125,2,128]{3,2,1,0:T(2,128)} %param.10) | copy-start | bytes 24576004
  0.0 23.2 %copy-start.4 = (f32[125,125]{1,0:T(8,128)S(1)}, f32[125,125]{1,0:T(8,128)}, u32[]{:S(2)}) copy-start(f32[125,125]{1,0:T(8,128)} %param.13) | copy-start | bytes 187504
  15.3 18.1 %collective-permute-start.3 = (f32[64,1,128]{2,1,0:T(1,128)S(1)}, f32[64,1,128]{2,1,0:T(1,128)S(1)}, u32[]{:S(2)}, u32[]{:S(2)}) collective-permute-start(f32[64,1,128]{2,1,0:T(1,128)S(1)} %get-tuple-element.282), channel_id=1, source_target_pairs={{1,0},{2,1},{3,2},{4,3},{5,4},{6,5},{7,6},{9,8},{10,9},{11,10},{12... | collective-permute-start | bytes 98312 | tf_op jit(solution)/shard_map/ppermute | solution.py:20
  17.9 15.5 %collective-permute-start.4 = (f32[64,1,128]{2,1,0:T(1,128)S(1)}, f32[64,1,128]{2,1,0:T(1,128)S(1)}, u32[]{:S(2)}, u32[]{:S(2)}) collective-permute-start(f32[64,1,128]{2,1,0:T(1,128)S(1)} %get-tuple-element.283), channel_id=1, source_target_pairs={{0,1},{1,2},{2,3},{3,4},{4,5},{5,6},{6,7},{8,9},{9,10},{10,11},{11... | collective-permute-start | bytes 98312 | tf_op jit(solution)/shard_map/ppermute | solution.py:18
  21.0 12.4 %collective-permute-start.1 = (f32[1,2,128]{2,1,0:T(2,128)S(1)}, f32[1,2,128]{2,1,0:T(2,128)S(1)}, u32[]{:S(2)}, u32[]{:S(2)}) collective-permute-start(f32[1,2,128]{2,1,0:T(2,128)S(1)} %get-tuple-element.280), channel_id=1, source_target_pairs={{8,0},{16,8},{24,16},{0,24},{9,1},{17,9},{25,17},{1,25},{10,2},{18... | collective-permute-start | bytes 3080 | tf_op jit(solution)/shard_map/ppermute | solution.py:20
  23.2 10.2 %collective-permute-start.2 = (f32[1,2,128]{2,1,0:T(2,128)S(1)}, f32[1,2,128]{2,1,0:T(2,128)S(1)}, u32[]{:S(2)}, u32[]{:S(2)}) collective-permute-start(f32[1,2,128]{2,1,0:T(2,128)S(1)} %get-tuple-element.281), channel_id=1, source_target_pairs={{0,8},{8,16},{16,24},{24,0},{1,9},{9,17},{17,25},{25,1},{2,10},{10... | collective-permute-start | bytes 3080 | tf_op jit(solution)/shard_map/ppermute | solution.py:18
  33.6 14.6 %copy-start.3 = (f32[64,125,125]{2,0,1:T(8,128)S(1)}, f32[64,125,125]{2,0,1:T(8,128)}, u32[]{:S(2)}) copy-start(f32[64,125,125]{2,0,1:T(8,128)} %param.15) | copy-start | bytes 12000004
  324.1 194.3 %all-to-all-start = ((f32[64,125,2,128]{3,2,1,0:T(2,128)}), f32[64,125,2,128]{3,2,1,0:T(2,128)}, u32[]{:S(2)}, u32[]{:S(2)}) async-start(f32[64,125,2,128]{3,2,1,0:T(2,128)} %get-tuple-element.187), calls=%async_computation | async-start | bytes 16384000 | tf_op jit(solution)/shard_map/all_to_all | solution.py:79
  329.1 6.2 %collective-permute-start = (f32[125,2,128]{2,0,1:T(8,128)S(1)}, f32[125,2,128]{2,0,1:T(8,128)S(1)}, u32[]{:S(2)}, u32[]{:S(2)}) collective-permute-start(f32[125,2,128]{2,0,1:T(8,128)S(1)} %broadcast_select_fusion.2), channel_id=1, source_target_pairs={{0,8},{8,16},{16,24},{24,0},{1,9},{9,17},{17,25},{25,1},{2,10},{10... | collective-permute-start | bytes 384008 | tf_op jit(solution)/shard_map/while/body/eval_jaxpr/ppermute | solution.py:29
  335.6 5.4 %collective-permute-start = (f32[125,2,128]{2,0,1:T(8,128)S(1)}, f32[125,2,128]{2,0,1:T(8,128)S(1)}, u32[]{:S(2)}, u32[]{:S(2)}) collective-permute-start(f32[125,2,128]{2,0,1:T(8,128)S(1)} %broadcast_select_fusion.2), channel_id=1, source_target_pairs={{0,8},{8,16},{16,24},{24,0},{1,9},{9,17},{17,25},{25,1},{2,10},{10... | collective-permute-start | bytes 384008 | tf_op jit(solution)/shard_map/while/body/eval_jaxpr/ppermute | solution.py:29
  341.4 5.2 collective-permute-start
  346.9 5.2 collective-permute-start
  352.5 4.8 collective-permute-start
  357.6 4.8 collective-permute-start
  362.7 5.6 %collective-permute-start = (f32[125,2,128]{2,0,1:T(8,128)S(1)}, f32[125,2,128]{2,0,1:T(8,128)S(1)}, u32[]{:S(2)}, u32[]{:S(2)}) collective-permute-start(f32[125,2,128]{2,0,1:T(8,128)S(1)} %broadcast_select_fusion.2), channel_id=1, source_target_pairs={{0,8},{8,16},{16,24},{24,0},{1,9},{9,17},{17,25},{25,1},{2,10},{10... | collective-permute-start | bytes 384008 | tf_op jit(solution)/shard_map/while/body/eval_jaxpr/ppermute | solution.py:29
  368.6 5.9 %collective-permute-start = (f32[125,2,128]{2,0,1:T(8,128)S(1)}, f32[125,2,128]{2,0,1:T(8,128)S(1)}, u32[]{:S(2)}, u32[]{:S(2)}) collective-permute-start(f32[125,2,128]{2,0,1:T(8,128)S(1)} %broadcast_select_fusion.2), channel_id=1, source_target_pairs={{0,8},{8,16},{16,24},{24,0},{1,9},{9,17},{17,25},{25,1},{2,10},{10... | collective-permute-start | bytes 384008 | tf_op jit(solution)/shard_map/while/body/eval_jaxpr/ppermute | solution.py:29
  523.0 16.0 %copy-start.1 = (f32[125,125]{1,0:T(8,128)S(1)}, f32[125,125]{1,0:T(8,128)}, u32[]{:S(2)}) copy-start(f32[125,125]{1,0:T(8,128)} %param.12) | copy-start | bytes 187504
where the time goes:
time: 545 us; the launch traced here: 539 us
  local copies, waits for them, and re-layouts  198 us (36%)
  blocking collectives  144 us (26%)
  matrix products  123 us (23%)
  waiting for transfers between devices  40.9 us (8%)
  other arithmetic  16 us (3%)
  starting transfers between devices  14.8 us (3%)
    all_gather x1, blocking collectives, body(): incoming_all = lax.all_gather(incoming, 'elem', axis=1, tiled=True)  144 us
    dynamic_slice x192, local copies, waits for them, and re-layouts, body(): lax.scan(local_step, (identity, zero_field), (sweep_gain, coupled))  135 us
    dot_general x64, matrix products, local_step(): product = jnp.dot(matrix, product, precision=highest)  53.2 us
    dynamic_update_slice x64, local copies, waits for them, and re-layouts, body(): lax.scan(local_step, (identity, zero_field), (sweep_gain, coupled))  48.4 us
    ppermute x8, waiting for transfers between devices, shifted(): lax.ppermute(array, axis, [(i, (i + by) % length) for i in range(length)])  40.9 us
    dot_general x1, matrix products, body(): coupled = jnp.einsum('kmn,knja->kmja', inv_blocks, force, precision=highest)  19.4 us
    dot_general x72, matrix products, apply_block(): jnp.einsum('mn,nja->mja', matrix, field, precision=lax.Precision.HIGHEST)  18.9 us
    add x1, other arithmetic, body(): force = rhs + smooth[:, None] * viscous  14.6 us
  transfers between devices with their start and end apart: 13, of which 8 were waited for; matrix products, arithmetic and copies ran while one was open for 2% of the time, Pallas kernels for 0%

commit v1 on v0

v1 whole, which is shorter than its diff:
```python
import functools

import jax
import jax.numpy as jnp
from jax import lax
from jax.experimental import pallas as pl
from jax.experimental.pallas import tpu as pltpu
from jax.sharding import PartitionSpec as P

ORDER = 4
F32 = jnp.float32
BF16 = jnp.bfloat16
VMEM_LIMIT = 36 * 1024 * 1024
TILE = 8
LANES = 128


def operand_left(a):
    high = a.astype(BF16)
    low = (a - high.astype(F32)).astype(BF16)
    return jnp.concatenate([jnp.concatenate([high, high], axis=1), jnp.concatenate([low, low], axis=1)], axis=0)


def operand_right(x):
    high = x.astype(BF16)
    return jnp.concatenate([high, (x - high.astype(F32)).astype(BF16)], axis=0)


def product(left, right):
    both = jnp.dot(left, right, preferred_element_type=F32)
    half = left.shape[0] // 2
    return both[:half] + both[half:]


def spec_any():
    return pl.BlockSpec(memory_space=pl.ANY)


def spec_vmem():
    return pl.BlockSpec(memory_space=pltpu.VMEM)


def spec_smem():
    return pl.BlockSpec(memory_space=pltpu.SMEM)


def call(kernel, name, outs, in_specs, out_specs, scratch, flops, nbytes, aliases=None):
    return pl.pallas_call(
        kernel,
        name=name,
        out_shape=outs,
        in_specs=in_specs,
        out_specs=out_specs,
        scratch_shapes=scratch,
        input_output_aliases=aliases or {},
        compiler_params=pltpu.CompilerParams(vmem_limit_bytes=VMEM_LIMIT),
        cost_estimate=pl.CostEstimate(flops=int(flops), bytes_accessed=int(nbytes), transcendentals=0),
    )


def f32(*shape):
    return jax.ShapeDtypeStruct(shape, F32)


def up(value, unit):
    return -(-value // unit) * unit


class Sizes:
    def __init__(self, state, segments, groups):
        count, self.nodes, self.rows, self.ax = state.shape
        self.count = count
        self.segments = segments
        self.groups = groups
        self.steps = count // segments
        self.cols = self.rows * self.ax
        self.height = self.nodes * self.rows
        self.pad = up(self.nodes, LANES)
        self.spill = up((self.pad - self.nodes) * self.rows, TILE)
        self.flops = 2 * 4 * self.pad * self.pad * self.cols

    def window(self, low, high):
        first = low * self.height // TILE * TILE
        return first, up(high * self.height, TILE) - first

    def message(self, count):
        return up(count * self.height, TILE)

    def rows_masked(self, x):
        cut = self.nodes // TILE * TILE
        rest = x[cut:]
        inside = lax.broadcasted_iota(jnp.int32, rest.shape, 0) < self.nodes - cut
        return jnp.concatenate([x[:cut], jnp.where(inside, rest, 0.0)], axis=0)

    def square(self, x):
        x = jnp.concatenate([x, jnp.zeros((self.nodes, self.pad - self.nodes), F32)], axis=1)
        return jnp.concatenate([x, jnp.zeros((self.pad - self.nodes, self.pad), F32)], axis=0)


def read_field(z, ref, lead, offset):
    parts = [ref[lead + (pl.ds(offset + j, z.pad, stride=z.rows), slice(None))] for j in range(z.rows)]
    return z.rows_masked(jnp.concatenate(parts, axis=1))


def read_exact(z, ref, lead, offset):
    parts = [ref[lead + (pl.ds(offset + j, z.nodes, stride=z.rows), slice(None))] for j in range(z.rows)]
    return jnp.concatenate(parts, axis=1)


def write_field(z, ref, lead, offset, value):
    for j in range(z.rows):
        rows = pl.ds(offset + j, z.nodes, stride=z.rows)
        ref[lead + (rows, slice(None))] = value[: z.nodes, j * z.ax : (j + 1) * z.ax]


def read_matrix(z, ref, k):
    return z.square(ref[:, k, :])


def sensor_call(z, state, to_modal, after, low, high):
    first, size = z.window(low, high)
    count = high - low

    def kernel(state_ref, modal_ref, *refs):
        sensor_ref, head_ref, tail_ref, buf, sem = refs[len(after) :]
        copies = [
            pltpu.make_async_copy(state_ref.at[e, pl.ds(first, size)], buf.at[e, pl.ds(0, size)], sem.at[e])
            for e in range(z.segments)
        ]
        for copy in copies:
            copy.start()
        matrix = operand_left(z.square(modal_ref[...]))
        for e in range(z.segments):
            copies[e].wait()
            for i in range(low, high):
                field = read_field(z, buf, (e,), i * z.height - first)
                modal = product(matrix, operand_right(field))
                squares = modal * modal
                lower = jnp.sum(squares[: ORDER**3], axis=0, keepdims=True)
                upper = jnp.sum(squares[ORDER**3 :], axis=0, keepdims=True)
                sensor = (upper / z.nodes) / ((lower + upper) / z.nodes + 1e-6)
                sensor_ref[i - low, e : e + 1, :] = sensor
                head_ref[i - low, e : e + 1, :] = sensor[:, : z.ax]
                tail_ref[i - low, e : e + 1, :] = sensor[:, z.cols - z.ax :]

    outs = [f32(count, z.segments, z.cols), f32(count, z.segments, z.ax), f32(count, z.segments, z.ax)]
    return call(
        kernel,
        f"sensor_{low}",
        outs,
        [spec_any(), spec_vmem()] + [spec_any()] * len(after),
        [spec_vmem()] * 3,
        [pltpu.VMEM((z.segments, size + z.spill, z.ax), F32), pltpu.SemaphoreType.DMA((z.segments,))],
        z.flops * count * z.segments,
        4 * z.segments * size * z.ax,
    )(state, to_modal, *after)


def smoothed(z, sensor, before, after, left, right):
    inner = sensor[:, : z.cols - z.ax]
    outer = sensor[:, z.ax :]
    from_left = jnp.concatenate([left, inner], axis=1)
    from_right = jnp.concatenate([outer, right], axis=1)
    return (4.0 * sensor + before + after + from_left + from_right) / 8.0


def sweep_call(z, chunk, whole, me, state, rhs, viscous, gain, inverse, sensors, lefts, rights, ring, carry, after):
    low, high = chunk
    with_first = high == z.steps
    first, size = z.window(low, high)
    count = high - low
    first0, size0 = z.window(0, 1)
    arrays = []

    def place(array):
        for n, known in enumerate(arrays):
            if known is array:
                return n
        arrays.append(array)
        return len(arrays) - 1

    steps = list(range(low, high)) + ([0] if with_first else [])
    plan = []
    for i in steps:
        beside = []
        for k in (i, (i - 1) % z.steps, (i + 1) % z.steps):
            beside.append((place(sensors[k][0]), sensors[k][1]))
        for side in (lefts, rights):
            beside.append((place(side[i][0]), side[i][1]))
        plan.append(beside)
    ring_places = [place(array) for array in ring] if with_first else []
    small = len(arrays)
    has_carry = carry is not None
    needs_gain = has_carry or count > 1
    sent = 1 if whole else z.segments
    message = z.message(count)

    def kernel(*refs):
        me_ref, state_ref, rhs_ref, viscous_ref, inverse_ref = refs[:5]
        refs = refs[5:]
        if needs_gain:
            gain_ref, refs = refs[0], refs[1:]
        small_refs, refs = refs[:small], refs[small:]
        if has_carry:
            carry_ref, refs = refs[0], refs[1:]
        refs = refs[len(after) :]
        out_refs, refs = refs[:sent], refs[sent:]
        end_ref, refs = refs[0], refs[1:]
        if with_first:
            start_ref, refs = refs[0], refs[1:]
        state_buf, rhs_buf, smooth_buf, stage, sem, out_sem = refs[:6]
        if with_first:
            state0, rhs0 = refs[6:]
        mine = me_ref[0]
        batch = 4 if z.segments % 4 == 0 else 1
        places = [e if whole else lax.rem(mine + e, z.segments) for e in range(z.segments)]
        copies = []
        for s, e in enumerate(places):
            moves = [
                (state_ref.at[e, pl.ds(first, size)], state_buf.at[s, pl.ds(0, size)]),
                (rhs_ref.at[e, pl.ds(first, size)], rhs_buf.at[s, pl.ds(0, size)]),
            ]
            if with_first:
                moves.append((state_ref.at[e, pl.ds(first0, size0)], state0.at[s, pl.ds(0, size0)]))
                moves.append((rhs_ref.at[e, pl.ds(first0, size0)], rhs0.at[s, pl.ds(0, size0)]))
            started = []
            for n, (source, target) in enumerate(moves):
                copy = pltpu.make_async_copy(source, target, sem.at[s, n])
                copy.start()
                started.append(copy)
            copies.append(started)
        for n, i in enumerate(steps):
            (a0, p0), (a1, p1), (a2, p2), (al, pL), (ar, pR) = plan[n]
            here = small_refs[a0][p0]
            before = small_refs[a1][p1]
            later = small_refs[a2][p2]
            if i == 0:
                before = jnp.concatenate([small_refs[ring_places[0]][...], before[: z.segments - 1]], axis=0)
            if i == z.steps - 1:
                later = jnp.concatenate([later[1:], small_refs[ring_places[1]][...]], axis=0)
            smooth_buf[n] = smoothed(z, here, before, later, small_refs[al][pL], small_refs[ar][pR])
        operator = operand_left(z.square(viscous_ref[...]))

        def source(field, force, matrix, smooth):
            force = force + smooth * product(operator, operand_right(field))
            return product(operand_left(matrix), operand_right(force))

        sends = []
        for s0 in range(0, z.segments, batch):
            group = range(s0, s0 + batch)
            for s in group:
                for copy in copies[s]:
                    copy.wait()
            fields = [carry_ref[places[s]] if has_carry else None for s in group]
            for n in range(count):
                offset = (low + n) * z.height - first
                for g, s in enumerate(group):
                    k = places[s] * z.steps + low + n
                    smooth = smooth_buf[n, pl.ds(places[s], 1), :]
                    value = source(
                        read_field(z, state_buf, (s,), offset),
                        read_field(z, rhs_buf, (s,), offset),
                        read_matrix(z, inverse_ref, k),
                        smooth,
                    )
                    if fields[g] is not None:
                        value = value + product(
                            operand_left(read_matrix(z, gain_ref, k)), operand_right(fields[g])
                        )
                    fields[g] = value
                    write_field(z, stage, (s,), n * z.height, value)
            for g, s in enumerate(group):
                target = out_refs[0].at[s] if whole else out_refs[s]
                copy = pltpu.make_async_copy(stage.at[s], target, out_sem.at[s])
                copy.start()
                sends.append(copy)
                end_ref[places[s]] = fields[g]
                if with_first:
                    smooth = smooth_buf[count, pl.ds(places[s], 1), :]
                    start_ref[places[s]] = source(
                        read_field(z, state0, (s,), -first0),
                        read_field(z, rhs0, (s,), -first0),
                        read_matrix(z, inverse_ref, places[s] * z.steps),
                        smooth,
                    )
        for copy in sends:
            copy.wait()

    field = f32(z.segments, z.pad, z.cols)
    outs = [f32(z.segments, message, z.ax)] if whole else [f32(message, z.ax) for _ in range(z.segments)]
    outs += [field] * (2 if with_first else 1)
    operands = [me, state, rhs, viscous, inverse] + ([gain] if needs_gain else [])
    in_specs = [spec_smem(), spec_any(), spec_any()] + [spec_vmem()] * (len(operands) - 3)
    operands += arrays + ([carry] if has_carry else []) + after
    in_specs += [spec_vmem()] * (small + (1 if has_carry else 0)) + [spec_any()] * len(after)
    out_specs = [spec_any()] * sent + [spec_vmem()] * (2 if with_first else 1)
    scratch = [
        pltpu.VMEM((z.segments, size + z.spill, z.ax), F32),
        pltpu.VMEM((z.segments, size + z.spill, z.ax), F32),
        pltpu.VMEM((len(steps), z.segments, z.cols), F32),
        pltpu.VMEM((z.segments, message, z.ax), F32),
        pltpu.SemaphoreType.DMA((z.segments, 4)),
        pltpu.SemaphoreType.DMA((z.segments,)),
    ]
    if with_first:
        scratch += [pltpu.VMEM((z.segments, size0 + z.spill, z.ax), F32)] * 2
    result = call(
        kernel,
        f"sweep_{low}",
        outs,
        in_specs,
        out_specs,
        scratch,
        z.flops * len(steps) * z.segments * 3,
        4 * z.segments * size * z.ax * 4,
    )(*operands)
    return result[:sent], result[sent:]


def maps_call(z, me, gain, after):
    def kernel(me_ref, gain_ref, *refs):
        own_ref, tail_ref, whole_ref, prefix_ref, group_ref = refs[len(after) :]
        mine = me_ref[0]

        def times(a, b):
            return product(operand_left(a), operand_right(b))

        own_ref[0] = read_matrix(z, gain_ref, mine * z.steps)
        values = [read_matrix(z, gain_ref, e * z.steps + 1) for e in range(z.segments)]
        for i in range(1, z.steps):
            for e in range(z.segments):
                if i > 1:
                    values[e] = times(read_matrix(z, gain_ref, e * z.steps + i), values[e])

                @pl.when(e == mine)
                def _(i=i, value=values[e]):
                    own_ref[i] = value

        for e in range(z.segments):
            tail_ref[e] = values[e]
            whole_ref[e] = times(values[e], read_matrix(z, gain_ref, e * z.steps))
        value = whole_ref[0]
        prefix_ref[0] = value
        for e in range(1, z.segments):
            prefix_ref[e] = value
            value = times(whole_ref[e], value)
        group_ref[...] = value

    square = (z.pad, z.pad)
    outs = [f32(z.steps, *square)] + [f32(z.segments, *square)] * 3 + [f32(*square)]
    return call(
        kernel,
        "maps",
        outs,
        [spec_smem(), spec_vmem()] + [spec_any()] * len(after),
        [spec_vmem()] * 5,
        [],
        z.flops * z.segments * (z.steps + 1) // 2,
        4 * z.segments * z.steps * z.pad * z.pad,
    )(me, gain, *after)


def chain_call(z, starts, ends, tails, wholes, group):
    def kernel(start_ref, end_ref, tail_ref, whole_ref, group_ref, before_ref, pack_ref):
        value = None
        for e in range(z.segments):
            shift = end_ref[e] + product(operand_left(tail_ref[e]), operand_right(start_ref[e]))
            if e > 0:
                before_ref[e] = value
                shift = shift + product(operand_left(whole_ref[e]), operand_right(value))
            else:
                before_ref[0] = jnp.zeros_like(shift)
            value = shift
        pack_ref[:, : z.cols] = value
        pack_ref[:, z.cols :] = group_ref[...]

    return call(
        kernel,
        "chain",
        [f32(z.segments, z.pad, z.cols), f32(z.pad, z.cols + z.pad)],
        [spec_vmem()] * 5,
        [spec_vmem()] * 2,
        [],
        z.flops * z.segments * 2,
        4 * z.segments * z.pad * z.cols * 4,
    )(starts, ends, tails, wholes, group)


def first_call(z, places, packs, before, prefix, gain, starts, held):
    message = z.message(1)

    def kernel(*refs):
        places_ref, refs = refs[0], refs[1:]
        pack_refs, refs = refs[: z.groups], refs[z.groups :]
        before_ref, prefix_ref, gain_ref, start_ref, _ = refs[:5]
        out_refs = refs[5 : 5 + z.segments]
        mine = places_ref[0]
        group = places_ref[1]
        value = jnp.zeros((z.pad, z.cols), F32)
        matrices = [operand_left(ref[:, z.cols :]) for ref in pack_refs]
        for t in range(2 * z.groups - 1, 0, -1):
            n = t % z.groups
            moved = product(matrices[n], operand_right(value)) + pack_refs[n][:, : z.cols]
            value = jnp.where(t <= z.groups + group, moved, 0.0)
        incoming = operand_right(value)
        for s in range(z.segments):
            e = lax.rem(mine + s, z.segments)
            arriving = jnp.where(e == 0, value, before_ref[e] + product(operand_left(prefix_ref[e]), incoming))
            matrix = operand_left(read_matrix(z, gain_ref, e * z.steps))
            solved = start_ref[e] + product(matrix, operand_right(arriving))
            write_field(z, out_refs[s], (), 0, solved)

    result = call(
        kernel,
        "first",
        [f32(message, z.ax) for _ in range(z.segments)] + [jax.ShapeDtypeStruct(held.shape, F32)],
        [spec_smem()] + [spec_vmem()] * (z.groups + 4) + [spec_any()],
        [spec_vmem()] * z.segments + [spec_any()],
        [],
        z.flops * (z.segments * 2 + 2 * z.groups),
        4 * z.segments * z.pad * z.cols * 4,
        {z.groups + 5: z.segments},
    )(places, *packs, before, prefix, gain, starts, held)
    return result[: z.segments], result[z.segments]


def finish_call(z, chunk, me, own, firsts, messages, out):
    low, high = chunk
    count = high - low
    radial = z.segments * z.rows
    tall = z.nodes * radial
    only_first = messages is None
    has_out = out is not None
    whole = not only_first and len(messages) == 1
    sent = 0 if only_first else len(messages)

    def kernel(*refs):
        me_ref, own_ref, refs = refs[0], refs[1], refs[2:]
        first_refs, refs = refs[: z.segments], refs[z.segments :]
        message_refs, refs = refs[:sent], refs[sent:]
        if has_out:
            refs = refs[1:]
        out_ref, stage, sem = refs
        mine = me_ref[0]
        matrices = None if only_first else [operand_left(own_ref[i]) for i in range(low, high)]
        for s in range(z.segments):
            src = lax.rem(mine - s + z.segments, z.segments)
            field = read_exact(z, first_refs[s], (), 0)
            if not only_first:
                empty = jnp.zeros((z.pad - z.nodes, z.cols), F32)
                parts = operand_right(jnp.concatenate([field, empty], axis=0))
            for n in range(count):
                if only_first:
                    value = field
                else:
                    ref, lead = (message_refs[0], (src,)) if whole else (message_refs[s], ())
                    value = product(matrices[n], parts)[: z.nodes] + read_exact(z, ref, lead, n * z.height)
                for j in range(z.rows):
                    rows = pl.ds(src * z.rows + j, z.nodes, stride=radial)
                    stage[n, rows, :] = value[:, j * z.ax : (j + 1) * z.ax]
        copies = []
        for n in range(count):
            copy = pltpu.make_async_copy(stage.at[n], out_ref.at[low + n], sem.at[n])
            copy.start()
            copies.append(copy)
        for copy in copies:
            copy.wait()

    operands = [me, own] + list(firsts) + ([] if only_first else list(messages))
    in_specs = [spec_smem()] + [spec_vmem()] * (len(operands) - 1)
    aliases = {}
    if has_out:
        aliases = {len(operands): 0}
        operands.append(out)
        in_specs.append(spec_any())
    return call(
        kernel,
        f"finish_{low}",
        f32(z.steps, tall, z.ax),
        in_specs,
        spec_any(),
        [pltpu.VMEM((count, tall, z.ax), F32), pltpu.SemaphoreType.DMA((count,))],
        z.flops * count * z.segments,
        4 * 2 * count * tall * z.ax,
        aliases,
    )(*operands)


def shift_by(array, axis, by):
    size = lax.axis_size(axis)
    return lax.ppermute(array, axis, [(i, (i + by) % size) for i in range(size)])


def neighbours(head, tail):
    size = lax.axis_size("elem")
    left = lax.ppermute(tail, "elem", [(i, i + 1) for i in range(size - 1)])
    right = lax.ppermute(head, "elem", [(i + 1, i) for i in range(size - 1)])
    return left, right


def exchange(z, messages):
    if len(messages) == 1:
        return [lax.all_to_all(messages[0], "elem", 0, 0, tiled=True)]
    order = sorted(range(1, z.segments), key=lambda s: abs(s - z.segments // 2))
    moved = {0: messages[0]}
    for s in order:
        moved[s] = shift_by(messages[s], "elem", s)
    return [moved[s] for s in range(z.segments)]


def chunks_of(steps):
    if steps >= 8:
        return [(1, 2), (2, 5), (5, steps)]
    return [(1, 2), (2, 3), (3, steps)]


def body(state, rhs, to_modal, viscous_op, sweep_gain, inv_blocks):
    segments = lax.axis_size("elem")
    groups = lax.axis_size("blk")
    z = Sizes(state, segments, groups)
    state = state.reshape(segments, z.steps * z.height, z.ax)
    rhs = rhs.reshape(segments, z.steps * z.height, z.ax)
    gain = jnp.transpose(sweep_gain, (1, 0, 2))
    inverse = jnp.transpose(inv_blocks, (1, 0, 2))
    here = lax.axis_index("elem").astype(jnp.int32)
    me = here.reshape(1)
    places = jnp.stack([here, lax.axis_index("blk").astype(jnp.int32)])
    sensors, lefts, rights = {}, {}, {}

    def sense(low, high, after):
        sensor, head, tail = sensor_call(z, state, to_modal, after, low, high)
        left, right = neighbours(head, tail)
        for i in range(low, high):
            sensors[i], lefts[i], rights[i] = (sensor, i - low), (left, i - low), (right, i - low)

    def sweep(chunk, whole, ring, carry, after):
        return sweep_call(
            z, chunk, whole, me, state, rhs, viscous_op, gain, inverse, sensors, lefts, rights, ring, carry, after
        )

    one, two, three = chunks_of(z.steps)
    sense(0, 3, [])
    messages_one, (carry,) = sweep(one, False, None, None, [])
    sense(3, z.steps, [carry])
    last, place = sensors[z.steps - 1]
    ring = [
        shift_by(last[place, segments - 1 :], "blk", 1),
        shift_by(sensors[0][0][0, :1], "blk", -1),
    ]
    messages_two, (carry,) = sweep(two, True, None, carry, [])
    received_one = exchange(z, messages_one)
    own, tails, wholes, prefix, group = maps_call(z, me, gain, [carry])
    messages_three, (carry, starts) = sweep(three, True, ring, carry, received_one[1:])
    before, pack = chain_call(z, starts, carry, tails, wholes, group)
    packs = [pack] + [shift_by(pack, "blk", s) for s in range(1, groups)]
    firsts, held = first_call(z, places, packs, before, prefix, gain, starts, messages_three[0])
    received_two = exchange(z, messages_two)
    firsts = exchange(z, firsts)
    received_three = exchange(z, [held])
    out = finish_call(z, (0, 1), me, own, firsts, None, None)
    for chunk, messages in ((one, received_one), (two, received_two), (three, received_three)):
        out = finish_call(z, chunk, me, own, firsts, messages, out)
    return out.reshape(z.steps, z.nodes, segments * z.rows, z.ax)


def solution(mesh):
    in_specs = (
        P("blk", None, "elem", None),
        P("blk", None, "elem", None),
        P(),
        P(),
        P("blk", None, None),
        P("blk", None, None),
    )
    out_specs = P(("blk", "elem"), None, None, None)
    return jax.shard_map(body, mesh=mesh, in_specs=in_specs, out_specs=out_specs, check_vma=False)
```

time: 545 us -> 326 us (0.60)
  local copies, waits for them, and re-layouts: 198 us -> 44.4 us
  blocking collectives: 144 us -> 0 us
  waiting for transfers between devices: 40.9 us -> 176 us
  matrix products: 123 us -> 0 us
  Pallas kernels: 0 us -> 67.2 us
  starting transfers between devices: 14.8 us -> 36.1 us
  other arithmetic: 16 us -> 0.07 us
    all_gather x1 -> x0, blocking collectives: 144 us -> none  [body(): incoming_all = lax.all_gather(incoming, 'elem', axis=1, tiled=True)]
    dynamic_slice x192 -> x0, local copies, waits for them, and re-layouts: 135 us -> none  [body(): lax.scan(local_step, (identity, zero_field), (sweep_gain, coupled))]
    ppermute x12 -> x23, waiting for transfers between devices: 40.9 us -> 176 us  [the longest x19 170 us: shift_by(): lax.ppermute(array, axis, [(i, (i + by) % size) for i in range(size)])]
    dot_general x140 -> x0, matrix products: 123 us -> none  [the longest x64 53.2 us: local_step(): product = jnp.dot(matrix, product, precision=highest)]
    pallas_call x0 -> x12, Pallas kernels: none -> 67.2 us  [the longest x3 27 us: sweep_call(): call(kernel, f'sweep_{low}', outs, in_specs, out_specs, scratch, z.flops...]
    dynamic_update_slice x64 -> x0, local copies, waits for them, and re-layouts: 48.4 us -> none  [body(): lax.scan(local_step, (identity, zero_field), (sweep_gain, coupled))]
    unnamed x10 -> x130, local copies, waits for them, and re-layouts: 0.85 us -> 44.4 us
    ppermute x12 -> x23, starting transfers between devices: 9.91 us -> 25.4 us  [the longest x19 15.4 us: shift_by(): lax.ppermute(array, axis, [(i, (i + by) % size) for i in range(size)])]
  transfers between devices with their start and end apart: 13 -> 25, of which waited for: 8 -> 13; matrix products, arithmetic and copies ran while one was open for 2% -> 0% of each run, Pallas kernels for 0% -> 12%
where the time goes in v1:
time: 326 us; the launch traced here: 325 us
  waiting for transfers between devices  176 us (54%)
  Pallas kernels  67.2 us (21%)
  local copies, waits for them, and re-layouts  44.4 us (14%)
  starting transfers between devices  36.1 us (11%)
    ppermute x19, waiting for transfers between devices, shift_by(): lax.ppermute(array, axis, [(i, (i + by) % size) for i in range(size)])  170 us
    unnamed x130, local copies, waits for them, and re-layouts  44.4 us
    pallas_call x3, Pallas kernels, sweep_call(): call(kernel, f'sweep_{low}', outs, in_specs, out_specs, scratch, z.flops...  27 us
    ppermute x19, starting transfers between devices, shift_by(): lax.ppermute(array, axis, [(i, (i + by) % size) for i in range(size)])  15.4 us
    pallas_call x1, Pallas kernels, maps_call(): call(kernel, 'maps', outs, [spec_smem(), spec_vmem()] + [spec_any()] * le...  13.4 us
    pallas_call x4, Pallas kernels, finish_call(): call(kernel, f'finish_{low}', f32(z.steps, tall, z.ax), in_specs, spec_an...  12 us
    all_to_all x2, starting transfers between devices, exchange(): return [lax.all_to_all(messages[0], 'elem', 0, 0, tiled=True)]  10.8 us
    pallas_call x2, Pallas kernels, sensor_call(): call(kernel, f'sensor_{low}', outs, [spec_any(), spec_vmem()] + [spec_any...  8.83 us
  transfers between devices with their start and end apart: 25, of which 13 were waited for; matrix products, arithmetic and copies ran while one was open for 0% of the time, Pallas kernels for 12%

profile of v1, /device:TPU:9, one launch (start us, length us, event | category | flops | bytes accessed | tf_op | source)
XLA Modules:
  0.0 324.7 jit_solution(11099396682773362639)
XLA Ops:
  0.0 3.3 %copy-done = f32[64,125,2,128]{3,2,1,0:T(2,128)S(1)} copy-done((f32[64,125,2,128]{3,2,1,0:T(2,128)S(1)}, f32[64,125,2,128]{3,2,1,0:T(2,128)}, u32[]{:S(2)}) %copy-start) | copy-done | bytes 8192024
  3.3 0.8 copy-done.50
  4.2 4.0 %sensor_0.1 = (f32[3,8,256]{2,1,0:T(8,128)S(1)}, f32[3,8,128]{2,1,0:T(8,128)S(1)}, f32[3,8,128]{2,1,0:T(8,128)S(1)}) custom-call(f32[8,2000,128]{2,1,0:T(8,128)S(1)} %bitcast.13, f32[125,125]{1,0:T(8,128)S(1)} %copy-done.50), custom_call_target="tpu_custom_call" | custom-call | flops 805306368 | bytes 3080192 | tf_op jit(solution)/shard_map/sensor_0/pallas_call | solution.py:147
  8.2 3.8 %collective-permute-start = (f32[3,8,128]{2,1,0:T(8,128)S(1)}, f32[3,8,128]{2,1,0:T(8,128)S(1)}, u32[]{:S(2)}, u32[]{:S(2)}) collective-permute-start(f32[3,8,128]{2,1,0:T(8,128)S(1)} %get-tuple-element.42), channel_id=1, source_target_pairs={{0,1},{1,2},{2,3},{3,4},{4,5},{5,6},{6,7},{8,9},{9,10},{10,11},{11... | collective-permute-start | bytes 36872 | tf_op jit(solution)/shard_map/ppermute | solution.py:496
  12.0 1.9 collective-permute-start.1
  13.9 3.1 collective-permute-done.1.refs_7_.refs_9_.refs_11_
  17.0 3.3 %copy-done.1 = f32[64,125,2,128]{3,2,1,0:T(2,128)S(1)} copy-done((f32[64,125,2,128]{3,2,1,0:T(2,128)S(1)}, f32[64,125,2,128]{3,2,1,0:T(2,128)}, u32[]{:S(2)}) %copy-start.1) | copy-done | bytes 8192024
  20.3 2.2 copy-done.6
  22.5 5.1 %sweep_1.1 = (f32[256,128]{1,0:T(8,128)S(1)}, f32[256,128]{1,0:T(8,128)S(1)}, f32[256,128]{1,0:T(8,128)S(1)}, f32[256,128]{1,0:T(8,128)S(1)}, f32[256,128]{1,0:T...) custom-call(s32[1]{0:T(128)} %bitcast.refs_0_.me_ref, ...), custom_call_target="tpu_custom_call" | custom-call | flops 805306368 | bytes 4194304 | tf_op jit(solution)/shard_map/sweep_1/pallas_call | solution.py:307
  28.9 4.8 %sensor_3.1 = (f32[5,8,256]{2,1,0:T(8,128)S(1)}, f32[5,8,128]{2,1,0:T(8,128)S(1)}, f32[5,8,128]{2,1,0:T(8,128)S(1)}) custom-call(f32[8,2000,128]{2,1,0:T(8,128)S(1)} %bitcast.15, f32[125,125]{1,0:T(8,128)S(1)} %copy-done.51, f32[8,128,256]{2,1,0:T(8,128)S(1)} %get-tuple-element.44.refs_0_.refs_12_), custom_call_target="tpu_custom_call" | custom-call | flops 1342177280 | bytes 5144576 | tf_op jit(solution)/shard_map/sensor_3/pallas_call | solution.py:147
  33.8 1.9 collective-permute-start.2
  35.7 2.4 collective-permute-start.3
  38.1 2.7 collective-permute-done.3.refs_11_.refs_8_
  40.8 9.1 %sweep_2.1 = (f32[8,752,128]{2,1,0:T(8,128)S(1)}, f32[8,128,256]{2,1,0:T(8,128)S(1)}) custom-call(s32[1]{0:T(128)} %bitcast.refs_0_.me_ref, f32[8,2000,128]{2,1,0:T(8,128)} %bitcast.11, f32[8,2000,128]{2,1,0:T(8,128)} %bitcast.24, f32[125,125]{1,0:T(8,128)S(1)} %copy-done.33, f32[125,64,125]{2,1,0:T(8,128)S(1)} %bitcast.21, f32[125,64,125]{2,1,0:T(8,128)S(1)} %bitcast.16, ...), custom_call_target="tpu_custom_call" | custom-call | flops 2415919104 | bytes 12451840 | tf_op jit(solution)/shard_map/sweep_2/pallas_call | solution.py:307
  49.9 1.0 copy-done.15
  50.9 1.7 copy-done.20
  52.6 4.1 %all-to-all-start.1 = ((f32[8,752,128]{2,1,0:T(8,128)}), f32[8,752,128]{2,1,0:T(8,128)S(1)}, u32[]{:S(2)}, u32[]{:S(2)}) async-start(f32[8,752,128]{2,1,0:T(8,128)} %copy-done.20), calls=%async_computation.1 | async-start | bytes 6160384 | tf_op jit(solution)/shard_map/all_to_all | solution.py:503
  56.6 2.2 collective-permute-start.5
  58.8 1.7 collective-permute-start.6
  60.5 1.2 collective-permute-start.7
  61.7 1.5 collective-permute-start.9
  63.2 2.1 collective-permute-done.4.refs_12_
  65.6 71.7 %collective-permute-done.6.refs_15_.refs_11_ = f32[256,128]{1,0:T(8,128)S(1)} collective-permute-done((f32[256,128]{1,0:T(8,128)}, f32[256,128]{1,0:T(8,128)S(1)}, u32[]{:S(2)}, u32[]{:S(2)}) %collective-permute-start.6) | collective-permute-done | bytes 131104 | tf_op jit(solution)/shard_map/ppermute | solution.py:491
  137.3 2.8 collective-permute-done.7.refs_16_.refs_12_
  140.1 2.2 copy-done.3
  142.3 1.2 copy-done.16
  143.5 13.4 %maps.1 = (f32[8,128,128]{2,1,0:T(8,128)S(1)}, f32[8,128,128]{2,1,0:T(8,128)S(1)}, f32[8,128,128]{2,1,0:T(8,128)S(1)}, f32[8,128,128]{2,1,0:T(8,128)S(1)}, f32[128,128]{1,0:T(8,128)S(1)}) custom-call(s32[1]{0:T(128)} %bitcast.refs_0_.me_ref, f32[125,64,125]{2,1,0:T(8,128)S(1)} %bitcast.17, f32[8,128,256]{2,1,0:T(8,128)S(1)} %copy-done.16), custom_call_target="tpu_custom_call" | custom-call | flops 1207959552 | bytes 4194304 | tf_op jit(solution)/shard_map/maps/pallas_call | solution.py:351
  158.7 2.3 copy-done.8
  160.9 12.8 %sweep_5.1 = (f32[8,752,128]{2,1,0:T(8,128)S(1)}, f32[8,128,256]{2,1,0:T(8,128)S(1)}, f32[8,128,256]{2,1,0:T(8,128)S(1)}) custom-call(s32[1]{0:T(128)} %bitcast.refs_0_.me_ref, f32[8,2000,128]{2,1,0:T(8,128)} %bitcast.12, f32[8,2000,128]{2,1,0:T(8,128)} %bitcast.25, f32[125,125]{1,0:T(8,128)S(1)} %copy-done.33, f32[125,64,125]{2,1,0:T(8,128)S(1)} %bitcast.22, ...), custom_call_target="tpu_custom_call" | custom-call | flops 3221225472 | bytes 12320768 | tf_op jit(solution)/shard_map/sweep_5/pallas_call | solution.py:307
  173.8 1.6 copy-done.9
  175.5 1.7 chain.1
  177.2 1.0 copy-done.18
  178.2 1.0 copy-done.31
  179.2 2.2 collective-permute-start.15
  182.0 4.2 %collective-permute-done.15.refs_4_ = f32[128,384]{1,0:T(8,128)} collective-permute-done((f32[128,384]{1,0:T(8,128)S(1)}, f32[128,384]{1,0:T(8,128)}, u32[]{:S(2)}, u32[]{:S(2)}) %collective-permute-start.15) | collective-permute-done | bytes 196640 | tf_op jit(solution)/shard_map/ppermute | solution.py:491
  186.2 4.6 %collective-permute-done.14.refs_3_ = f32[128,384]{1,0:T(8,128)} collective-permute-done((f32[128,384]{1,0:T(8,128)S(1)}, f32[128,384]{1,0:T(8,128)}, u32[]{:S(2)}, u32[]{:S(2)}) %collective-permute-start.14) | collective-permute-done | bytes 196640 | tf_op jit(solution)/shard_map/ppermute | solution.py:491
  190.7 2.2 copy-done.5
  192.9 1.9 copy-done.10
  194.8 1.2 copy-done.19
  196.0 1.2 copy-done.32
  197.2 1.0 copy-done.49
  198.3 4.2 %first.1 = (f32[256,128]{1,0:T(8,128)S(1)}, f32[256,128]{1,0:T(8,128)}, f32[256,128]{1,0:T(8,128)S(1)}, f32[256,128]{1,0:T(8,128)S(1)}, f32[256,128]{1,0:T(8,128...) custom-call(s32[2]{0:T(128)S(1)} %pad_add_fusion.refs_0_, ...), custom_call_target="tpu_custom_call", output_to_operand_aliasing={{8}: (9, {})} | custom-call | flops 805306368 | bytes 4194304 | tf_op jit(solution)/shard_map/first/pallas_call | solution.py:413
  202.5 1.7 copy-done.11
  208.0 6.7 %all-to-all-start = ((f32[8,752,128]{2,1,0:T(8,128)}), f32[8,752,128]{2,1,0:T(8,128)}, u32[]{:S(2)}, u32[]{:S(2)}) async-start(f32[8,752,128]{2,1,0:T(8,128)} %copy-done.11), calls=%async_computation | async-start | bytes 6160384 | tf_op jit(solution)/shard_map/all_to_all | solution.py:503
  214.8 1.7 collective-permute-start.16
  216.5 0.9 collective-permute-start.17
  217.6 1.6 collective-permute-start.19
  219.2 1.4 collective-permute-start.20
  220.6 74.8 %collective-permute-done.16.refs_3_ = f32[256,128]{1,0:T(8,128)S(1)} collective-permute-done((f32[256,128]{1,0:T(8,128)}, f32[256,128]{1,0:T(8,128)S(1)}, u32[]{:S(2)}, u32[]{:S(2)}) %collective-permute-start.16) | collective-permute-done | bytes 131104 | tf_op jit(solution)/shard_map/ppermute | solution.py:491
  295.4 2.8 collective-permute-done.17.refs_4_
  298.2 2.8 collective-permute-done.18.refs_5_
  301.0 2.8 collective-permute-done.19.refs_6_
  303.8 1.2 collective-permute-done.21.refs_8_
  305.6 1.1 copy-done.13
  306.8 1.5 finish_0.1.refs_18_
  308.4 1.7 finish_1.1.refs_11_
  310.1 3.5 %finish_2.1.refs_11_ = f32[8,2000,128]{2,1,0:T(8,128)} custom-call(s32[1]{0:T(128)} %bitcast.refs_0_.me_ref, f32[8,128,128]{2,1,0:T(8,128)S(1)} %copy-done.13, f32[256,128]{1,0:T(8,128)S(1)} %get-tuple-element.66.refs_2_, f32[256,128]{1,0:T(8,128)S(1)} %collective-permute-done.16.refs_3_, ...), custom_call_target="tpu_custom_call", output_to_operand_aliasing={{}: (11, {})} | custom-call | flops 805306368 | bytes 6144000 | tf_op jit(solution)/shard_map/finish_2/pallas_call | solution.py:476
  313.6 1.0 copy-done.14
  314.7 0.9 copy-done.22
  315.6 0.9 copy-done.24
  316.5 0.9 copy-done.26
  317.4 0.9 copy-done.28
  318.3 0.9 copy-done.30
  319.2 5.4 %finish_5.1 = f32[8,2000,128]{2,1,0:T(8,128)} custom-call(s32[1]{0:T(128)} %bitcast.refs_0_.me_ref, f32[8,128,128]{2,1,0:T(8,128)S(1)} %copy-done.14, f32[256,128]{1,0:T(8,128)S(1)} %get-tuple-element.66.refs_2_, f32[256,128]{1,0:T(8,128)S(1)} %collective-permute-done.16.refs_3_, ...), custom_call_target="tpu_custom_call", output_to_operand_aliasing={{}: (11, {})} | custom-call | flops 805306368 | bytes 6144000 | tf_op jit(solution)/shard_map/finish_5/pallas_call | solution.py:476
  (131 shorter events, 8.8 us)
Async XLA Ops:
  0.0 3.3 %copy-start = (f32[64,125,2,128]{3,2,1,0:T(2,128)S(1)}, f32[64,125,2,128]{3,2,1,0:T(2,128)}, u32[]{:S(2)}) copy-start(f32[64,125,2,128]{3,2,1,0:T(2,128)} %param.6) | copy-start | bytes 24576004
  4.2 12.8 %copy-start.33 = (f32[125,125]{1,0:T(8,128)S(1)}, f32[125,125]{1,0:T(8,128)}, u32[]{:S(2)}) copy-start(f32[125,125]{1,0:T(8,128)} %refs_3_.5) | copy-start | bytes 187504
  8.2 5.7 %collective-permute-start = (f32[3,8,128]{2,1,0:T(8,128)S(1)}, f32[3,8,128]{2,1,0:T(8,128)S(1)}, u32[]{:S(2)}, u32[]{:S(2)}) collective-permute-start(f32[3,8,128]{2,1,0:T(8,128)S(1)} %get-tuple-element.42), channel_id=1, source_target_pairs={{0,1},{1,2},{2,3},{3,4},{4,5},{5,6},{6,7},{8,9},{9,10},{10,11},{11... | collective-permute-start | bytes 36872 | tf_op jit(solution)/shard_map/ppermute | solution.py:496
  12.0 5.0 %collective-permute-start.1 = (f32[3,8,128]{2,1,0:T(8,128)S(1)}, f32[3,8,128]{2,1,0:T(8,128)S(1)}, u32[]{:S(2)}, u32[]{:S(2)}) collective-permute-start(f32[3,8,128]{2,1,0:T(8,128)S(1)} %get-tuple-element.43), channel_id=1, source_target_pairs={{1,0},{2,1},{3,2},{4,3},{5,4},{6,5},{7,6},{9,8},{10,9},{11,10},{12... | collective-permute-start | bytes 36872 | tf_op jit(solution)/shard_map/ppermute | solution.py:497
  17.0 3.3 %copy-start.1 = (f32[64,125,2,128]{3,2,1,0:T(2,128)S(1)}, f32[64,125,2,128]{3,2,1,0:T(2,128)}, u32[]{:S(2)}) copy-start(f32[64,125,2,128]{3,2,1,0:T(2,128)} %param.6) | copy-start | bytes 24576004
  20.3 2.2 copy-start.6
  22.5 6.4 %copy-start.51 = (f32[125,125]{1,0:T(8,128)S(1)}, f32[125,125]{1,0:T(8,128)}, u32[]{:S(2)}) copy-start(f32[125,125]{1,0:T(8,128)} %modal_ref.3) | copy-start | bytes 187504
  28.9 4.8 %copy-start.54 = (f32[256,128]{1,0:T(8,128)}, f32[256,128]{1,0:T(8,128)S(1)}, u32[]{:S(2)}) copy-start(f32[256,128]{1,0:T(8,128)S(1)} %get-tuple-element.54) | copy-start | bytes 393220
  28.9 4.8 %copy-start.55 = (f32[256,128]{1,0:T(8,128)}, f32[256,128]{1,0:T(8,128)S(1)}, u32[]{:S(2)}) copy-start(f32[256,128]{1,0:T(8,128)S(1)} %get-tuple-element.53) | copy-start | bytes 393220
  28.9 4.9 %copy-start.56 = (f32[256,128]{1,0:T(8,128)}, f32[256,128]{1,0:T(8,128)S(1)}, u32[]{:S(2)}) copy-start(f32[256,128]{1,0:T(8,128)S(1)} %get-tuple-element.52) | copy-start | bytes 393220
  28.9 4.9 %copy-start.57 = (f32[256,128]{1,0:T(8,128)}, f32[256,128]{1,0:T(8,128)S(1)}, u32[]{:S(2)}) copy-start(f32[256,128]{1,0:T(8,128)S(1)} %get-tuple-element.51) | copy-start | bytes 393220
  28.9 11.9 %copy-start.2 = (f32[64,125,125]{2,0,1:T(8,128)S(1)}, f32[64,125,125]{2,0,1:T(8,128)}, u32[]{:S(2)}) copy-start(f32[64,125,125]{2,0,1:T(8,128)} %param.10) | copy-start | bytes 12000004
  28.9 11.9 %copy-start.7 = (f32[64,125,125]{2,0,1:T(8,128)S(1)}, f32[64,125,125]{2,0,1:T(8,128)}, u32[]{:S(2)}) copy-start(f32[64,125,125]{2,0,1:T(8,128)} %param.11) | copy-start | bytes 12000004
  33.8 4.3 %collective-permute-start.2 = (f32[5,8,128]{2,1,0:T(8,128)S(1)}, f32[5,8,128]{2,1,0:T(8,128)S(1)}, u32[]{:S(2)}, u32[]{:S(2)}) collective-permute-start(f32[5,8,128]{2,1,0:T(8,128)S(1)} %get-tuple-element.46), channel_id=1, source_target_pairs={{0,1},{1,2},{2,3},{3,4},{4,5},{5,6},{6,7},{8,9},{9,10},{10,11},{11... | collective-permute-start | bytes 61448 | tf_op jit(solution)/shard_map/ppermute | solution.py:496
  35.7 5.1 %collective-permute-start.3 = (f32[5,8,128]{2,1,0:T(8,128)S(1)}, f32[5,8,128]{2,1,0:T(8,128)S(1)}, u32[]{:S(2)}, u32[]{:S(2)}) collective-permute-start(f32[5,8,128]{2,1,0:T(8,128)S(1)} %get-tuple-element.47), channel_id=1, source_target_pairs={{1,0},{2,1},{3,2},{4,3},{5,4},{6,5},{7,6},{9,8},{10,9},{11,10},{12... | collective-permute-start | bytes 61448 | tf_op jit(solution)/shard_map/ppermute | solution.py:497
  50.9 1.7 copy-start.20
  52.6 155.5 %all-to-all-start.1 = ((f32[8,752,128]{2,1,0:T(8,128)}), f32[8,752,128]{2,1,0:T(8,128)S(1)}, u32[]{:S(2)}, u32[]{:S(2)}) async-start(f32[8,752,128]{2,1,0:T(8,128)} %copy-done.20), calls=%async_computation.1 | async-start | bytes 6160384 | tf_op jit(solution)/shard_map/all_to_all | solution.py:503
  56.6 5.1 %collective-permute-start.5 = (f32[1,256]{1,0:T(1,128)S(1)}, f32[1,256]{1,0:T(1,128)S(1)}, u32[]{:S(2)}, u32[]{:S(2)}) collective-permute-start(f32[1,256]{1,0:T(1,128)S(1)} %slice_bitcast_fusion), channel_id=1, source_target_pairs={{0,24},{8,0},{16,8},{24,16},{1,25},{9,1},{17,9},{25,17},{2,26},{10... | collective-permute-start | bytes 3080 | tf_op jit(solution)/shard_map/ppermute | solution.py:491
  58.8 78.4 %collective-permute-start.6 = (f32[256,128]{1,0:T(8,128)}, f32[256,128]{1,0:T(8,128)S(1)}, u32[]{:S(2)}, u32[]{:S(2)}) collective-permute-start(f32[256,128]{1,0:T(8,128)} %copy-done.58), channel_id=1, source_target_pairs={{0,1},{1,2},{2,3},{3,4},{4,5},{5,6},{6,7},{7,0},{8,9},{9,10},{10,1... | collective-permute-start | bytes 393224 | tf_op jit(solution)/shard_map/ppermute | solution.py:491
  60.5 79.5 %collective-permute-start.7 = (f32[256,128]{1,0:T(8,128)}, f32[256,128]{1,0:T(8,128)S(1)}, u32[]{:S(2)}, u32[]{:S(2)}) collective-permute-start(f32[256,128]{1,0:T(8,128)} %copy-done.57), channel_id=1, source_target_pairs={{0,2},{1,3},{2,4},{3,5},{4,6},{5,7},{6,0},{7,1},{8,10},{9,11},{10,... | collective-permute-start | bytes 393224 | tf_op jit(solution)/shard_map/ppermute | solution.py:491
  61.7 3.6 %collective-permute-start.4 = (f32[1,256]{1,0:T(1,128)S(1)}, f32[1,256]{1,0:T(1,128)S(1)}, u32[]{:S(2)}, u32[]{:S(2)}) collective-permute-start(f32[1,256]{1,0:T(1,128)S(1)} %slice_bitcast_fusion.1), channel_id=1, source_target_pairs={{0,8},{8,16},{16,24},{24,0},{1,9},{9,17},{17,25},{25,1},{2,10},{10... | collective-permute-start | bytes 3080 | tf_op jit(solution)/shard_map/ppermute | solution.py:491
  61.7 96.9 %collective-permute-start.8 = (f32[256,128]{1,0:T(8,128)}, f32[256,128]{1,0:T(8,128)S(1)}, u32[]{:S(2)}, u32[]{:S(2)}) collective-permute-start(f32[256,128]{1,0:T(8,128)} %copy-done.56), channel_id=1, source_target_pairs={{0,3},{1,4},{2,5},{3,6},{4,7},{5,0},{6,1},{7,2},{8,11},{9,12},{10,... | collective-permute-start | bytes 393224 | tf_op jit(solution)/shard_map/ppermute | solution.py:491
  61.7 96.8 %collective-permute-start.9 = (f32[256,128]{1,0:T(8,128)}, f32[256,128]{1,0:T(8,128)S(1)}, u32[]{:S(2)}, u32[]{:S(2)}) collective-permute-start(f32[256,128]{1,0:T(8,128)} %copy-done.55), channel_id=1, source_target_pairs={{0,4},{1,5},{2,6},{3,7},{4,0},{5,1},{6,2},{7,3},{8,12},{9,13},{10,... | collective-permute-start | bytes 393224 | tf_op jit(solution)/shard_map/ppermute | solution.py:491
  65.3 93.3 %collective-permute-start.10 = (f32[256,128]{1,0:T(8,128)}, f32[256,128]{1,0:T(8,128)S(1)}, u32[]{:S(2)}, u32[]{:S(2)}) collective-permute-start(f32[256,128]{1,0:T(8,128)} %copy-done.54), channel_id=1, source_target_pairs={{0,5},{1,6},{2,7},{3,0},{4,1},{5,2},{6,3},{7,4},{8,13},{9,14},{10,... | collective-permute-start | bytes 393224 | tf_op jit(solution)/shard_map/ppermute | solution.py:491
  137.3 36.5 %copy-start.34 = (f32[256,128]{1,0:T(8,128)}, f32[256,128]{1,0:T(8,128)S(1)}, u32[]{:S(2)}) copy-start(f32[256,128]{1,0:T(8,128)S(1)} %collective-permute-done.6.refs_15_.refs_11_) | copy-start | bytes 393220
  137.3 21.3 %collective-permute-start.11 = (f32[256,128]{1,0:T(8,128)S(1)}, f32[256,128]{1,0:T(8,128)S(1)}, u32[]{:S(2)}, u32[]{:S(2)}) collective-permute-start(f32[256,128]{1,0:T(8,128)S(1)} %get-tuple-element.55), channel_id=1, source_target_pairs={{0,6},{1,7},{2,0},{3,1},{4,2},{5,3},{6,4},{7,5},{8,14},{9,15},{10,... | collective-permute-start | bytes 393224 | tf_op jit(solution)/shard_map/ppermute | solution.py:491
  140.1 33.7 %copy-start.36 = (f32[256,128]{1,0:T(8,128)}, f32[256,128]{1,0:T(8,128)S(1)}, u32[]{:S(2)}) copy-start(f32[256,128]{1,0:T(8,128)S(1)} %collective-permute-done.7.refs_16_.refs_12_) | copy-start | bytes 393220
  140.1 18.6 %collective-permute-start.12 = (f32[256,128]{1,0:T(8,128)S(1)}, f32[256,128]{1,0:T(8,128)S(1)}, u32[]{:S(2)}, u32[]{:S(2)}) collective-permute-start(f32[256,128]{1,0:T(8,128)S(1)} %get-tuple-element.56), channel_id=1, source_target_pairs={{0,7},{1,0},{2,1},{3,2},{4,3},{5,4},{6,5},{7,6},{8,15},{9,8},{10,9... | collective-permute-start | bytes 393224 | tf_op jit(solution)/shard_map/ppermute | solution.py:491
  140.1 2.2 copy-start.3
  143.5 15.1 %copy-start.4 = (f32[64,125,125]{2,0,1:T(8,128)S(1)}, f32[64,125,125]{2,0,1:T(8,128)}, u32[]{:S(2)}) copy-start(f32[64,125,125]{2,0,1:T(8,128)} %param.10) | copy-start | bytes 12000004
  143.5 15.1 %copy-start.17 = (f32[8,128,256]{2,1,0:T(8,128)S(1)}, f32[8,128,256]{2,1,0:T(8,128)}, u32[]{:S(2)}) copy-start(f32[8,128,256]{2,1,0:T(8,128)} %copy-done.15) | copy-start | bytes 3145732
  158.6 15.2 %copy-start.38 = (f32[256,128]{1,0:T(8,128)}, f32[256,128]{1,0:T(8,128)S(1)}, u32[]{:S(2)}) copy-start(f32[256,128]{1,0:T(8,128)S(1)} %collective-permute-done.8.refs_17_.refs_13_) | copy-start | bytes 393220
  158.6 15.2 %copy-start.40 = (f32[256,128]{1,0:T(8,128)}, f32[256,128]{1,0:T(8,128)S(1)}, u32[]{:S(2)}) copy-start(f32[256,128]{1,0:T(8,128)S(1)} %collective-permute-done.9.refs_18_.refs_14_) | copy-start | bytes 393220
  158.6 15.2 %copy-start.42 = (f32[256,128]{1,0:T(8,128)}, f32[256,128]{1,0:T(8,128)S(1)}, u32[]{:S(2)}) copy-start(f32[256,128]{1,0:T(8,128)S(1)} %collective-permute-done.10.refs_19_.refs_15_) | copy-start | bytes 393220
  158.6 15.2 %copy-start.44 = (f32[256,128]{1,0:T(8,128)}, f32[256,128]{1,0:T(8,128)S(1)}, u32[]{:S(2)}) copy-start(f32[256,128]{1,0:T(8,128)S(1)} %collective-permute-done.11.refs_20_.refs_16_) | copy-start | bytes 393220
  158.7 2.3 copy-start.8
  160.9 12.9 %copy-start.46 = (f32[256,128]{1,0:T(8,128)}, f32[256,128]{1,0:T(8,128)S(1)}, u32[]{:S(2)}) copy-start(f32[256,128]{1,0:T(8,128)S(1)} %collective-permute-done.12.refs_21_.refs_17_) | copy-start | bytes 393220
  173.8 1.6 copy-start.9
  179.2 7.0 %collective-permute-start.15 = (f32[128,384]{1,0:T(8,128)S(1)}, f32[128,384]{1,0:T(8,128)}, u32[]{:S(2)}, u32[]{:S(2)}) collective-permute-start(f32[128,384]{1,0:T(8,128)S(1)} %get-tuple-element.62.refs_1_), channel_id=1, source_target_pairs={{0,24},{8,0},{16,8},{24,16},{1,25},{9,1},{17,9},{25,17},{2,26},{10... | collective-permute-start | bytes 589832 | tf_op jit(solution)/shard_map/ppermute | solution.py:491
  181.4 9.4 %collective-permute-start.14 = (f32[128,384]{1,0:T(8,128)S(1)}, f32[128,384]{1,0:T(8,128)}, u32[]{:S(2)}, u32[]{:S(2)}) collective-permute-start(f32[128,384]{1,0:T(8,128)S(1)} %get-tuple-element.62.refs_1_), channel_id=1, source_target_pairs={{0,16},{8,24},{16,0},{24,8},{1,17},{9,25},{17,1},{25,9},{2,18},{10... | collective-permute-start | bytes 589832 | tf_op jit(solution)/shard_map/ppermute | solution.py:491
  181.6 9.2 %collective-permute-start.13 = (f32[128,384]{1,0:T(8,128)S(1)}, f32[128,384]{1,0:T(8,128)}, u32[]{:S(2)}, u32[]{:S(2)}) collective-permute-start(f32[128,384]{1,0:T(8,128)S(1)} %get-tuple-element.62.refs_1_), channel_id=1, source_target_pairs={{0,8},{8,16},{16,24},{24,0},{1,9},{9,17},{17,25},{25,1},{2,10},{10... | collective-permute-start | bytes 589832 | tf_op jit(solution)/shard_map/ppermute | solution.py:491
  190.7 2.2 copy-start.5
  192.9 1.9 copy-start.10
  202.5 1.7 copy-start.11
  208.0 105.6 %all-to-all-start = ((f32[8,752,128]{2,1,0:T(8,128)}), f32[8,752,128]{2,1,0:T(8,128)}, u32[]{:S(2)}, u32[]{:S(2)}) async-start(f32[8,752,128]{2,1,0:T(8,128)} %copy-done.11), calls=%async_computation | async-start | bytes 6160384 | tf_op jit(solution)/shard_map/all_to_all | solution.py:503
  214.8 80.6 %collective-permute-start.16 = (f32[256,128]{1,0:T(8,128)}, f32[256,128]{1,0:T(8,128)S(1)}, u32[]{:S(2)}, u32[]{:S(2)}) collective-permute-start(f32[256,128]{1,0:T(8,128)} %get-tuple-element.67), channel_id=1, source_target_pairs={{0,1},{1,2},{2,3},{3,4},{4,5},{5,6},{6,7},{7,0},{8,9},{9,10},{10,1... | collective-permute-start | bytes 393224 | tf_op jit(solution)/shard_map/ppermute | solution.py:491
  216.5 81.7 %collective-permute-start.17 = (f32[256,128]{1,0:T(8,128)}, f32[256,128]{1,0:T(8,128)S(1)}, u32[]{:S(2)}, u32[]{:S(2)}) collective-permute-start(f32[256,128]{1,0:T(8,128)} %copy-done.64), channel_id=1, source_target_pairs={{0,2},{1,3},{2,4},{3,5},{4,6},{5,7},{6,0},{7,1},{8,10},{9,11},{10,... | collective-permute-start | bytes 393224 | tf_op jit(solution)/shard_map/ppermute | solution.py:491
  217.4 83.6 %collective-permute-start.18 = (f32[256,128]{1,0:T(8,128)}, f32[256,128]{1,0:T(8,128)S(1)}, u32[]{:S(2)}, u32[]{:S(2)}) collective-permute-start(f32[256,128]{1,0:T(8,128)} %copy-done.63), channel_id=1, source_target_pairs={{0,3},{1,4},{2,5},{3,6},{4,7},{5,0},{6,1},{7,2},{8,11},{9,12},{10,... | collective-permute-start | bytes 393224 | tf_op jit(solution)/shard_map/ppermute | solution.py:491
  217.6 86.2 %collective-permute-start.19 = (f32[256,128]{1,0:T(8,128)}, f32[256,128]{1,0:T(8,128)S(1)}, u32[]{:S(2)}, u32[]{:S(2)}) collective-permute-start(f32[256,128]{1,0:T(8,128)} %copy-done.62), channel_id=1, source_target_pairs={{0,4},{1,5},{2,6},{3,7},{4,0},{5,1},{6,2},{7,3},{8,12},{9,13},{10,... | collective-permute-start | bytes 393224 | tf_op jit(solution)/shard_map/ppermute | solution.py:491
  219.2 84.6 %collective-permute-start.20 = (f32[256,128]{1,0:T(8,128)}, f32[256,128]{1,0:T(8,128)S(1)}, u32[]{:S(2)}, u32[]{:S(2)}) collective-permute-start(f32[256,128]{1,0:T(8,128)} %copy-done.61), channel_id=1, source_target_pairs={{0,5},{1,6},{2,7},{3,0},{4,1},{5,2},{6,3},{7,4},{8,13},{9,14},{10,... | collective-permute-start | bytes 393224 | tf_op jit(solution)/shard_map/ppermute | solution.py:491
  295.4 9.6 %collective-permute-start.21 = (f32[256,128]{1,0:T(8,128)}, f32[256,128]{1,0:T(8,128)S(1)}, u32[]{:S(2)}, u32[]{:S(2)}) collective-permute-start(f32[256,128]{1,0:T(8,128)} %copy-done.60), channel_id=1, source_target_pairs={{0,6},{1,7},{2,0},{3,1},{4,2},{5,3},{6,4},{7,5},{8,14},{9,15},{10,... | collective-permute-start | bytes 393224 | tf_op jit(solution)/shard_map/ppermute | solution.py:491
  298.2 7.4 %collective-permute-start.22 = (f32[256,128]{1,0:T(8,128)}, f32[256,128]{1,0:T(8,128)S(1)}, u32[]{:S(2)}, u32[]{:S(2)}) collective-permute-start(f32[256,128]{1,0:T(8,128)} %copy-done.59), channel_id=1, source_target_pairs={{0,7},{1,0},{2,1},{3,2},{4,3},{5,4},{6,5},{7,6},{8,15},{9,8},{10,9... | collective-permute-start | bytes 393224 | tf_op jit(solution)/shard_map/ppermute | solution.py:491
  301.0 9.1 %copy-start.21 = (f32[256,128]{1,0:T(8,128)}, f32[256,128]{1,0:T(8,128)S(1)}, u32[]{:S(2)}) copy-start(f32[256,128]{1,0:T(8,128)S(1)} %collective-permute-done.18.refs_5_) | copy-start | bytes 393220
  303.8 6.3 %copy-start.23 = (f32[256,128]{1,0:T(8,128)}, f32[256,128]{1,0:T(8,128)S(1)}, u32[]{:S(2)}) copy-start(f32[256,128]{1,0:T(8,128)S(1)} %collective-permute-done.19.refs_6_) | copy-start | bytes 393220
  303.8 6.3 %copy-start.25 = (f32[256,128]{1,0:T(8,128)}, f32[256,128]{1,0:T(8,128)S(1)}, u32[]{:S(2)}) copy-start(f32[256,128]{1,0:T(8,128)S(1)} %collective-permute-done.20.refs_7_) | copy-start | bytes 393220
  305.0 5.1 %copy-start.27 = (f32[256,128]{1,0:T(8,128)}, f32[256,128]{1,0:T(8,128)S(1)}, u32[]{:S(2)}) copy-start(f32[256,128]{1,0:T(8,128)S(1)} %collective-permute-done.21.refs_8_) | copy-start | bytes 393220
  305.6 4.5 %copy-start.29 = (f32[256,128]{1,0:T(8,128)}, f32[256,128]{1,0:T(8,128)S(1)}, u32[]{:S(2)}) copy-start(f32[256,128]{1,0:T(8,128)S(1)} %collective-permute-done.22.refs_9_) | copy-start | bytes 393220
  306.7 1.6 copy-start.37
  306.7 1.6 copy-start.39
  306.7 1.6 copy-start.41
  306.7 1.6 copy-start.43
  306.7 1.6 copy-start.45
  306.7 1.6 copy-start.47
  306.8 1.6 copy-start.53
  (26 other events, 23.6 us)

commit v2 on v1

--- a/solution.py
+++ b/solution.py
@@ -10,7 +10,7 @@
 ORDER = 4
 F32 = jnp.float32
 BF16 = jnp.bfloat16
-VMEM_LIMIT = 36 * 1024 * 1024
+MIB = 1024 * 1024
 TILE = 8
 LANES = 128
 
@@ -36,6 +36,10 @@
     return pl.BlockSpec(memory_space=pl.ANY)
 
 
+def spec_hbm():
+    return pl.BlockSpec(memory_space=pltpu.HBM)
+
+
 def spec_vmem():
     return pl.BlockSpec(memory_space=pltpu.VMEM)
 
@@ -44,7 +48,7 @@
     return pl.BlockSpec(memory_space=pltpu.SMEM)
 
 
-def call(kernel, name, outs, in_specs, out_specs, scratch, flops, nbytes, aliases=None):
+def call(kernel, name, outs, in_specs, out_specs, scratch, flops, nbytes, aliases=None, limit=24):
     return pl.pallas_call(
         kernel,
         name=name,
@@ -53,7 +57,7 @@
         out_specs=out_specs,
         scratch_shapes=scratch,
         input_output_aliases=aliases or {},
-        compiler_params=pltpu.CompilerParams(vmem_limit_bytes=VMEM_LIMIT),
+        compiler_params=pltpu.CompilerParams(vmem_limit_bytes=limit * MIB),
         cost_estimate=pl.CostEstimate(flops=int(flops), bytes_accessed=int(nbytes), transcendentals=0),
     )
 
@@ -148,11 +152,12 @@
         kernel,
         f"sensor_{low}",
         outs,
-        [spec_any(), spec_vmem()] + [spec_any()] * len(after),
+        [spec_hbm(), spec_vmem()] + [spec_any()] * len(after),
         [spec_vmem()] * 3,
         [pltpu.VMEM((z.segments, size + z.spill, z.ax), F32), pltpu.SemaphoreType.DMA((z.segments,))],
         z.flops * count * z.segments,
         4 * z.segments * size * z.ax,
+        limit=56,
     )(state, to_modal, *after)
 
 
@@ -164,7 +169,7 @@
     return (4.0 * sensor + before + after + from_left + from_right) / 8.0
 
 
-def sweep_call(z, chunk, whole, me, state, rhs, viscous, gain, inverse, sensors, lefts, rights, ring, carry, after):
+def sweep_call(z, chunk, state, rhs, viscous, gain, inverse, sensors, lefts, rights, ring, carry, after):
     low, high = chunk
     with_first = high == z.steps
     first, size = z.window(low, high)
@@ -192,37 +197,34 @@
     small = len(arrays)
     has_carry = carry is not None
     needs_gain = has_carry or count > 1
-    sent = 1 if whole else z.segments
     message = z.message(count)
 
     def kernel(*refs):
-        me_ref, state_ref, rhs_ref, viscous_ref, inverse_ref = refs[:5]
-        refs = refs[5:]
+        state_ref, rhs_ref, viscous_ref, inverse_ref = refs[:4]
+        refs = refs[4:]
         if needs_gain:
             gain_ref, refs = refs[0], refs[1:]
         small_refs, refs = refs[:small], refs[small:]
         if has_carry:
             carry_ref, refs = refs[0], refs[1:]
         refs = refs[len(after) :]
-        out_refs, refs = refs[:sent], refs[sent:]
+        out_ref, refs = refs[0], refs[1:]
         end_ref, refs = refs[0], refs[1:]
         if with_first:
             start_ref, refs = refs[0], refs[1:]
         state_buf, rhs_buf, smooth_buf, stage, sem, out_sem = refs[:6]
         if with_first:
             state0, rhs0 = refs[6:]
-        mine = me_ref[0]
         batch = 4 if z.segments % 4 == 0 else 1
-        places = [e if whole else lax.rem(mine + e, z.segments) for e in range(z.segments)]
         copies = []
-        for s, e in enumerate(places):
+        for s in range(z.segments):
             moves = [
-                (state_ref.at[e, pl.ds(first, size)], state_buf.at[s, pl.ds(0, size)]),
-                (rhs_ref.at[e, pl.ds(first, size)], rhs_buf.at[s, pl.ds(0, size)]),
+                (state_ref.at[s, pl.ds(first, size)], state_buf.at[s, pl.ds(0, size)]),
+                (rhs_ref.at[s, pl.ds(first, size)], rhs_buf.at[s, pl.ds(0, size)]),
             ]
             if with_first:
-                moves.append((state_ref.at[e, pl.ds(first0, size0)], state0.at[s, pl.ds(0, size0)]))
-                moves.append((rhs_ref.at[e, pl.ds(first0, size0)], rhs0.at[s, pl.ds(0, size0)]))
+                moves.append((state_ref.at[s, pl.ds(first0, size0)], state0.at[s, pl.ds(0, size0)]))
+                moves.append((rhs_ref.at[s, pl.ds(first0, size0)], rhs0.at[s, pl.ds(0, size0)]))
             started = []
             for n, (source, target) in enumerate(moves):
                 copy = pltpu.make_async_copy(source, target, sem.at[s, n])
@@ -251,12 +253,12 @@
             for s in group:
                 for copy in copies[s]:
                     copy.wait()
-            fields = [carry_ref[places[s]] if has_carry else None for s in group]
+            fields = [carry_ref[s] if has_carry else None for s in group]
             for n in range(count):
                 offset = (low + n) * z.height - first
                 for g, s in enumerate(group):
-                    k = places[s] * z.steps + low + n
-                    smooth = smooth_buf[n, pl.ds(places[s], 1), :]
+                    k = s * z.steps + low + n
+                    smooth = smooth_buf[n, s : s + 1, :]
                     value = source(
                         read_field(z, state_buf, (s,), offset),
                         read_field(z, rhs_buf, (s,), offset),
@@ -270,30 +272,28 @@
                     fields[g] = value
                     write_field(z, stage, (s,), n * z.height, value)
             for g, s in enumerate(group):
-                target = out_refs[0].at[s] if whole else out_refs[s]
-                copy = pltpu.make_async_copy(stage.at[s], target, out_sem.at[s])
+                copy = pltpu.make_async_copy(stage.at[s], out_ref.at[s], out_sem.at[s])
                 copy.start()
                 sends.append(copy)
-                end_ref[places[s]] = fields[g]
+                end_ref[s] = fields[g]
                 if with_first:
-                    smooth = smooth_buf[count, pl.ds(places[s], 1), :]
-                    start_ref[places[s]] = source(
+                    smooth = smooth_buf[count, s : s + 1, :]
+                    start_ref[s] = source(
                         read_field(z, state0, (s,), -first0),
                         read_field(z, rhs0, (s,), -first0),
-                        read_matrix(z, inverse_ref, places[s] * z.steps),
+                        read_matrix(z, inverse_ref, s * z.steps),
                         smooth,
                     )
         for copy in sends:
             copy.wait()
 
     field = f32(z.segments, z.pad, z.cols)
-    outs = [f32(z.segments, message, z.ax)] if whole else [f32(message, z.ax) for _ in range(z.segments)]
-    outs += [field] * (2 if with_first else 1)
-    operands = [me, state, rhs, viscous, inverse] + ([gain] if needs_gain else [])
-    in_specs = [spec_smem(), spec_any(), spec_any()] + [spec_vmem()] * (len(operands) - 3)
+    outs = [f32(z.segments, message, z.ax)] + [field] * (2 if with_first else 1)
+    operands = [state, rhs, viscous, inverse] + ([gain] if needs_gain else [])
+    in_specs = [spec_hbm(), spec_hbm()] + [spec_vmem()] * (len(operands) - 2)
     operands += arrays + ([carry] if has_carry else []) + after
     in_specs += [spec_vmem()] * (small + (1 if has_carry else 0)) + [spec_any()] * len(after)
-    out_specs = [spec_any()] * sent + [spec_vmem()] * (2 if with_first else 1)
+    out_specs = [spec_hbm()] + [spec_vmem()] * (2 if with_first else 1)
     scratch = [
         pltpu.VMEM((z.segments, size + z.spill, z.ax), F32),
         pltpu.VMEM((z.segments, size + z.spill, z.ax), F32),
@@ -313,8 +313,9 @@
         scratch,
         z.flops * len(steps) * z.segments * 3,
         4 * z.segments * size * z.ax * 4,
+        limit=52,
     )(*operands)
-    return result[:sent], result[sent:]
+    return result[0], result[1:]
 
 
 def maps_call(z, me, gain, after):
@@ -387,13 +388,14 @@
 
 
 def first_call(z, places, packs, before, prefix, gain, starts, held):
+    pairs = z.segments // 2
     message = z.message(1)
 
     def kernel(*refs):
         places_ref, refs = refs[0], refs[1:]
         pack_refs, refs = refs[: z.groups], refs[z.groups :]
         before_ref, prefix_ref, gain_ref, start_ref, _ = refs[:5]
-        out_refs = refs[5 : 5 + z.segments]
+        keep_ref, give_ref = refs[5:7]
         mine = places_ref[0]
         group = places_ref[1]
         value = jnp.zeros((z.pad, z.cols), F32)
@@ -403,87 +405,127 @@
             moved = product(matrices[n], operand_right(value)) + pack_refs[n][:, : z.cols]
             value = jnp.where(t <= z.groups + group, moved, 0.0)
         incoming = operand_right(value)
-        for s in range(z.segments):
-            e = lax.rem(mine + s, z.segments)
-            arriving = jnp.where(e == 0, value, before_ref[e] + product(operand_left(prefix_ref[e]), incoming))
-            matrix = operand_left(read_matrix(z, gain_ref, e * z.steps))
-            solved = start_ref[e] + product(matrix, operand_right(arriving))
-            write_field(z, out_refs[s], (), 0, solved)
-
-    result = call(
+        side = lax.rem(mine, 2)
+        for d in range(pairs):
+            for ref, part in ((give_ref, 1 - side), (keep_ref, side)):
+                e = lax.rem(mine - side + 2 * d, z.segments) + part
+                arriving = jnp.where(e == 0, value, before_ref[e] + product(operand_left(prefix_ref[e]), incoming))
+                matrix = operand_left(read_matrix(z, gain_ref, e * z.steps))
+                solved = start_ref[e] + product(matrix, operand_right(arriving))
+                write_field(z, ref, (d,), 0, solved)
+
+    return call(
         kernel,
         "first",
-        [f32(message, z.ax) for _ in range(z.segments)] + [jax.ShapeDtypeStruct(held.shape, F32)],
-        [spec_smem()] + [spec_vmem()] * (z.groups + 4) + [spec_any()],
-        [spec_vmem()] * z.segments + [spec_any()],
+        [f32(pairs, message, z.ax)] * 2 + [jax.ShapeDtypeStruct(held.shape, F32)],
+        [spec_smem()] + [spec_vmem()] * (z.groups + 4) + [spec_hbm()],
+        [spec_vmem()] * 2 + [spec_hbm()],
         [],
         z.flops * (z.segments * 2 + 2 * z.groups),
         4 * z.segments * z.pad * z.cols * 4,
-        {z.groups + 5: z.segments},
+        {z.groups + 5: 2},
     )(places, *packs, before, prefix, gain, starts, held)
-    return result[: z.segments], result[z.segments]
-
-
-def finish_call(z, chunk, me, own, firsts, messages, out):
+
+
+def couple_call(z, keep, got):
+    pairs = z.segments // 2
+    message = z.message(1)
+
+    def kernel(keep_ref, got_ref, *refs):
+        for d in range(pairs):
+            refs[d][0] = keep_ref[d]
+            refs[d][1] = got_ref[d]
+
+    return call(
+        kernel,
+        "couple",
+        [f32(2, message, z.ax)] * pairs,
+        [spec_vmem()] * 2,
+        [spec_vmem()] * pairs,
+        [],
+        0,
+        4 * 4 * pairs * message * z.ax,
+    )(keep, got)
+
+
+def open_call(z, me, firsts):
+    radial = z.segments * z.rows
+    tall = z.nodes * radial
+    pairs = z.segments // 2
+
+    def kernel(*refs):
+        me_ref, refs = refs[0], refs[1:]
+        first_refs, refs = refs[:pairs], refs[pairs:]
+        out_ref, operand_ref, stage, sem = refs
+        mine = me_ref[0]
+        side = lax.rem(mine, 2)
+        for d in range(pairs):
+            for part in range(2):
+                src = lax.rem(mine - side - 2 * d + z.segments, z.segments) + (side if part == 0 else 1 - side)
+                field = read_exact(z, first_refs[d], (part,), 0)
+                empty = jnp.zeros((z.pad - z.nodes, z.cols), F32)
+                operand_ref[src] = operand_right(jnp.concatenate([field, empty], axis=0))
+                for j in range(z.rows):
+                    stage[pl.ds(src * z.rows + j, z.nodes, stride=radial), :] = field[:, j * z.ax : (j + 1) * z.ax]
+        copy = pltpu.make_async_copy(stage, out_ref.at[0], sem)
+        copy.start()
+        copy.wait()
+
+    return call(
+        kernel,
+        "finish_0",
+        [f32(z.steps, tall, z.ax), jax.ShapeDtypeStruct((z.segments, 2 * z.pad, z.cols), BF16)],
+        [spec_smem()] + [spec_vmem()] * pairs,
+        [spec_hbm(), spec_vmem()],
+        [pltpu.VMEM((tall, z.ax), F32), pltpu.SemaphoreType.DMA],
+        0,
+        4 * 2 * tall * z.ax,
+    )(me, *firsts)
+
+
+def finish_call(z, chunk, own, operands, messages, out):
     low, high = chunk
     count = high - low
     radial = z.segments * z.rows
     tall = z.nodes * radial
-    only_first = messages is None
-    has_out = out is not None
-    whole = not only_first and len(messages) == 1
-    sent = 0 if only_first else len(messages)
-
-    def kernel(*refs):
-        me_ref, own_ref, refs = refs[0], refs[1], refs[2:]
-        first_refs, refs = refs[: z.segments], refs[z.segments :]
-        message_refs, refs = refs[:sent], refs[sent:]
-        if has_out:
-            refs = refs[1:]
-        out_ref, stage, sem = refs
-        mine = me_ref[0]
-        matrices = None if only_first else [operand_left(own_ref[i]) for i in range(low, high)]
-        for s in range(z.segments):
-            src = lax.rem(mine - s + z.segments, z.segments)
-            field = read_exact(z, first_refs[s], (), 0)
-            if not only_first:
-                empty = jnp.zeros((z.pad - z.nodes, z.cols), F32)
-                parts = operand_right(jnp.concatenate([field, empty], axis=0))
-            for n in range(count):
-                if only_first:
-                    value = field
-                else:
-                    ref, lead = (message_refs[0], (src,)) if whole else (message_refs[s], ())
-                    value = product(matrices[n], parts)[: z.nodes] + read_exact(z, ref, lead, n * z.height)
+    message = z.message(count)
+
+    def kernel(own_ref, operand_ref, message_ref, _, out_ref, buf, stage, sem, out_sem):
+        copies = [pltpu.make_async_copy(message_ref.at[e], buf.at[e], sem.at[e]) for e in range(z.segments)]
+        for copy in copies:
+            copy.start()
+        sends = []
+        for n in range(count):
+            matrix = operand_left(own_ref[low + n])
+            for e in range(z.segments):
+                if n == 0:
+                    copies[e].wait()
+                value = product(matrix, operand_ref[e])[: z.nodes] + read_exact(z, buf, (e,), n * z.height)
                 for j in range(z.rows):
-                    rows = pl.ds(src * z.rows + j, z.nodes, stride=radial)
+                    rows = pl.ds(e * z.rows + j, z.nodes, stride=radial)
                     stage[n, rows, :] = value[:, j * z.ax : (j + 1) * z.ax]
-        copies = []
-        for n in range(count):
-            copy = pltpu.make_async_copy(stage.at[n], out_ref.at[low + n], sem.at[n])
+            copy = pltpu.make_async_copy(stage.at[n], out_ref.at[low + n], out_sem.at[n])
             copy.start()
-            copies.append(copy)
-        for copy in copies:
+            sends.append(copy)
+        for copy in sends:
             copy.wait()
 
-    operands = [me, own] + list(firsts) + ([] if only_first else list(messages))
-    in_specs = [spec_smem()] + [spec_vmem()] * (len(operands) - 1)
-    aliases = {}
-    if has_out:
-        aliases = {len(operands): 0}
-        operands.append(out)
-        in_specs.append(spec_any())
     return call(
         kernel,
         f"finish_{low}",
         f32(z.steps, tall, z.ax),
-        in_specs,
-        spec_any(),
-        [pltpu.VMEM((count, tall, z.ax), F32), pltpu.SemaphoreType.DMA((count,))],
+        [spec_vmem(), spec_vmem(), spec_hbm(), spec_hbm()],
+        spec_hbm(),
+        [
+            pltpu.VMEM((z.segments, message, z.ax), F32),
+            pltpu.VMEM((count, tall, z.ax), F32),
+            pltpu.SemaphoreType.DMA((z.segments,)),
+            pltpu.SemaphoreType.DMA((count,)),
+        ],
         z.flops * count * z.segments,
         4 * 2 * count * tall * z.ax,
-        aliases,
-    )(*operands)
+        {3: 0},
+    )(own, operands, messages, out)
 
 
 def shift_by(array, axis, by):
@@ -498,14 +540,8 @@
     return left, right
 
 
-def exchange(z, messages):
-    if len(messages) == 1:
-        return [lax.all_to_all(messages[0], "elem", 0, 0, tiled=True)]
-    order = sorted(range(1, z.segments), key=lambda s: abs(s - z.segments // 2))
-    moved = {0: messages[0]}
-    for s in order:
-        moved[s] = shift_by(messages[s], "elem", s)
-    return [moved[s] for s in range(z.segments)]
+def spread(messages):
+    return lax.all_to_all(messages, "elem", 0, 0, tiled=True)
 
 
 def chunks_of(steps):
@@ -533,33 +569,35 @@
         for i in range(low, high):
             sensors[i], lefts[i], rights[i] = (sensor, i - low), (left, i - low), (right, i - low)
 
-    def sweep(chunk, whole, ring, carry, after):
+    def sweep(chunk, ring, carry):
         return sweep_call(
-            z, chunk, whole, me, state, rhs, viscous_op, gain, inverse, sensors, lefts, rights, ring, carry, after
+            z, chunk, state, rhs, viscous_op, gain, inverse, sensors, lefts, rights, ring, carry, []
         )
 
     one, two, three = chunks_of(z.steps)
     sense(0, 3, [])
-    messages_one, (carry,) = sweep(one, False, None, None, [])
+    messages_one, (carry,) = sweep(one, None, None)
     sense(3, z.steps, [carry])
     last, place = sensors[z.steps - 1]
     ring = [
         shift_by(last[place, segments - 1 :], "blk", 1),
         shift_by(sensors[0][0][0, :1], "blk", -1),
     ]
-    messages_two, (carry,) = sweep(two, True, None, carry, [])
-    received_one = exchange(z, messages_one)
+    messages_two, (carry,) = sweep(two, None, carry)
     own, tails, wholes, prefix, group = maps_call(z, me, gain, [carry])
-    messages_three, (carry, starts) = sweep(three, True, ring, carry, received_one[1:])
+    messages_three, (carry, starts) = sweep(three, ring, carry)
     before, pack = chain_call(z, starts, carry, tails, wholes, group)
     packs = [pack] + [shift_by(pack, "blk", s) for s in range(1, groups)]
-    firsts, held = first_call(z, places, packs, before, prefix, gain, starts, messages_three[0])
-    received_two = exchange(z, messages_two)
-    firsts = exchange(z, firsts)
-    received_three = exchange(z, [held])
-    out = finish_call(z, (0, 1), me, own, firsts, None, None)
+    keep, give, held = first_call(z, places, packs, before, prefix, gain, starts, messages_three)
+    got = lax.ppermute(give, "elem", [(i, i ^ 1) for i in range(segments)])
+    firsts = couple_call(z, keep, got)
+    firsts = [firsts[0]] + [shift_by(firsts[d], "elem", 2 * d) for d in range(1, segments // 2)]
+    received_one = spread(messages_one)
+    received_two = spread(messages_two)
+    received_three = spread(held)
+    out, operands = open_call(z, me, firsts)
     for chunk, messages in ((one, received_one), (two, received_two), (three, received_three)):
-        out = finish_call(z, chunk, me, own, firsts, messages, out)
+        out = finish_call(z, chunk, own, operands, messages, out)
     return out.reshape(z.steps, z.nodes, segments * z.rows, z.ax)
 
 

time: 326 us -> 257 us (0.79)
  waiting for transfers between devices: 176 us -> 113 us
  local copies, waits for them, and re-layouts: 44.4 us -> 27.4 us
  Pallas kernels: 67.2 us -> 78.7 us
    ppermute x19 -> x8, waiting for transfers between devices: 170 us -> 92 us  [shift_by(): lax.ppermute(array, axis, [(i, (i + by) % size) for i in range(size)])]
    unnamed x130 -> x54, local copies, waits for them, and re-layouts: 44.4 us -> 27.4 us
    ppermute x2, waiting for transfers between devices: 0.01 us -> 12.2 us  [neighbours(): left = lax.ppermute(tail, 'elem', [(i, i + 1) for i in range(size - 1)])]
    ppermute x19 -> x8, starting transfers between devices: 15.4 us -> 8.49 us  [shift_by(): lax.ppermute(array, axis, [(i, (i + by) % size) for i in range(size)])]
    pallas_call x3, Pallas kernels: 27 us -> 33.4 us  [sweep_call(): call(kernel, f'sweep_{low}', outs, in_specs, out_specs, scratch, z.flops...]
    pallas_call x7 -> x8, Pallas kernels: 25.1 us -> 30.3 us  [the longest x3 14.1 us: finish_call(): call(kernel, f'finish_{low}', f32(z.steps, tall, z.ax), [spec_vmem(), spe...]
    all_to_all x2 -> x3, starting transfers between devices: 10.8 us -> 15.6 us  [spread(): return lax.all_to_all(messages, 'elem', 0, 0, tiled=True)]
  transfers between devices with their start and end apart: 25 -> 16, of which waited for: 13 -> 11; matrix products, arithmetic and copies ran while one was open for 0% -> 0% of each run, Pallas kernels for 12% -> 24%
where the time goes in v2:
time: 257 us; the launch traced here: 255 us
  waiting for transfers between devices  113 us (44%)
  Pallas kernels  78.7 us (31%)
  starting transfers between devices  35.4 us (14%)
  local copies, waits for them, and re-layouts  27.4 us (11%)
    ppermute x8, waiting for transfers between devices, shift_by(): lax.ppermute(array, axis, [(i, (i + by) % size) for i in range(size)])  92 us
    pallas_call x3, Pallas kernels, sweep_call(): call(kernel, f'sweep_{low}', outs, in_specs, out_specs, scratch, z.flops...  33.4 us
    unnamed x54, local copies, waits for them, and re-layouts  27.4 us
    all_to_all x3, starting transfers between devices, spread(): return lax.all_to_all(messages, 'elem', 0, 0, tiled=True)  15.6 us
    pallas_call x3, Pallas kernels, finish_call(): call(kernel, f'finish_{low}', f32(z.steps, tall, z.ax), [spec_vmem(), spe...  14.1 us
    pallas_call x1, Pallas kernels, maps_call(): call(kernel, 'maps', outs, [spec_smem(), spec_vmem()] + [spec_any()] * le...  13.4 us
    ppermute x2, waiting for transfers between devices, neighbours(): left = lax.ppermute(tail, 'elem', [(i, i + 1) for i in range(size - 1)])  12.2 us
    pallas_call x2, Pallas kernels, sensor_call(): call(kernel, f'sensor_{low}', outs, [spec_hbm(), spec_vmem()] + [spec_any...  10.9 us
  transfers between devices with their start and end apart: 16, of which 11 were waited for; matrix products, arithmetic and copies ran while one was open for 0% of the time, Pallas kernels for 24%

profile of v2, /device:TPU:9, one launch (start us, length us, event | category | flops | bytes accessed | tf_op | source)
XLA Modules:
  0.0 255.5 jit_solution(12950692410586267684)
XLA Ops:
  0.0 5.1 %sensor_0.1 = (f32[3,8,256]{2,1,0:T(8,128)}, f32[3,8,128]{2,1,0:T(8,128)}, f32[3,8,128]{2,1,0:T(8,128)}) custom-call(f32[8,2000,128]{2,1,0:T(8,128)} %bitcast.15, f32[125,125]{1,0:T(8,128)} %modal_ref.3), custom_call_target="tpu_custom_call" | custom-call | flops 805306368 | bytes 3080192 | tf_op jit(solution)/shard_map/sensor_0/pallas_call | solution.py:151
  5.1 3.8 %collective-permute-start = (f32[3,8,128]{2,1,0:T(8,128)}, f32[3,8,128]{2,1,0:T(8,128)S(1)}, u32[]{:S(2)}, u32[]{:S(2)}) collective-permute-start(f32[3,8,128]{2,1,0:T(8,128)} %get-tuple-element.35), channel_id=1, source_target_pairs={{0,1},{1,2},{2,3},{3,4},{4,5},{5,6},{6,7},{8,9},{9,10},{10,11},{11... | collective-permute-start | bytes 36872 | tf_op jit(solution)/shard_map/ppermute | solution.py:538
  8.9 1.9 collective-permute-start.1
  10.8 3.3 %collective-permute-done.1.refs_6_.refs_8_.refs_10_ = f32[3,8,128]{2,1,0:T(8,128)S(1)} collective-permute-done((f32[3,8,128]{2,1,0:T(8,128)}, f32[3,8,128]{2,1,0:T(8,128)S(1)}, u32[]{:S(2)}, u32[]{:S(2)}) %collective-permute-start.1) | collective-permute-done | bytes 12320 | tf_op jit(solution)/shard_map/ppermute | solution.py:539
  14.1 0.7 copy-done.22
  14.9 7.0 %sweep_1.1 = (f32[8,256,128]{2,1,0:T(8,128)}, f32[8,128,256]{2,1,0:T(8,128)}) custom-call(f32[8,2000,128]{2,1,0:T(8,128)} %bitcast.16, f32[8,2000,128]{2,1,0:T(8,128)} %bitcast.20, f32[125,125]{1,0:T(8,128)S(1)} %copy-done.17, f32[125,64,125]{2,1,0:T(8,128)} %bitcast.23, f32[3,8,256]{2,1,0:T(8,128)S(1)} %copy-done.22, ...), custom_call_target="tpu_custom_call" | custom-call | flops 805306368 | bytes 4194304 | tf_op jit(solution)/shard_map/sweep_1/pallas_call | solution.py:307
  21.9 4.1 %all-to-all-start.2 = ((f32[8,256,128]{2,1,0:T(8,128)}), f32[8,256,128]{2,1,0:T(8,128)S(1)}, u32[]{:S(2)}, u32[]{:S(2)}) async-start(f32[8,256,128]{2,1,0:T(8,128)} %get-tuple-element.61), calls=%async_computation.2 | async-start | bytes 2097152 | tf_op jit(solution)/shard_map/all_to_all | solution.py:544
  25.9 5.8 %sensor_3.1 = (f32[5,8,256]{2,1,0:T(8,128)}, f32[5,8,128]{2,1,0:T(8,128)}, f32[5,8,128]{2,1,0:T(8,128)}) custom-call(f32[8,2000,128]{2,1,0:T(8,128)} %bitcast.17, f32[125,125]{1,0:T(8,128)} %modal_ref.3, f32[8,128,256]{2,1,0:T(8,128)} %get-tuple-element.37.refs_0_.refs_11_), custom_call_target="tpu_custom_call" | custom-call | flops 1342177280 | bytes 5144576 | tf_op jit(solution)/shard_map/sensor_3/pallas_call | solution.py:151
  31.7 3.3 %collective-permute-start.2 = (f32[5,8,128]{2,1,0:T(8,128)}, f32[5,8,128]{2,1,0:T(8,128)S(1)}, u32[]{:S(2)}, u32[]{:S(2)}) collective-permute-start(f32[5,8,128]{2,1,0:T(8,128)} %get-tuple-element.39), channel_id=1, source_target_pairs={{0,1},{1,2},{2,3},{3,4},{4,5},{5,6},{6,7},{8,9},{9,10},{10,11},{11... | collective-permute-start | bytes 61448 | tf_op jit(solution)/shard_map/ppermute | solution.py:538
  35.1 1.9 collective-permute-start.3
  37.0 12.2 %collective-permute-done.2.refs_9_.refs_6_ = f32[5,8,128]{2,1,0:T(8,128)S(1)} collective-permute-done((f32[5,8,128]{2,1,0:T(8,128)}, f32[5,8,128]{2,1,0:T(8,128)S(1)}, u32[]{:S(2)}, u32[]{:S(2)}) %collective-permute-start.2) | collective-permute-done | bytes 20512 | tf_op jit(solution)/shard_map/ppermute | solution.py:538
  49.2 1.8 collective-permute-done.3.refs_10_.refs_7_
  51.0 0.8 copy-done.24
  51.7 12.4 %sweep_2.1 = (f32[8,752,128]{2,1,0:T(8,128)}, f32[8,128,256]{2,1,0:T(8,128)S(1)}) custom-call(f32[8,2000,128]{2,1,0:T(8,128)} %bitcast.18, f32[8,2000,128]{2,1,0:T(8,128)} %bitcast.21, f32[125,125]{1,0:T(8,128)S(1)} %copy-done.17, f32[125,64,125]{2,1,0:T(8,128)} %bitcast.24, f32[125,64,125]{2,1,0:T(8,128)} %bitcast.11, f32[3,8,256]{2,1,0:T(8,128)S(1)} %copy-done.22, ...), custom_call_target="tpu_custom_call" | custom-call | flops 2415919104 | bytes 12451840 | tf_op jit(solution)/shard_map/sweep_2/pallas_call | solution.py:307
  64.1 1.0 copy-done.11
  65.1 1.0 copy-done.9
  66.1 3.6 %all-to-all-start.1 = ((f32[8,752,128]{2,1,0:T(8,128)}), f32[8,752,128]{2,1,0:T(8,128)S(1)}, u32[]{:S(2)}, u32[]{:S(2)}) async-start(f32[8,752,128]{2,1,0:T(8,128)} %get-tuple-element.60), calls=%async_computation.1 | async-start | bytes 6160384 | tf_op jit(solution)/shard_map/all_to_all | solution.py:544
  69.7 2.2 collective-permute-start.5
  71.9 0.0 copy-start
  71.9 2.2 copy-done
  74.1 1.2 copy-done.12
  75.3 13.4 %maps.1 = (f32[8,128,128]{2,1,0:T(8,128)S(1)}, f32[8,128,128]{2,1,0:T(8,128)S(1)}, f32[8,128,128]{2,1,0:T(8,128)S(1)}, f32[8,128,128]{2,1,0:T(8,128)S(1)}, f32[128,128]{1,0:T(8,128)S(1)}) custom-call(s32[1]{0:T(128)} %bitcast.me_ref.refs_0_, f32[125,64,125]{2,1,0:T(8,128)S(1)} %bitcast.13, f32[8,128,256]{2,1,0:T(8,128)S(1)} %copy-done.12), custom_call_target="tpu_custom_call" | custom-call | flops 1207959552 | bytes 4194304 | tf_op jit(solution)/shard_map/maps/pallas_call | solution.py:352
  88.7 0.8 copy-done.6
  89.5 0.8 copy-done.20
  90.4 14.0 %sweep_5.1 = (f32[8,752,128]{2,1,0:T(8,128)}, f32[8,128,256]{2,1,0:T(8,128)S(1)}, f32[8,128,256]{2,1,0:T(8,128)}) custom-call(f32[8,2000,128]{2,1,0:T(8,128)} %bitcast.19, f32[8,2000,128]{2,1,0:T(8,128)} %bitcast.22, f32[125,125]{1,0:T(8,128)S(1)} %copy-done.17, f32[125,64,125]{2,1,0:T(8,128)} %bitcast.25, f32[125,64,125]{2,1,0:T(8,128)} %bitcast.12, ...), custom_call_target="tpu_custom_call" | custom-call | flops 3221225472 | bytes 12320768 | tf_op jit(solution)/shard_map/sweep_5/pallas_call | solution.py:307
  104.4 1.2 copy-done.13
  105.6 1.7 chain.1
  107.3 1.0 copy-done.15
  108.3 2.4 collective-permute-start.8
  110.6 0.2 collective-permute-start.7
  110.9 0.1 collective-permute-start.6
  110.9 0.1 pad_add_fusion.refs_0_
  111.0 3.3 %collective-permute-done.8.refs_4_ = f32[128,384]{1,0:T(8,128)S(1)} collective-permute-done((f32[128,384]{1,0:T(8,128)S(1)}, f32[128,384]{1,0:T(8,128)S(1)}, u32[]{:S(2)}, u32[]{:S(2)}) %collective-permute-start.8) | collective-permute-done | bytes 196640 | tf_op jit(solution)/shard_map/ppermute | solution.py:533
  114.3 2.6 %collective-permute-done.7.refs_3_ = f32[128,384]{1,0:T(8,128)} collective-permute-done((f32[128,384]{1,0:T(8,128)S(1)}, f32[128,384]{1,0:T(8,128)}, u32[]{:S(2)}, u32[]{:S(2)}) %collective-permute-start.7) | collective-permute-done | bytes 196640 | tf_op jit(solution)/shard_map/ppermute | solution.py:533
  116.9 2.6 %collective-permute-done.6.refs_2_ = f32[128,384]{1,0:T(8,128)} collective-permute-done((f32[128,384]{1,0:T(8,128)S(1)}, f32[128,384]{1,0:T(8,128)}, u32[]{:S(2)}, u32[]{:S(2)}) %collective-permute-start.6) | collective-permute-done | bytes 196640 | tf_op jit(solution)/shard_map/ppermute | solution.py:533
  119.6 2.2 copy-done.1
  121.7 1.9 copy-done.2
  123.6 1.2 copy-done.14
  124.8 1.2 copy-done.16
  126.0 1.0 copy-done.21
  127.1 3.6 %first.1 = (f32[4,256,128]{2,1,0:T(8,128)S(1)}, f32[4,256,128]{2,1,0:T(8,128)S(1)}, f32[8,752,128]{2,1,0:T(8,128)S(1)}) custom-call(s32[2]{0:T(128)S(1)} %pad_add_fusion.refs_0_, f32[128,384]{1,0:T(8,128)S(1)} %get-tuple-element.48.refs_1_, f32[128,384]{1,0:T(8,128)} %collective-permute-done.6.refs_2_, ...), custom_call_target="tpu_custom_call", output_to_operand_aliasing={{2}: (9, {})} | custom-call | flops 805306368 | bytes 4194304 | tf_op jit(solution)/shard_map/first/pallas_call | solution.py:417
  130.7 1.7 copy-done.3
  132.4 0.8 copy-done.18
  133.2 0.8 copy-done.26
  134.0 2.1 all-to-all-done.1.message_ref
  136.1 7.9 %all-to-all-start = ((f32[8,752,128]{2,1,0:T(8,128)}), f32[8,752,128]{2,1,0:T(8,128)}, u32[]{:S(2)}, u32[]{:S(2)}) async-start(f32[8,752,128]{2,1,0:T(8,128)} %copy-done.3), calls=%async_computation | async-start | bytes 6160384 | tf_op jit(solution)/shard_map/all_to_all | solution.py:544
  144.0 0.4 collective-permute-start.9
  144.3 2.2 collective-permute-done.9.got_ref
  146.5 1.0 copy-done.19
  147.5 0.1 couple.1
  147.6 1.2 collective-permute-start.10
  148.9 1.0 collective-permute-start.11
  149.9 1.4 collective-permute-start.12
  151.3 76.1 %collective-permute-done.10.refs_2_ = f32[2,256,128]{2,1,0:T(8,128)S(1)} collective-permute-done((f32[2,256,128]{2,1,0:T(8,128)S(1)}, f32[2,256,128]{2,1,0:T(8,128)S(1)}, u32[]{:S(2)}, u32[]{:S(2)}) %collective-permute-start.10) | collective-permute-done | bytes 262176 | tf_op jit(solution)/shard_map/ppermute | solution.py:533
  227.3 5.6 %collective-permute-done.11.refs_3_ = f32[2,256,128]{2,1,0:T(8,128)S(1)} collective-permute-done((f32[2,256,128]{2,1,0:T(8,128)S(1)}, f32[2,256,128]{2,1,0:T(8,128)S(1)}, u32[]{:S(2)}, u32[]{:S(2)}) %collective-permute-start.11) | collective-permute-done | bytes 262176 | tf_op jit(solution)/shard_map/ppermute | solution.py:533
  232.9 1.7 collective-permute-done.12.refs_4_
  234.6 1.6 finish_0.1
  236.2 1.4 copy-done.7
  237.6 1.2 copy-done.10
  238.9 4.2 %finish_1.1._ = f32[8,2000,128]{2,1,0:T(8,128)} custom-call(f32[8,128,128]{2,1,0:T(8,128)S(1)} %copy-done.7, bf16[8,256,256]{2,1,0:T(8,128)(2,1)S(1)} %get-tuple-element.58.operand_ref, f32[8,256,128]{2,1,0:T(8,128)S(1)} %copy-done.10, f32[8,2000,128]{2,1,0:T(8,128)} %get-tuple-element.62._), custom_call_target="tpu_custom_call", output_to_operand_aliasing={{}: (3, {})} | custom-call | flops 268435456 | bytes 2048000 | tf_op jit(solution)/shard_map/finish_1/pallas_call | solution.py:513
  243.1 5.2 %finish_2.1._ = f32[8,2000,128]{2,1,0:T(8,128)} custom-call(f32[8,128,128]{2,1,0:T(8,128)S(1)} %copy-done.7, bf16[8,256,256]{2,1,0:T(8,128)(2,1)S(1)} %get-tuple-element.58.operand_ref, f32[8,752,128]{2,1,0:T(8,128)S(1)} %all-to-all-done.1.message_ref, f32[8,2000,128]{2,1,0:T(8,128)} %finish_1.1._), custom_call_target="tpu_custom_call", output_to_operand_aliasing={{}: (3, {})} | custom-call | flops 805306368 | bytes 6144000 | tf_op jit(solution)/shard_map/finish_2/pallas_call | solution.py:513
  248.3 1.2 copy-done.5
  249.5 1.0 copy-done.8
  250.6 4.7 %finish_5.1 = f32[8,2000,128]{2,1,0:T(8,128)} custom-call(f32[8,128,128]{2,1,0:T(8,128)S(1)} %copy-done.8, bf16[8,256,256]{2,1,0:T(8,128)(2,1)S(1)} %copy-done.5, f32[8,752,128]{2,1,0:T(8,128)} %all-to-all-done.message_ref, f32[8,2000,128]{2,1,0:T(8,128)} %finish_2.1._), custom_call_target="tpu_custom_call", output_to_operand_aliasing={{}: (3, {})} | custom-call | flops 805306368 | bytes 6144000 | tf_op jit(solution)/shard_map/finish_5/pallas_call | solution.py:513
  (38 shorter events, 0.1 us)
Async XLA Ops:
  0.0 14.1 %copy-start.17 = (f32[125,125]{1,0:T(8,128)S(1)}, f32[125,125]{1,0:T(8,128)}, u32[]{:S(2)}) copy-start(f32[125,125]{1,0:T(8,128)} %refs_2_.5) | copy-start | bytes 187504
  5.1 5.7 %collective-permute-start = (f32[3,8,128]{2,1,0:T(8,128)}, f32[3,8,128]{2,1,0:T(8,128)S(1)}, u32[]{:S(2)}, u32[]{:S(2)}) collective-permute-start(f32[3,8,128]{2,1,0:T(8,128)} %get-tuple-element.35), channel_id=1, source_target_pairs={{0,1},{1,2},{2,3},{3,4},{4,5},{5,6},{6,7},{8,9},{9,10},{10,11},{11... | collective-permute-start | bytes 36872 | tf_op jit(solution)/shard_map/ppermute | solution.py:538
  8.9 5.2 %collective-permute-start.1 = (f32[3,8,128]{2,1,0:T(8,128)}, f32[3,8,128]{2,1,0:T(8,128)S(1)}, u32[]{:S(2)}, u32[]{:S(2)}) collective-permute-start(f32[3,8,128]{2,1,0:T(8,128)} %get-tuple-element.36), channel_id=1, source_target_pairs={{1,0},{2,1},{3,2},{4,3},{5,4},{6,5},{7,6},{9,8},{10,9},{11,10},{12... | collective-permute-start | bytes 36872 | tf_op jit(solution)/shard_map/ppermute | solution.py:539
  14.1 0.7 copy-start.22
  21.9 43.3 %all-to-all-start.2 = ((f32[8,256,128]{2,1,0:T(8,128)}), f32[8,256,128]{2,1,0:T(8,128)S(1)}, u32[]{:S(2)}, u32[]{:S(2)}) async-start(f32[8,256,128]{2,1,0:T(8,128)} %get-tuple-element.61), calls=%async_computation.2 | async-start | bytes 2097152 | tf_op jit(solution)/shard_map/all_to_all | solution.py:544
  31.7 17.4 %collective-permute-start.2 = (f32[5,8,128]{2,1,0:T(8,128)}, f32[5,8,128]{2,1,0:T(8,128)S(1)}, u32[]{:S(2)}, u32[]{:S(2)}) collective-permute-start(f32[5,8,128]{2,1,0:T(8,128)} %get-tuple-element.39), channel_id=1, source_target_pairs={{0,1},{1,2},{2,3},{3,4},{4,5},{5,6},{6,7},{8,9},{9,10},{10,11},{11... | collective-permute-start | bytes 61448 | tf_op jit(solution)/shard_map/ppermute | solution.py:538
  35.1 15.9 %collective-permute-start.3 = (f32[5,8,128]{2,1,0:T(8,128)}, f32[5,8,128]{2,1,0:T(8,128)S(1)}, u32[]{:S(2)}, u32[]{:S(2)}) collective-permute-start(f32[5,8,128]{2,1,0:T(8,128)} %get-tuple-element.40), channel_id=1, source_target_pairs={{1,0},{2,1},{3,2},{4,3},{5,4},{6,5},{7,6},{9,8},{10,9},{11,10},{12... | collective-permute-start | bytes 61448 | tf_op jit(solution)/shard_map/ppermute | solution.py:539
  51.0 0.8 copy-start.24
  64.1 1.0 copy-start.11
  65.1 4.6 %copy-start.23 = (f32[3,8,256]{2,1,0:T(8,128)S(1)}, f32[3,8,256]{2,1,0:T(8,128)}, u32[]{:S(2)}) copy-start(f32[3,8,256]{2,1,0:T(8,128)} %get-tuple-element.34.refs_4_.refs_5_.refs_8_) | copy-start | bytes 73732
  65.1 6.8 %copy-start.25 = (f32[5,8,256]{2,1,0:T(8,128)S(1)}, f32[5,8,256]{2,1,0:T(8,128)}, u32[]{:S(2)}) copy-start(f32[5,8,256]{2,1,0:T(8,128)} %get-tuple-element.38.refs_6_.refs_5_) | copy-start | bytes 122884
  65.1 1.0 copy-start.9
  66.1 70.0 %all-to-all-start.1 = ((f32[8,752,128]{2,1,0:T(8,128)}), f32[8,752,128]{2,1,0:T(8,128)S(1)}, u32[]{:S(2)}, u32[]{:S(2)}) async-start(f32[8,752,128]{2,1,0:T(8,128)} %get-tuple-element.60), calls=%async_computation.1 | async-start | bytes 6160384 | tf_op jit(solution)/shard_map/all_to_all | solution.py:544
  69.7 20.6 %collective-permute-start.5 = (f32[1,256]{1,0:T(1,128)S(1)}, f32[1,256]{1,0:T(1,128)S(1)}, u32[]{:S(2)}, u32[]{:S(2)}) collective-permute-start(f32[1,256]{1,0:T(1,128)S(1)} %slice_bitcast_fusion), channel_id=1, source_target_pairs={{0,24},{8,0},{16,8},{24,16},{1,25},{9,1},{17,9},{25,17},{2,26},{10... | collective-permute-start | bytes 3080 | tf_op jit(solution)/shard_map/ppermute | solution.py:533
  71.9 18.4 %collective-permute-start.4 = (f32[1,256]{1,0:T(1,128)S(1)}, f32[1,256]{1,0:T(1,128)S(1)}, u32[]{:S(2)}, u32[]{:S(2)}) collective-permute-start(f32[1,256]{1,0:T(1,128)S(1)} %slice_bitcast_fusion.1), channel_id=1, source_target_pairs={{0,8},{8,16},{16,24},{24,0},{1,9},{9,17},{17,25},{25,1},{2,10},{10... | collective-permute-start | bytes 3080 | tf_op jit(solution)/shard_map/ppermute | solution.py:533
  71.9 2.2 copy-start
  74.1 1.2 copy-start.12
  88.7 0.8 copy-start.6
  89.5 0.8 copy-start.20
  104.4 1.2 copy-start.13
  107.3 1.0 copy-start.15
  108.3 6.0 %collective-permute-start.8 = (f32[128,384]{1,0:T(8,128)S(1)}, f32[128,384]{1,0:T(8,128)S(1)}, u32[]{:S(2)}, u32[]{:S(2)}) collective-permute-start(f32[128,384]{1,0:T(8,128)S(1)} %get-tuple-element.48.refs_1_), channel_id=1, source_target_pairs={{0,24},{8,0},{16,8},{24,16},{1,25},{9,1},{17,9},{25,17},{2,26},{10... | collective-permute-start | bytes 589832 | tf_op jit(solution)/shard_map/ppermute | solution.py:533
  110.6 6.3 %collective-permute-start.7 = (f32[128,384]{1,0:T(8,128)S(1)}, f32[128,384]{1,0:T(8,128)}, u32[]{:S(2)}, u32[]{:S(2)}) collective-permute-start(f32[128,384]{1,0:T(8,128)S(1)} %get-tuple-element.48.refs_1_), channel_id=1, source_target_pairs={{0,16},{8,24},{16,0},{24,8},{1,17},{9,25},{17,1},{25,9},{2,18},{10... | collective-permute-start | bytes 589832 | tf_op jit(solution)/shard_map/ppermute | solution.py:533
  110.9 8.7 %collective-permute-start.6 = (f32[128,384]{1,0:T(8,128)S(1)}, f32[128,384]{1,0:T(8,128)}, u32[]{:S(2)}, u32[]{:S(2)}) collective-permute-start(f32[128,384]{1,0:T(8,128)S(1)} %get-tuple-element.48.refs_1_), channel_id=1, source_target_pairs={{0,8},{8,16},{16,24},{24,0},{1,9},{9,17},{17,25},{25,1},{2,10},{10... | collective-permute-start | bytes 589832 | tf_op jit(solution)/shard_map/ppermute | solution.py:533
  119.6 2.2 copy-start.1
  121.7 1.9 copy-start.2
  123.6 1.2 copy-start.14
  124.8 1.2 copy-start.16
  126.0 1.0 copy-start.21
  130.7 1.7 copy-start.3
  132.4 0.8 copy-start.18
  133.2 0.8 copy-start.26
  136.1 112.2 %all-to-all-start = ((f32[8,752,128]{2,1,0:T(8,128)}), f32[8,752,128]{2,1,0:T(8,128)}, u32[]{:S(2)}, u32[]{:S(2)}) async-start(f32[8,752,128]{2,1,0:T(8,128)} %copy-done.3), calls=%async_computation | async-start | bytes 6160384 | tf_op jit(solution)/shard_map/all_to_all | solution.py:544
  144.0 2.5 collective-permute-start.9
  146.5 1.0 copy-start.19
  147.6 79.7 %collective-permute-start.10 = (f32[2,256,128]{2,1,0:T(8,128)S(1)}, f32[2,256,128]{2,1,0:T(8,128)S(1)}, u32[]{:S(2)}, u32[]{:S(2)}) collective-permute-start(f32[2,256,128]{2,1,0:T(8,128)S(1)} %get-tuple-element.55), channel_id=1, source_target_pairs={{0,2},{1,3},{2,4},{3,5},{4,6},{5,7},{6,0},{7,1},{8,10},{9,11},{10,... | collective-permute-start | bytes 786440 | tf_op jit(solution)/shard_map/ppermute | solution.py:533
  148.9 84.1 %collective-permute-start.11 = (f32[2,256,128]{2,1,0:T(8,128)S(1)}, f32[2,256,128]{2,1,0:T(8,128)S(1)}, u32[]{:S(2)}, u32[]{:S(2)}) collective-permute-start(f32[2,256,128]{2,1,0:T(8,128)S(1)} %get-tuple-element.56), channel_id=1, source_target_pairs={{0,4},{1,5},{2,6},{3,7},{4,0},{5,1},{6,2},{7,3},{8,12},{9,13},{10,... | collective-permute-start | bytes 786440 | tf_op jit(solution)/shard_map/ppermute | solution.py:533
  149.9 84.8 %collective-permute-start.12 = (f32[2,256,128]{2,1,0:T(8,128)S(1)}, f32[2,256,128]{2,1,0:T(8,128)S(1)}, u32[]{:S(2)}, u32[]{:S(2)}) collective-permute-start(f32[2,256,128]{2,1,0:T(8,128)S(1)} %get-tuple-element.57), channel_id=1, source_target_pairs={{0,6},{1,7},{2,0},{3,1},{4,2},{5,3},{6,4},{7,5},{8,14},{9,15},{10,... | collective-permute-start | bytes 786440 | tf_op jit(solution)/shard_map/ppermute | solution.py:533
  236.2 6.9 %copy-start.4 = (bf16[8,256,256]{2,1,0:T(8,128)(2,1)}, bf16[8,256,256]{2,1,0:T(8,128)(2,1)S(1)}, u32[]{:S(2)}) copy-start(bf16[8,256,256]{2,1,0:T(8,128)(2,1)S(1)} %get-tuple-element.58.operand_ref) | copy-start | bytes 3145732
  236.2 1.4 copy-start.7
  237.6 1.2 copy-start.10
  248.3 1.2 copy-start.5
  249.5 1.0 copy-start.8

commit v3 on v2

--- a/solution.py
+++ b/solution.py
@@ -10,7 +10,7 @@
 ORDER = 4
 F32 = jnp.float32
 BF16 = jnp.bfloat16
-MIB = 1024 * 1024
+VMEM_LIMIT = 57 * 1024 * 1024
 TILE = 8
 LANES = 128
 
@@ -48,7 +48,7 @@
     return pl.BlockSpec(memory_space=pltpu.SMEM)
 
 
-def call(kernel, name, outs, in_specs, out_specs, scratch, flops, nbytes, aliases=None, limit=24):
+def call(kernel, name, outs, in_specs, out_specs, scratch, flops, nbytes, aliases=None):
     return pl.pallas_call(
         kernel,
         name=name,
@@ -57,7 +57,7 @@
         out_specs=out_specs,
         scratch_shapes=scratch,
         input_output_aliases=aliases or {},
-        compiler_params=pltpu.CompilerParams(vmem_limit_bytes=limit * MIB),
+        compiler_params=pltpu.CompilerParams(vmem_limit_bytes=VMEM_LIMIT),
         cost_estimate=pl.CostEstimate(flops=int(flops), bytes_accessed=int(nbytes), transcendentals=0),
     )
 
@@ -121,11 +121,13 @@
     return z.square(ref[:, k, :])
 
 
-def sensor_call(z, state, to_modal, after, low, high):
+def sensor_call(z, state, to_modal, after, earlier, low, high):
     first, size = z.window(low, high)
     count = high - low
+    before = sum(array.shape[0] for array in earlier)
 
     def kernel(state_ref, modal_ref, *refs):
+        earlier_refs, refs = refs[: len(earlier)], refs[len(earlier) :]
         sensor_ref, head_ref, tail_ref, buf, sem = refs[len(after) :]
         copies = [
             pltpu.make_async_copy(state_ref.at[e, pl.ds(first, size)], buf.at[e, pl.ds(0, size)], sem.at[e])
@@ -133,6 +135,12 @@
         ]
         for copy in copies:
             copy.start()
+        place = 0
+        for ref in earlier_refs:
+            for n in range(ref.shape[0]):
+                head_ref[place] = ref[n, :, : z.ax]
+                tail_ref[place] = ref[n, :, z.cols - z.ax :]
+                place += 1
         matrix = operand_left(z.square(modal_ref[...]))
         for e in range(z.segments):
             copies[e].wait()
@@ -143,22 +151,22 @@
                 lower = jnp.sum(squares[: ORDER**3], axis=0, keepdims=True)
                 upper = jnp.sum(squares[ORDER**3 :], axis=0, keepdims=True)
                 sensor = (upper / z.nodes) / ((lower + upper) / z.nodes + 1e-6)
-                sensor_ref[i - low, e : e + 1, :] = sensor
-                head_ref[i - low, e : e + 1, :] = sensor[:, : z.ax]
-                tail_ref[i - low, e : e + 1, :] = sensor[:, z.cols - z.ax :]
-
-    outs = [f32(count, z.segments, z.cols), f32(count, z.segments, z.ax), f32(count, z.segments, z.ax)]
+                n = i - low
+                sensor_ref[n, e : e + 1, :] = sensor
+                head_ref[before + n, e : e + 1, :] = sensor[:, : z.ax]
+                tail_ref[before + n, e : e + 1, :] = sensor[:, z.cols - z.ax :]
+
+    outs = [f32(count, z.segments, z.cols)] + [f32(before + count, z.segments, z.ax)] * 2
     return call(
         kernel,
         f"sensor_{low}",
         outs,
-        [spec_hbm(), spec_vmem()] + [spec_any()] * len(after),
+        [spec_hbm()] + [spec_vmem()] * (1 + len(earlier)) + [spec_any()] * len(after),
         [spec_vmem()] * 3,
         [pltpu.VMEM((z.segments, size + z.spill, z.ax), F32), pltpu.SemaphoreType.DMA((z.segments,))],
         z.flops * count * z.segments,
         4 * z.segments * size * z.ax,
-        limit=56,
-    )(state, to_modal, *after)
+    )(state, to_modal, *earlier, *after)
 
 
 def smoothed(z, sensor, before, after, left, right):
@@ -169,7 +177,7 @@
     return (4.0 * sensor + before + after + from_left + from_right) / 8.0
 
 
-def sweep_call(z, chunk, state, rhs, viscous, gain, inverse, sensors, lefts, rights, ring, carry, after):
+def sweep_call(z, chunk, state, rhs, viscous, gain, inverse, sensors, lefts, rights, ring, carry, held):
     low, high = chunk
     with_first = high == z.steps
     first, size = z.window(low, high)
@@ -207,17 +215,31 @@
         small_refs, refs = refs[:small], refs[small:]
         if has_carry:
             carry_ref, refs = refs[0], refs[1:]
-        refs = refs[len(after) :]
+        if held is not None:
+            refs = refs[1:]
         out_ref, refs = refs[0], refs[1:]
         end_ref, refs = refs[0], refs[1:]
         if with_first:
             start_ref, refs = refs[0], refs[1:]
-        state_buf, rhs_buf, smooth_buf, stage, sem, out_sem = refs[:6]
+        if held is not None:
+            refs = refs[1:]
+        state_buf, rhs_buf, inverse_buf, gain_buf, smooth_buf, stage, sem, matrix_sem, out_sem = refs[:9]
         if with_first:
-            state0, rhs0 = refs[6:]
-        batch = 4 if z.segments % 4 == 0 else 1
+            state0, rhs0 = refs[9:]
+        batch = next(n for n in (4, 8, z.segments) if z.segments % n == 0 and n * z.steps % TILE == 0)
         copies = []
         for s in range(z.segments):
+            if s % batch == 0:
+                part = pl.ds(s * z.steps, batch * z.steps)
+                sources = [(inverse_ref, inverse_buf)] + ([(gain_ref, gain_buf)] if needs_gain else [])
+                pieces = []
+                for n, (source, target) in enumerate(sources):
+                    copy = pltpu.make_async_copy(source.at[:, part], target.at[:, part], matrix_sem.at[s, n])
+                    copy.start()
+                    pieces.append(copy)
+                copies.append(pieces)
+            else:
+                copies.append([])
             moves = [
                 (state_ref.at[s, pl.ds(first, size)], state_buf.at[s, pl.ds(0, size)]),
                 (rhs_ref.at[s, pl.ds(first, size)], rhs_buf.at[s, pl.ds(0, size)]),
@@ -230,7 +252,7 @@
                 copy = pltpu.make_async_copy(source, target, sem.at[s, n])
                 copy.start()
                 started.append(copy)
-            copies.append(started)
+            copies[s] += started
         for n, i in enumerate(steps):
             (a0, p0), (a1, p1), (a2, p2), (al, pL), (ar, pR) = plan[n]
             here = small_refs[a0][p0]
@@ -262,12 +284,12 @@
                     value = source(
                         read_field(z, state_buf, (s,), offset),
                         read_field(z, rhs_buf, (s,), offset),
-                        read_matrix(z, inverse_ref, k),
+                        read_matrix(z, inverse_buf, k),
                         smooth,
                     )
                     if fields[g] is not None:
                         value = value + product(
-                            operand_left(read_matrix(z, gain_ref, k)), operand_right(fields[g])
+                            operand_left(read_matrix(z, gain_buf, k)), operand_right(fields[g])
                         )
                     fields[g] = value
                     write_field(z, stage, (s,), n * z.height, value)
@@ -281,7 +303,7 @@
                     start_ref[s] = source(
                         read_field(z, state0, (s,), -first0),
                         read_field(z, rhs0, (s,), -first0),
-                        read_matrix(z, inverse_ref, s * z.steps),
+                        read_matrix(z, inverse_buf, s * z.steps),
                         smooth,
                     )
         for copy in sends:
@@ -290,16 +312,26 @@
     field = f32(z.segments, z.pad, z.cols)
     outs = [f32(z.segments, message, z.ax)] + [field] * (2 if with_first else 1)
     operands = [state, rhs, viscous, inverse] + ([gain] if needs_gain else [])
-    in_specs = [spec_hbm(), spec_hbm()] + [spec_vmem()] * (len(operands) - 2)
-    operands += arrays + ([carry] if has_carry else []) + after
-    in_specs += [spec_vmem()] * (small + (1 if has_carry else 0)) + [spec_any()] * len(after)
+    in_specs = [spec_hbm(), spec_hbm(), spec_vmem()] + [spec_hbm()] * (len(operands) - 3)
+    operands += arrays + ([carry] if has_carry else [])
+    in_specs += [spec_vmem()] * (small + (1 if has_carry else 0))
+    aliases = {}
     out_specs = [spec_hbm()] + [spec_vmem()] * (2 if with_first else 1)
+    if held is not None:
+        aliases = {len(operands): len(outs)}
+        operands.append(held)
+        in_specs.append(spec_hbm())
+        outs.append(f32(*held.shape))
+        out_specs.append(spec_hbm())
     scratch = [
         pltpu.VMEM((z.segments, size + z.spill, z.ax), F32),
         pltpu.VMEM((z.segments, size + z.spill, z.ax), F32),
+        pltpu.VMEM(inverse.shape, F32),
+        pltpu.VMEM(gain.shape, F32),
         pltpu.VMEM((len(steps), z.segments, z.cols), F32),
         pltpu.VMEM((z.segments, message, z.ax), F32),
         pltpu.SemaphoreType.DMA((z.segments, 4)),
+        pltpu.SemaphoreType.DMA((z.segments, 2)),
         pltpu.SemaphoreType.DMA((z.segments,)),
     ]
     if with_first:
@@ -313,14 +345,14 @@
         scratch,
         z.flops * len(steps) * z.segments * 3,
         4 * z.segments * size * z.ax * 4,
-        limit=52,
+        aliases,
     )(*operands)
     return result[0], result[1:]
 
 
 def maps_call(z, me, gain, after):
     def kernel(me_ref, gain_ref, *refs):
-        own_ref, tail_ref, whole_ref, prefix_ref, group_ref = refs[len(after) :]
+        own_ref, head_ref, tail_ref, whole_ref, prefix_ref, group_ref = refs[len(after) :]
         mine = me_ref[0]
 
         def times(a, b):
@@ -338,8 +370,9 @@
                     own_ref[i] = value
 
         for e in range(z.segments):
+            head_ref[e] = read_matrix(z, gain_ref, e * z.steps)
             tail_ref[e] = values[e]
-            whole_ref[e] = times(values[e], read_matrix(z, gain_ref, e * z.steps))
+            whole_ref[e] = times(values[e], head_ref[e])
         value = whole_ref[0]
         prefix_ref[0] = value
         for e in range(1, z.segments):
@@ -348,13 +381,13 @@
         group_ref[...] = value
 
     square = (z.pad, z.pad)
-    outs = [f32(z.steps, *square)] + [f32(z.segments, *square)] * 3 + [f32(*square)]
+    outs = [f32(z.steps, *square)] + [f32(z.segments, *square)] * 4 + [f32(*square)]
     return call(
         kernel,
         "maps",
         outs,
         [spec_smem(), spec_vmem()] + [spec_any()] * len(after),
-        [spec_vmem()] * 5,
+        [spec_vmem()] * 6,
         [],
         z.flops * z.segments * (z.steps + 1) // 2,
         4 * z.segments * z.steps * z.pad * z.pad,
@@ -387,15 +420,14 @@
     )(starts, ends, tails, wholes, group)
 
 
-def first_call(z, places, packs, before, prefix, gain, starts, held):
+def first_call(z, places, packs, before, prefix, heads, starts):
     pairs = z.segments // 2
     message = z.message(1)
 
     def kernel(*refs):
         places_ref, refs = refs[0], refs[1:]
         pack_refs, refs = refs[: z.groups], refs[z.groups :]
-        before_ref, prefix_ref, gain_ref, start_ref, _ = refs[:5]
-        keep_ref, give_ref = refs[5:7]
+        before_ref, prefix_ref, head_ref, start_ref, keep_ref, give_ref = refs
         mine = places_ref[0]
         group = places_ref[1]
         value = jnp.zeros((z.pad, z.cols), F32)
@@ -410,28 +442,27 @@
             for ref, part in ((give_ref, 1 - side), (keep_ref, side)):
                 e = lax.rem(mine - side + 2 * d, z.segments) + part
                 arriving = jnp.where(e == 0, value, before_ref[e] + product(operand_left(prefix_ref[e]), incoming))
-                matrix = operand_left(read_matrix(z, gain_ref, e * z.steps))
+                matrix = operand_left(head_ref[e])
                 solved = start_ref[e] + product(matrix, operand_right(arriving))
                 write_field(z, ref, (d,), 0, solved)
 
     return call(
         kernel,
         "first",
-        [f32(pairs, message, z.ax)] * 2 + [jax.ShapeDtypeStruct(held.shape, F32)],
-        [spec_smem()] + [spec_vmem()] * (z.groups + 4) + [spec_hbm()],
-        [spec_vmem()] * 2 + [spec_hbm()],
+        [f32(pairs, message, z.ax)] * 2,
+        [spec_smem()] + [spec_vmem()] * (z.groups + 4),
+        [spec_vmem()] * 2,
         [],
         z.flops * (z.segments * 2 + 2 * z.groups),
         4 * z.segments * z.pad * z.cols * 4,
-        {z.groups + 5: 2},
-    )(places, *packs, before, prefix, gain, starts, held)
-
-
-def couple_call(z, keep, got):
+    )(places, *packs, before, prefix, heads, starts)
+
+
+def couple_call(z, keep, got, held):
     pairs = z.segments // 2
     message = z.message(1)
 
-    def kernel(keep_ref, got_ref, *refs):
+    def kernel(keep_ref, got_ref, _, *refs):
         for d in range(pairs):
             refs[d][0] = keep_ref[d]
             refs[d][1] = got_ref[d]
@@ -439,13 +470,14 @@
     return call(
         kernel,
         "couple",
-        [f32(2, message, z.ax)] * pairs,
-        [spec_vmem()] * 2,
-        [spec_vmem()] * pairs,
+        [f32(2, message, z.ax)] * pairs + [f32(*held.shape)],
+        [spec_vmem()] * 2 + [spec_hbm()],
+        [spec_vmem()] * pairs + [spec_hbm()],
         [],
         0,
         4 * 4 * pairs * message * z.ax,
-    )(keep, got)
+        {2: pairs},
+    )(keep, got, held)
 
 
 def open_call(z, me, firsts):
@@ -546,7 +578,7 @@
 
 def chunks_of(steps):
     if steps >= 8:
-        return [(1, 2), (2, 5), (5, steps)]
+        return [(1, 3), (3, 6), (6, steps)]
     return [(1, 2), (2, 3), (3, steps)]
 
 
@@ -563,38 +595,50 @@
     places = jnp.stack([here, lax.axis_index("blk").astype(jnp.int32)])
     sensors, lefts, rights = {}, {}, {}
 
-    def sense(low, high, after):
-        sensor, head, tail = sensor_call(z, state, to_modal, after, low, high)
+    def sense(low, high, after, earlier=()):
+        sensor, head, tail = sensor_call(z, state, to_modal, after, earlier, low, high)
+        for i in range(low, high):
+            sensors[i] = (sensor, i - low)
+        return sensor, head, tail
+
+    def edges(low, high, head, tail):
         left, right = neighbours(head, tail)
         for i in range(low, high):
-            sensors[i], lefts[i], rights[i] = (sensor, i - low), (left, i - low), (right, i - low)
-
-    def sweep(chunk, ring, carry):
+            lefts[i], rights[i] = (left, i - low), (right, i - low)
+
+    def sweep(chunk, ring, carry, held):
         return sweep_call(
-            z, chunk, state, rhs, viscous_op, gain, inverse, sensors, lefts, rights, ring, carry, []
+            z, chunk, state, rhs, viscous_op, gain, inverse, sensors, lefts, rights, ring, carry, held
         )
 
     one, two, three = chunks_of(z.steps)
-    sense(0, 3, [])
-    messages_one, (carry,) = sweep(one, None, None)
-    sense(3, z.steps, [carry])
-    last, place = sensors[z.steps - 1]
+    opening, head, tail = sense(0, 3, [])
+    edges(0, 3, head, tail)
+    known = 3
+    earlier = []
+    if one[1] >= known:
+        more, _, _ = sense(known, one[1] + 1, [opening])
+        earlier = [more]
+        known = one[1] + 1
+    messages_one, (carry,) = sweep(one, None, None, None)
+    last, head, tail = sense(known, z.steps, [carry], earlier)
+    edges(3, z.steps, head, tail)
     ring = [
-        shift_by(last[place, segments - 1 :], "blk", 1),
-        shift_by(sensors[0][0][0, :1], "blk", -1),
+        shift_by(last[z.steps - 1 - known, segments - 1 :], "blk", 1),
+        shift_by(opening[0, :1], "blk", -1),
     ]
-    messages_two, (carry,) = sweep(two, None, carry)
-    own, tails, wholes, prefix, group = maps_call(z, me, gain, [carry])
-    messages_three, (carry, starts) = sweep(three, ring, carry)
+    own, heads, tails, wholes, prefix, group = maps_call(z, me, gain, [carry])
+    messages_two, (carry,) = sweep(two, None, carry, None)
+    messages_three, (carry, starts, messages_two) = sweep(three, ring, carry, messages_two)
     before, pack = chain_call(z, starts, carry, tails, wholes, group)
     packs = [pack] + [shift_by(pack, "blk", s) for s in range(1, groups)]
-    keep, give, held = first_call(z, places, packs, before, prefix, gain, starts, messages_three)
+    keep, give = first_call(z, places, packs, before, prefix, heads, starts)
     got = lax.ppermute(give, "elem", [(i, i ^ 1) for i in range(segments)])
-    firsts = couple_call(z, keep, got)
+    *firsts, messages_three = couple_call(z, keep, got, messages_three)
     firsts = [firsts[0]] + [shift_by(firsts[d], "elem", 2 * d) for d in range(1, segments // 2)]
     received_one = spread(messages_one)
     received_two = spread(messages_two)
-    received_three = spread(held)
+    received_three = spread(messages_three)
     out, operands = open_call(z, me, firsts)
     for chunk, messages in ((one, received_one), (two, received_two), (three, received_three)):
         out = finish_call(z, chunk, own, operands, messages, out)

time: 257 us -> 276 us (1.074)
  local copies, waits for them, and re-layouts: 27.4 us -> 6.02 us
  Pallas kernels: 78.7 us -> 99.1 us
  waiting for transfers between devices: 113 us -> 129 us
  starting transfers between devices: 35.4 us -> 39.9 us
    unnamed x54 -> x30, local copies, waits for them, and re-layouts: 27.4 us -> 4.63 us
    all_to_all x3, waiting for transfers between devices: 2.06 us -> 21.3 us  [spread(): return lax.all_to_all(messages, 'elem', 0, 0, tiled=True)]
    ppermute x2, waiting for transfers between devices: 12.2 us -> 30.7 us  [neighbours(): left = lax.ppermute(tail, 'elem', [(i, i + 1) for i in range(size - 1)])]
    ppermute x8, waiting for transfers between devices: 92 us -> 73.6 us  [shift_by(): lax.ppermute(array, axis, [(i, (i + by) % size) for i in range(size)])]
    pallas_call x4 -> x5, Pallas kernels: 14.6 us -> 22.2 us  [the longest x3 14.6 us: sensor_call(): call(kernel, f'sensor_{low}', outs, [spec_hbm()] + [spec_vmem()] * (1 + l...]
    ppermute x2, waiting for transfers between devices: 5.07 us -> 1.79 us  [neighbours(): right = lax.ppermute(head, 'elem', [(i + 1, i) for i in range(size - 1)])]
    pallas_call x3, Pallas kernels: 14.1 us -> 17.4 us  [finish_call(): call(kernel, f'finish_{low}', f32(z.steps, tall, z.ax), [spec_vmem(), spe...]
    pallas_call x1, Pallas kernels: 13.4 us -> 16.2 us  [maps_call(): call(kernel, 'maps', outs, [spec_smem(), spec_vmem()] + [spec_any()] * le...]
  transfers between devices with their start and end apart: 16 -> 16, of which waited for: 11 -> 10; matrix products, arithmetic and copies ran while one was open for 0% -> 1% of each run, Pallas kernels for 24% -> 29%
where the time goes in v3:
time: 276 us; the launch traced here: 275 us
  waiting for transfers between devices  129 us (47%)
  Pallas kernels  99.1 us (36%)
  starting transfers between devices  39.9 us (14%)
  local copies, waits for them, and re-layouts  6.02 us (2%)
    ppermute x8, waiting for transfers between devices, shift_by(): lax.ppermute(array, axis, [(i, (i + by) % size) for i in range(size)])  73.6 us
    pallas_call x3, Pallas kernels, sweep_call(): call(kernel, f'sweep_{low}', outs, in_specs, out_specs, scratch, z.flops...  35.2 us
    ppermute x2, waiting for transfers between devices, neighbours(): left = lax.ppermute(tail, 'elem', [(i, i + 1) for i in range(size - 1)])  30.7 us
    all_to_all x3, waiting for transfers between devices, spread(): return lax.all_to_all(messages, 'elem', 0, 0, tiled=True)  21.3 us
    pallas_call x3, Pallas kernels, finish_call(): call(kernel, f'finish_{low}', f32(z.steps, tall, z.ax), [spec_vmem(), spe...  17.4 us
    all_to_all x3, starting transfers between devices, spread(): return lax.all_to_all(messages, 'elem', 0, 0, tiled=True)  17.4 us
    pallas_call x1, Pallas kernels, maps_call(): call(kernel, 'maps', outs, [spec_smem(), spec_vmem()] + [spec_any()] * le...  16.2 us
    pallas_call x3, Pallas kernels, sensor_call(): call(kernel, f'sensor_{low}', outs, [spec_hbm()] + [spec_vmem()] * (1 + l...  14.6 us
  transfers between devices with their start and end apart: 16, of which 10 were waited for; matrix products, arithmetic and copies ran while one was open for 1% of the time, Pallas kernels for 29%

profile of v3, /device:TPU:9, one launch (start us, length us, event | category | flops | bytes accessed | tf_op | source)
XLA Modules:
  0.0 275.2 jit_solution(3822522810042060201)
XLA Ops:
  0.0 5.1 %sensor_0.1 = (f32[3,8,256]{2,1,0:T(8,128)}, f32[3,8,128]{2,1,0:T(8,128)}, f32[3,8,128]{2,1,0:T(8,128)}) custom-call(f32[8,2000,128]{2,1,0:T(8,128)} %bitcast.11, f32[125,125]{1,0:T(8,128)} %modal_ref.5), custom_call_target="tpu_custom_call" | custom-call | flops 805306368 | bytes 3080192 | tf_op jit(solution)/shard_map/sensor_0/pallas_call | solution.py:160
  5.1 3.8 %collective-permute-start = (f32[3,8,128]{2,1,0:T(8,128)}, f32[3,8,128]{2,1,0:T(8,128)S(1)}, u32[]{:S(2)}, u32[]{:S(2)}) collective-permute-start(f32[3,8,128]{2,1,0:T(8,128)} %get-tuple-element.38), channel_id=1, source_target_pairs={{0,1},{1,2},{2,3},{3,4},{4,5},{5,6},{6,7},{8,9},{9,10},{10,11},{11... | collective-permute-start | bytes 36872 | tf_op jit(solution)/shard_map/ppermute | solution.py:570
  8.9 1.9 collective-permute-start.1
  10.8 4.3 %sensor_3.1 = (f32[1,8,256]{2,1,0:T(8,128)}, f32[1,8,128]{2,1,0:T(8,128)}, f32[1,8,128]{2,1,0:T(8,128)}) custom-call(f32[8,2000,128]{2,1,0:T(8,128)} %bitcast.12, f32[125,125]{1,0:T(8,128)} %modal_ref.5, f32[3,8,256]{2,1,0:T(8,128)} %get-tuple-element.37.refs_0_.refs_5_.refs_6_.refs_8_), custom_call_target="tpu_custom_call" | custom-call | flops 268435456 | bytes 1048576 | tf_op jit(solution)/shard_map/sensor_3/pallas_call | solution.py:160
  15.1 0.0 collective-permute-done.refs_6_.refs_9_
  15.1 0.0 copy-start.10
  15.2 0.0 collective-permute-done.1.refs_7_.refs_10_
  15.2 0.0 copy-start.11
  15.2 0.6 copy-done.10
  15.7 0.0 copy-done.11
  15.8 9.6 %sweep_1.1 = (f32[8,504,128]{2,1,0:T(8,128)}, f32[8,128,256]{2,1,0:T(8,128)}) custom-call(f32[8,2000,128]{2,1,0:T(8,128)} %bitcast.13, f32[8,2000,128]{2,1,0:T(8,128)} %bitcast.17, f32[125,125]{1,0:T(8,128)} %refs_2_.5, f32[125,64,125]{2,1,0:T(8,128)} %bitcast.24, f32[125,64,125]{2,1,0:T(8,128)} %bitcast.20, ...), custom_call_target="tpu_custom_call" | custom-call | flops 1610612736 | bytes 8257536 | tf_op jit(solution)/shard_map/sweep_1/pallas_call | solution.py:339
  25.4 5.5 %all-to-all-start.2 = ((f32[8,504,128]{2,1,0:T(8,128)}), f32[8,504,128]{2,1,0:T(8,128)S(1)}, u32[]{:S(2)}, u32[]{:S(2)}) async-start(f32[8,504,128]{2,1,0:T(8,128)} %get-tuple-element.67), calls=%async_computation.2 | async-start | bytes 4128768 | tf_op jit(solution)/shard_map/all_to_all | solution.py:576
  30.9 0.7 slice_bitcast_fusion
  31.6 2.2 collective-permute-start.5
  33.7 5.2 %sensor_4.1 = (f32[4,8,256]{2,1,0:T(8,128)}, f32[5,8,128]{2,1,0:T(8,128)}, f32[5,8,128]{2,1,0:T(8,128)}) custom-call(f32[8,2000,128]{2,1,0:T(8,128)} %bitcast.14, f32[125,125]{1,0:T(8,128)} %modal_ref.5, f32[1,8,256]{2,1,0:T(8,128)} %get-tuple-element.40.refs_8_.refs_0_.refs_5_, f32[8,128,256]{2,1,0:T(8,128)} %get-tuple-element.41.refs_0_.refs_1_.refs_10_), custom_call_target="tpu_custom_call" | custom-call | flops 1073741824 | bytes 4096000 | tf_op jit(solution)/shard_map/sensor_4/pallas_call | solution.py:160
  39.0 3.6 %collective-permute-start.2 = (f32[5,8,128]{2,1,0:T(8,128)}, f32[5,8,128]{2,1,0:T(8,128)S(1)}, u32[]{:S(2)}, u32[]{:S(2)}) collective-permute-start(f32[5,8,128]{2,1,0:T(8,128)} %get-tuple-element.44), channel_id=1, source_target_pairs={{0,1},{1,2},{2,3},{3,4},{4,5},{5,6},{6,7},{8,9},{9,10},{10,11},{11... | collective-permute-start | bytes 61448 | tf_op jit(solution)/shard_map/ppermute | solution.py:570
  42.6 1.9 collective-permute-start.3
  44.5 0.7 slice_bitcast_fusion.1
  45.2 0.0 collective-permute-start.4
  45.2 30.7 %collective-permute-done.2.refs_8_.refs_6_ = f32[5,8,128]{2,1,0:T(8,128)S(1)} collective-permute-done((f32[5,8,128]{2,1,0:T(8,128)}, f32[5,8,128]{2,1,0:T(8,128)S(1)}, u32[]{:S(2)}, u32[]{:S(2)}) %collective-permute-start.2) | collective-permute-done | bytes 20512 | tf_op jit(solution)/shard_map/ppermute | solution.py:570
  75.9 1.8 collective-permute-done.3.refs_9_.refs_7_
  77.7 0.0 copy-done.8
  77.7 0.6 copy-done.9
  78.3 13.2 %sweep_3.1 = (f32[8,752,128]{2,1,0:T(8,128)}, f32[8,128,256]{2,1,0:T(8,128)}) custom-call(f32[8,2000,128]{2,1,0:T(8,128)} %bitcast.15, f32[8,2000,128]{2,1,0:T(8,128)} %bitcast.18, f32[125,125]{1,0:T(8,128)} %refs_2_.5, f32[125,64,125]{2,1,0:T(8,128)} %bitcast.25, f32[125,64,125]{2,1,0:T(8,128)} %bitcast.21, ...), custom_call_target="tpu_custom_call" | custom-call | flops 2415919104 | bytes 12451840 | tf_op jit(solution)/shard_map/sweep_3/pallas_call | solution.py:339
  91.5 0.0 collective-permute-done.5.refs_12_
  91.5 0.0 copy-start.12
  91.5 0.0 collective-permute-done.4.refs_11_
  91.5 0.0 copy-start.13
  91.5 0.6 copy-done.12
  92.1 0.0 copy-done.13
  92.1 12.4 %sweep_6.1 = (f32[8,504,128]{2,1,0:T(8,128)}, f32[8,128,256]{2,1,0:T(8,128)}, f32[8,128,256]{2,1,0:T(8,128)}, f32[8,752,128]{2,1,0:T(8,128)}) custom-call(f32[8,2000,128]{2,1,0:T(8,128)} %bitcast.16, f32[8,2000,128]{2,1,0:T(8,128)} %bitcast.19, f32[125,125]{1,0:T(8,128)} %refs_2_.5, f32[125,64,125]{2,1,0:T(8,128)} %bitcast.26, ...), custom_call_target="tpu_custom_call", output_to_operand_aliasing={{3}: (14, {})} | custom-call | flops 2415919104 | bytes 8257536 | tf_op jit(solution)/shard_map/sweep_6/pallas_call | solution.py:339
  104.5 0.0 all-to-all-done.2.message_ref
  104.5 0.0 copy-start.1
  104.5 1.3 copy-done.1
  105.9 4.0 %all-to-all-start.1 = ((f32[8,752,128]{2,1,0:T(8,128)}), f32[8,752,128]{2,1,0:T(8,128)S(1)}, u32[]{:S(2)}, u32[]{:S(2)}) async-start(f32[8,752,128]{2,1,0:T(8,128)} %get-tuple-element.66), calls=%async_computation.1 | async-start | bytes 6160384 | tf_op jit(solution)/shard_map/all_to_all | solution.py:576
  109.9 16.2 %maps.1 = (f32[8,128,128]{2,1,0:T(8,128)}, f32[8,128,128]{2,1,0:T(8,128)}, f32[8,128,128]{2,1,0:T(8,128)}, f32[8,128,128]{2,1,0:T(8,128)}, f32[8,128,128]{2,1,0:T(8,128)}, /*index=5*/f32[128,128]{1,0:T(8,128)}) custom-call(s32[1]{0:T(128)} %bitcast.me_ref.refs_0_, f32[125,64,125]{2,1,0:T(8,128)} %bitcast.23, ...), custom_call_target="tpu_custom_call" | custom-call | flops 1207959552 | bytes 4194304 | tf_op jit(solution)/shard_map/maps/pallas_call | solution.py:385
  126.1 4.3 %chain.1 = (f32[8,128,256]{2,1,0:T(8,128)}, f32[128,384]{1,0:T(8,128)}) custom-call(f32[8,128,256]{2,1,0:T(8,128)} %get-tuple-element.48.start_ref.refs_8_, f32[8,128,256]{2,1,0:T(8,128)} %get-tuple-element.49.end_ref, f32[8,128,128]{2,1,0:T(8,128)} %get-tuple-element.50.tail_ref, f32[8,128,128]{2,1,0:T(8,128)} %get-tuple-element.51.whole_ref, ...), custom_call_target="tpu_custom_call" | custom-call | flops 536870912 | bytes 4194304 | tf_op jit(solution)/shard_map/chain/pallas_call | solution.py:411
  130.4 2.2 collective-permute-start.8
  132.6 0.2 collective-permute-start.7
  132.8 0.3 collective-permute-start.6
  133.1 0.6 pad_add_fusion.refs_0_
  133.8 3.1 %collective-permute-done.8.refs_4_ = f32[128,384]{1,0:T(8,128)S(1)} collective-permute-done((f32[128,384]{1,0:T(8,128)}, f32[128,384]{1,0:T(8,128)S(1)}, u32[]{:S(2)}, u32[]{:S(2)}) %collective-permute-start.8) | collective-permute-done | bytes 196640 | tf_op jit(solution)/shard_map/ppermute | solution.py:565
  136.9 2.6 collective-permute-done.7.refs_3_
  139.5 2.6 collective-permute-done.6.refs_2_
  142.1 0.0 copy-done.6
  142.1 5.4 %first.1 = (f32[4,256,128]{2,1,0:T(8,128)}, f32[4,256,128]{2,1,0:T(8,128)}) custom-call(s32[2]{0:T(128)} %pad_add_fusion.refs_0_, f32[128,384]{1,0:T(8,128)} %get-tuple-element.53.refs_1_, f32[128,384]{1,0:T(8,128)} %collective-permute-done.6.refs_2_, f32[128,384]{1,0:T(8,128)} %copy-done.7, f32[128,384]{1,0:T(8,128)} %copy-done.6, ...), custom_call_target="tpu_custom_call" | custom-call | flops 805306368 | bytes 4194304 | tf_op jit(solution)/shard_map/first/pallas_call | solution.py:449
  147.5 2.9 %collective-permute-start.9 = (f32[4,256,128]{2,1,0:T(8,128)}, f32[4,256,128]{2,1,0:T(8,128)S(1)}, u32[]{:S(2)}, u32[]{:S(2)}) collective-permute-start(f32[4,256,128]{2,1,0:T(8,128)} %get-tuple-element.58), channel_id=1, source_target_pairs={{0,1},{1,0},{2,3},{3,2},{4,5},{5,4},{6,7},{7,6},{8,9},{9,8},{10,11... | collective-permute-start | bytes 1572872 | tf_op jit(solution)/shard_map/ppermute | solution.py:636
  150.4 1.7 collective-permute-done.9.got_ref
  152.1 0.8 copy-done.2
  153.0 2.2 couple.1
  155.2 21.3 %all-to-all-done.1.message_ref = f32[8,752,128]{2,1,0:T(8,128)S(1)} async-done(((f32[8,752,128]{2,1,0:T(8,128)}), f32[8,752,128]{2,1,0:T(8,128)S(1)}, u32[]{:S(2)}, u32[]{:S(2)}) %all-to-all-start.1) | async-done | bytes 3080224 | tf_op jit(solution)/shard_map/all_to_all | solution.py:576
  176.5 7.8 %all-to-all-start = ((f32[8,504,128]{2,1,0:T(8,128)}), f32[8,504,128]{2,1,0:T(8,128)}, u32[]{:S(2)}, u32[]{:S(2)}) async-start(f32[8,504,128]{2,1,0:T(8,128)} %get-tuple-element.65), calls=%async_computation | async-start | bytes 4128768 | tf_op jit(solution)/shard_map/all_to_all | solution.py:576
  184.3 1.2 collective-permute-start.10
  185.5 1.0 collective-permute-start.11
  186.4 1.4 collective-permute-start.12
  187.8 58.1 %collective-permute-done.10.refs_2_ = f32[2,256,128]{2,1,0:T(8,128)S(1)} collective-permute-done((f32[2,256,128]{2,1,0:T(8,128)}, f32[2,256,128]{2,1,0:T(8,128)S(1)}, u32[]{:S(2)}, u32[]{:S(2)}) %collective-permute-start.10) | collective-permute-done | bytes 262176 | tf_op jit(solution)/shard_map/ppermute | solution.py:565
  245.9 5.6 %collective-permute-done.11.refs_3_ = f32[2,256,128]{2,1,0:T(8,128)S(1)} collective-permute-done((f32[2,256,128]{2,1,0:T(8,128)}, f32[2,256,128]{2,1,0:T(8,128)S(1)}, u32[]{:S(2)}, u32[]{:S(2)}) %collective-permute-start.11) | collective-permute-done | bytes 262176 | tf_op jit(solution)/shard_map/ppermute | solution.py:565
  251.5 1.6 collective-permute-done.12.refs_4_
  253.2 0.7 copy-done.5
  253.8 3.7 %finish_0.1 = (f32[8,2000,128]{2,1,0:T(8,128)}, bf16[8,256,256]{2,1,0:T(8,128)(2,1)}) custom-call(s32[1]{0:T(128)} %bitcast.me_ref.refs_0_, f32[2,256,128]{2,1,0:T(8,128)} %get-tuple-element.60.refs_1_, f32[2,256,128]{2,1,0:T(8,128)} %copy-done.3, f32[2,256,128]{2,1,0:T(8,128)} %copy-done.4, f32[2,256,128]{2,1,0:T(8,128)} %copy-done.5), custom_call_target="tpu_custom_call" | custom-call | bytes 2048000 | tf_op jit(solution)/shard_map/finish_0/pallas_call | solution.py:506
  257.6 5.6 %finish_1.1._ = f32[8,2000,128]{2,1,0:T(8,128)} custom-call(f32[8,128,128]{2,1,0:T(8,128)} %get-tuple-element.42.own_ref, bf16[8,256,256]{2,1,0:T(8,128)(2,1)} %get-tuple-element.64.operand_ref, f32[8,504,128]{2,1,0:T(8,128)} %copy-done.1, f32[8,2000,128]{2,1,0:T(8,128)} %get-tuple-element.68._), custom_call_target="tpu_custom_call", output_to_operand_aliasing={{}: (3, {})} | custom-call | flops 536870912 | bytes 4096000 | tf_op jit(solution)/shard_map/finish_1/pallas_call | solution.py:545
  263.2 6.1 %finish_3.1._ = f32[8,2000,128]{2,1,0:T(8,128)} custom-call(f32[8,128,128]{2,1,0:T(8,128)} %get-tuple-element.42.own_ref, bf16[8,256,256]{2,1,0:T(8,128)(2,1)} %get-tuple-element.64.operand_ref, f32[8,752,128]{2,1,0:T(8,128)} %copy-done, f32[8,2000,128]{2,1,0:T(8,128)} %finish_1.1._), custom_call_target="tpu_custom_call", output_to_operand_aliasing={{}: (3, {})} | custom-call | flops 805306368 | bytes 6144000 | tf_op jit(solution)/shard_map/finish_3/pallas_call | solution.py:545
  269.4 0.0 all-to-all-done.message_ref
  269.4 5.6 %finish_6.1 = f32[8,2000,128]{2,1,0:T(8,128)} custom-call(f32[8,128,128]{2,1,0:T(8,128)} %get-tuple-element.42.own_ref, bf16[8,256,256]{2,1,0:T(8,128)(2,1)} %get-tuple-element.64.operand_ref, f32[8,504,128]{2,1,0:T(8,128)} %all-to-all-done.message_ref, f32[8,2000,128]{2,1,0:T(8,128)} %finish_3.1._), custom_call_target="tpu_custom_call", output_to_operand_aliasing={{}: (3, {})} | custom-call | flops 536870912 | bytes 4096000 | tf_op jit(solution)/shard_map/finish_6/pallas_call | solution.py:545
  (15 shorter events, 0.0 us)
Async XLA Ops:
  5.1 10.0 %collective-permute-start = (f32[3,8,128]{2,1,0:T(8,128)}, f32[3,8,128]{2,1,0:T(8,128)S(1)}, u32[]{:S(2)}, u32[]{:S(2)}) collective-permute-start(f32[3,8,128]{2,1,0:T(8,128)} %get-tuple-element.38), channel_id=1, source_target_pairs={{0,1},{1,2},{2,3},{3,4},{4,5},{5,6},{6,7},{8,9},{9,10},{10,11},{11... | collective-permute-start | bytes 36872 | tf_op jit(solution)/shard_map/ppermute | solution.py:570
  8.9 6.3 %collective-permute-start.1 = (f32[3,8,128]{2,1,0:T(8,128)}, f32[3,8,128]{2,1,0:T(8,128)S(1)}, u32[]{:S(2)}, u32[]{:S(2)}) collective-permute-start(f32[3,8,128]{2,1,0:T(8,128)} %get-tuple-element.39), channel_id=1, source_target_pairs={{1,0},{2,1},{3,2},{4,3},{5,4},{6,5},{7,6},{9,8},{10,9},{11,10},{12... | collective-permute-start | bytes 36872 | tf_op jit(solution)/shard_map/ppermute | solution.py:571
  15.1 0.6 copy-start.10
  15.2 0.6 copy-start.11
  25.4 79.2 %all-to-all-start.2 = ((f32[8,504,128]{2,1,0:T(8,128)}), f32[8,504,128]{2,1,0:T(8,128)S(1)}, u32[]{:S(2)}, u32[]{:S(2)}) async-start(f32[8,504,128]{2,1,0:T(8,128)} %get-tuple-element.67), calls=%async_computation.2 | async-start | bytes 4128768 | tf_op jit(solution)/shard_map/all_to_all | solution.py:576
  31.6 59.9 %collective-permute-start.5 = (f32[1,256]{1,0:T(1,128)S(1)}, f32[1,256]{1,0:T(1,128)S(1)}, u32[]{:S(2)}, u32[]{:S(2)}) collective-permute-start(f32[1,256]{1,0:T(1,128)S(1)} %slice_bitcast_fusion), channel_id=1, source_target_pairs={{0,24},{8,0},{16,8},{24,16},{1,25},{9,1},{17,9},{25,17},{2,26},{10... | collective-permute-start | bytes 3080 | tf_op jit(solution)/shard_map/ppermute | solution.py:565
  39.0 36.9 %collective-permute-start.2 = (f32[5,8,128]{2,1,0:T(8,128)}, f32[5,8,128]{2,1,0:T(8,128)S(1)}, u32[]{:S(2)}, u32[]{:S(2)}) collective-permute-start(f32[5,8,128]{2,1,0:T(8,128)} %get-tuple-element.44), channel_id=1, source_target_pairs={{0,1},{1,2},{2,3},{3,4},{4,5},{5,6},{6,7},{8,9},{9,10},{10,11},{11... | collective-permute-start | bytes 61448 | tf_op jit(solution)/shard_map/ppermute | solution.py:570
  42.6 35.1 %collective-permute-start.3 = (f32[5,8,128]{2,1,0:T(8,128)}, f32[5,8,128]{2,1,0:T(8,128)S(1)}, u32[]{:S(2)}, u32[]{:S(2)}) collective-permute-start(f32[5,8,128]{2,1,0:T(8,128)} %get-tuple-element.45), channel_id=1, source_target_pairs={{1,0},{2,1},{3,2},{4,3},{5,4},{6,5},{7,6},{9,8},{10,9},{11,10},{12... | collective-permute-start | bytes 61448 | tf_op jit(solution)/shard_map/ppermute | solution.py:571
  45.2 46.3 %collective-permute-start.4 = (f32[1,256]{1,0:T(1,128)S(1)}, f32[1,256]{1,0:T(1,128)S(1)}, u32[]{:S(2)}, u32[]{:S(2)}) collective-permute-start(f32[1,256]{1,0:T(1,128)S(1)} %slice_bitcast_fusion.1), channel_id=1, source_target_pairs={{0,8},{8,16},{16,24},{24,0},{1,9},{9,17},{17,25},{25,1},{2,10},{10... | collective-permute-start | bytes 3080 | tf_op jit(solution)/shard_map/ppermute | solution.py:565
  75.9 1.8 copy-start.8
  77.7 0.6 copy-start.9
  91.5 0.6 copy-start.12
  91.5 0.6 copy-start.13
  104.5 1.3 copy-start.1
  105.9 70.6 %all-to-all-start.1 = ((f32[8,752,128]{2,1,0:T(8,128)}), f32[8,752,128]{2,1,0:T(8,128)S(1)}, u32[]{:S(2)}, u32[]{:S(2)}) async-start(f32[8,752,128]{2,1,0:T(8,128)} %get-tuple-element.66), calls=%async_computation.1 | async-start | bytes 6160384 | tf_op jit(solution)/shard_map/all_to_all | solution.py:576
  130.4 6.4 %collective-permute-start.8 = (f32[128,384]{1,0:T(8,128)}, f32[128,384]{1,0:T(8,128)S(1)}, u32[]{:S(2)}, u32[]{:S(2)}) collective-permute-start(f32[128,384]{1,0:T(8,128)} %get-tuple-element.53.refs_1_), channel_id=1, source_target_pairs={{0,24},{8,0},{16,8},{24,16},{1,25},{9,1},{17,9},{25,17},{2,26},{10... | collective-permute-start | bytes 589832 | tf_op jit(solution)/shard_map/ppermute | solution.py:565
  132.6 6.9 %collective-permute-start.7 = (f32[128,384]{1,0:T(8,128)}, f32[128,384]{1,0:T(8,128)S(1)}, u32[]{:S(2)}, u32[]{:S(2)}) collective-permute-start(f32[128,384]{1,0:T(8,128)} %get-tuple-element.53.refs_1_), channel_id=1, source_target_pairs={{0,16},{8,24},{16,0},{24,8},{1,17},{9,25},{17,1},{25,9},{2,18},{10... | collective-permute-start | bytes 589832 | tf_op jit(solution)/shard_map/ppermute | solution.py:565
  132.8 9.3 %collective-permute-start.6 = (f32[128,384]{1,0:T(8,128)}, f32[128,384]{1,0:T(8,128)}, u32[]{:S(2)}, u32[]{:S(2)}) collective-permute-start(f32[128,384]{1,0:T(8,128)} %get-tuple-element.53.refs_1_), channel_id=1, source_target_pairs={{0,8},{8,16},{16,24},{24,0},{1,9},{9,17},{17,25},{25,1},{2,10},{10... | collective-permute-start | bytes 589832 | tf_op jit(solution)/shard_map/ppermute | solution.py:565
  136.9 5.2 %copy-start.6 = (f32[128,384]{1,0:T(8,128)}, f32[128,384]{1,0:T(8,128)S(1)}, u32[]{:S(2)}) copy-start(f32[128,384]{1,0:T(8,128)S(1)} %collective-permute-done.8.refs_4_) | copy-start | bytes 589828
  139.5 2.6 copy-start.7
  147.5 4.7 %collective-permute-start.9 = (f32[4,256,128]{2,1,0:T(8,128)}, f32[4,256,128]{2,1,0:T(8,128)S(1)}, u32[]{:S(2)}, u32[]{:S(2)}) collective-permute-start(f32[4,256,128]{2,1,0:T(8,128)} %get-tuple-element.58), channel_id=1, source_target_pairs={{0,1},{1,0},{2,3},{3,2},{4,5},{5,4},{6,7},{7,6},{8,9},{9,8},{10,11... | collective-permute-start | bytes 1572872 | tf_op jit(solution)/shard_map/ppermute | solution.py:636
  152.1 0.8 copy-start.2
  155.2 31.3 %copy-start.14 = (f32[2,256,128]{2,1,0:T(8,128)S(1)}, f32[2,256,128]{2,1,0:T(8,128)}, u32[]{:S(2)}) copy-start(f32[2,256,128]{2,1,0:T(8,128)} %get-tuple-element.63) | copy-start | bytes 786436
  176.5 86.8 %copy-start = (f32[8,752,128]{2,1,0:T(8,128)}, f32[8,752,128]{2,1,0:T(8,128)S(1)}, u32[]{:S(2)}) copy-start(f32[8,752,128]{2,1,0:T(8,128)S(1)} %all-to-all-done.1.message_ref) | copy-start | bytes 9240580
  176.5 92.9 %all-to-all-start = ((f32[8,504,128]{2,1,0:T(8,128)}), f32[8,504,128]{2,1,0:T(8,128)}, u32[]{:S(2)}, u32[]{:S(2)}) async-start(f32[8,504,128]{2,1,0:T(8,128)} %get-tuple-element.65), calls=%async_computation | async-start | bytes 4128768 | tf_op jit(solution)/shard_map/all_to_all | solution.py:576
  184.3 61.7 %collective-permute-start.10 = (f32[2,256,128]{2,1,0:T(8,128)}, f32[2,256,128]{2,1,0:T(8,128)S(1)}, u32[]{:S(2)}, u32[]{:S(2)}) collective-permute-start(f32[2,256,128]{2,1,0:T(8,128)} %get-tuple-element.61), channel_id=1, source_target_pairs={{0,2},{1,3},{2,4},{3,5},{4,6},{5,7},{6,0},{7,1},{8,10},{9,11},{10,... | collective-permute-start | bytes 786440 | tf_op jit(solution)/shard_map/ppermute | solution.py:565
  185.5 66.1 %collective-permute-start.11 = (f32[2,256,128]{2,1,0:T(8,128)}, f32[2,256,128]{2,1,0:T(8,128)S(1)}, u32[]{:S(2)}, u32[]{:S(2)}) collective-permute-start(f32[2,256,128]{2,1,0:T(8,128)} %get-tuple-element.62), channel_id=1, source_target_pairs={{0,4},{1,5},{2,6},{3,7},{4,0},{5,1},{6,2},{7,3},{8,12},{9,13},{10,... | collective-permute-start | bytes 786440 | tf_op jit(solution)/shard_map/ppermute | solution.py:565
  186.4 66.7 %collective-permute-start.12 = (f32[2,256,128]{2,1,0:T(8,128)S(1)}, f32[2,256,128]{2,1,0:T(8,128)S(1)}, u32[]{:S(2)}, u32[]{:S(2)}) collective-permute-start(f32[2,256,128]{2,1,0:T(8,128)S(1)} %copy-done.14), channel_id=1, source_target_pairs={{0,6},{1,7},{2,0},{3,1},{4,2},{5,3},{6,4},{7,5},{8,14},{9,15},{10,... | collective-permute-start | bytes 786440 | tf_op jit(solution)/shard_map/ppermute | solution.py:565
  245.9 7.2 %copy-start.3 = (f32[2,256,128]{2,1,0:T(8,128)}, f32[2,256,128]{2,1,0:T(8,128)S(1)}, u32[]{:S(2)}) copy-start(f32[2,256,128]{2,1,0:T(8,128)S(1)} %collective-permute-done.10.refs_2_) | copy-start | bytes 786436
  251.5 1.6 copy-start.4
  253.2 0.7 copy-start.5

commit v4 on v1

v4 whole, which is shorter than its diff:
```python
import functools

import jax
import jax.numpy as jnp
from jax import lax
from jax.experimental import pallas as pl
from jax.experimental.pallas import tpu as pltpu
from jax.sharding import PartitionSpec as P

ORDER = 4
F32 = jnp.float32
BF16 = jnp.bfloat16
MIB = 1024 * 1024
TILE = 8
LANES = 128


def operand_left(a):
    high = a.astype(BF16)
    low = (a - high.astype(F32)).astype(BF16)
    return jnp.concatenate([jnp.concatenate([high, high], axis=1), jnp.concatenate([low, low], axis=1)], axis=0)


def operand_right(x):
    high = x.astype(BF16)
    return jnp.concatenate([high, (x - high.astype(F32)).astype(BF16)], axis=0)


def product(left, right):
    both = jnp.dot(left, right, preferred_element_type=F32)
    half = left.shape[0] // 2
    return both[:half] + both[half:]


def spec_any():
    return pl.BlockSpec(memory_space=pl.ANY)


def spec_hbm():
    return pl.BlockSpec(memory_space=pltpu.HBM)


def spec_vmem():
    return pl.BlockSpec(memory_space=pltpu.VMEM)


def spec_smem():
    return pl.BlockSpec(memory_space=pltpu.SMEM)


def call(kernel, name, outs, in_specs, out_specs, scratch, flops, nbytes, aliases=None, limit=57):
    return pl.pallas_call(
        kernel,
        name=name,
        out_shape=outs,
        in_specs=in_specs,
        out_specs=out_specs,
        scratch_shapes=scratch,
        input_output_aliases=aliases or {},
        compiler_params=pltpu.CompilerParams(vmem_limit_bytes=limit * MIB),
        cost_estimate=pl.CostEstimate(flops=int(flops), bytes_accessed=int(nbytes), transcendentals=0),
    )


def f32(*shape):
    return jax.ShapeDtypeStruct(shape, F32)


def up(value, unit):
    return -(-value // unit) * unit


class Sizes:
    def __init__(self, state, segments, groups):
        count, self.nodes, self.rows, self.ax = state.shape
        self.count = count
        self.segments = segments
        self.groups = groups
        self.steps = count // segments
        self.cols = self.rows * self.ax
        self.height = self.nodes * self.rows
        self.pad = up(self.nodes, LANES)
        self.spill = up((self.pad - self.nodes) * self.rows, TILE)
        self.flops = 2 * 4 * self.pad * self.pad * self.cols

    def window(self, low, high):
        first = low * self.height // TILE * TILE
        return first, up(high * self.height, TILE) - first

    def message(self, count):
        return up(count * self.height, TILE)

    def rows_masked(self, x):
        cut = self.nodes // TILE * TILE
        rest = x[cut:]
        inside = lax.broadcasted_iota(jnp.int32, rest.shape, 0) < self.nodes - cut
        return jnp.concatenate([x[:cut], jnp.where(inside, rest, 0.0)], axis=0)

    def square(self, x):
        x = jnp.concatenate([x, jnp.zeros((self.nodes, self.pad - self.nodes), F32)], axis=1)
        return jnp.concatenate([x, jnp.zeros((self.pad - self.nodes, self.pad), F32)], axis=0)


def read_field(z, ref, lead, offset):
    parts = [ref[lead + (pl.ds(offset + j, z.pad, stride=z.rows), slice(None))] for j in range(z.rows)]
    return z.rows_masked(jnp.concatenate(parts, axis=1))


def read_exact(z, ref, lead, offset):
    parts = [ref[lead + (pl.ds(offset + j, z.nodes, stride=z.rows), slice(None))] for j in range(z.rows)]
    return jnp.concatenate(parts, axis=1)


def write_field(z, ref, lead, offset, value):
    for j in range(z.rows):
        rows = pl.ds(offset + j, z.nodes, stride=z.rows)
        ref[lead + (rows, slice(None))] = value[: z.nodes, j * z.ax : (j + 1) * z.ax]


def read_matrix(z, ref, k):
    return z.square(ref[:, k, :])


def sensor_call(z, state, to_modal):
    batch = 4 if z.segments % 4 == 0 else 1
    tall = z.steps * z.height

    def kernel(state_ref, modal_ref, sensor_ref, head_ref, tail_ref, buf, modal_buf, sem, modal_sem):
        modal_copy = pltpu.make_async_copy(modal_ref, modal_buf, modal_sem)
        modal_copy.start()
        copies = [
            pltpu.make_async_copy(state_ref.at[e], buf.at[e, pl.ds(0, tall)], sem.at[e]) for e in range(z.segments)
        ]
        for copy in copies:
            copy.start()
        modal_copy.wait()
        matrix = operand_left(z.square(modal_buf[...]))
        for e0 in range(0, z.segments, batch):
            for e in range(e0, e0 + batch):
                copies[e].wait()
            for e in range(e0, e0 + batch):
                for i in range(z.steps):
                    modal = product(matrix, operand_right(read_field(z, buf, (e,), i * z.height)))
                    squares = modal * modal
                    lower = jnp.sum(squares[: ORDER**3], axis=0, keepdims=True)
                    upper = jnp.sum(squares[ORDER**3 :], axis=0, keepdims=True)
                    sensor = (upper / z.nodes) / ((lower + upper) / z.nodes + 1e-6)
                    sensor_ref[i, e : e + 1, :] = sensor
                    head_ref[i, e : e + 1, :] = sensor[:, : z.ax]
                    tail_ref[i, e : e + 1, :] = sensor[:, z.cols - z.ax :]

    outs = [f32(z.steps, z.segments, z.cols)] + [f32(z.steps, z.segments, z.ax)] * 2
    return call(
        kernel,
        "sensor",
        outs,
        [spec_hbm()] * 2,
        [spec_vmem()] * 3,
        [
            pltpu.VMEM((z.segments, tall + z.spill, z.ax), F32),
            pltpu.VMEM((z.nodes, z.nodes), F32),
            pltpu.SemaphoreType.DMA((z.segments,)),
            pltpu.SemaphoreType.DMA,
        ],
        z.flops * z.steps * z.segments,
        4 * z.segments * tall * z.ax,
    )(state, to_modal)


def smoothed(z, sensor, before, after, left, right):
    inner = sensor[:, : z.cols - z.ax]
    outer = sensor[:, z.ax :]
    from_left = jnp.concatenate([left, inner], axis=1)
    from_right = jnp.concatenate([outer, right], axis=1)
    return (4.0 * sensor + before + after + from_left + from_right) / 8.0


def sweep_call(z, chunk, mode, me, state, rhs, viscous, gain, inverse, sensors, lefts, rights, ring, carry, after):
    low, high = chunk
    opened = mode == "open"
    first, size = z.window(low, high)
    count = high - low
    first0, size0 = z.window(0, 1)
    steps = list(range(low, high)) + ([0] if opened else [])
    has_carry = carry is not None
    needs_gain = has_carry or count > 1
    message = z.message(count + (1 if opened else 0))
    edge_outs = low == 1
    pairs = z.segments // 2
    batch = next(n for n in (4, 8, z.segments) if z.segments % n == 0 and n * z.steps % TILE == 0)

    def kernel(*refs):
        me_ref, state_ref, rhs_ref, viscous_ref, inverse_ref, gain_ref, sensor_ref, left_ref, right_ref = refs[:9]
        refs = refs[9:]
        if opened:
            before_ref, behind_ref, refs = refs[0], refs[1], refs[2:]
        if has_carry:
            carry_ref, refs = refs[0], refs[1:]
        refs = refs[len(after) :]
        if mode == "pairs":
            keep_ref, give_ref, refs = refs[0], refs[1], refs[2:]
        else:
            out_ref, refs = refs[0], refs[1:]
        end_ref, refs = refs[0], refs[1:]
        if opened:
            start_ref, refs = refs[0], refs[1:]
        if edge_outs:
            low_ref, high_ref, refs = refs[0], refs[1], refs[2:]
        state_buf, rhs_buf, inverse_buf, gain_buf, viscous_buf, smooth_buf, stage, sem, matrix_sem, out_sem = refs[:10]
        if opened:
            state0, rhs0 = refs[10:]
        viscous_copy = pltpu.make_async_copy(viscous_ref, viscous_buf, out_sem.at[0])
        viscous_copy.start()
        copies = [[] for _ in range(z.segments)]
        for s0 in range(0, z.segments, batch):
            for s in range(s0, s0 + batch):
                moves = [
                    (state_ref.at[s, pl.ds(first, size)], state_buf.at[s, pl.ds(0, size)]),
                    (rhs_ref.at[s, pl.ds(first, size)], rhs_buf.at[s, pl.ds(0, size)]),
                ]
                if opened:
                    moves.append((state_ref.at[s, pl.ds(first0, size0)], state0.at[s, pl.ds(0, size0)]))
                    moves.append((rhs_ref.at[s, pl.ds(first0, size0)], rhs0.at[s, pl.ds(0, size0)]))
                for n, (source, target) in enumerate(moves):
                    copies[s].append(pltpu.make_async_copy(source, target, sem.at[s, n]))
            part = pl.ds(s0 * z.steps, batch * z.steps)
            sources = [(inverse_ref, inverse_buf)] + ([(gain_ref, gain_buf)] if needs_gain else [])
            for n, (source, target) in enumerate(sources):
                copies[s0].append(pltpu.make_async_copy(source.at[:, part], target.at[:, part], matrix_sem.at[s0, n]))
            for s in range(s0, s0 + batch):
                for copy in copies[s]:
                    copy.start()
        for n, i in enumerate(steps):
            before = sensor_ref[(i - 1) % z.steps]
            later = sensor_ref[(i + 1) % z.steps]
            if i == 0:
                before = jnp.concatenate([before_ref[...], before[: z.segments - 1]], axis=0)
            if i == z.steps - 1:
                later = jnp.concatenate([later[1:], behind_ref[...]], axis=0)
            smooth_buf[n] = smoothed(z, sensor_ref[i], before, later, left_ref[i], right_ref[i])
        if edge_outs:
            low_ref[...] = sensor_ref[0, :1]
            high_ref[...] = sensor_ref[z.steps - 1, z.segments - 1 :]
        viscous_copy.wait()
        operator = operand_left(z.square(viscous_buf[...]))
        sends = []
        for s0 in range(0, z.segments, batch):
            group = range(s0, s0 + batch)
            for s in group:
                for copy in copies[s]:
                    copy.wait()
            fields = [carry_ref[s] if has_carry else None for s in group]
            for n, i in enumerate(steps):
                bufs = (state0, rhs0, -first0) if i == 0 else (state_buf, rhs_buf, i * z.height - first)
                moved = [product(operator, operand_right(read_field(z, bufs[0], (s,), bufs[2]))) for s in group]
                forces = [
                    operand_right(read_field(z, bufs[1], (s,), bufs[2]) + smooth_buf[n, s : s + 1, :] * value)
                    for s, value in zip(group, moved)
                ]
                values = [
                    product(operand_left(read_matrix(z, inverse_buf, s * z.steps + i)), force)
                    for s, force in zip(group, forces)
                ]
                if i == 0:
                    for s, value in zip(group, values):
                        start_ref[s] = value
                    continue
                if fields[0] is not None:
                    swept = [
                        product(operand_left(read_matrix(z, gain_buf, s * z.steps + i)), operand_right(field))
                        for s, field in zip(group, fields)
                    ]
                    values = [value + more for value, more in zip(values, swept)]
                fields = values
                for s, value in zip(group, values):
                    write_field(z, stage, (s,), n * z.height, value)
            for s, value in zip(group, fields):
                end_ref[s] = value
                if mode != "pairs":
                    copy = pltpu.make_async_copy(stage.at[s], out_ref.at[s], out_sem.at[s])
                    copy.start()
                    sends.append(copy)
                    continue
                side = lax.rem(me_ref[0], 2)
                place = lax.rem(s // 2 - me_ref[0] // 2 + pairs, pairs)
                own = side == s % 2

                @pl.when(own)
                def _(s=s, place=place):
                    pltpu.make_async_copy(stage.at[s], keep_ref.at[place], out_sem.at[s]).start()

                @pl.when(jnp.logical_not(own))
                def _(s=s, place=place):
                    pltpu.make_async_copy(stage.at[s], give_ref.at[place], out_sem.at[s]).start()

                sends.append(pltpu.make_async_copy(stage.at[s], keep_ref.at[place], out_sem.at[s]))
        for copy in sends:
            copy.wait()

    field = f32(z.segments, z.pad, z.cols)
    outs = [f32(pairs, message, z.ax)] * 2 if mode == "pairs" else [f32(z.segments, message, z.ax)]
    out_specs = [spec_hbm()] * len(outs)
    more = [field] * (2 if opened else 1) + ([f32(1, z.cols)] * 2 if edge_outs else [])
    operands = [me, state, rhs, viscous, inverse, gain, sensors, lefts, rights]
    in_specs = [spec_smem()] + [spec_hbm()] * 5 + [spec_vmem()] * 3
    extra = (list(ring) if opened else []) + ([carry] if has_carry else [])
    scratch = [
        pltpu.VMEM((z.segments, size + z.spill, z.ax), F32),
        pltpu.VMEM((z.segments, size + z.spill, z.ax), F32),
        pltpu.VMEM(inverse.shape, F32),
        pltpu.VMEM(gain.shape, F32),
        pltpu.VMEM(viscous.shape, F32),
        pltpu.VMEM((len(steps), z.segments, z.cols), F32),
        pltpu.VMEM((z.segments, message, z.ax), F32),
        pltpu.SemaphoreType.DMA((z.segments, 4)),
        pltpu.SemaphoreType.DMA((z.segments, 2)),
        pltpu.SemaphoreType.DMA((z.segments,)),
    ]
    if opened:
        scratch += [pltpu.VMEM((z.segments, size0 + z.spill, z.ax), F32)] * 2
    return call(
        kernel,
        f"sweep_{low}",
        outs + more,
        in_specs + [spec_vmem()] * len(extra) + [spec_any()] * len(after),
        out_specs + [spec_vmem()] * len(more),
        scratch,
        z.flops * len(steps) * z.segments * 3,
        4 * z.segments * size * z.ax * 4,
    )(*operands, *extra, *after)


def maps_call(z, me, gain, after):
    def kernel(me_ref, gain_ref, *refs):
        own_ref, head_ref, tail_ref, whole_ref, prefix_ref, group_ref, gain_buf, kept, sem = refs[len(after) :]
        copy = pltpu.make_async_copy(gain_ref, gain_buf, sem)
        copy.start()
        copy.wait()

        def times(a, b):
            return product(operand_left(a), operand_right(b))

        values = [read_matrix(z, gain_buf, e * z.steps + 1) for e in range(z.segments)]
        for i in range(1, z.steps):
            if i > 1:
                values = [
                    times(read_matrix(z, gain_buf, e * z.steps + i), values[e]) for e in range(z.segments)
                ]
            for e in range(z.segments):
                kept[e, i] = values[e]
        heads = [read_matrix(z, gain_buf, e * z.steps) for e in range(z.segments)]
        for e in range(z.segments):
            kept[e, 0] = heads[e]
            head_ref[e] = heads[e]
            tail_ref[e] = values[e]
            whole_ref[e] = times(values[e], heads[e])
        own_ref[...] = kept[me_ref[0]]
        value = whole_ref[0]
        prefix_ref[0] = value
        for e in range(1, z.segments):
            prefix_ref[e] = value
            value = times(whole_ref[e], value)
        group_ref[...] = value

    square = (z.pad, z.pad)
    outs = [f32(z.steps, *square)] + [f32(z.segments, *square)] * 4 + [f32(*square)]
    return call(
        kernel,
        "maps",
        outs,
        [spec_smem(), spec_hbm()] + [spec_any()] * len(after),
        [spec_vmem()] * 6,
        [
            pltpu.VMEM(gain.shape, F32),
            pltpu.VMEM((z.segments, z.steps) + square, F32),
            pltpu.SemaphoreType.DMA,
        ],
        z.flops * z.segments * (z.steps + 1) // 2,
        4 * z.segments * z.steps * z.pad * z.pad,
    )(me, gain, *after)


def chain_call(z, starts, ends, tails, wholes, group):
    def kernel(start_ref, end_ref, tail_ref, whole_ref, group_ref, before_ref, pack_ref):
        value = None
        for e in range(z.segments):
            shift = end_ref[e] + product(operand_left(tail_ref[e]), operand_right(start_ref[e]))
            if e > 0:
                before_ref[e] = value
                shift = shift + product(operand_left(whole_ref[e]), operand_right(value))
            else:
                before_ref[0] = jnp.zeros_like(shift)
            value = shift
        pack_ref[:, : z.cols] = value
        pack_ref[:, z.cols :] = group_ref[...]

    return call(
        kernel,
        "chain",
        [f32(z.segments, z.pad, z.cols), f32(z.pad, z.cols + z.pad)],
        [spec_vmem()] * 5,
        [spec_vmem()] * 2,
        [],
        z.flops * z.segments * 2,
        4 * z.segments * z.pad * z.cols * 4,
    )(starts, ends, tails, wholes, group)


def first_call(z, places, packs, before, prefix, heads, starts, messages, place):
    offset = place * z.height
    base = offset // TILE * TILE
    size = messages.shape[1] - base

    def kernel(*refs):
        places_ref, refs = refs[0], refs[1:]
        pack_refs, refs = refs[: z.groups], refs[z.groups :]
        before_ref, prefix_ref, head_ref, start_ref, message_ref, out_ref, stage, sem = refs
        copies = [
            pltpu.make_async_copy(message_ref.at[e, pl.ds(base, size)], stage.at[e], sem.at[e])
            for e in range(z.segments)
        ]
        for copy in copies:
            copy.start()
        group = places_ref[1]
        value = jnp.zeros((z.pad, z.cols), F32)
        matrices = [operand_left(ref[:, z.cols :]) for ref in pack_refs]
        for t in range(2 * z.groups - 1, 0, -1):
            n = t % z.groups
            moved = product(matrices[n], operand_right(value)) + pack_refs[n][:, : z.cols]
            value = jnp.where(t <= z.groups + group, moved, 0.0)
        incoming = operand_right(value)
        arriving = [value] + [
            before_ref[e] + product(operand_left(prefix_ref[e]), incoming) for e in range(1, z.segments)
        ]
        solved = [
            start_ref[e] + product(operand_left(head_ref[e]), operand_right(arriving[e])) for e in range(z.segments)
        ]
        sends = []
        for e in range(z.segments):
            copies[e].wait()
            write_field(z, stage, (e,), offset - base, solved[e])
            copy = pltpu.make_async_copy(stage.at[e], out_ref.at[e, pl.ds(base, size)], sem.at[e])
            copy.start()
            sends.append(copy)
        for copy in sends:
            copy.wait()

    return call(
        kernel,
        "first",
        f32(*messages.shape),
        [spec_smem()] + [spec_vmem()] * (z.groups + 4) + [spec_hbm()],
        spec_hbm(),
        [pltpu.VMEM((z.segments, size, z.ax), F32), pltpu.SemaphoreType.DMA((z.segments,))],
        z.flops * (z.segments * 2 + 2 * z.groups),
        4 * z.segments * z.pad * z.cols * 4,
        {z.groups + 5: 0},
    )(places, *packs, before, prefix, heads, starts, messages)


def couple_call(z, keep, got):
    pairs, message, _ = keep.shape

    def kernel(*refs):
        sources, refs = refs[:2], refs[2:]
        outs, sem = refs[:pairs], refs[pairs]
        copies = []
        for d in range(pairs):
            for n in range(2):
                copies.append(pltpu.make_async_copy(sources[n].at[d], outs[d].at[n], sem.at[d, n]))
        for copy in copies:
            copy.start()
        for copy in copies:
            copy.wait()

    return call(
        kernel,
        "couple",
        [f32(2, message, z.ax)] * pairs,
        [spec_hbm()] * 2,
        [spec_hbm()] * pairs,
        [pltpu.SemaphoreType.DMA((pairs, 2))],
        0,
        4 * 4 * pairs * message * z.ax,
    )(keep, got)


def finish_call(z, chunk, mode, me, own, messages, place, operands, out):
    low, high = chunk
    count = high - low
    radial = z.segments * z.rows
    tall = z.nodes * radial
    opened = mode == "open"
    paired = mode == "pairs"
    pairs = z.segments // 2
    if paired:
        message = messages[0].shape[1]
    else:
        message = messages.shape[1]
        messages = [messages]
    steps = list(range(low, high)) + ([0] if opened else [])

    def kernel(*refs):
        me_ref, own_ref, refs = refs[0], refs[1], refs[2:]
        message_refs, refs = refs[: len(messages)], refs[len(messages) :]
        if opened:
            out_ref, operand_ref, refs = refs[0], refs[1], refs[2:]
        else:
            operand_ref, _, out_ref, refs = refs[0], refs[1], refs[2], refs[3:]
        buf, own_buf, operand_buf, stage, sem, in_sem, out_sem = refs
        copies = []
        own_copy = pltpu.make_async_copy(own_ref, own_buf, in_sem.at[0])
        own_copy.start()
        if not opened:
            operand_copy = pltpu.make_async_copy(operand_ref, operand_buf, in_sem.at[1])
            operand_copy.start()
        if paired:
            mine = me_ref[0]
            side = lax.rem(mine, 2)
            for d in range(pairs):
                pair = lax.rem(mine // 2 - d + pairs, pairs) * 2
                for n in range(2):
                    e = pair + (side if n == 0 else 1 - side)
                    copies.append(pltpu.make_async_copy(message_refs[d].at[n], buf.at[e], sem.at[2 * d + n]))
        else:
            copies = [pltpu.make_async_copy(message_refs[0].at[e], buf.at[e], sem.at[e]) for e in range(z.segments)]
        for copy in copies:
            copy.start()
        own_copy.wait()
        if not opened:
            operand_copy.wait()
        for copy in copies:
            copy.wait()
        sends = []

        def put(n, i, e, value):
            for j in range(z.rows):
                rows = pl.ds(e * z.rows + j, z.nodes, stride=radial)
                stage[n, rows, :] = value[: z.nodes, j * z.ax : (j + 1) * z.ax]

        def send(n, i):
            copy = pltpu.make_async_copy(stage.at[n], out_ref.at[i], out_sem.at[n])
            copy.start()
            sends.append(copy)

        if opened:
            for e in range(z.segments):
                field = read_exact(z, buf, (e,), count * z.height)
                empty = jnp.zeros((z.pad - z.nodes, z.cols), F32)
                operand_buf[e] = operand_right(jnp.concatenate([field, empty], axis=0))
                put(count, 0, e, field)
            send(count, 0)
            operand_copy = pltpu.make_async_copy(operand_buf, operand_ref, in_sem.at[1])
            operand_copy.start()
            sends.append(operand_copy)
        for n in range(count):
            matrix = operand_left(own_buf[low + n])
            for e in range(z.segments):
                value = product(matrix, operand_buf[e])[: z.nodes]
                put(n, low + n, e, value + read_exact(z, buf, (e,), (place + n) * z.height))
            send(n, low + n)
        for copy in sends:
            copy.wait()

    result = f32(z.steps, tall, z.ax)
    operand_shape = (z.segments, 2 * z.pad, z.cols)
    inputs = [me, own] + list(messages)
    in_specs = [spec_smem()] + [spec_hbm()] * (len(inputs) - 1)
    aliases = {}
    if opened:
        outs = [result, jax.ShapeDtypeStruct(operand_shape, BF16)]
        out_specs = [spec_hbm()] * 2
    else:
        inputs += [operands, out]
        in_specs += [spec_hbm()] * 2
        aliases = {len(inputs) - 1: 0}
        outs = result
        out_specs = spec_hbm()
    return call(
        kernel,
        f"finish_{low}",
        outs,
        in_specs,
        out_specs,
        [
            pltpu.VMEM((z.segments, message, z.ax), F32),
            pltpu.VMEM((z.steps, z.pad, z.pad), F32),
            pltpu.VMEM(operand_shape, BF16),
            pltpu.VMEM((len(steps), tall, z.ax), F32),
            pltpu.SemaphoreType.DMA((z.segments,)),
            pltpu.SemaphoreType.DMA((2,)),
            pltpu.SemaphoreType.DMA((len(steps),)),
        ],
        z.flops * count * z.segments,
        4 * 2 * count * tall * z.ax,
        aliases,
    )(*inputs)


def shift_by(array, axis, by):
    size = lax.axis_size(axis)
    return lax.ppermute(array, axis, [(i, (i + by) % size) for i in range(size)])


def neighbours(head, tail):
    size = lax.axis_size("elem")
    left = lax.ppermute(tail, "elem", [(i, i + 1) for i in range(size - 1)])
    right = lax.ppermute(head, "elem", [(i + 1, i) for i in range(size - 1)])
    return left, right


def spread(messages):
    return lax.all_to_all(messages, "elem", 0, 0, tiled=True)


def chunks_of(steps):
    if steps >= 8:
        return [(1, 3), (3, 5), (5, steps)]
    return [(1, 2), (2, 3), (3, steps)]


def body(state, rhs, to_modal, viscous_op, sweep_gain, inv_blocks):
    segments = lax.axis_size("elem")
    groups = lax.axis_size("blk")
    z = Sizes(state, segments, groups)
    state = state.reshape(segments, z.steps * z.height, z.ax)
    rhs = rhs.reshape(segments, z.steps * z.height, z.ax)
    gain = jnp.transpose(sweep_gain, (1, 0, 2))
    inverse = jnp.transpose(inv_blocks, (1, 0, 2))
    here = lax.axis_index("elem").astype(jnp.int32)
    me = here.reshape(1)
    places = jnp.stack([here, lax.axis_index("blk").astype(jnp.int32)])
    one, two, three = chunks_of(z.steps)
    sensors, head, tail = sensor_call(z, state, to_modal)
    lefts, rights = neighbours(head, tail)

    def sweep(chunk, mode, ring, carry, after):
        return sweep_call(
            z, chunk, mode, me, state, rhs, viscous_op, gain, inverse, sensors, lefts, rights, ring, carry, after
        )

    messages_one, carry, low, high = sweep(one, "all", None, None, [])
    ring = [shift_by(high, "blk", 1), shift_by(low, "blk", -1)]
    own, heads, tails, wholes, prefix, group = maps_call(z, me, gain, [carry])
    keep, give, carry = sweep(two, "pairs", None, carry, [group])
    messages_three, carry, starts = sweep(three, "open", ring, carry, [])
    before, pack = chain_call(z, starts, carry, tails, wholes, group)
    packs = [pack] + [shift_by(pack, "blk", s) for s in range(1, groups)]
    place = three[1] - three[0]
    messages_three = first_call(z, places, packs, before, prefix, heads, starts, messages_three, place)
    got = lax.ppermute(give, "elem", [(i, i ^ 1) for i in range(segments)])
    coupled = couple_call(z, keep, got)
    coupled = [coupled[0]] + [shift_by(coupled[d], "elem", 2 * d) for d in range(1, segments // 2)]
    received_one = spread(messages_one)
    received_three = spread(messages_three)
    out, operands = finish_call(z, three, "open", me, own, received_three, 0, None, None)
    out = finish_call(z, one, "all", me, own, received_one, 0, operands, out)
    out = finish_call(z, two, "pairs", me, own, coupled, 0, operands, out)
    return out.reshape(z.steps, z.nodes, segments * z.rows, z.ax)


def solution(mesh):
    in_specs = (
        P("blk", None, "elem", None),
        P("blk", None, "elem", None),
        P(),
        P(),
        P("blk", None, None),
        P("blk", None, None),
    )
    out_specs = P(("blk", "elem"), None, None, None)
    return jax.shard_map(body, mesh=mesh, in_specs=in_specs, out_specs=out_specs, check_vma=False)
```

time: 326 us -> 306 us (0.939)
  waiting for transfers between devices: 176 us -> 48.5 us
  blocking collectives: 0 us -> 94.1 us
  Pallas kernels: 67.2 us -> 136 us
  local copies, waits for them, and re-layouts: 44.4 us -> 4.23 us
  starting transfers between devices: 36.1 us -> 20.9 us
    ppermute x19 -> x8, waiting for transfers between devices: 170 us -> 42.5 us  [shift_by(): lax.ppermute(array, axis, [(i, (i + by) % size) for i in range(size)])]
    all_to_all x0 -> x1, blocking collectives: none -> 94.1 us  [spread(): return lax.all_to_all(messages, 'elem', 0, 0, tiled=True)]
    pallas_call x11 -> x10, Pallas kernels: 65.5 us -> 132 us  [the longest x1 63.7 us: couple_call(): call(kernel, 'couple', [f32(2, message, z.ax)] * pairs, [spec_hbm()] * 2,...]
    unnamed x130 -> x24, local copies, waits for them, and re-layouts: 44.4 us -> 4.23 us
    ppermute x19 -> x8, starting transfers between devices: 15.4 us -> 8.74 us  [shift_by(): lax.ppermute(array, axis, [(i, (i + by) % size) for i in range(size)])]
    all_to_all x2 -> x1, starting transfers between devices: 10.8 us -> 6.09 us  [spread(): return lax.all_to_all(messages, 'elem', 0, 0, tiled=True)]
  transfers between devices with their start and end apart: 25 -> 12, of which waited for: 13 -> 6; matrix products, arithmetic and copies ran while one was open for 0% -> 0% of each run, Pallas kernels for 12% -> 30%
where the time goes in v4:
time: 306 us; the launch traced here: 305 us
  Pallas kernels  136 us (44%)
  blocking collectives  94.1 us (31%)
  waiting for transfers between devices  48.5 us (16%)
  starting transfers between devices  20.9 us (7%)
  local copies, waits for them, and re-layouts  4.23 us (1%)
    all_to_all x1, blocking collectives, spread(): return lax.all_to_all(messages, 'elem', 0, 0, tiled=True)  94.1 us
    pallas_call x1, Pallas kernels, couple_call(): call(kernel, 'couple', [f32(2, message, z.ax)] * pairs, [spec_hbm()] * 2,...  63.7 us
    ppermute x8, waiting for transfers between devices, shift_by(): lax.ppermute(array, axis, [(i, (i + by) % size) for i in range(size)])  42.5 us
    pallas_call x3, Pallas kernels, sweep_call(): call(kernel, f'sweep_{low}', outs + more, in_specs + [spec_vmem()] * len(...  35.1 us
    pallas_call x3, Pallas kernels, finish_call(): call(kernel, f'finish_{low}', outs, in_specs, out_specs, [pltpu.VMEM((z.s...  13.4 us
    ppermute x8, starting transfers between devices, shift_by(): lax.ppermute(array, axis, [(i, (i + by) % size) for i in range(size)])  8.74 us
    pallas_call x1, Pallas kernels, maps_call(): call(kernel, 'maps', outs, [spec_smem(), spec_hbm()] + [spec_any()] * len...  8.24 us
    pallas_call x1, Pallas kernels, sensor_call(): call(kernel, 'sensor', outs, [spec_hbm()] * 2, [spec_vmem()] * 3, [pltpu....  6.3 us
  transfers between devices with their start and end apart: 12, of which 6 were waited for; matrix products, arithmetic and copies ran while one was open for 0% of the time, Pallas kernels for 30%

profile of v4, /device:TPU:9, one launch (start us, length us, event | category | flops | bytes accessed | tf_op | source)
XLA Modules:
  0.0 305.2 jit_solution(8814302651713416291)
XLA Ops:
  0.0 6.3 %sensor.1 = (f32[8,8,256]{2,1,0:T(8,128)}, f32[8,8,128]{2,1,0:T(8,128)}, f32[8,8,128]{2,1,0:T(8,128)}) custom-call(f32[8,2000,128]{2,1,0:T(8,128)} %bitcast.7, f32[125,125]{1,0:T(8,128)} %modal_ref.1), custom_call_target="tpu_custom_call" | custom-call | flops 2147483648 | bytes 8192000 | tf_op jit(solution)/shard_map/sensor/pallas_call | solution.py:153
  6.3 3.8 %collective-permute-start = (f32[8,8,128]{2,1,0:T(8,128)}, f32[8,8,128]{2,1,0:T(8,128)S(1)}, u32[]{:S(2)}, u32[]{:S(2)}) collective-permute-start(f32[8,8,128]{2,1,0:T(8,128)} %get-tuple-element.33), channel_id=1, source_target_pairs={{0,1},{1,2},{2,3},{3,4},{4,5},{5,6},{6,7},{8,9},{9,10},{10,11},{11... | collective-permute-start | bytes 98312 | tf_op jit(solution)/shard_map/ppermute | solution.py:607
  10.1 1.9 collective-permute-start.1
  12.0 0.0 collective-permute-done.refs_7_
  12.0 0.0 copy-start.4
  12.0 3.5 %collective-permute-done.1.refs_8_ = f32[8,8,128]{2,1,0:T(8,128)S(1)} collective-permute-done((f32[8,8,128]{2,1,0:T(8,128)}, f32[8,8,128]{2,1,0:T(8,128)S(1)}, u32[]{:S(2)}, u32[]{:S(2)}) %collective-permute-start.1) | collective-permute-done | bytes 32800 | tf_op jit(solution)/shard_map/ppermute | solution.py:608
  15.5 0.0 copy-start.5
  15.5 0.0 copy-done.4
  15.5 0.6 copy-done.5
  16.1 9.8 %sweep_1.1 = (f32[8,504,128]{2,1,0:T(8,128)}, f32[8,128,256]{2,1,0:T(8,128)}, f32[1,256]{1,0:T(1,128)}, f32[1,256]{1,0:T(1,128)}) custom-call(s32[1]{0:T(128)} %bitcast.refs_0_.me_ref, f32[8,2000,128]{2,1,0:T(8,128)} %bitcast.8, f32[8,2000,128]{2,1,0:T(8,128)} %bitcast.11, f32[125,125]{1,0:T(8,128)} %refs_3_.5, f32[125,64,125]{2,1,0:T(8,128)} %bitcast.18, ...), custom_call_target="tpu_custom_call" | custom-call | flops 1610612736 | bytes 8257536 | tf_op jit(solution)/shard_map/sweep_1/pallas_call | solution.py:321
  26.0 1.3 collective-permute-start.6
  27.2 1.2 collective-permute-start.7
  28.4 8.2 %maps.1 = (f32[8,128,128]{2,1,0:T(8,128)}, f32[8,128,128]{2,1,0:T(8,128)}, f32[8,128,128]{2,1,0:T(8,128)}, f32[8,128,128]{2,1,0:T(8,128)}, f32[8,128,128]{2,1,0:T(8,128)}, /*index=5*/f32[128,128]{1,0:T(8,128)}) custom-call(s32[1]{0:T(128)} %bitcast.refs_0_.me_ref, f32[125,64,125]{2,1,0:T(8,128)} %bitcast.15, f32[8,128,256]{2,1,0:T(8,128)} %get-tuple-element.35.refs_0_.refs_9_), custom_call_target="tpu_custom_call" | custom-call | flops 1207959552 | bytes 4194304 | tf_op jit(solution)/shard_map/maps/pallas_call | solution.py:367
  36.7 10.7 %sweep_3.1 = (f32[4,504,128]{2,1,0:T(8,128)}, f32[4,504,128]{2,1,0:T(8,128)}, f32[8,128,256]{2,1,0:T(8,128)}) custom-call(s32[1]{0:T(128)} %bitcast.refs_0_.me_ref, f32[8,2000,128]{2,1,0:T(8,128)} %bitcast.9, f32[8,2000,128]{2,1,0:T(8,128)} %bitcast.12, f32[125,125]{1,0:T(8,128)} %refs_3_.5, f32[125,64,125]{2,1,0:T(8,128)} %bitcast.19, ...), custom_call_target="tpu_custom_call" | custom-call | flops 1610612736 | bytes 8388608 | tf_op jit(solution)/shard_map/sweep_3/pallas_call | solution.py:321
  47.4 0.0 collective-permute-done.6.refs_9_
  47.4 0.0 copy-start.9
  47.4 0.0 collective-permute-done.7.refs_10_
  47.4 0.0 copy-start.10
  47.4 0.5 copy-done.9
  47.9 0.0 copy-done.10
  47.9 14.6 %sweep_5.1 = (f32[8,1000,128]{2,1,0:T(8,128)}, f32[8,128,256]{2,1,0:T(8,128)}, f32[8,128,256]{2,1,0:T(8,128)}) custom-call(s32[1]{0:T(128)} %bitcast.refs_0_.me_ref, f32[8,2000,128]{2,1,0:T(8,128)} %bitcast.10, f32[8,2000,128]{2,1,0:T(8,128)} %bitcast.13, f32[125,125]{1,0:T(8,128)} %refs_3_.5, f32[125,64,125]{2,1,0:T(8,128)} %bitcast.20, ...), custom_call_target="tpu_custom_call" | custom-call | flops 3221225472 | bytes 12320768 | tf_op jit(solution)/shard_map/sweep_5/pallas_call | solution.py:321
  62.5 4.4 %chain.1 = (f32[8,128,256]{2,1,0:T(8,128)}, f32[128,384]{1,0:T(8,128)}) custom-call(f32[8,128,256]{2,1,0:T(8,128)} %get-tuple-element.47.start_ref.refs_8_, f32[8,128,256]{2,1,0:T(8,128)} %get-tuple-element.48.end_ref, f32[8,128,128]{2,1,0:T(8,128)} %get-tuple-element.49.tail_ref, f32[8,128,128]{2,1,0:T(8,128)} %get-tuple-element.50.whole_ref, ...), custom_call_target="tpu_custom_call" | custom-call | flops 536870912 | bytes 4194304 | tf_op jit(solution)/shard_map/chain/pallas_call | solution.py:397
  66.9 1.2 collective-permute-start.10
  68.1 0.2 collective-permute-start.9
  68.3 1.2 collective-permute-start.8
  69.6 0.6 pad_add_fusion.refs_0_
  70.2 3.8 %collective-permute-done.10.refs_4_ = f32[128,384]{1,0:T(8,128)S(1)} collective-permute-done((f32[128,384]{1,0:T(8,128)}, f32[128,384]{1,0:T(8,128)S(1)}, u32[]{:S(2)}, u32[]{:S(2)}) %collective-permute-start.10) | collective-permute-done | bytes 196640 | tf_op jit(solution)/shard_map/ppermute | solution.py:602
  74.0 0.0 copy-start.6
  74.0 5.2 %collective-permute-done.9.refs_3_ = f32[128,384]{1,0:T(8,128)S(1)} collective-permute-done((f32[128,384]{1,0:T(8,128)}, f32[128,384]{1,0:T(8,128)S(1)}, u32[]{:S(2)}, u32[]{:S(2)}) %collective-permute-start.9) | collective-permute-done | bytes 196640 | tf_op jit(solution)/shard_map/ppermute | solution.py:602
  79.2 0.0 copy-start.7
  79.2 0.0 collective-permute-done.8.refs_2_
  79.2 0.0 copy-start.8
  79.2 0.0 copy-done.6
  79.2 0.7 copy-done.7
  79.9 0.1 copy-done.8
  80.0 5.3 %first.1 = f32[8,1000,128]{2,1,0:T(8,128)} custom-call(s32[2]{0:T(128)} %pad_add_fusion.refs_0_, f32[128,384]{1,0:T(8,128)} %get-tuple-element.51.refs_1_, f32[128,384]{1,0:T(8,128)} %copy-done.8, f32[128,384]{1,0:T(8,128)} %copy-done.7, f32[128,384]{1,0:T(8,128)} %copy-done.6, ...), custom_call_target="tpu_custom_call", output_to_operand_aliasing={{}: (9, {})} | custom-call | flops 805306368 | bytes 4194304 | tf_op jit(solution)/shard_map/first/pallas_call | solution.py:448
  85.3 94.1 %all_to_all.10.refs_2_ = f32[8,1000,128]{2,1,0:T(8,128)} all-to-all(f32[8,1000,128]{2,1,0:T(8,128)} %first.1), channel_id=1, replica_groups=mesh['blk'=4,'elem'=8] {'elem'}, dimensions={0} | all-to-all | bytes 8192000 | tf_op jit(solution)/shard_map/all_to_all | solution.py:613
  179.5 0.0 copy-start.11
  179.5 6.1 %all-to-all-start.1 = ((f32[8,504,128]{2,1,0:T(8,128)}), f32[8,504,128]{2,1,0:T(8,128)S(1)}, u32[]{:S(2)}, u32[]{:S(2)}) async-start(f32[8,504,128]{2,1,0:T(8,128)} %get-tuple-element.57), calls=%async_computation.1 | async-start | bytes 4128768 | tf_op jit(solution)/shard_map/all_to_all | solution.py:613
  185.5 0.0 copy-done.11
  185.5 0.4 collective-permute-start.2
  185.9 2.5 collective-permute-done.2.refs_1_
  188.4 0.0 copy-start.1
  188.4 1.0 copy-done.1
  189.4 63.7 %couple.1 = (f32[2,504,128]{2,1,0:T(8,128)}, f32[2,504,128]{2,1,0:T(8,128)}, f32[2,504,128]{2,1,0:T(8,128)}, f32[2,504,128]{2,1,0:T(8,128)}) custom-call(f32[4,504,128]{2,1,0:T(8,128)} %get-tuple-element.38.refs_0_, f32[4,504,128]{2,1,0:T(8,128)} %copy-done.1), custom_call_target="tpu_custom_call" | custom-call | bytes 4128768 | tf_op jit(solution)/shard_map/couple/pallas_call | solution.py:476
  253.1 1.2 collective-permute-start.3
  254.3 1.0 collective-permute-start.4
  255.3 1.4 collective-permute-start.5
  256.7 5.3 %finish_5.1 = (f32[8,2000,128]{2,1,0:T(8,128)}, bf16[8,256,256]{2,1,0:T(8,128)(2,1)}) custom-call(s32[1]{0:T(128)} %bitcast.refs_0_.me_ref, f32[8,128,128]{2,1,0:T(8,128)} %get-tuple-element.36.refs_1_, f32[8,1000,128]{2,1,0:T(8,128)} %all_to_all.10.refs_2_), custom_call_target="tpu_custom_call" | custom-call | flops 805306368 | bytes 6144000 | tf_op jit(solution)/shard_map/finish_5/pallas_call | solution.py:579
  262.0 0.0 all-to-all-done.1.refs_2_
  262.0 0.0 copy-start
  262.0 1.3 copy-done
  263.3 4.1 %finish_1.1.refs_7_ = f32[8,2000,128]{2,1,0:T(8,128)} custom-call(s32[1]{0:T(128)} %bitcast.refs_0_.me_ref, f32[8,128,128]{2,1,0:T(8,128)} %get-tuple-element.36.refs_1_, f32[8,504,128]{2,1,0:T(8,128)} %copy-done, bf16[8,256,256]{2,1,0:T(8,128)(2,1)} %get-tuple-element.56.refs_3_.refs_6_, ...), custom_call_target="tpu_custom_call", output_to_operand_aliasing={{}: (4, {})} | custom-call | flops 536870912 | bytes 4096000 | tf_op jit(solution)/shard_map/finish_1/pallas_call | solution.py:579
  267.5 0.0 collective-permute-done.3.refs_3_
  267.5 0.0 copy-start.2
  267.5 31.3 %collective-permute-done.4.refs_4_ = f32[2,504,128]{2,1,0:T(8,128)S(1)} collective-permute-done((f32[2,504,128]{2,1,0:T(8,128)}, f32[2,504,128]{2,1,0:T(8,128)S(1)}, u32[]{:S(2)}, u32[]{:S(2)}) %collective-permute-start.4) | collective-permute-done | bytes 516128 | tf_op jit(solution)/shard_map/ppermute | solution.py:602
  298.8 0.0 copy-start.3
  298.8 2.2 collective-permute-done.5.refs_5_
  301.0 0.0 copy-done.2
  301.0 0.0 copy-done.3
  301.0 4.0 %finish_3.1 = f32[8,2000,128]{2,1,0:T(8,128)} custom-call(s32[1]{0:T(128)} %bitcast.refs_0_.me_ref, f32[8,128,128]{2,1,0:T(8,128)} %get-tuple-element.36.refs_1_, f32[2,504,128]{2,1,0:T(8,128)} %get-tuple-element.40.refs_2_, f32[2,504,128]{2,1,0:T(8,128)} %copy-done.2, f32[2,504,128]{2,1,0:T(8,128)} %copy-done.3, ...), custom_call_target="tpu_custom_call", output_to_operand_aliasing={{}: (7, {})} | custom-call | flops 536870912 | bytes 4096000 | tf_op jit(solution)/shard_map/finish_3/pallas_call | solution.py:579
Async XLA Ops:
  6.3 5.7 %collective-permute-start = (f32[8,8,128]{2,1,0:T(8,128)}, f32[8,8,128]{2,1,0:T(8,128)S(1)}, u32[]{:S(2)}, u32[]{:S(2)}) collective-permute-start(f32[8,8,128]{2,1,0:T(8,128)} %get-tuple-element.33), channel_id=1, source_target_pairs={{0,1},{1,2},{2,3},{3,4},{4,5},{5,6},{6,7},{8,9},{9,10},{10,11},{11... | collective-permute-start | bytes 98312 | tf_op jit(solution)/shard_map/ppermute | solution.py:607
  10.1 5.4 %collective-permute-start.1 = (f32[8,8,128]{2,1,0:T(8,128)}, f32[8,8,128]{2,1,0:T(8,128)S(1)}, u32[]{:S(2)}, u32[]{:S(2)}) collective-permute-start(f32[8,8,128]{2,1,0:T(8,128)} %get-tuple-element.34), channel_id=1, source_target_pairs={{1,0},{2,1},{3,2},{4,3},{5,4},{6,5},{7,6},{9,8},{10,9},{11,10},{12... | collective-permute-start | bytes 98312 | tf_op jit(solution)/shard_map/ppermute | solution.py:608
  12.0 3.5 %copy-start.4 = (f32[8,8,128]{2,1,0:T(8,128)}, f32[8,8,128]{2,1,0:T(8,128)S(1)}, u32[]{:S(2)}) copy-start(f32[8,8,128]{2,1,0:T(8,128)S(1)} %collective-permute-done.refs_7_) | copy-start | bytes 98308
  15.5 0.6 copy-start.5
  26.0 21.4 %collective-permute-start.6 = (f32[1,256]{1,0:T(1,128)}, f32[1,256]{1,0:T(1,128)S(1)}, u32[]{:S(2)}, u32[]{:S(2)}) collective-permute-start(f32[1,256]{1,0:T(1,128)} %get-tuple-element.44), channel_id=1, source_target_pairs={{0,8},{8,16},{16,24},{24,0},{1,9},{9,17},{17,25},{25,1},{2,10},{10... | collective-permute-start | bytes 3080 | tf_op jit(solution)/shard_map/ppermute | solution.py:602
  27.2 20.1 %collective-permute-start.7 = (f32[1,256]{1,0:T(1,128)}, f32[1,256]{1,0:T(1,128)S(1)}, u32[]{:S(2)}, u32[]{:S(2)}) collective-permute-start(f32[1,256]{1,0:T(1,128)} %get-tuple-element.45), channel_id=1, source_target_pairs={{0,24},{8,0},{16,8},{24,16},{1,25},{9,1},{17,9},{25,17},{2,26},{10... | collective-permute-start | bytes 3080 | tf_op jit(solution)/shard_map/ppermute | solution.py:602
  47.4 0.6 copy-start.9
  47.4 0.6 copy-start.10
  66.9 7.1 %collective-permute-start.10 = (f32[128,384]{1,0:T(8,128)}, f32[128,384]{1,0:T(8,128)S(1)}, u32[]{:S(2)}, u32[]{:S(2)}) collective-permute-start(f32[128,384]{1,0:T(8,128)} %get-tuple-element.51.refs_1_), channel_id=1, source_target_pairs={{0,24},{8,0},{16,8},{24,16},{1,25},{9,1},{17,9},{25,17},{2,26},{10... | collective-permute-start | bytes 589832 | tf_op jit(solution)/shard_map/ppermute | solution.py:602
  68.1 11.1 %collective-permute-start.9 = (f32[128,384]{1,0:T(8,128)}, f32[128,384]{1,0:T(8,128)S(1)}, u32[]{:S(2)}, u32[]{:S(2)}) collective-permute-start(f32[128,384]{1,0:T(8,128)} %get-tuple-element.51.refs_1_), channel_id=1, source_target_pairs={{0,16},{8,24},{16,0},{24,8},{1,17},{9,25},{17,1},{25,9},{2,18},{10... | collective-permute-start | bytes 589832 | tf_op jit(solution)/shard_map/ppermute | solution.py:602
  68.3 10.9 %collective-permute-start.8 = (f32[128,384]{1,0:T(8,128)}, f32[128,384]{1,0:T(8,128)S(1)}, u32[]{:S(2)}, u32[]{:S(2)}) collective-permute-start(f32[128,384]{1,0:T(8,128)} %get-tuple-element.51.refs_1_), channel_id=1, source_target_pairs={{0,8},{8,16},{16,24},{24,0},{1,9},{9,17},{17,25},{25,1},{2,10},{10... | collective-permute-start | bytes 589832 | tf_op jit(solution)/shard_map/ppermute | solution.py:602
  74.0 5.2 %copy-start.6 = (f32[128,384]{1,0:T(8,128)}, f32[128,384]{1,0:T(8,128)S(1)}, u32[]{:S(2)}) copy-start(f32[128,384]{1,0:T(8,128)S(1)} %collective-permute-done.10.refs_4_) | copy-start | bytes 589828
  79.2 0.7 copy-start.7
  79.2 0.8 copy-start.8
  179.5 6.1 %copy-start.11 = (f32[4,504,128]{2,1,0:T(8,128)S(1)}, f32[4,504,128]{2,1,0:T(8,128)}, u32[]{:S(2)}) copy-start(f32[4,504,128]{2,1,0:T(8,128)} %get-tuple-element.39) | copy-start | bytes 3096580
  179.5 82.5 %all-to-all-start.1 = ((f32[8,504,128]{2,1,0:T(8,128)}), f32[8,504,128]{2,1,0:T(8,128)S(1)}, u32[]{:S(2)}, u32[]{:S(2)}) async-start(f32[8,504,128]{2,1,0:T(8,128)} %get-tuple-element.57), calls=%async_computation.1 | async-start | bytes 4128768 | tf_op jit(solution)/shard_map/all_to_all | solution.py:613
  185.5 2.9 collective-permute-start.2
  188.4 1.0 copy-start.1
  253.1 14.4 %collective-permute-start.3 = (f32[2,504,128]{2,1,0:T(8,128)}, f32[2,504,128]{2,1,0:T(8,128)S(1)}, u32[]{:S(2)}, u32[]{:S(2)}) collective-permute-start(f32[2,504,128]{2,1,0:T(8,128)} %get-tuple-element.41), channel_id=1, source_target_pairs={{0,2},{1,3},{2,4},{3,5},{4,6},{5,7},{6,0},{7,1},{8,10},{9,11},{10,... | collective-permute-start | bytes 1548296 | tf_op jit(solution)/shard_map/ppermute | solution.py:602
  254.3 44.5 %collective-permute-start.4 = (f32[2,504,128]{2,1,0:T(8,128)}, f32[2,504,128]{2,1,0:T(8,128)S(1)}, u32[]{:S(2)}, u32[]{:S(2)}) collective-permute-start(f32[2,504,128]{2,1,0:T(8,128)} %get-tuple-element.42), channel_id=1, source_target_pairs={{0,4},{1,5},{2,6},{3,7},{4,0},{5,1},{6,2},{7,3},{8,12},{9,13},{10,... | collective-permute-start | bytes 1548296 | tf_op jit(solution)/shard_map/ppermute | solution.py:602
  255.3 45.7 %collective-permute-start.5 = (f32[2,504,128]{2,1,0:T(8,128)}, f32[2,504,128]{2,1,0:T(8,128)}, u32[]{:S(2)}, u32[]{:S(2)}) collective-permute-start(f32[2,504,128]{2,1,0:T(8,128)} %get-tuple-element.43), channel_id=1, source_target_pairs={{0,6},{1,7},{2,0},{3,1},{4,2},{5,3},{6,4},{7,5},{8,14},{9,15},{10,... | collective-permute-start | bytes 1548296 | tf_op jit(solution)/shard_map/ppermute | solution.py:602
  262.0 1.3 copy-start
  267.5 33.5 %copy-start.2 = (f32[2,504,128]{2,1,0:T(8,128)}, f32[2,504,128]{2,1,0:T(8,128)S(1)}, u32[]{:S(2)}) copy-start(f32[2,504,128]{2,1,0:T(8,128)S(1)} %collective-permute-done.3.refs_3_) | copy-start | bytes 1548292
  298.8 2.2 copy-start.3

commit v5 on v4

--- a/solution.py
+++ b/solution.py
@@ -175,19 +175,23 @@
     return (4.0 * sensor + before + after + from_left + from_right) / 8.0
 
 
-def sweep_call(z, chunk, mode, me, state, rhs, viscous, gain, inverse, sensors, lefts, rights, ring, carry, after):
+def sweep_call(z, chunk, paired, me, state, rhs, viscous, gain, inverse, sensors, lefts, rights, ring, carry, after):
     low, high = chunk
-    opened = mode == "open"
+    opened = high == z.steps
     first, size = z.window(low, high)
     count = high - low
     first0, size0 = z.window(0, 1)
     steps = list(range(low, high)) + ([0] if opened else [])
     has_carry = carry is not None
-    needs_gain = has_carry or count > 1
-    message = z.message(count + (1 if opened else 0))
+    gains = list(range(low if has_carry else low + 1, high))
+    rest = count - paired
+    message = z.message(rest + (1 if opened else 0))
+    paired_message = z.message(paired)
     edge_outs = low == 1
     pairs = z.segments // 2
+    last, last_size = z.window(low - 2, low - 1)
     batch = next(n for n in (4, 8, z.segments) if z.segments % n == 0 and n * z.steps % TILE == 0)
+    narrow = low == 1
 
     def kernel(*refs):
         me_ref, state_ref, rhs_ref, viscous_ref, inverse_ref, gain_ref, sensor_ref, left_ref, right_ref = refs[:9]
@@ -197,18 +201,21 @@
         if has_carry:
             carry_ref, refs = refs[0], refs[1:]
         refs = refs[len(after) :]
-        if mode == "pairs":
+        out_ref, refs = refs[0], refs[1:]
+        if paired:
             keep_ref, give_ref, refs = refs[0], refs[1], refs[2:]
-        else:
-            out_ref, refs = refs[0], refs[1:]
-        end_ref, refs = refs[0], refs[1:]
         if opened:
-            start_ref, refs = refs[0], refs[1:]
+            end_ref, start_ref, refs = refs[0], refs[1], refs[2:]
         if edge_outs:
             low_ref, high_ref, refs = refs[0], refs[1], refs[2:]
         state_buf, rhs_buf, inverse_buf, gain_buf, viscous_buf, smooth_buf, stage, sem, matrix_sem, out_sem = refs[:10]
+        refs = refs[10:]
         if opened:
-            state0, rhs0 = refs[10:]
+            state0, rhs0, refs = refs[0], refs[1], refs[2:]
+        if paired:
+            pair_stage, pair_sem, refs = refs[0], refs[1], refs[2:]
+        if has_carry:
+            carry_buf = refs[0]
         viscous_copy = pltpu.make_async_copy(viscous_ref, viscous_buf, out_sem.at[0])
         viscous_copy.start()
         copies = [[] for _ in range(z.segments)]
@@ -221,12 +228,20 @@
                 if opened:
                     moves.append((state_ref.at[s, pl.ds(first0, size0)], state0.at[s, pl.ds(0, size0)]))
                     moves.append((rhs_ref.at[s, pl.ds(first0, size0)], rhs0.at[s, pl.ds(0, size0)]))
+                if has_carry:
+                    moves.append((carry_ref.at[s, pl.ds(last, last_size)], carry_buf.at[s, pl.ds(0, last_size)]))
+                if narrow:
+                    for source, target, needed in ((inverse_ref, inverse_buf, steps), (gain_ref, gain_buf, gains)):
+                        if needed:
+                            part = pl.ds(s * z.steps + needed[0], len(needed))
+                            moves.append((source.at[:, part], target.at[:, part]))
                 for n, (source, target) in enumerate(moves):
                     copies[s].append(pltpu.make_async_copy(source, target, sem.at[s, n]))
-            part = pl.ds(s0 * z.steps, batch * z.steps)
-            sources = [(inverse_ref, inverse_buf)] + ([(gain_ref, gain_buf)] if needs_gain else [])
-            for n, (source, target) in enumerate(sources):
-                copies[s0].append(pltpu.make_async_copy(source.at[:, part], target.at[:, part], matrix_sem.at[s0, n]))
+            if not narrow:
+                part = pl.ds(s0 * z.steps, batch * z.steps)
+                for n, (source, target) in enumerate(((inverse_ref, inverse_buf), (gain_ref, gain_buf))):
+                    copy = pltpu.make_async_copy(source.at[:, part], target.at[:, part], matrix_sem.at[s0, n])
+                    copies[s0].append(copy)
             for s in range(s0, s0 + batch):
                 for copy in copies[s]:
                     copy.start()
@@ -244,12 +259,28 @@
         viscous_copy.wait()
         operator = operand_left(z.square(viscous_buf[...]))
         sends = []
+
+        def send_pairs(s):
+            side = lax.rem(me_ref[0], 2)
+            place = lax.rem(s // 2 - me_ref[0] // 2 + pairs, pairs)
+            own = side == s % 2
+
+            @pl.when(own)
+            def _():
+                pltpu.make_async_copy(pair_stage.at[s], keep_ref.at[place], pair_sem.at[s]).start()
+
+            @pl.when(jnp.logical_not(own))
+            def _():
+                pltpu.make_async_copy(pair_stage.at[s], give_ref.at[place], pair_sem.at[s]).start()
+
+            sends.append(pltpu.make_async_copy(pair_stage.at[s], keep_ref.at[place], pair_sem.at[s]))
+
         for s0 in range(0, z.segments, batch):
             group = range(s0, s0 + batch)
             for s in group:
                 for copy in copies[s]:
                     copy.wait()
-            fields = [carry_ref[s] if has_carry else None for s in group]
+            sources = []
             for n, i in enumerate(steps):
                 bufs = (state0, rhs0, -first0) if i == 0 else (state_buf, rhs_buf, i * z.height - first)
                 moved = [product(operator, operand_right(read_field(z, bufs[0], (s,), bufs[2]))) for s in group]
@@ -257,15 +288,22 @@
                     operand_right(read_field(z, bufs[1], (s,), bufs[2]) + smooth_buf[n, s : s + 1, :] * value)
                     for s, value in zip(group, moved)
                 ]
-                values = [
+                sources.append(forces)
+            for n, i in enumerate(steps):
+                sources[n] = [
                     product(operand_left(read_matrix(z, inverse_buf, s * z.steps + i)), force)
-                    for s, force in zip(group, forces)
+                    for s, force in zip(group, sources[n])
                 ]
+            fields = None
+            if has_carry:
+                fields = [read_field(z, carry_buf, (s,), (low - 2) * z.height - last) for s in group]
+            for n, i in enumerate(steps):
+                values = sources[n]
                 if i == 0:
                     for s, value in zip(group, values):
                         start_ref[s] = value
                     continue
-                if fields[0] is not None:
+                if fields is not None:
                     swept = [
                         product(operand_left(read_matrix(z, gain_buf, s * z.steps + i)), operand_right(field))
                         for s, field in zip(group, fields)
@@ -273,37 +311,33 @@
                     values = [value + more for value, more in zip(values, swept)]
                 fields = values
                 for s, value in zip(group, values):
-                    write_field(z, stage, (s,), n * z.height, value)
+                    if n >= rest:
+                        write_field(z, pair_stage, (s,), (n - rest) * z.height, value)
+                    else:
+                        write_field(z, stage, (s,), n * z.height, value)
             for s, value in zip(group, fields):
-                end_ref[s] = value
-                if mode != "pairs":
-                    copy = pltpu.make_async_copy(stage.at[s], out_ref.at[s], out_sem.at[s])
-                    copy.start()
-                    sends.append(copy)
-                    continue
-                side = lax.rem(me_ref[0], 2)
-                place = lax.rem(s // 2 - me_ref[0] // 2 + pairs, pairs)
-                own = side == s % 2
-
-                @pl.when(own)
-                def _(s=s, place=place):
-                    pltpu.make_async_copy(stage.at[s], keep_ref.at[place], out_sem.at[s]).start()
-
-                @pl.when(jnp.logical_not(own))
-                def _(s=s, place=place):
-                    pltpu.make_async_copy(stage.at[s], give_ref.at[place], out_sem.at[s]).start()
-
-                sends.append(pltpu.make_async_copy(stage.at[s], keep_ref.at[place], out_sem.at[s]))
+                if opened:
+                    end_ref[s] = value
+                copy = pltpu.make_async_copy(stage.at[s], out_ref.at[s], out_sem.at[s])
+                copy.start()
+                sends.append(copy)
+            if paired:
+                for s in group:
+                    send_pairs(s)
         for copy in sends:
             copy.wait()
 
     field = f32(z.segments, z.pad, z.cols)
-    outs = [f32(pairs, message, z.ax)] * 2 if mode == "pairs" else [f32(z.segments, message, z.ax)]
+    outs = [f32(z.segments, message, z.ax)] + [f32(pairs, paired_message, z.ax)] * (2 if paired else 0)
     out_specs = [spec_hbm()] * len(outs)
-    more = [field] * (2 if opened else 1) + ([f32(1, z.cols)] * 2 if edge_outs else [])
+    more = [field] * (2 if opened else 0) + ([f32(1, z.cols)] * 2 if edge_outs else [])
     operands = [me, state, rhs, viscous, inverse, gain, sensors, lefts, rights]
     in_specs = [spec_smem()] + [spec_hbm()] * 5 + [spec_vmem()] * 3
-    extra = (list(ring) if opened else []) + ([carry] if has_carry else [])
+    extra = list(ring) if opened else []
+    extra_specs = [spec_vmem()] * len(extra)
+    if has_carry:
+        extra.append(carry)
+        extra_specs.append(spec_hbm())
     scratch = [
         pltpu.VMEM((z.segments, size + z.spill, z.ax), F32),
         pltpu.VMEM((z.segments, size + z.spill, z.ax), F32),
@@ -312,21 +346,26 @@
         pltpu.VMEM(viscous.shape, F32),
         pltpu.VMEM((len(steps), z.segments, z.cols), F32),
         pltpu.VMEM((z.segments, message, z.ax), F32),
-        pltpu.SemaphoreType.DMA((z.segments, 4)),
+        pltpu.SemaphoreType.DMA((z.segments, 7)),
         pltpu.SemaphoreType.DMA((z.segments, 2)),
         pltpu.SemaphoreType.DMA((z.segments,)),
     ]
     if opened:
         scratch += [pltpu.VMEM((z.segments, size0 + z.spill, z.ax), F32)] * 2
+    if paired:
+        scratch += [pltpu.VMEM((z.segments, paired_message, z.ax), F32), pltpu.SemaphoreType.DMA((z.segments,))]
+    if has_carry:
+        scratch.append(pltpu.VMEM((z.segments, last_size + z.spill, z.ax), F32))
     return call(
         kernel,
         f"sweep_{low}",
         outs + more,
-        in_specs + [spec_vmem()] * len(extra) + [spec_any()] * len(after),
+        in_specs + extra_specs + [spec_any()] * len(after),
         out_specs + [spec_vmem()] * len(more),
         scratch,
         z.flops * len(steps) * z.segments * 3,
         4 * z.segments * size * z.ax * 4,
+        limit=54,
     )(*operands, *extra, *after)
 
 
@@ -463,14 +502,22 @@
 
     def kernel(*refs):
         sources, refs = refs[:2], refs[2:]
-        outs, sem = refs[:pairs], refs[pairs]
-        copies = []
+        outs, buf, sem = refs[:pairs], refs[pairs], refs[pairs + 1]
+        loads = [
+            [pltpu.make_async_copy(sources[n].at[d], buf.at[d, n], sem.at[d, n]) for n in range(2)]
+            for d in range(pairs)
+        ]
+        for load in loads:
+            for copy in load:
+                copy.start()
+        stores = []
         for d in range(pairs):
-            for n in range(2):
-                copies.append(pltpu.make_async_copy(sources[n].at[d], outs[d].at[n], sem.at[d, n]))
-        for copy in copies:
+            for copy in loads[d]:
+                copy.wait()
+            copy = pltpu.make_async_copy(buf.at[d], outs[d], sem.at[d, 0])
             copy.start()
-        for copy in copies:
+            stores.append(copy)
+        for copy in stores:
             copy.wait()
 
     return call(
@@ -479,41 +526,116 @@
         [f32(2, message, z.ax)] * pairs,
         [spec_hbm()] * 2,
         [spec_hbm()] * pairs,
-        [pltpu.SemaphoreType.DMA((pairs, 2))],
+        [pltpu.VMEM((pairs, 2, message, z.ax), F32), pltpu.SemaphoreType.DMA((pairs, 2))],
         0,
         4 * 4 * pairs * message * z.ax,
     )(keep, got)
 
 
-def finish_call(z, chunk, mode, me, own, messages, place, operands, out):
+def gate_call(held, after):
+    def kernel(*refs):
+        pass
+
+    return call(
+        kernel,
+        "gate",
+        f32(*held.shape),
+        [spec_hbm()] + [spec_any()] * len(after),
+        spec_hbm(),
+        [],
+        0,
+        0,
+        {0: 0},
+    )(held, *after)
+
+
+def open_call(z, one, two, own, received_one, received_two):
+    radial = z.segments * z.rows
+    tall = z.nodes * radial
+    operand_shape = (z.segments, 2 * z.pad, z.cols)
+    low, middle, high = one[0], two[0], two[1]
+    messages = (received_one, received_two)
+
+    def kernel(own_ref, one_ref, two_ref, out_ref, operand_ref, own_buf, one_buf, two_buf, stage, sem, own_sem, out_sem):
+        own_copy = pltpu.make_async_copy(own_ref, own_buf, own_sem)
+        own_copy.start()
+        copies = []
+        for n, (source, target) in enumerate(((two_ref, two_buf), (one_ref, one_buf))):
+            copies.append(
+                [pltpu.make_async_copy(source.at[e], target.at[e], sem.at[e, n]) for e in range(z.segments)]
+            )
+            for copy in copies[n]:
+                copy.start()
+        sends = []
+
+        def put(i, e, value):
+            for j in range(z.rows):
+                rows = pl.ds(e * z.rows + j, z.nodes, stride=radial)
+                stage[i, rows, :] = value[: z.nodes, j * z.ax : (j + 1) * z.ax]
+
+        def send(i):
+            copy = pltpu.make_async_copy(stage.at[i], out_ref.at[i], out_sem.at[i])
+            copy.start()
+            sends.append(copy)
+
+        for e in range(z.segments):
+            copies[0][e].wait()
+            field = read_exact(z, two_buf, (e,), (high - middle) * z.height)
+            empty = jnp.zeros((z.pad - z.nodes, z.cols), F32)
+            operand_ref[e] = operand_right(jnp.concatenate([field, empty], axis=0))
+            put(0, e, field)
+        send(0)
+        own_copy.wait()
+        for i in list(range(middle, high)) + list(range(low, middle)):
+            if i == low:
+                for copy in copies[1]:
+                    copy.wait()
+            buf, offset = (two_buf, i - middle) if i >= middle else (one_buf, i - low)
+            matrix = operand_left(own_buf[i])
+            for e in range(z.segments):
+                value = product(matrix, operand_ref[e])[: z.nodes]
+                put(i, e, value + read_exact(z, buf, (e,), offset * z.height))
+            send(i)
+        for copy in sends:
+            copy.wait()
+
+    return call(
+        kernel,
+        "finish_0",
+        [f32(z.steps, tall, z.ax), jax.ShapeDtypeStruct(operand_shape, BF16)],
+        [spec_hbm()] * 3,
+        [spec_hbm(), spec_vmem()],
+        [
+            pltpu.VMEM((z.steps, z.pad, z.pad), F32),
+            pltpu.VMEM(received_one.shape, F32),
+            pltpu.VMEM(received_two.shape, F32),
+            pltpu.VMEM((high, tall, z.ax), F32),
+            pltpu.SemaphoreType.DMA((z.segments, 2)),
+            pltpu.SemaphoreType.DMA,
+            pltpu.SemaphoreType.DMA((high,)),
+        ],
+        z.flops * (high - 1) * z.segments,
+        4 * 2 * high * tall * z.ax,
+    )(own, *messages)
+
+
+def finish_call(z, chunk, me, own, messages, operands, out):
     low, high = chunk
     count = high - low
     radial = z.segments * z.rows
     tall = z.nodes * radial
-    opened = mode == "open"
-    paired = mode == "pairs"
     pairs = z.segments // 2
-    if paired:
-        message = messages[0].shape[1]
-    else:
-        message = messages.shape[1]
-        messages = [messages]
-    steps = list(range(low, high)) + ([0] if opened else [])
-
-    def kernel(*refs):
-        me_ref, own_ref, refs = refs[0], refs[1], refs[2:]
+    paired = len(messages) > 1
+    message = messages[0].shape[1]
+
+    def kernel(me_ref, own_ref, operand_ref, *refs):
         message_refs, refs = refs[: len(messages)], refs[len(messages) :]
-        if opened:
-            out_ref, operand_ref, refs = refs[0], refs[1], refs[2:]
-        else:
-            operand_ref, _, out_ref, refs = refs[0], refs[1], refs[2], refs[3:]
-        buf, own_buf, operand_buf, stage, sem, in_sem, out_sem = refs
+        _, out_ref, buf, own_buf, operand_buf, stage, sem, in_sem, out_sem = refs
+        own_copy = pltpu.make_async_copy(own_ref.at[pl.ds(low, count)], own_buf, in_sem.at[0])
+        operand_copy = pltpu.make_async_copy(operand_ref, operand_buf, in_sem.at[1])
+        own_copy.start()
+        operand_copy.start()
         copies = []
-        own_copy = pltpu.make_async_copy(own_ref, own_buf, in_sem.at[0])
-        own_copy.start()
-        if not opened:
-            operand_copy = pltpu.make_async_copy(operand_ref, operand_buf, in_sem.at[1])
-            operand_copy.start()
         if paired:
             mine = me_ref[0]
             side = lax.rem(mine, 2)
@@ -527,73 +649,45 @@
         for copy in copies:
             copy.start()
         own_copy.wait()
-        if not opened:
-            operand_copy.wait()
-        for copy in copies:
-            copy.wait()
+        operand_copy.wait()
+        if paired:
+            for copy in copies:
+                copy.wait()
         sends = []
-
-        def put(n, i, e, value):
-            for j in range(z.rows):
-                rows = pl.ds(e * z.rows + j, z.nodes, stride=radial)
-                stage[n, rows, :] = value[: z.nodes, j * z.ax : (j + 1) * z.ax]
-
-        def send(n, i):
-            copy = pltpu.make_async_copy(stage.at[n], out_ref.at[i], out_sem.at[n])
+        for n in range(count):
+            matrix = operand_left(own_buf[n])
+            for e in range(z.segments):
+                if n == 0 and not paired:
+                    copies[e].wait()
+                value = product(matrix, operand_buf[e])[: z.nodes] + read_exact(z, buf, (e,), n * z.height)
+                for j in range(z.rows):
+                    rows = pl.ds(e * z.rows + j, z.nodes, stride=radial)
+                    stage[n, rows, :] = value[:, j * z.ax : (j + 1) * z.ax]
+            copy = pltpu.make_async_copy(stage.at[n], out_ref.at[low + n], out_sem.at[n])
             copy.start()
             sends.append(copy)
-
-        if opened:
-            for e in range(z.segments):
-                field = read_exact(z, buf, (e,), count * z.height)
-                empty = jnp.zeros((z.pad - z.nodes, z.cols), F32)
-                operand_buf[e] = operand_right(jnp.concatenate([field, empty], axis=0))
-                put(count, 0, e, field)
-            send(count, 0)
-            operand_copy = pltpu.make_async_copy(operand_buf, operand_ref, in_sem.at[1])
-            operand_copy.start()
-            sends.append(operand_copy)
-        for n in range(count):
-            matrix = operand_left(own_buf[low + n])
-            for e in range(z.segments):
-                value = product(matrix, operand_buf[e])[: z.nodes]
-                put(n, low + n, e, value + read_exact(z, buf, (e,), (place + n) * z.height))
-            send(n, low + n)
         for copy in sends:
             copy.wait()
 
-    result = f32(z.steps, tall, z.ax)
-    operand_shape = (z.segments, 2 * z.pad, z.cols)
-    inputs = [me, own] + list(messages)
-    in_specs = [spec_smem()] + [spec_hbm()] * (len(inputs) - 1)
-    aliases = {}
-    if opened:
-        outs = [result, jax.ShapeDtypeStruct(operand_shape, BF16)]
-        out_specs = [spec_hbm()] * 2
-    else:
-        inputs += [operands, out]
-        in_specs += [spec_hbm()] * 2
-        aliases = {len(inputs) - 1: 0}
-        outs = result
-        out_specs = spec_hbm()
+    inputs = [me, own, operands] + list(messages) + [out]
     return call(
         kernel,
         f"finish_{low}",
-        outs,
-        in_specs,
-        out_specs,
+        f32(z.steps, tall, z.ax),
+        [spec_smem()] + [spec_hbm()] * (len(inputs) - 1),
+        spec_hbm(),
         [
             pltpu.VMEM((z.segments, message, z.ax), F32),
-            pltpu.VMEM((z.steps, z.pad, z.pad), F32),
-            pltpu.VMEM(operand_shape, BF16),
-            pltpu.VMEM((len(steps), tall, z.ax), F32),
+            pltpu.VMEM((count, z.pad, z.pad), F32),
+            pltpu.VMEM(operands.shape, BF16),
+            pltpu.VMEM((count, tall, z.ax), F32),
             pltpu.SemaphoreType.DMA((z.segments,)),
             pltpu.SemaphoreType.DMA((2,)),
-            pltpu.SemaphoreType.DMA((len(steps),)),
+            pltpu.SemaphoreType.DMA((count,)),
         ],
         z.flops * count * z.segments,
         4 * 2 * count * tall * z.ax,
-        aliases,
+        {len(inputs) - 1: 0},
     )(*inputs)
 
 
@@ -615,8 +709,8 @@
 
 def chunks_of(steps):
     if steps >= 8:
-        return [(1, 3), (3, 5), (5, steps)]
-    return [(1, 2), (2, 3), (3, steps)]
+        return (1, 4), (4, steps), 1
+    return (1, 2), (2, steps), 1
 
 
 def body(state, rhs, to_modal, viscous_op, sweep_gain, inv_blocks):
@@ -630,32 +724,30 @@
     here = lax.axis_index("elem").astype(jnp.int32)
     me = here.reshape(1)
     places = jnp.stack([here, lax.axis_index("blk").astype(jnp.int32)])
-    one, two, three = chunks_of(z.steps)
+    one, two, paired = chunks_of(z.steps)
     sensors, head, tail = sensor_call(z, state, to_modal)
     lefts, rights = neighbours(head, tail)
 
-    def sweep(chunk, mode, ring, carry, after):
+    def sweep(chunk, paired, ring, carry, after):
         return sweep_call(
-            z, chunk, mode, me, state, rhs, viscous_op, gain, inverse, sensors, lefts, rights, ring, carry, after
+            z, chunk, paired, me, state, rhs, viscous_op, gain, inverse, sensors, lefts, rights, ring, carry, after
         )
 
-    messages_one, carry, low, high = sweep(one, "all", None, None, [])
+    messages_one, low, high = sweep(one, 0, None, None, [])
     ring = [shift_by(high, "blk", 1), shift_by(low, "blk", -1)]
-    own, heads, tails, wholes, prefix, group = maps_call(z, me, gain, [carry])
-    keep, give, carry = sweep(two, "pairs", None, carry, [group])
-    messages_three, carry, starts = sweep(three, "open", ring, carry, [])
-    before, pack = chain_call(z, starts, carry, tails, wholes, group)
+    own, heads, tails, wholes, prefix, group = maps_call(z, me, gain, [messages_one])
+    messages_two, keep, give, ends, starts = sweep(two, paired, ring, messages_one, [group])
+    before, pack = chain_call(z, starts, ends, tails, wholes, group)
     packs = [pack] + [shift_by(pack, "blk", s) for s in range(1, groups)]
-    place = three[1] - three[0]
-    messages_three = first_call(z, places, packs, before, prefix, heads, starts, messages_three, place)
+    middle = two[1] - paired
+    messages_two = first_call(z, places, packs, before, prefix, heads, starts, messages_two, middle - two[0])
     got = lax.ppermute(give, "elem", [(i, i ^ 1) for i in range(segments)])
     coupled = couple_call(z, keep, got)
     coupled = [coupled[0]] + [shift_by(coupled[d], "elem", 2 * d) for d in range(1, segments // 2)]
     received_one = spread(messages_one)
-    received_three = spread(messages_three)
-    out, operands = finish_call(z, three, "open", me, own, received_three, 0, None, None)
-    out = finish_call(z, one, "all", me, own, received_one, 0, operands, out)
-    out = finish_call(z, two, "pairs", me, own, coupled, 0, operands, out)
+    received_two = spread(gate_call(messages_two, [received_one, coupled[0]]))
+    out, operands = open_call(z, one, (two[0], middle), own, received_one, received_two)
+    out = finish_call(z, (middle, two[1]), me, own, coupled, operands, out)
     return out.reshape(z.steps, z.nodes, segments * z.rows, z.ax)
 
 

time: 306 us -> 225 us (0.74)
  blocking collectives: 94.1 us -> 0 us
  waiting for transfers between devices: 48.5 us -> 127 us
  Pallas kernels: 136 us -> 65 us
  starting transfers between devices: 20.9 us -> 27.5 us
    all_to_all x1 -> x2, waiting for transfers between devices: 0.01 us -> 110 us  [spread(): return lax.all_to_all(messages, 'elem', 0, 0, tiled=True)]
    all_to_all x1 -> x0, blocking collectives: 94.1 us -> none  [spread(): return lax.all_to_all(messages, 'elem', 0, 0, tiled=True)]
    pallas_call x1, Pallas kernels: 63.7 us -> 2.12 us  [couple_call(): call(kernel, 'couple', [f32(2, message, z.ax)] * pairs, [spec_hbm()] * 2,...]
    ppermute x8, waiting for transfers between devices: 42.5 us -> 13.4 us  [shift_by(): lax.ppermute(array, axis, [(i, (i + by) % size) for i in range(size)])]
    pallas_call x6 -> x5, Pallas kernels: 48.5 us -> 38.7 us  [the longest x2 27.3 us: sweep_call(): call(kernel, f'sweep_{low}', outs + more, in_specs + extra_specs + [spec_...]
    all_to_all x1 -> x2, starting transfers between devices: 6.09 us -> 12.2 us  [spread(): return lax.all_to_all(messages, 'elem', 0, 0, tiled=True)]
  transfers between devices with their start and end apart: 12 -> 13, of which waited for: 6 -> 8; matrix products, arithmetic and copies ran while one was open for 0% -> 0% of each run, Pallas kernels for 30% -> 20%
where the time goes in v5:
time: 225 us; the launch traced here: 224 us
  waiting for transfers between devices  127 us (56%)
  Pallas kernels  65 us (29%)
  starting transfers between devices  27.5 us (12%)
  local copies, waits for them, and re-layouts  3.58 us (2%)
    all_to_all x2, waiting for transfers between devices, spread(): return lax.all_to_all(messages, 'elem', 0, 0, tiled=True)  110 us
    pallas_call x2, Pallas kernels, sweep_call(): call(kernel, f'sweep_{low}', outs + more, in_specs + extra_specs + [spec_...  27.3 us
    ppermute x8, waiting for transfers between devices, shift_by(): lax.ppermute(array, axis, [(i, (i + by) % size) for i in range(size)])  13.4 us
    all_to_all x2, starting transfers between devices, spread(): return lax.all_to_all(messages, 'elem', 0, 0, tiled=True)  12.2 us
    ppermute x8, starting transfers between devices, shift_by(): lax.ppermute(array, axis, [(i, (i + by) % size) for i in range(size)])  8.7 us
    pallas_call x1, Pallas kernels, maps_call(): call(kernel, 'maps', outs, [spec_smem(), spec_hbm()] + [spec_any()] * len...  8.23 us
    pallas_call x1, Pallas kernels, open_call(): call(kernel, 'finish_0', [f32(z.steps, tall, z.ax), jax.ShapeDtypeStruct(...  8.19 us
    pallas_call x1, Pallas kernels, sensor_call(): call(kernel, 'sensor', outs, [spec_hbm()] * 2, [spec_vmem()] * 3, [pltpu....  6.29 us
  transfers between devices with their start and end apart: 13, of which 8 were waited for; matrix products, arithmetic and copies ran while one was open for 0% of the time, Pallas kernels for 20%

profile of v5, /device:TPU:9, one launch (start us, length us, event | category | flops | bytes accessed | tf_op | source)
XLA Modules:
  0.0 223.7 jit_solution(15421647852141325862)
XLA Ops:
  0.0 6.3 %sensor.1 = (f32[8,8,256]{2,1,0:T(8,128)}, f32[8,8,128]{2,1,0:T(8,128)}, f32[8,8,128]{2,1,0:T(8,128)}) custom-call(f32[8,2000,128]{2,1,0:T(8,128)} %bitcast.7, f32[125,125]{1,0:T(8,128)} %modal_ref.1), custom_call_target="tpu_custom_call" | custom-call | flops 2147483648 | bytes 8192000 | tf_op jit(solution)/shard_map/sensor/pallas_call | solution.py:153
  6.3 3.8 %collective-permute-start = (f32[8,8,128]{2,1,0:T(8,128)}, f32[8,8,128]{2,1,0:T(8,128)S(1)}, u32[]{:S(2)}, u32[]{:S(2)}) collective-permute-start(f32[8,8,128]{2,1,0:T(8,128)} %get-tuple-element.31), channel_id=1, source_target_pairs={{0,1},{1,2},{2,3},{3,4},{4,5},{5,6},{6,7},{8,9},{9,10},{10,11},{11... | collective-permute-start | bytes 98312 | tf_op jit(solution)/shard_map/ppermute | solution.py:701
  10.1 1.9 collective-permute-start.1
  12.0 0.0 collective-permute-done.refs_7_
  12.0 0.0 copy-start.6
  12.0 3.5 %collective-permute-done.1.refs_8_ = f32[8,8,128]{2,1,0:T(8,128)S(1)} collective-permute-done((f32[8,8,128]{2,1,0:T(8,128)}, f32[8,8,128]{2,1,0:T(8,128)S(1)}, u32[]{:S(2)}, u32[]{:S(2)}) %collective-permute-start.1) | collective-permute-done | bytes 32800 | tf_op jit(solution)/shard_map/ppermute | solution.py:702
  15.5 0.0 copy-start.7
  15.5 0.0 copy-done.6
  15.5 0.6 copy-done.7
  16.1 10.6 %sweep_1.1 = (f32[8,752,128]{2,1,0:T(8,128)}, f32[1,256]{1,0:T(1,128)}, f32[1,256]{1,0:T(1,128)}) custom-call(s32[1]{0:T(128)} %bitcast.refs_0_.me_ref, f32[8,2000,128]{2,1,0:T(8,128)} %bitcast.8, f32[8,2000,128]{2,1,0:T(8,128)} %bitcast.13, f32[125,125]{1,0:T(8,128)} %refs_3_.3, f32[125,64,125]{2,1,0:T(8,128)} %bitcast.15, f32[125,64,125]{2,1,0:T(8,128)} %bitcast.10, ...), custom_call_target="tpu_custom_call" | custom-call | flops 2415919104 | bytes 12320768 | tf_op jit(solution)/shard_map/sweep_1/pallas_call | solution.py:359
  26.8 0.0 copy-start.14
  26.8 0.0 copy-start.13
  26.8 4.1 %all-to-all-start = ((f32[8,752,128]{2,1,0:T(8,128)}), f32[8,752,128]{2,1,0:T(8,128)S(1)}, u32[]{:S(2)}, u32[]{:S(2)}) async-start(f32[8,752,128]{2,1,0:T(8,128)} %get-tuple-element.33.refs_0_.refs_11_), calls=%async_computation | async-start | bytes 6160384 | tf_op jit(solution)/shard_map/all_to_all | solution.py:707
  30.9 0.0 copy-done.14
  30.9 1.2 collective-permute-start.2
  32.1 0.0 copy-done.13
  32.1 1.2 collective-permute-start.3
  33.3 8.2 %maps.1 = (f32[8,128,128]{2,1,0:T(8,128)}, f32[8,128,128]{2,1,0:T(8,128)}, f32[8,128,128]{2,1,0:T(8,128)}, f32[8,128,128]{2,1,0:T(8,128)}, f32[8,128,128]{2,1,0:T(8,128)}, /*index=5*/f32[128,128]{1,0:T(8,128)}) custom-call(s32[1]{0:T(128)} %bitcast.refs_0_.me_ref, f32[125,64,125]{2,1,0:T(8,128)} %bitcast.11, f32[8,752,128]{2,1,0:T(8,128)} %get-tuple-element.33.refs_0_.refs_11_), custom_call_target="tpu_custom_call" | custom-call | flops 1207959552 | bytes 4194304 | tf_op jit(solution)/shard_map/maps/pallas_call | solution.py:406
  41.5 0.0 collective-permute-done.2.refs_9_
  41.5 0.0 copy-start.8
  41.5 0.0 collective-permute-done.3.refs_10_
  41.5 0.0 copy-start.9
  41.6 0.5 copy-done.8
  42.1 0.0 copy-done.9
  42.1 16.7 %sweep_4.1 = (f32[8,1000,128]{2,1,0:T(8,128)}, f32[4,256,128]{2,1,0:T(8,128)}, f32[4,256,128]{2,1,0:T(8,128)}, f32[8,128,256]{2,1,0:T(8,128)}, f32[8,128,256]{2,1,0:T(8,128)}) custom-call(s32[1]{0:T(128)} %bitcast.refs_0_.me_ref, f32[8,2000,128]{2,1,0:T(8,128)} %bitcast.9, f32[8,2000,128]{2,1,0:T(8,128)} %bitcast.14, f32[125,125]{1,0:T(8,128)} %refs_3_.3, ...), custom_call_target="tpu_custom_call" | custom-call | flops 4026531840 | bytes 16384000 | tf_op jit(solution)/shard_map/sweep_4/pallas_call | solution.py:359
  58.8 0.9 collective-permute-start.7
  59.8 4.4 %chain.1 = (f32[8,128,256]{2,1,0:T(8,128)}, f32[128,384]{1,0:T(8,128)}) custom-call(f32[8,128,256]{2,1,0:T(8,128)} %get-tuple-element.38.start_ref.refs_8_, f32[8,128,256]{2,1,0:T(8,128)} %get-tuple-element.39.end_ref, f32[8,128,128]{2,1,0:T(8,128)} %get-tuple-element.40.tail_ref, f32[8,128,128]{2,1,0:T(8,128)} %get-tuple-element.41.whole_ref, ...), custom_call_target="tpu_custom_call" | custom-call | flops 536870912 | bytes 4194304 | tf_op jit(solution)/shard_map/chain/pallas_call | solution.py:436
  64.2 1.3 collective-permute-start.6
  65.4 0.2 collective-permute-start.5
  65.7 1.2 collective-permute-start.4
  66.9 0.6 pad_add_fusion.refs_0_
  67.5 3.4 %collective-permute-done.6.refs_4_ = f32[128,384]{1,0:T(8,128)S(1)} collective-permute-done((f32[128,384]{1,0:T(8,128)}, f32[128,384]{1,0:T(8,128)S(1)}, u32[]{:S(2)}, u32[]{:S(2)}) %collective-permute-start.6) | collective-permute-done | bytes 196640 | tf_op jit(solution)/shard_map/ppermute | solution.py:696
  70.9 0.0 copy-start.4
  70.9 1.0 collective-permute-done.5.refs_3_
  71.8 0.0 copy-start.5
  71.8 4.4 %collective-permute-done.4.refs_2_ = f32[128,384]{1,0:T(8,128)} collective-permute-done((f32[128,384]{1,0:T(8,128)}, f32[128,384]{1,0:T(8,128)}, u32[]{:S(2)}, u32[]{:S(2)}) %collective-permute-start.4) | collective-permute-done | bytes 196640 | tf_op jit(solution)/shard_map/ppermute | solution.py:696
  76.2 0.0 copy-done.4
  76.2 0.0 copy-done.5
  76.2 5.3 %first.1.refs_0_ = f32[8,1000,128]{2,1,0:T(8,128)} custom-call(s32[2]{0:T(128)} %pad_add_fusion.refs_0_, f32[128,384]{1,0:T(8,128)} %get-tuple-element.42.refs_1_, f32[128,384]{1,0:T(8,128)} %collective-permute-done.4.refs_2_, f32[128,384]{1,0:T(8,128)} %copy-done.5, f32[128,384]{1,0:T(8,128)} %copy-done.4, ...), custom_call_target="tpu_custom_call", output_to_operand_aliasing={{}: (9, {})} | custom-call | flops 805306368 | bytes 4194304 | tf_op jit(solution)/shard_map/first/pallas_call | solution.py:487
  81.5 0.0 collective-permute-done.7.refs_1_
  81.6 2.1 couple.1
  83.7 13.8 %all-to-all-done.refs_1_.one_ref = f32[8,752,128]{2,1,0:T(8,128)S(1)} async-done(((f32[8,752,128]{2,1,0:T(8,128)}), f32[8,752,128]{2,1,0:T(8,128)S(1)}, u32[]{:S(2)}, u32[]{:S(2)}) %all-to-all-start) | async-done | bytes 3080224 | tf_op jit(solution)/shard_map/all_to_all | solution.py:707
  97.4 0.0 copy-start
  97.4 1.6 copy-done
  99.1 0.0 copy-start.12
  99.1 0.0 copy-start.11
  99.1 8.1 %all-to-all-start.1 = ((f32[8,1000,128]{2,1,0:T(8,128)}), f32[8,1000,128]{2,1,0:T(8,128)}, u32[]{:S(2)}, u32[]{:S(2)}) async-start(f32[8,1000,128]{2,1,0:T(8,128)} %gate.1), calls=%async_computation.1 | async-start | bytes 8192000 | tf_op jit(solution)/shard_map/all_to_all | solution.py:707
  107.2 0.0 copy-done.12
  107.2 1.2 collective-permute-start.8
  108.4 0.0 copy-done.11
  108.4 1.0 collective-permute-start.9
  109.4 0.0 copy-done.10
  109.4 1.4 collective-permute-start.10
  110.8 96.0 %all-to-all-done.1.two_ref = f32[8,1000,128]{2,1,0:T(8,128)} async-done(((f32[8,1000,128]{2,1,0:T(8,128)}), f32[8,1000,128]{2,1,0:T(8,128)}, u32[]{:S(2)}, u32[]{:S(2)}) %all-to-all-start.1) | async-done | bytes 4096032 | tf_op jit(solution)/shard_map/all_to_all | solution.py:707
  206.8 8.2 %finish_0.1 = (f32[8,2000,128]{2,1,0:T(8,128)}, bf16[8,256,256]{2,1,0:T(8,128)(2,1)}) custom-call(f32[8,128,128]{2,1,0:T(8,128)} %get-tuple-element.34.own_ref, f32[8,752,128]{2,1,0:T(8,128)} %copy-done, f32[8,1000,128]{2,1,0:T(8,128)} %all-to-all-done.1.two_ref), custom_call_target="tpu_custom_call" | custom-call | flops 1610612736 | bytes 14336000 | tf_op jit(solution)/shard_map/finish_0/pallas_call | solution.py:602
  215.0 0.0 collective-permute-done.8.refs_1_
  215.0 0.0 copy-start.1
  215.0 2.9 %collective-permute-done.9.refs_2_ = f32[2,256,128]{2,1,0:T(8,128)S(1)} collective-permute-done((f32[2,256,128]{2,1,0:T(8,128)S(1)}, f32[2,256,128]{2,1,0:T(8,128)S(1)}, u32[]{:S(2)}, u32[]{:S(2)}) %collective-permute-start.9) | collective-permute-done | bytes 262176 | tf_op jit(solution)/shard_map/ppermute | solution.py:696
  217.9 0.0 copy-start.2
  217.9 1.7 collective-permute-done.10.refs_3_
  219.6 0.0 copy-done.1
  219.6 0.0 copy-done.2
  219.6 0.7 copy-done.3
  220.3 3.2 %finish_7.1 = f32[8,2000,128]{2,1,0:T(8,128)} custom-call(s32[1]{0:T(128)} %bitcast.refs_0_.me_ref, f32[8,128,128]{2,1,0:T(8,128)} %get-tuple-element.34.own_ref, bf16[8,256,256]{2,1,0:T(8,128)(2,1)} %get-tuple-element.50.operand_ref, f32[2,256,128]{2,1,0:T(8,128)} %get-tuple-element.49.refs_2_.refs_0_, ...), custom_call_target="tpu_custom_call", output_to_operand_aliasing={{}: (7, {})} | custom-call | flops 268435456 | bytes 2048000 | tf_op jit(solution)/shard_map/finish_7/pallas_call | solution.py:673
  (3 shorter events, 0.0 us)
Async XLA Ops:
  6.3 5.7 %collective-permute-start = (f32[8,8,128]{2,1,0:T(8,128)}, f32[8,8,128]{2,1,0:T(8,128)S(1)}, u32[]{:S(2)}, u32[]{:S(2)}) collective-permute-start(f32[8,8,128]{2,1,0:T(8,128)} %get-tuple-element.31), channel_id=1, source_target_pairs={{0,1},{1,2},{2,3},{3,4},{4,5},{5,6},{6,7},{8,9},{9,10},{10,11},{11... | collective-permute-start | bytes 98312 | tf_op jit(solution)/shard_map/ppermute | solution.py:701
  10.1 5.4 %collective-permute-start.1 = (f32[8,8,128]{2,1,0:T(8,128)}, f32[8,8,128]{2,1,0:T(8,128)S(1)}, u32[]{:S(2)}, u32[]{:S(2)}) collective-permute-start(f32[8,8,128]{2,1,0:T(8,128)} %get-tuple-element.32), channel_id=1, source_target_pairs={{1,0},{2,1},{3,2},{4,3},{5,4},{6,5},{7,6},{9,8},{10,9},{11,10},{12... | collective-permute-start | bytes 98312 | tf_op jit(solution)/shard_map/ppermute | solution.py:702
  12.0 3.5 %copy-start.6 = (f32[8,8,128]{2,1,0:T(8,128)}, f32[8,8,128]{2,1,0:T(8,128)S(1)}, u32[]{:S(2)}) copy-start(f32[8,8,128]{2,1,0:T(8,128)S(1)} %collective-permute-done.refs_7_) | copy-start | bytes 98308
  15.5 0.6 copy-start.7
  26.8 4.1 %copy-start.14 = (f32[1,256]{1,0:T(1,128)S(1)}, f32[1,256]{1,0:T(1,128)}, u32[]{:S(2)}) copy-start(f32[1,256]{1,0:T(1,128)} %get-tuple-element.35) | copy-start | bytes 3076
  26.8 5.3 %copy-start.13 = (f32[1,256]{1,0:T(1,128)S(1)}, f32[1,256]{1,0:T(1,128)}, u32[]{:S(2)}) copy-start(f32[1,256]{1,0:T(1,128)} %get-tuple-element.36) | copy-start | bytes 3076
  26.8 70.6 %all-to-all-start = ((f32[8,752,128]{2,1,0:T(8,128)}), f32[8,752,128]{2,1,0:T(8,128)S(1)}, u32[]{:S(2)}, u32[]{:S(2)}) async-start(f32[8,752,128]{2,1,0:T(8,128)} %get-tuple-element.33.refs_0_.refs_11_), calls=%async_computation | async-start | bytes 6160384 | tf_op jit(solution)/shard_map/all_to_all | solution.py:707
  30.9 10.7 %collective-permute-start.2 = (f32[1,256]{1,0:T(1,128)S(1)}, f32[1,256]{1,0:T(1,128)S(1)}, u32[]{:S(2)}, u32[]{:S(2)}) collective-permute-start(f32[1,256]{1,0:T(1,128)S(1)} %copy-done.14), channel_id=1, source_target_pairs={{0,8},{8,16},{16,24},{24,0},{1,9},{9,17},{17,25},{25,1},{2,10},{10... | collective-permute-start | bytes 3080 | tf_op jit(solution)/shard_map/ppermute | solution.py:696
  32.1 9.5 %collective-permute-start.3 = (f32[1,256]{1,0:T(1,128)S(1)}, f32[1,256]{1,0:T(1,128)S(1)}, u32[]{:S(2)}, u32[]{:S(2)}) collective-permute-start(f32[1,256]{1,0:T(1,128)S(1)} %copy-done.13), channel_id=1, source_target_pairs={{0,24},{8,0},{16,8},{24,16},{1,25},{9,1},{17,9},{25,17},{2,26},{10... | collective-permute-start | bytes 3080 | tf_op jit(solution)/shard_map/ppermute | solution.py:696
  41.5 0.6 copy-start.8
  41.5 0.6 copy-start.9
  58.8 22.7 %collective-permute-start.7 = (f32[4,256,128]{2,1,0:T(8,128)}, f32[4,256,128]{2,1,0:T(8,128)}, u32[]{:S(2)}, u32[]{:S(2)}) collective-permute-start(f32[4,256,128]{2,1,0:T(8,128)} %get-tuple-element.48), channel_id=1, source_target_pairs={{0,1},{1,0},{2,3},{3,2},{4,5},{5,4},{6,7},{7,6},{8,9},{9,8},{10,11... | collective-permute-start | bytes 1572872 | tf_op jit(solution)/shard_map/ppermute | solution.py:744
  64.2 6.7 %collective-permute-start.6 = (f32[128,384]{1,0:T(8,128)}, f32[128,384]{1,0:T(8,128)S(1)}, u32[]{:S(2)}, u32[]{:S(2)}) collective-permute-start(f32[128,384]{1,0:T(8,128)} %get-tuple-element.42.refs_1_), channel_id=1, source_target_pairs={{0,24},{8,0},{16,8},{24,16},{1,25},{9,1},{17,9},{25,17},{2,26},{10... | collective-permute-start | bytes 589832 | tf_op jit(solution)/shard_map/ppermute | solution.py:696
  65.4 6.4 %collective-permute-start.5 = (f32[128,384]{1,0:T(8,128)}, f32[128,384]{1,0:T(8,128)S(1)}, u32[]{:S(2)}, u32[]{:S(2)}) collective-permute-start(f32[128,384]{1,0:T(8,128)} %get-tuple-element.42.refs_1_), channel_id=1, source_target_pairs={{0,16},{8,24},{16,0},{24,8},{1,17},{9,25},{17,1},{25,9},{2,18},{10... | collective-permute-start | bytes 589832 | tf_op jit(solution)/shard_map/ppermute | solution.py:696
  65.7 10.5 %collective-permute-start.4 = (f32[128,384]{1,0:T(8,128)}, f32[128,384]{1,0:T(8,128)}, u32[]{:S(2)}, u32[]{:S(2)}) collective-permute-start(f32[128,384]{1,0:T(8,128)} %get-tuple-element.42.refs_1_), channel_id=1, source_target_pairs={{0,8},{8,16},{16,24},{24,0},{1,9},{9,17},{17,25},{25,1},{2,10},{10... | collective-permute-start | bytes 589832 | tf_op jit(solution)/shard_map/ppermute | solution.py:696
  70.9 5.3 %copy-start.4 = (f32[128,384]{1,0:T(8,128)}, f32[128,384]{1,0:T(8,128)S(1)}, u32[]{:S(2)}) copy-start(f32[128,384]{1,0:T(8,128)S(1)} %collective-permute-done.6.refs_4_) | copy-start | bytes 589828
  71.8 4.4 %copy-start.5 = (f32[128,384]{1,0:T(8,128)}, f32[128,384]{1,0:T(8,128)S(1)}, u32[]{:S(2)}) copy-start(f32[128,384]{1,0:T(8,128)S(1)} %collective-permute-done.5.refs_3_) | copy-start | bytes 589828
  97.4 1.7 copy-start
  99.1 8.1 %copy-start.12 = (f32[2,256,128]{2,1,0:T(8,128)S(1)}, f32[2,256,128]{2,1,0:T(8,128)}, u32[]{:S(2)}) copy-start(f32[2,256,128]{2,1,0:T(8,128)} %get-tuple-element.51) | copy-start | bytes 786436
  99.1 9.3 %copy-start.11 = (f32[2,256,128]{2,1,0:T(8,128)S(1)}, f32[2,256,128]{2,1,0:T(8,128)}, u32[]{:S(2)}) copy-start(f32[2,256,128]{2,1,0:T(8,128)} %get-tuple-element.52) | copy-start | bytes 786436
  99.1 10.3 %copy-start.10 = (f32[2,256,128]{2,1,0:T(8,128)S(1)}, f32[2,256,128]{2,1,0:T(8,128)}, u32[]{:S(2)}) copy-start(f32[2,256,128]{2,1,0:T(8,128)} %get-tuple-element.53) | copy-start | bytes 786436
  99.1 107.7 %all-to-all-start.1 = ((f32[8,1000,128]{2,1,0:T(8,128)}), f32[8,1000,128]{2,1,0:T(8,128)}, u32[]{:S(2)}, u32[]{:S(2)}) async-start(f32[8,1000,128]{2,1,0:T(8,128)} %gate.1), calls=%async_computation.1 | async-start | bytes 8192000 | tf_op jit(solution)/shard_map/all_to_all | solution.py:707
  107.2 107.8 %collective-permute-start.8 = (f32[2,256,128]{2,1,0:T(8,128)S(1)}, f32[2,256,128]{2,1,0:T(8,128)S(1)}, u32[]{:S(2)}, u32[]{:S(2)}) collective-permute-start(f32[2,256,128]{2,1,0:T(8,128)S(1)} %copy-done.12), channel_id=1, source_target_pairs={{0,2},{1,3},{2,4},{3,5},{4,6},{5,7},{6,0},{7,1},{8,10},{9,11},{10,... | collective-permute-start | bytes 786440 | tf_op jit(solution)/shard_map/ppermute | solution.py:696
  108.4 109.5 %collective-permute-start.9 = (f32[2,256,128]{2,1,0:T(8,128)S(1)}, f32[2,256,128]{2,1,0:T(8,128)S(1)}, u32[]{:S(2)}, u32[]{:S(2)}) collective-permute-start(f32[2,256,128]{2,1,0:T(8,128)S(1)} %copy-done.11), channel_id=1, source_target_pairs={{0,4},{1,5},{2,6},{3,7},{4,0},{5,1},{6,2},{7,3},{8,12},{9,13},{10,... | collective-permute-start | bytes 786440 | tf_op jit(solution)/shard_map/ppermute | solution.py:696
  109.4 110.2 %collective-permute-start.10 = (f32[2,256,128]{2,1,0:T(8,128)S(1)}, f32[2,256,128]{2,1,0:T(8,128)S(1)}, u32[]{:S(2)}, u32[]{:S(2)}) collective-permute-start(f32[2,256,128]{2,1,0:T(8,128)S(1)} %copy-done.10), channel_id=1, source_target_pairs={{0,6},{1,7},{2,0},{3,1},{4,2},{5,3},{6,4},{7,5},{8,14},{9,15},{10,... | collective-permute-start | bytes 786440 | tf_op jit(solution)/shard_map/ppermute | solution.py:696
  215.0 4.6 %copy-start.1 = (f32[2,256,128]{2,1,0:T(8,128)}, f32[2,256,128]{2,1,0:T(8,128)S(1)}, u32[]{:S(2)}) copy-start(f32[2,256,128]{2,1,0:T(8,128)S(1)} %collective-permute-done.8.refs_1_) | copy-start | bytes 786436
  217.9 1.7 copy-start.2
  219.6 0.7 copy-start.3

commit v6 on v5

--- a/solution.py
+++ b/solution.py
@@ -119,6 +119,34 @@
 
 def read_matrix(z, ref, k):
     return z.square(ref[:, k, :])
+
+
+def send_pair(z, mine, e, stage, keep_ref, give_ref, sem):
+    pairs = z.segments // 2
+    place = lax.rem(e // 2 - mine // 2 + pairs, pairs)
+    own = lax.rem(mine, 2) == e % 2
+
+    @pl.when(own)
+    def _():
+        pltpu.make_async_copy(stage.at[e], keep_ref.at[place], sem.at[e]).start()
+
+    @pl.when(jnp.logical_not(own))
+    def _():
+        pltpu.make_async_copy(stage.at[e], give_ref.at[place], sem.at[e]).start()
+
+    return pltpu.make_async_copy(stage.at[e], keep_ref.at[place], sem.at[e])
+
+
+def load_pairs(z, mine, sources, buf, sem):
+    pairs = z.segments // 2
+    side = lax.rem(mine, 2)
+    copies = []
+    for d in range(pairs):
+        pair = lax.rem(mine // 2 - d + pairs, pairs) * 2
+        for n in range(2):
+            e = pair + (side if n == 0 else 1 - side)
+            copies.append(pltpu.make_async_copy(sources[d].at[n], buf.at[e], sem.at[2 * d + n]))
+    return copies
 
 
 def sensor_call(z, state, to_modal):
@@ -164,6 +192,7 @@
         ],
         z.flops * z.steps * z.segments,
         4 * z.segments * tall * z.ax,
+        limit=57,
     )(state, to_modal)
 
 
@@ -175,7 +204,7 @@
     return (4.0 * sensor + before + after + from_left + from_right) / 8.0
 
 
-def sweep_call(z, chunk, paired, me, state, rhs, viscous, gain, inverse, sensors, lefts, rights, ring, carry, after):
+def sweep_call(z, chunk, parts, me, state, rhs, viscous, gain, inverse, sensors, lefts, rights, ring, carry, after):
     low, high = chunk
     opened = high == z.steps
     first, size = z.window(low, high)
@@ -184,14 +213,17 @@
     steps = list(range(low, high)) + ([0] if opened else [])
     has_carry = carry is not None
     gains = list(range(low if has_carry else low + 1, high))
-    rest = count - paired
-    message = z.message(rest + (1 if opened else 0))
-    paired_message = z.message(paired)
+    messages = [z.message(stop - start) for start, stop in parts or [chunk]]
     edge_outs = low == 1
     pairs = z.segments // 2
     last, last_size = z.window(low - 2, low - 1)
     batch = next(n for n in (4, 8, z.segments) if z.segments % n == 0 and n * z.steps % TILE == 0)
     narrow = low == 1
+
+    if parts:
+        outs = [f32(pairs, message, z.ax) for message in messages for _ in range(2)]
+    else:
+        outs = [f32(z.segments, messages[0], z.ax)]
 
     def kernel(*refs):
         me_ref, state_ref, rhs_ref, viscous_ref, inverse_ref, gain_ref, sensor_ref, left_ref, right_ref = refs[:9]
@@ -201,22 +233,18 @@
         if has_carry:
             carry_ref, refs = refs[0], refs[1:]
         refs = refs[len(after) :]
-        out_ref, refs = refs[0], refs[1:]
-        if paired:
-            keep_ref, give_ref, refs = refs[0], refs[1], refs[2:]
+        out_refs, refs = refs[: len(outs)], refs[len(outs) :]
         if opened:
             end_ref, start_ref, refs = refs[0], refs[1], refs[2:]
         if edge_outs:
             low_ref, high_ref, refs = refs[0], refs[1], refs[2:]
-        state_buf, rhs_buf, inverse_buf, gain_buf, viscous_buf, smooth_buf, stage, sem, matrix_sem, out_sem = refs[:10]
-        refs = refs[10:]
+        state_buf, rhs_buf, inverse_buf, gain_buf, viscous_buf, smooth_buf, sem, matrix_sem, out_sem = refs[:9]
+        stages, refs = refs[9 : 9 + len(messages)], refs[9 + len(messages) :]
         if opened:
             state0, rhs0, refs = refs[0], refs[1], refs[2:]
-        if paired:
-            pair_stage, pair_sem, refs = refs[0], refs[1], refs[2:]
         if has_carry:
             carry_buf = refs[0]
-        viscous_copy = pltpu.make_async_copy(viscous_ref, viscous_buf, out_sem.at[0])
+        viscous_copy = pltpu.make_async_copy(viscous_ref, viscous_buf, out_sem.at[0, 0])
         viscous_copy.start()
         copies = [[] for _ in range(z.segments)]
         for s0 in range(0, z.segments, batch):
@@ -260,21 +288,6 @@
         operator = operand_left(z.square(viscous_buf[...]))
         sends = []
 
-        def send_pairs(s):
-            side = lax.rem(me_ref[0], 2)
-            place = lax.rem(s // 2 - me_ref[0] // 2 + pairs, pairs)
-            own = side == s % 2
-
-            @pl.when(own)
-            def _():
-                pltpu.make_async_copy(pair_stage.at[s], keep_ref.at[place], pair_sem.at[s]).start()
-
-            @pl.when(jnp.logical_not(own))
-            def _():
-                pltpu.make_async_copy(pair_stage.at[s], give_ref.at[place], pair_sem.at[s]).start()
-
-            sends.append(pltpu.make_async_copy(pair_stage.at[s], keep_ref.at[place], pair_sem.at[s]))
-
         for s0 in range(0, z.segments, batch):
             group = range(s0, s0 + batch)
             for s in group:
@@ -311,24 +324,24 @@
                     values = [value + more for value, more in zip(values, swept)]
                 fields = values
                 for s, value in zip(group, values):
-                    if n >= rest:
-                        write_field(z, pair_stage, (s,), (n - rest) * z.height, value)
-                    else:
-                        write_field(z, stage, (s,), n * z.height, value)
+                    for (start, stop), stage in zip(parts or [chunk], stages):
+                        if start <= i < stop:
+                            write_field(z, stage, (s,), (i - start) * z.height, value)
             for s, value in zip(group, fields):
                 if opened:
                     end_ref[s] = value
-                copy = pltpu.make_async_copy(stage.at[s], out_ref.at[s], out_sem.at[s])
-                copy.start()
-                sends.append(copy)
-            if paired:
+                if not parts:
+                    copy = pltpu.make_async_copy(stages[0].at[s], out_refs[0].at[s], out_sem.at[0, s])
+                    copy.start()
+                    sends.append(copy)
+            for p, stage in enumerate(stages if parts else []):
                 for s in group:
-                    send_pairs(s)
+                    keep_ref, give_ref = out_refs[2 * p], out_refs[2 * p + 1]
+                    sends.append(send_pair(z, me_ref[0], s, stage, keep_ref, give_ref, out_sem.at[p]))
         for copy in sends:
             copy.wait()
 
     field = f32(z.segments, z.pad, z.cols)
-    outs = [f32(z.segments, message, z.ax)] + [f32(pairs, paired_message, z.ax)] * (2 if paired else 0)
     out_specs = [spec_hbm()] * len(outs)
     more = [field] * (2 if opened else 0) + ([f32(1, z.cols)] * 2 if edge_outs else [])
     operands = [me, state, rhs, viscous, inverse, gain, sensors, lefts, rights]
@@ -345,15 +358,13 @@
         pltpu.VMEM(gain.shape, F32),
         pltpu.VMEM(viscous.shape, F32),
         pltpu.VMEM((len(steps), z.segments, z.cols), F32),
-        pltpu.VMEM((z.segments, message, z.ax), F32),
         pltpu.SemaphoreType.DMA((z.segments, 7)),
         pltpu.SemaphoreType.DMA((z.segments, 2)),
-        pltpu.SemaphoreType.DMA((z.segments,)),
+        pltpu.SemaphoreType.DMA((len(messages), z.segments)),
     ]
+    scratch += [pltpu.VMEM((z.segments, message, z.ax), F32) for message in messages]
     if opened:
         scratch += [pltpu.VMEM((z.segments, size0 + z.spill, z.ax), F32)] * 2
-    if paired:
-        scratch += [pltpu.VMEM((z.segments, paired_message, z.ax), F32), pltpu.SemaphoreType.DMA((z.segments,))]
     if has_carry:
         scratch.append(pltpu.VMEM((z.segments, last_size + z.spill, z.ax), F32))
     return call(
@@ -445,21 +456,15 @@
     )(starts, ends, tails, wholes, group)
 
 
-def first_call(z, places, packs, before, prefix, heads, starts, messages, place):
-    offset = place * z.height
-    base = offset // TILE * TILE
-    size = messages.shape[1] - base
+def first_call(z, places, packs, before, prefix, heads, starts):
+    rows = z.message(1)
+    pairs = z.segments // 2
 
     def kernel(*refs):
         places_ref, refs = refs[0], refs[1:]
         pack_refs, refs = refs[: z.groups], refs[z.groups :]
-        before_ref, prefix_ref, head_ref, start_ref, message_ref, out_ref, stage, sem = refs
-        copies = [
-            pltpu.make_async_copy(message_ref.at[e, pl.ds(base, size)], stage.at[e], sem.at[e])
-            for e in range(z.segments)
-        ]
-        for copy in copies:
-            copy.start()
+        before_ref, prefix_ref, head_ref, start_ref, keep_ref, give_ref, stage, sem = refs
+        mine = places_ref[0]
         group = places_ref[1]
         value = jnp.zeros((z.pad, z.cols), F32)
         matrices = [operand_left(ref[:, z.cols :]) for ref in pack_refs]
@@ -474,27 +479,22 @@
         solved = [
             start_ref[e] + product(operand_left(head_ref[e]), operand_right(arriving[e])) for e in range(z.segments)
         ]
-        sends = []
         for e in range(z.segments):
-            copies[e].wait()
-            write_field(z, stage, (e,), offset - base, solved[e])
-            copy = pltpu.make_async_copy(stage.at[e], out_ref.at[e, pl.ds(base, size)], sem.at[e])
-            copy.start()
-            sends.append(copy)
+            write_field(z, stage, (e,), 0, solved[e])
+        sends = [send_pair(z, mine, e, stage, keep_ref, give_ref, sem) for e in range(z.segments)]
         for copy in sends:
             copy.wait()
 
     return call(
         kernel,
         "first",
-        f32(*messages.shape),
-        [spec_smem()] + [spec_vmem()] * (z.groups + 4) + [spec_hbm()],
-        spec_hbm(),
-        [pltpu.VMEM((z.segments, size, z.ax), F32), pltpu.SemaphoreType.DMA((z.segments,))],
+        [f32(pairs, rows, z.ax)] * 2,
+        [spec_smem()] + [spec_vmem()] * (z.groups + 4),
+        [spec_hbm()] * 2,
+        [pltpu.VMEM((z.segments, rows, z.ax), F32), pltpu.SemaphoreType.DMA((z.segments,))],
         z.flops * (z.segments * 2 + 2 * z.groups),
         4 * z.segments * z.pad * z.cols * 4,
-        {z.groups + 5: 0},
-    )(places, *packs, before, prefix, heads, starts, messages)
+    )(places, *packs, before, prefix, heads, starts)
 
 
 def couple_call(z, keep, got):
@@ -539,33 +539,34 @@
     return call(
         kernel,
         "gate",
-        f32(*held.shape),
-        [spec_hbm()] + [spec_any()] * len(after),
-        spec_hbm(),
+        [f32(*array.shape) for array in held],
+        [spec_hbm()] * len(held) + [spec_any()] * len(after),
+        [spec_hbm()] * len(held),
         [],
         0,
         0,
-        {0: 0},
-    )(held, *after)
-
-
-def open_call(z, one, two, own, received_one, received_two):
+        {n: n for n in range(len(held))},
+    )(*held, *after)
+
+
+def open_call(z, one, me, own, received_one, received_first):
     radial = z.segments * z.rows
     tall = z.nodes * radial
     operand_shape = (z.segments, 2 * z.pad, z.cols)
-    low, middle, high = one[0], two[0], two[1]
-    messages = (received_one, received_two)
-
-    def kernel(own_ref, one_ref, two_ref, out_ref, operand_ref, own_buf, one_buf, two_buf, stage, sem, own_sem, out_sem):
+    low, high = one
+    pairs = z.segments // 2
+    message = received_first[0].shape[1]
+
+    def kernel(me_ref, own_ref, one_ref, *refs):
+        first_refs, refs = refs[:pairs], refs[pairs:]
+        out_ref, operand_ref, own_buf, one_buf, first_buf, stage, one_sem, first_sem, own_sem, out_sem = refs
+        first_copies = load_pairs(z, me_ref[0], first_refs, first_buf, first_sem)
+        one_copies = [pltpu.make_async_copy(one_ref.at[e], one_buf.at[e], one_sem.at[e]) for e in range(z.segments)]
         own_copy = pltpu.make_async_copy(own_ref, own_buf, own_sem)
-        own_copy.start()
-        copies = []
-        for n, (source, target) in enumerate(((two_ref, two_buf), (one_ref, one_buf))):
-            copies.append(
-                [pltpu.make_async_copy(source.at[e], target.at[e], sem.at[e, n]) for e in range(z.segments)]
-            )
-            for copy in copies[n]:
-                copy.start()
+        for copy in first_copies + [own_copy] + one_copies:
+            copy.start()
+        for copy in first_copies:
+            copy.wait()
         sends = []
 
         def put(i, e, value):
@@ -579,22 +580,19 @@
             sends.append(copy)
 
         for e in range(z.segments):
-            copies[0][e].wait()
-            field = read_exact(z, two_buf, (e,), (high - middle) * z.height)
+            field = read_exact(z, first_buf, (e,), 0)
             empty = jnp.zeros((z.pad - z.nodes, z.cols), F32)
             operand_ref[e] = operand_right(jnp.concatenate([field, empty], axis=0))
             put(0, e, field)
         send(0)
         own_copy.wait()
-        for i in list(range(middle, high)) + list(range(low, middle)):
-            if i == low:
-                for copy in copies[1]:
-                    copy.wait()
-            buf, offset = (two_buf, i - middle) if i >= middle else (one_buf, i - low)
+        for copy in one_copies:
+            copy.wait()
+        for i in range(low, high):
             matrix = operand_left(own_buf[i])
             for e in range(z.segments):
                 value = product(matrix, operand_ref[e])[: z.nodes]
-                put(i, e, value + read_exact(z, buf, (e,), offset * z.height))
+                put(i, e, value + read_exact(z, one_buf, (e,), (i - low) * z.height))
             send(i)
         for copy in sends:
             copy.wait()
@@ -603,20 +601,21 @@
         kernel,
         "finish_0",
         [f32(z.steps, tall, z.ax), jax.ShapeDtypeStruct(operand_shape, BF16)],
-        [spec_hbm()] * 3,
+        [spec_smem()] + [spec_hbm()] * (2 + pairs),
         [spec_hbm(), spec_vmem()],
         [
             pltpu.VMEM((z.steps, z.pad, z.pad), F32),
             pltpu.VMEM(received_one.shape, F32),
-            pltpu.VMEM(received_two.shape, F32),
+            pltpu.VMEM((z.segments, message, z.ax), F32),
             pltpu.VMEM((high, tall, z.ax), F32),
-            pltpu.SemaphoreType.DMA((z.segments, 2)),
+            pltpu.SemaphoreType.DMA((z.segments,)),
+            pltpu.SemaphoreType.DMA((z.segments,)),
             pltpu.SemaphoreType.DMA,
             pltpu.SemaphoreType.DMA((high,)),
         ],
         z.flops * (high - 1) * z.segments,
         4 * 2 * high * tall * z.ax,
-    )(own, *messages)
+    )(me, own, received_one, *received_first)
 
 
 def finish_call(z, chunk, me, own, messages, operands, out):
@@ -624,8 +623,6 @@
     count = high - low
     radial = z.segments * z.rows
     tall = z.nodes * radial
-    pairs = z.segments // 2
-    paired = len(messages) > 1
     message = messages[0].shape[1]
 
     def kernel(me_ref, own_ref, operand_ref, *refs):
@@ -635,30 +632,17 @@
         operand_copy = pltpu.make_async_copy(operand_ref, operand_buf, in_sem.at[1])
         own_copy.start()
         operand_copy.start()
-        copies = []
-        if paired:
-            mine = me_ref[0]
-            side = lax.rem(mine, 2)
-            for d in range(pairs):
-                pair = lax.rem(mine // 2 - d + pairs, pairs) * 2
-                for n in range(2):
-                    e = pair + (side if n == 0 else 1 - side)
-                    copies.append(pltpu.make_async_copy(message_refs[d].at[n], buf.at[e], sem.at[2 * d + n]))
-        else:
-            copies = [pltpu.make_async_copy(message_refs[0].at[e], buf.at[e], sem.at[e]) for e in range(z.segments)]
+        copies = load_pairs(z, me_ref[0], message_refs, buf, sem)
         for copy in copies:
             copy.start()
         own_copy.wait()
         operand_copy.wait()
-        if paired:
-            for copy in copies:
-                copy.wait()
+        for copy in copies:
+            copy.wait()
         sends = []
         for n in range(count):
             matrix = operand_left(own_buf[n])
             for e in range(z.segments):
-                if n == 0 and not paired:
-                    copies[e].wait()
                 value = product(matrix, operand_buf[e])[: z.nodes] + read_exact(z, buf, (e,), n * z.height)
                 for j in range(z.rows):
                     rows = pl.ds(e * z.rows + j, z.nodes, stride=radial)
@@ -707,10 +691,19 @@
     return lax.all_to_all(messages, "elem", 0, 0, tiled=True)
 
 
+def spread_pairs(z, keep, give, after):
+    got = lax.ppermute(give, "elem", [(i, i ^ 1) for i in range(z.segments)])
+    coupled = couple_call(z, keep, got)
+    if after:
+        coupled = gate_call(coupled, after)
+    return [coupled[0]] + [shift_by(coupled[d], "elem", 2 * d) for d in range(1, z.segments // 2)]
+
+
 def chunks_of(steps):
-    if steps >= 8:
-        return (1, 4), (4, steps), 1
-    return (1, 2), (2, steps), 1
+    middle = 4 if steps >= 8 else 2
+    last = steps - 1
+    parts = [(middle, last), (last, steps)] if last > middle else [(middle, steps)]
+    return (1, middle), (middle, steps), parts
 
 
 def body(state, rhs, to_modal, viscous_op, sweep_gain, inv_blocks):
@@ -724,30 +717,30 @@
     here = lax.axis_index("elem").astype(jnp.int32)
     me = here.reshape(1)
     places = jnp.stack([here, lax.axis_index("blk").astype(jnp.int32)])
-    one, two, paired = chunks_of(z.steps)
+    one, two, parts = chunks_of(z.steps)
     sensors, head, tail = sensor_call(z, state, to_modal)
     lefts, rights = neighbours(head, tail)
 
-    def sweep(chunk, paired, ring, carry, after):
+    def sweep(chunk, parts, ring, carry, after):
         return sweep_call(
-            z, chunk, paired, me, state, rhs, viscous_op, gain, inverse, sensors, lefts, rights, ring, carry, after
+            z, chunk, parts, me, state, rhs, viscous_op, gain, inverse, sensors, lefts, rights, ring, carry, after
         )
 
-    messages_one, low, high = sweep(one, 0, None, None, [])
+    messages_one, low, high = sweep(one, [], None, None, [])
     ring = [shift_by(high, "blk", 1), shift_by(low, "blk", -1)]
     own, heads, tails, wholes, prefix, group = maps_call(z, me, gain, [messages_one])
-    messages_two, keep, give, ends, starts = sweep(two, paired, ring, messages_one, [group])
+    *pairs, ends, starts = sweep(two, parts, ring, messages_one, [group])
     before, pack = chain_call(z, starts, ends, tails, wholes, group)
     packs = [pack] + [shift_by(pack, "blk", s) for s in range(1, groups)]
-    middle = two[1] - paired
-    messages_two = first_call(z, places, packs, before, prefix, heads, starts, messages_two, middle - two[0])
-    got = lax.ppermute(give, "elem", [(i, i ^ 1) for i in range(segments)])
-    coupled = couple_call(z, keep, got)
-    coupled = [coupled[0]] + [shift_by(coupled[d], "elem", 2 * d) for d in range(1, segments // 2)]
+    keep_first, give_first = first_call(z, places, packs, before, prefix, heads, starts)
     received_one = spread(messages_one)
-    received_two = spread(gate_call(messages_two, [received_one, coupled[0]]))
-    out, operands = open_call(z, one, (two[0], middle), own, received_one, received_two)
-    out = finish_call(z, (middle, two[1]), me, own, coupled, operands, out)
+    received_first = spread_pairs(z, keep_first, give_first, [])
+    out, operands = open_call(z, one, me, own, received_one, received_first)
+    after = received_first[1:]
+    for n, part in enumerate(parts):
+        received = spread_pairs(z, pairs[2 * n], pairs[2 * n + 1], after)
+        out = finish_call(z, part, me, own, received, operands, out)
+        after = received[1:2]
     return out.reshape(z.steps, z.nodes, segments * z.rows, z.ax)
 
 

time: 225 us -> 218 us (0.969)
  waiting for transfers between devices: 127 us -> 108 us
  Pallas kernels: 65 us -> 72.7 us
  local copies, waits for them, and re-layouts: 3.58 us -> 6.01 us
    all_to_all x2 -> x1, waiting for transfers between devices: 110 us -> 0.01 us  [spread(): return lax.all_to_all(messages, 'elem', 0, 0, tiled=True)]
    ppermute x8 -> x14, waiting for transfers between devices: 13.4 us -> 101 us  [shift_by(): lax.ppermute(array, axis, [(i, (i + by) % size) for i in range(size)])]
    all_to_all x2 -> x1, starting transfers between devices: 12.2 us -> 4.08 us  [spread(): return lax.all_to_all(messages, 'elem', 0, 0, tiled=True)]
    ppermute x8 -> x14, starting transfers between devices: 8.7 us -> 15.8 us  [shift_by(): lax.ppermute(array, axis, [(i, (i + by) % size) for i in range(size)])]
    pallas_call x1 -> x3, Pallas kernels: 2.12 us -> 7.01 us  [couple_call(): call(kernel, 'couple', [f32(2, message, z.ax)] * pairs, [spec_hbm()] * 2,...]
    pallas_call x1 -> x2, Pallas kernels: 3.2 us -> 7.91 us  [finish_call(): call(kernel, f'finish_{low}', f32(z.steps, tall, z.ax), [spec_smem()] + [...]
    ppermute x1 -> x3, waiting for transfers between devices: 0.01 us -> 3.29 us  [spread_pairs(): got = lax.ppermute(give, 'elem', [(i, i ^ 1) for i in range(z.segments)])]
    ppermute x1 -> x3, starting transfers between devices: 0.93 us -> 3.91 us  [spread_pairs(): got = lax.ppermute(give, 'elem', [(i, i ^ 1) for i in range(z.segments)])]
  transfers between devices with their start and end apart: 13 -> 20, of which waited for: 8 -> 14; matrix products, arithmetic and copies ran while one was open for 0% -> 0% of each run, Pallas kernels for 20% -> 24%
where the time goes in v6:
time: 218 us; the launch traced here: 217 us
  waiting for transfers between devices  108 us (50%)
  Pallas kernels  72.7 us (33%)
  starting transfers between devices  29.4 us (13%)
  local copies, waits for them, and re-layouts  6.01 us (3%)
    ppermute x14, waiting for transfers between devices, shift_by(): lax.ppermute(array, axis, [(i, (i + by) % size) for i in range(size)])  101 us
    pallas_call x2, Pallas kernels, sweep_call(): call(kernel, f'sweep_{low}', outs + more, in_specs + extra_specs + [spec_...  27.2 us
    ppermute x14, starting transfers between devices, shift_by(): lax.ppermute(array, axis, [(i, (i + by) % size) for i in range(size)])  15.8 us
    pallas_call x1, Pallas kernels, maps_call(): call(kernel, 'maps', outs, [spec_smem(), spec_hbm()] + [spec_any()] * len...  8.26 us
    pallas_call x2, Pallas kernels, finish_call(): call(kernel, f'finish_{low}', f32(z.steps, tall, z.ax), [spec_smem()] + [...  7.91 us
    pallas_call x3, Pallas kernels, couple_call(): call(kernel, 'couple', [f32(2, message, z.ax)] * pairs, [spec_hbm()] * 2,...  7.01 us
    pallas_call x1, Pallas kernels, sensor_call(): call(kernel, 'sensor', outs, [spec_hbm()] * 2, [spec_vmem()] * 3, [pltpu....  6.28 us
    pallas_call x1, Pallas kernels, open_call(): call(kernel, 'finish_0', [f32(z.steps, tall, z.ax), jax.ShapeDtypeStruct(...  6.21 us
  transfers between devices with their start and end apart: 20, of which 14 were waited for; matrix products, arithmetic and copies ran while one was open for 0% of the time, Pallas kernels for 24%

profile of v6, /device:TPU:9, one launch (start us, length us, event | category | flops | bytes accessed | tf_op | source)
XLA Modules:
  0.0 217.1 jit_solution(8323900293097745216)
XLA Ops:
  0.0 6.3 %sensor.1 = (f32[8,8,256]{2,1,0:T(8,128)}, f32[8,8,128]{2,1,0:T(8,128)}, f32[8,8,128]{2,1,0:T(8,128)}) custom-call(f32[8,2000,128]{2,1,0:T(8,128)} %bitcast.7, f32[125,125]{1,0:T(8,128)} %modal_ref.1), custom_call_target="tpu_custom_call" | custom-call | flops 2147483648 | bytes 8192000 | tf_op jit(solution)/shard_map/sensor/pallas_call | solution.py:181
  6.3 3.8 %collective-permute-start = (f32[8,8,128]{2,1,0:T(8,128)}, f32[8,8,128]{2,1,0:T(8,128)S(1)}, u32[]{:S(2)}, u32[]{:S(2)}) collective-permute-start(f32[8,8,128]{2,1,0:T(8,128)} %get-tuple-element.50), channel_id=1, source_target_pairs={{0,1},{1,2},{2,3},{3,4},{4,5},{5,6},{6,7},{8,9},{9,10},{10,11},{11... | collective-permute-start | bytes 98312 | tf_op jit(solution)/shard_map/ppermute | solution.py:685
  10.1 1.9 collective-permute-start.1
  12.0 0.0 collective-permute-done.refs_7_
  12.0 0.0 copy-start.10
  12.0 3.5 %collective-permute-done.1.refs_8_ = f32[8,8,128]{2,1,0:T(8,128)S(1)} collective-permute-done((f32[8,8,128]{2,1,0:T(8,128)}, f32[8,8,128]{2,1,0:T(8,128)S(1)}, u32[]{:S(2)}, u32[]{:S(2)}) %collective-permute-start.1) | collective-permute-done | bytes 32800 | tf_op jit(solution)/shard_map/ppermute | solution.py:686
  15.5 0.6 copy-done.11
  16.1 10.6 %sweep_1.1 = (f32[8,752,128]{2,1,0:T(8,128)}, f32[1,256]{1,0:T(1,128)}, f32[1,256]{1,0:T(1,128)}) custom-call(s32[1]{0:T(128)} %bitcast.refs_0_.me_ref, f32[8,2000,128]{2,1,0:T(8,128)} %bitcast.8, f32[8,2000,128]{2,1,0:T(8,128)} %bitcast.13, f32[125,125]{1,0:T(8,128)} %refs_3_.3, f32[125,64,125]{2,1,0:T(8,128)} %bitcast.15, f32[125,64,125]{2,1,0:T(8,128)} %bitcast.10, ...), custom_call_target="tpu_custom_call" | custom-call | flops 2415919104 | bytes 12320768 | tf_op jit(solution)/shard_map/sweep_1/pallas_call | solution.py:370
  26.8 4.1 %all-to-all-start = ((f32[8,752,128]{2,1,0:T(8,128)}), f32[8,752,128]{2,1,0:T(8,128)S(1)}, u32[]{:S(2)}, u32[]{:S(2)}) async-start(f32[8,752,128]{2,1,0:T(8,128)} %get-tuple-element.52.refs_0_.refs_11_), calls=%async_computation | async-start | bytes 6160384 | tf_op jit(solution)/shard_map/all_to_all | solution.py:691
  30.9 0.0 copy-done.16
  30.9 1.2 collective-permute-start.2
  32.1 1.2 collective-permute-start.3
  33.3 8.3 %maps.1 = (f32[8,128,128]{2,1,0:T(8,128)}, f32[8,128,128]{2,1,0:T(8,128)}, f32[8,128,128]{2,1,0:T(8,128)}, f32[8,128,128]{2,1,0:T(8,128)}, f32[8,128,128]{2,1,0:T(8,128)}, /*index=5*/f32[128,128]{1,0:T(8,128)}) custom-call(s32[1]{0:T(128)} %bitcast.refs_0_.me_ref, f32[125,64,125]{2,1,0:T(8,128)} %bitcast.11, f32[8,752,128]{2,1,0:T(8,128)} %get-tuple-element.52.refs_0_.refs_11_), custom_call_target="tpu_custom_call" | custom-call | flops 1207959552 | bytes 4194304 | tf_op jit(solution)/shard_map/maps/pallas_call | solution.py:417
  41.5 0.0 collective-permute-done.2.refs_9_
  41.6 0.0 collective-permute-done.3.refs_10_
  41.6 0.0 copy-start.13
  41.6 0.5 copy-done.12
  42.1 0.0 copy-done.13
  42.1 16.6 %sweep_4.1 = (f32[4,752,128]{2,1,0:T(8,128)}, f32[4,752,128]{2,1,0:T(8,128)}, f32[4,256,128]{2,1,0:T(8,128)}, f32[4,256,128]{2,1,0:T(8,128)}, f32[8,128,256]{2,1,0:T(8,128)}, /*index=5*/f32[8,128,256]{2,1,0:T(8,128)}) custom-call(s32[1]{0:T(128)} %bitcast.refs_0_.me_ref, f32[8,2000,128]{2,1,0:T(8,128)} %bitcast.9, f32[8,2000,128]{2,1,0:T(8,128)} %bitcast.14, ...), custom_call_target="tpu_custom_call" | custom-call | flops 4026531840 | bytes 16384000 | tf_op jit(solution)/shard_map/sweep_4/pallas_call | solution.py:370
  58.7 1.0 collective-permute-start.12
  59.7 4.4 %chain.1 = (f32[8,128,256]{2,1,0:T(8,128)}, f32[128,384]{1,0:T(8,128)}) custom-call(f32[8,128,256]{2,1,0:T(8,128)} %get-tuple-element.57.start_ref.refs_8_, f32[8,128,256]{2,1,0:T(8,128)} %get-tuple-element.58.end_ref, f32[8,128,128]{2,1,0:T(8,128)} %get-tuple-element.59.tail_ref, f32[8,128,128]{2,1,0:T(8,128)} %get-tuple-element.60.whole_ref, ...), custom_call_target="tpu_custom_call" | custom-call | flops 536870912 | bytes 4194304 | tf_op jit(solution)/shard_map/chain/pallas_call | solution.py:447
  64.1 1.2 collective-permute-start.6
  65.3 0.2 collective-permute-start.5
  65.6 1.2 collective-permute-start.4
  66.8 0.6 pad_add_fusion.refs_0_
  67.4 3.4 %collective-permute-done.6.refs_4_ = f32[128,384]{1,0:T(8,128)S(1)} collective-permute-done((f32[128,384]{1,0:T(8,128)}, f32[128,384]{1,0:T(8,128)S(1)}, u32[]{:S(2)}, u32[]{:S(2)}) %collective-permute-start.6) | collective-permute-done | bytes 196640 | tf_op jit(solution)/shard_map/ppermute | solution.py:680
  70.8 0.9 collective-permute-done.5.refs_3_
  71.7 4.4 %collective-permute-done.4.refs_2_ = f32[128,384]{1,0:T(8,128)} collective-permute-done((f32[128,384]{1,0:T(8,128)}, f32[128,384]{1,0:T(8,128)}, u32[]{:S(2)}, u32[]{:S(2)}) %collective-permute-start.4) | collective-permute-done | bytes 196640 | tf_op jit(solution)/shard_map/ppermute | solution.py:680
  76.1 5.4 %first.1 = (f32[4,256,128]{2,1,0:T(8,128)}, f32[4,256,128]{2,1,0:T(8,128)}) custom-call(s32[2]{0:T(128)} %pad_add_fusion.refs_0_, f32[128,384]{1,0:T(8,128)} %get-tuple-element.61.refs_1_, f32[128,384]{1,0:T(8,128)} %collective-permute-done.4.refs_2_, f32[128,384]{1,0:T(8,128)} %copy-done.9, f32[128,384]{1,0:T(8,128)} %copy-done.8, ...), custom_call_target="tpu_custom_call" | custom-call | flops 805306368 | bytes 4194304 | tf_op jit(solution)/shard_map/first/pallas_call | solution.py:488
  81.5 1.7 collective-permute-start.7
  83.2 1.7 collective-permute-done.7.refs_1_
  84.9 0.8 copy-done.5
  85.8 2.1 couple.3
  87.8 1.2 collective-permute-start.8
  89.0 0.9 collective-permute-start.9
  89.9 1.4 collective-permute-start.10
  91.3 0.0 collective-permute-done.12.refs_1_
  91.3 2.9 %couple.5 = (f32[2,752,128]{2,1,0:T(8,128)}, f32[2,752,128]{2,1,0:T(8,128)}, f32[2,752,128]{2,1,0:T(8,128)}, f32[2,752,128]{2,1,0:T(8,128)}) custom-call(f32[4,752,128]{2,1,0:T(8,128)} %get-tuple-element.78.refs_0_, f32[4,752,128]{2,1,0:T(8,128)} %collective-permute-done.12.refs_1_), custom_call_target="tpu_custom_call" | custom-call | bytes 6160384 | tf_op jit(solution)/shard_map/couple/pallas_call | solution.py:523
  94.2 20.1 %collective-permute-done.8.refs_1_.refs_4_ = f32[2,256,128]{2,1,0:T(8,128)S(1)} collective-permute-done((f32[2,256,128]{2,1,0:T(8,128)}, f32[2,256,128]{2,1,0:T(8,128)S(1)}, u32[]{:S(2)}, u32[]{:S(2)}) %collective-permute-start.8) | collective-permute-done | bytes 262176 | tf_op jit(solution)/shard_map/ppermute | solution.py:680
  114.3 5.6 %collective-permute-done.9.refs_2_.refs_5_ = f32[2,256,128]{2,1,0:T(8,128)S(1)} collective-permute-done((f32[2,256,128]{2,1,0:T(8,128)}, f32[2,256,128]{2,1,0:T(8,128)S(1)}, u32[]{:S(2)}, u32[]{:S(2)}) %collective-permute-start.9) | collective-permute-done | bytes 262176 | tf_op jit(solution)/shard_map/ppermute | solution.py:680
  120.0 1.6 collective-permute-done.10.refs_3_.refs_6_
  121.5 0.7 copy-done.4
  122.2 0.0 collective-permute-start.13
  122.2 1.5 collective-permute-start.17
  123.7 1.5 collective-permute-start.18
  125.2 1.3 collective-permute-start.11
  126.5 1.5 collective-permute-done.11.refs_1_
  128.0 0.8 copy-done.6
  128.8 2.1 couple.4
  130.9 9.4 %collective-permute-done.13.refs_4_.refs_1_ = f32[2,752,128]{2,1,0:T(8,128)S(1)} collective-permute-done((f32[2,752,128]{2,1,0:T(8,128)}, f32[2,752,128]{2,1,0:T(8,128)S(1)}, u32[]{:S(2)}, u32[]{:S(2)}) %collective-permute-start.13) | collective-permute-done | bytes 770080 | tf_op jit(solution)/shard_map/ppermute | solution.py:680
  140.3 0.9 copy-done.1
  141.2 0.4 collective-permute-start.14
  141.6 3.7 %collective-permute-start.15 = (f32[2,256,128]{2,1,0:T(8,128)}, f32[2,256,128]{2,1,0:T(8,128)}, u32[]{:S(2)}, u32[]{:S(2)}) collective-permute-start(f32[2,256,128]{2,1,0:T(8,128)} %get-tuple-element.87), channel_id=1, source_target_pairs={{0,4},{1,5},{2,6},{3,7},{4,0},{5,1},{6,2},{7,3},{8,12},{9,13},{10,... | collective-permute-start | bytes 786440 | tf_op jit(solution)/shard_map/ppermute | solution.py:680
  145.4 0.0 collective-permute-start.16
  145.4 0.0 all-to-all-done.one_ref
  145.4 1.6 copy-done
  147.0 6.2 %finish_0.1 = (f32[8,2000,128]{2,1,0:T(8,128)}, bf16[8,256,256]{2,1,0:T(8,128)(2,1)}) custom-call(s32[1]{0:T(128)} %bitcast.refs_0_.me_ref, f32[8,128,128]{2,1,0:T(8,128)} %get-tuple-element.53.own_ref, f32[8,752,128]{2,1,0:T(8,128)} %copy-done, f32[2,256,128]{2,1,0:T(8,128)} %get-tuple-element.67.refs_0_, f32[2,256,128]{2,1,0:T(8,128)} %copy-done.2, ...), custom_call_target="tpu_custom_call" | custom-call | flops 805306368 | bytes 8192000 | tf_op jit(solution)/shard_map/finish_0/pallas_call | solution.py:600
  153.2 46.0 %collective-permute-done.17.refs_2_ = f32[2,752,128]{2,1,0:T(8,128)} collective-permute-done((f32[2,752,128]{2,1,0:T(8,128)}, f32[2,752,128]{2,1,0:T(8,128)}, u32[]{:S(2)}, u32[]{:S(2)}) %collective-permute-start.17) | collective-permute-done | bytes 770080 | tf_op jit(solution)/shard_map/ppermute | solution.py:680
  199.2 3.3 %collective-permute-done.18.refs_3_ = f32[2,752,128]{2,1,0:T(8,128)} collective-permute-done((f32[2,752,128]{2,1,0:T(8,128)}, f32[2,752,128]{2,1,0:T(8,128)}, u32[]{:S(2)}, u32[]{:S(2)}) %collective-permute-start.18) | collective-permute-done | bytes 770080 | tf_op jit(solution)/shard_map/ppermute | solution.py:680
  202.5 4.7 %finish_4.1.refs_4_ = f32[8,2000,128]{2,1,0:T(8,128)} custom-call(s32[1]{0:T(128)} %bitcast.refs_0_.me_ref, f32[8,128,128]{2,1,0:T(8,128)} %get-tuple-element.53.own_ref, bf16[8,256,256]{2,1,0:T(8,128)(2,1)} %get-tuple-element.71.operand_ref, f32[2,752,128]{2,1,0:T(8,128)} %get-tuple-element.89.refs_0_, ...), custom_call_target="tpu_custom_call", output_to_operand_aliasing={{}: (7, {})} | custom-call | flops 805306368 | bytes 6144000 | tf_op jit(solution)/shard_map/finish_4/pallas_call | solution.py:657
  207.2 0.0 collective-permute-done.14.refs_1_
  207.3 3.2 %collective-permute-done.15.refs_2_ = f32[2,256,128]{2,1,0:T(8,128)} collective-permute-done((f32[2,256,128]{2,1,0:T(8,128)}, f32[2,256,128]{2,1,0:T(8,128)}, u32[]{:S(2)}, u32[]{:S(2)}) %collective-permute-start.15) | collective-permute-done | bytes 262176 | tf_op jit(solution)/shard_map/ppermute | solution.py:680
  210.5 3.3 %collective-permute-done.16.refs_3_ = f32[2,256,128]{2,1,0:T(8,128)} collective-permute-done((f32[2,256,128]{2,1,0:T(8,128)}, f32[2,256,128]{2,1,0:T(8,128)}, u32[]{:S(2)}, u32[]{:S(2)}) %collective-permute-start.16) | collective-permute-done | bytes 262176 | tf_op jit(solution)/shard_map/ppermute | solution.py:680
  213.8 3.2 %finish_7.1 = f32[8,2000,128]{2,1,0:T(8,128)} custom-call(s32[1]{0:T(128)} %bitcast.refs_0_.me_ref, f32[8,128,128]{2,1,0:T(8,128)} %get-tuple-element.53.own_ref, bf16[8,256,256]{2,1,0:T(8,128)(2,1)} %get-tuple-element.71.operand_ref, f32[2,256,128]{2,1,0:T(8,128)} %get-tuple-element.85.refs_0_, ...), custom_call_target="tpu_custom_call", output_to_operand_aliasing={{}: (7, {})} | custom-call | flops 268435456 | bytes 2048000 | tf_op jit(solution)/shard_map/finish_7/pallas_call | solution.py:657
  (25 shorter events, 0.0 us)
Async XLA Ops:
  6.3 5.7 %collective-permute-start = (f32[8,8,128]{2,1,0:T(8,128)}, f32[8,8,128]{2,1,0:T(8,128)S(1)}, u32[]{:S(2)}, u32[]{:S(2)}) collective-permute-start(f32[8,8,128]{2,1,0:T(8,128)} %get-tuple-element.50), channel_id=1, source_target_pairs={{0,1},{1,2},{2,3},{3,4},{4,5},{5,6},{6,7},{8,9},{9,10},{10,11},{11... | collective-permute-start | bytes 98312 | tf_op jit(solution)/shard_map/ppermute | solution.py:685
  10.1 5.4 %collective-permute-start.1 = (f32[8,8,128]{2,1,0:T(8,128)}, f32[8,8,128]{2,1,0:T(8,128)S(1)}, u32[]{:S(2)}, u32[]{:S(2)}) collective-permute-start(f32[8,8,128]{2,1,0:T(8,128)} %get-tuple-element.51), channel_id=1, source_target_pairs={{1,0},{2,1},{3,2},{4,3},{5,4},{6,5},{7,6},{9,8},{10,9},{11,10},{12... | collective-permute-start | bytes 98312 | tf_op jit(solution)/shard_map/ppermute | solution.py:686
  12.0 3.5 %copy-start.10 = (f32[8,8,128]{2,1,0:T(8,128)}, f32[8,8,128]{2,1,0:T(8,128)S(1)}, u32[]{:S(2)}) copy-start(f32[8,8,128]{2,1,0:T(8,128)S(1)} %collective-permute-done.refs_7_) | copy-start | bytes 98308
  15.5 0.6 copy-start.11
  26.8 4.1 %copy-start.16 = (f32[1,256]{1,0:T(1,128)S(1)}, f32[1,256]{1,0:T(1,128)}, u32[]{:S(2)}) copy-start(f32[1,256]{1,0:T(1,128)} %get-tuple-element.54) | copy-start | bytes 3076
  26.8 5.3 %copy-start.15 = (f32[1,256]{1,0:T(1,128)S(1)}, f32[1,256]{1,0:T(1,128)}, u32[]{:S(2)}) copy-start(f32[1,256]{1,0:T(1,128)} %get-tuple-element.55) | copy-start | bytes 3076
  26.8 118.6 %all-to-all-start = ((f32[8,752,128]{2,1,0:T(8,128)}), f32[8,752,128]{2,1,0:T(8,128)S(1)}, u32[]{:S(2)}, u32[]{:S(2)}) async-start(f32[8,752,128]{2,1,0:T(8,128)} %get-tuple-element.52.refs_0_.refs_11_), calls=%async_computation | async-start | bytes 6160384 | tf_op jit(solution)/shard_map/all_to_all | solution.py:691
  30.9 10.7 %collective-permute-start.2 = (f32[1,256]{1,0:T(1,128)S(1)}, f32[1,256]{1,0:T(1,128)S(1)}, u32[]{:S(2)}, u32[]{:S(2)}) collective-permute-start(f32[1,256]{1,0:T(1,128)S(1)} %copy-done.16), channel_id=1, source_target_pairs={{0,8},{8,16},{16,24},{24,0},{1,9},{9,17},{17,25},{25,1},{2,10},{10... | collective-permute-start | bytes 3080 | tf_op jit(solution)/shard_map/ppermute | solution.py:680
  32.1 9.5 %collective-permute-start.3 = (f32[1,256]{1,0:T(1,128)S(1)}, f32[1,256]{1,0:T(1,128)S(1)}, u32[]{:S(2)}, u32[]{:S(2)}) collective-permute-start(f32[1,256]{1,0:T(1,128)S(1)} %copy-done.15), channel_id=1, source_target_pairs={{0,24},{8,0},{16,8},{24,16},{1,25},{9,1},{17,9},{25,17},{2,26},{10... | collective-permute-start | bytes 3080 | tf_op jit(solution)/shard_map/ppermute | solution.py:680
  41.5 0.5 copy-start.12
  41.6 0.5 copy-start.13
  58.7 32.6 %collective-permute-start.12 = (f32[4,752,128]{2,1,0:T(8,128)}, f32[4,752,128]{2,1,0:T(8,128)}, u32[]{:S(2)}, u32[]{:S(2)}) collective-permute-start(f32[4,752,128]{2,1,0:T(8,128)} %get-tuple-element.79), channel_id=1, source_target_pairs={{0,1},{1,0},{2,3},{3,2},{4,5},{5,4},{6,7},{7,6},{8,9},{9,8},{10,11... | collective-permute-start | bytes 4620296 | tf_op jit(solution)/shard_map/ppermute | solution.py:695
  64.1 6.7 %collective-permute-start.6 = (f32[128,384]{1,0:T(8,128)}, f32[128,384]{1,0:T(8,128)S(1)}, u32[]{:S(2)}, u32[]{:S(2)}) collective-permute-start(f32[128,384]{1,0:T(8,128)} %get-tuple-element.61.refs_1_), channel_id=1, source_target_pairs={{0,24},{8,0},{16,8},{24,16},{1,25},{9,1},{17,9},{25,17},{2,26},{10... | collective-permute-start | bytes 589832 | tf_op jit(solution)/shard_map/ppermute | solution.py:680
  65.3 6.4 %collective-permute-start.5 = (f32[128,384]{1,0:T(8,128)}, f32[128,384]{1,0:T(8,128)S(1)}, u32[]{:S(2)}, u32[]{:S(2)}) collective-permute-start(f32[128,384]{1,0:T(8,128)} %get-tuple-element.61.refs_1_), channel_id=1, source_target_pairs={{0,16},{8,24},{16,0},{24,8},{1,17},{9,25},{17,1},{25,9},{2,18},{10... | collective-permute-start | bytes 589832 | tf_op jit(solution)/shard_map/ppermute | solution.py:680
  65.6 10.6 %collective-permute-start.4 = (f32[128,384]{1,0:T(8,128)}, f32[128,384]{1,0:T(8,128)}, u32[]{:S(2)}, u32[]{:S(2)}) collective-permute-start(f32[128,384]{1,0:T(8,128)} %get-tuple-element.61.refs_1_), channel_id=1, source_target_pairs={{0,8},{8,16},{16,24},{24,0},{1,9},{9,17},{17,25},{25,1},{2,10},{10... | collective-permute-start | bytes 589832 | tf_op jit(solution)/shard_map/ppermute | solution.py:680
  70.8 5.3 %copy-start.8 = (f32[128,384]{1,0:T(8,128)}, f32[128,384]{1,0:T(8,128)S(1)}, u32[]{:S(2)}) copy-start(f32[128,384]{1,0:T(8,128)S(1)} %collective-permute-done.6.refs_4_) | copy-start | bytes 589828
  71.7 4.4 %copy-start.9 = (f32[128,384]{1,0:T(8,128)}, f32[128,384]{1,0:T(8,128)S(1)}, u32[]{:S(2)}) copy-start(f32[128,384]{1,0:T(8,128)S(1)} %collective-permute-done.5.refs_3_) | copy-start | bytes 589828
  81.5 43.7 %copy-start.14 = (f32[4,256,128]{2,1,0:T(8,128)S(1)}, f32[4,256,128]{2,1,0:T(8,128)}, u32[]{:S(2)}) copy-start(f32[4,256,128]{2,1,0:T(8,128)} %get-tuple-element.73) | copy-start | bytes 1572868
  81.5 3.4 %collective-permute-start.7 = (f32[4,256,128]{2,1,0:T(8,128)}, f32[4,256,128]{2,1,0:T(8,128)S(1)}, u32[]{:S(2)}, u32[]{:S(2)}) collective-permute-start(f32[4,256,128]{2,1,0:T(8,128)} %get-tuple-element.66), channel_id=1, source_target_pairs={{0,1},{1,0},{2,3},{3,2},{4,5},{5,4},{6,7},{7,6},{8,9},{9,8},{10,11... | collective-permute-start | bytes 1572872 | tf_op jit(solution)/shard_map/ppermute | solution.py:695
  84.9 0.8 copy-start.5
  87.8 26.5 %collective-permute-start.8 = (f32[2,256,128]{2,1,0:T(8,128)}, f32[2,256,128]{2,1,0:T(8,128)S(1)}, u32[]{:S(2)}, u32[]{:S(2)}) collective-permute-start(f32[2,256,128]{2,1,0:T(8,128)} %get-tuple-element.68), channel_id=1, source_target_pairs={{0,2},{1,3},{2,4},{3,5},{4,6},{5,7},{6,0},{7,1},{8,10},{9,11},{10,... | collective-permute-start | bytes 786440 | tf_op jit(solution)/shard_map/ppermute | solution.py:680
  89.0 30.9 %collective-permute-start.9 = (f32[2,256,128]{2,1,0:T(8,128)}, f32[2,256,128]{2,1,0:T(8,128)S(1)}, u32[]{:S(2)}, u32[]{:S(2)}) collective-permute-start(f32[2,256,128]{2,1,0:T(8,128)} %get-tuple-element.69), channel_id=1, source_target_pairs={{0,4},{1,5},{2,6},{3,7},{4,0},{5,1},{6,2},{7,3},{8,12},{9,13},{10,... | collective-permute-start | bytes 786440 | tf_op jit(solution)/shard_map/ppermute | solution.py:680
  89.9 31.6 %collective-permute-start.10 = (f32[2,256,128]{2,1,0:T(8,128)}, f32[2,256,128]{2,1,0:T(8,128)S(1)}, u32[]{:S(2)}, u32[]{:S(2)}) collective-permute-start(f32[2,256,128]{2,1,0:T(8,128)} %get-tuple-element.70), channel_id=1, source_target_pairs={{0,6},{1,7},{2,0},{3,1},{4,2},{5,3},{6,4},{7,5},{8,14},{9,15},{10,... | collective-permute-start | bytes 786440 | tf_op jit(solution)/shard_map/ppermute | solution.py:680
  114.3 7.2 %copy-start.2 = (f32[2,256,128]{2,1,0:T(8,128)}, f32[2,256,128]{2,1,0:T(8,128)S(1)}, u32[]{:S(2)}) copy-start(f32[2,256,128]{2,1,0:T(8,128)S(1)} %collective-permute-done.8.refs_1_.refs_4_) | copy-start | bytes 786436
  120.0 1.6 copy-start.3
  121.5 0.7 copy-start.4
  122.2 18.0 %collective-permute-start.13 = (f32[2,752,128]{2,1,0:T(8,128)}, f32[2,752,128]{2,1,0:T(8,128)S(1)}, u32[]{:S(2)}, u32[]{:S(2)}) collective-permute-start(f32[2,752,128]{2,1,0:T(8,128)} %get-tuple-element.84), channel_id=1, source_target_pairs={{0,2},{1,3},{2,4},{3,5},{4,6},{5,7},{6,0},{7,1},{8,10},{9,11},{10,... | collective-permute-start | bytes 2310152 | tf_op jit(solution)/shard_map/ppermute | solution.py:680
  122.2 77.0 %collective-permute-start.17 = (f32[2,752,128]{2,1,0:T(8,128)}, f32[2,752,128]{2,1,0:T(8,128)}, u32[]{:S(2)}, u32[]{:S(2)}) collective-permute-start(f32[2,752,128]{2,1,0:T(8,128)} %get-tuple-element.90), channel_id=1, source_target_pairs={{0,4},{1,5},{2,6},{3,7},{4,0},{5,1},{6,2},{7,3},{8,12},{9,13},{10,... | collective-permute-start | bytes 2310152 | tf_op jit(solution)/shard_map/ppermute | solution.py:680
  123.7 78.8 %collective-permute-start.18 = (f32[2,752,128]{2,1,0:T(8,128)}, f32[2,752,128]{2,1,0:T(8,128)}, u32[]{:S(2)}, u32[]{:S(2)}) collective-permute-start(f32[2,752,128]{2,1,0:T(8,128)} %get-tuple-element.91), channel_id=1, source_target_pairs={{0,6},{1,7},{2,0},{3,1},{4,2},{5,3},{6,4},{7,5},{8,14},{9,15},{10,... | collective-permute-start | bytes 2310152 | tf_op jit(solution)/shard_map/ppermute | solution.py:680
  125.2 2.8 %collective-permute-start.11 = (f32[4,256,128]{2,1,0:T(8,128)S(1)}, f32[4,256,128]{2,1,0:T(8,128)S(1)}, u32[]{:S(2)}, u32[]{:S(2)}) collective-permute-start(f32[4,256,128]{2,1,0:T(8,128)S(1)} %copy-done.14), channel_id=1, source_target_pairs={{0,1},{1,0},{2,3},{3,2},{4,5},{5,4},{6,7},{7,6},{8,9},{9,8},{10,11... | collective-permute-start | bytes 1572872 | tf_op jit(solution)/shard_map/ppermute | solution.py:695
  128.0 0.8 copy-start.6
  140.3 0.9 copy-start.1
  141.2 66.1 %collective-permute-start.14 = (f32[2,256,128]{2,1,0:T(8,128)}, f32[2,256,128]{2,1,0:T(8,128)S(1)}, u32[]{:S(2)}, u32[]{:S(2)}) collective-permute-start(f32[2,256,128]{2,1,0:T(8,128)} %get-tuple-element.86), channel_id=1, source_target_pairs={{0,2},{1,3},{2,4},{3,5},{4,6},{5,7},{6,0},{7,1},{8,10},{9,11},{10,... | collective-permute-start | bytes 786440 | tf_op jit(solution)/shard_map/ppermute | solution.py:680
  141.6 68.8 %collective-permute-start.15 = (f32[2,256,128]{2,1,0:T(8,128)}, f32[2,256,128]{2,1,0:T(8,128)}, u32[]{:S(2)}, u32[]{:S(2)}) collective-permute-start(f32[2,256,128]{2,1,0:T(8,128)} %get-tuple-element.87), channel_id=1, source_target_pairs={{0,4},{1,5},{2,6},{3,7},{4,0},{5,1},{6,2},{7,3},{8,12},{9,13},{10,... | collective-permute-start | bytes 786440 | tf_op jit(solution)/shard_map/ppermute | solution.py:680
  145.4 68.4 %collective-permute-start.16 = (f32[2,256,128]{2,1,0:T(8,128)}, f32[2,256,128]{2,1,0:T(8,128)}, u32[]{:S(2)}, u32[]{:S(2)}) collective-permute-start(f32[2,256,128]{2,1,0:T(8,128)} %get-tuple-element.88), channel_id=1, source_target_pairs={{0,6},{1,7},{2,0},{3,1},{4,2},{5,3},{6,4},{7,5},{8,14},{9,15},{10,... | collective-permute-start | bytes 786440 | tf_op jit(solution)/shard_map/ppermute | solution.py:680
  145.4 1.6 copy-start
  207.3 6.5 %copy-start.7 = (f32[2,256,128]{2,1,0:T(8,128)}, f32[2,256,128]{2,1,0:T(8,128)S(1)}, u32[]{:S(2)}) copy-start(f32[2,256,128]{2,1,0:T(8,128)S(1)} %collective-permute-done.14.refs_1_) | copy-start | bytes 786436

commit v7 on v6

--- a/solution.py
+++ b/solution.py
@@ -219,6 +219,10 @@
     last, last_size = z.window(low - 2, low - 1)
     batch = next(n for n in (4, 8, z.segments) if z.segments % n == 0 and n * z.steps % TILE == 0)
     narrow = low == 1
+    cuts = list(range(0, z.segments + 1, batch))
+    if narrow:
+        cuts[1:1] = [2]
+    batches = list(zip(cuts[:-1], cuts[1:]))
 
     if parts:
         outs = [f32(pairs, message, z.ax) for message in messages for _ in range(2)]
@@ -247,8 +251,8 @@
         viscous_copy = pltpu.make_async_copy(viscous_ref, viscous_buf, out_sem.at[0, 0])
         viscous_copy.start()
         copies = [[] for _ in range(z.segments)]
-        for s0 in range(0, z.segments, batch):
-            for s in range(s0, s0 + batch):
+        for s0, s1 in batches:
+            for s in range(s0, s1):
                 moves = [
                     (state_ref.at[s, pl.ds(first, size)], state_buf.at[s, pl.ds(0, size)]),
                     (rhs_ref.at[s, pl.ds(first, size)], rhs_buf.at[s, pl.ds(0, size)]),
@@ -266,11 +270,11 @@
                 for n, (source, target) in enumerate(moves):
                     copies[s].append(pltpu.make_async_copy(source, target, sem.at[s, n]))
             if not narrow:
-                part = pl.ds(s0 * z.steps, batch * z.steps)
+                part = pl.ds(s0 * z.steps, (s1 - s0) * z.steps)
                 for n, (source, target) in enumerate(((inverse_ref, inverse_buf), (gain_ref, gain_buf))):
                     copy = pltpu.make_async_copy(source.at[:, part], target.at[:, part], matrix_sem.at[s0, n])
                     copies[s0].append(copy)
-            for s in range(s0, s0 + batch):
+            for s in range(s0, s1):
                 for copy in copies[s]:
                     copy.start()
         for n, i in enumerate(steps):
@@ -288,8 +292,8 @@
         operator = operand_left(z.square(viscous_buf[...]))
         sends = []
 
-        for s0 in range(0, z.segments, batch):
-            group = range(s0, s0 + batch)
+        for s0, s1 in batches:
+            group = range(s0, s1)
             for s in group:
                 for copy in copies[s]:
                     copy.wait()
@@ -376,7 +380,7 @@
         scratch,
         z.flops * len(steps) * z.segments * 3,
         4 * z.segments * size * z.ax * 4,
-        limit=54,
+        limit=52,
     )(*operands, *extra, *after)
 
 
@@ -539,14 +543,14 @@
     return call(
         kernel,
         "gate",
-        [f32(*array.shape) for array in held],
-        [spec_hbm()] * len(held) + [spec_any()] * len(after),
-        [spec_hbm()] * len(held),
+        f32(*held.shape),
+        [spec_hbm(), spec_any()],
+        spec_hbm(),
         [],
         0,
         0,
-        {n: n for n in range(len(held))},
-    )(*held, *after)
+        {0: 0},
+    )(held, after)
 
 
 def open_call(z, one, me, own, received_one, received_first):
@@ -672,6 +676,7 @@
         z.flops * count * z.segments,
         4 * 2 * count * tall * z.ax,
         {len(inputs) - 1: 0},
+        limit=57 if count > 1 else 40,
     )(*inputs)
 
 
@@ -694,9 +699,11 @@
 def spread_pairs(z, keep, give, after):
     got = lax.ppermute(give, "elem", [(i, i ^ 1) for i in range(z.segments)])
     coupled = couple_call(z, keep, got)
-    if after:
-        coupled = gate_call(coupled, after)
-    return [coupled[0]] + [shift_by(coupled[d], "elem", 2 * d) for d in range(1, z.segments // 2)]
+    moved = [coupled[0]]
+    for d in range(1, z.segments // 2):
+        held = coupled[d] if after is None else gate_call(coupled[d], after[d])
+        moved.append(shift_by(held, "elem", 2 * d))
+    return moved
 
 
 def chunks_of(steps):
@@ -734,13 +741,13 @@
     packs = [pack] + [shift_by(pack, "blk", s) for s in range(1, groups)]
     keep_first, give_first = first_call(z, places, packs, before, prefix, heads, starts)
     received_one = spread(messages_one)
-    received_first = spread_pairs(z, keep_first, give_first, [])
+    received_first = spread_pairs(z, keep_first, give_first, None)
     out, operands = open_call(z, one, me, own, received_one, received_first)
-    after = received_first[1:]
+    after = received_first
     for n, part in enumerate(parts):
         received = spread_pairs(z, pairs[2 * n], pairs[2 * n + 1], after)
         out = finish_call(z, part, me, own, received, operands, out)
-        after = received[1:2]
+        after = [received[1]] * len(received)
     return out.reshape(z.steps, z.nodes, segments * z.rows, z.ax)
 
 

time: 218 us -> 212 us (0.972)
  waiting for transfers between devices: 108 us -> 104 us
  local copies, waits for them, and re-layouts: 6.01 us -> 9.86 us
  Pallas kernels: 72.7 us -> 68.9 us
    ppermute x14, waiting for transfers between devices: 101 us -> 97.2 us  [shift_by(): lax.ppermute(array, axis, [(i, (i + by) % size) for i in range(size)])]
    pallas_call x2, Pallas kernels: 27.2 us -> 23.3 us  [sweep_call(): call(kernel, f'sweep_{low}', outs + more, in_specs + extra_specs + [spec_...]
    unnamed x34 -> x40, local copies, waits for them, and re-layouts: 6.01 us -> 9.86 us
  transfers between devices with their start and end apart: 20 -> 20, of which waited for: 14 -> 13; matrix products, arithmetic and copies ran while one was open for 0% -> 0% of each run, Pallas kernels for 24% -> 25%
where the time goes in v7:
time: 212 us; the launch traced here: 211 us
  waiting for transfers between devices  104 us (49%)
  Pallas kernels  68.9 us (33%)
  starting transfers between devices  27.6 us (13%)
  local copies, waits for them, and re-layouts  9.86 us (5%)
    ppermute x14, waiting for transfers between devices, shift_by(): lax.ppermute(array, axis, [(i, (i + by) % size) for i in range(size)])  97.2 us
    pallas_call x2, Pallas kernels, sweep_call(): call(kernel, f'sweep_{low}', outs + more, in_specs + extra_specs + [spec_...  23.3 us
    ppermute x14, starting transfers between devices, shift_by(): lax.ppermute(array, axis, [(i, (i + by) % size) for i in range(size)])  14.7 us
    unnamed x40, local copies, waits for them, and re-layouts  9.86 us
    pallas_call x1, Pallas kernels, maps_call(): call(kernel, 'maps', outs, [spec_smem(), spec_hbm()] + [spec_any()] * len...  8.22 us
    pallas_call x2, Pallas kernels, finish_call(): call(kernel, f'finish_{low}', f32(z.steps, tall, z.ax), [spec_smem()] + [...  7.98 us
    pallas_call x3, Pallas kernels, couple_call(): call(kernel, 'couple', [f32(2, message, z.ax)] * pairs, [spec_hbm()] * 2,...  7 us
    pallas_call x1, Pallas kernels, sensor_call(): call(kernel, 'sensor', outs, [spec_hbm()] * 2, [spec_vmem()] * 3, [pltpu....  6.33 us
  transfers between devices with their start and end apart: 20, of which 13 were waited for; matrix products, arithmetic and copies ran while one was open for 0% of the time, Pallas kernels for 25%

profile of v7, /device:TPU:9, one launch (start us, length us, event | category | flops | bytes accessed | tf_op | source)
XLA Modules:
  0.0 211.3 jit_solution(1816405750520263612)
XLA Ops:
  0.0 6.3 %sensor.1 = (f32[8,8,256]{2,1,0:T(8,128)}, f32[8,8,128]{2,1,0:T(8,128)}, f32[8,8,128]{2,1,0:T(8,128)}) custom-call(f32[8,2000,128]{2,1,0:T(8,128)} %bitcast.7, f32[125,125]{1,0:T(8,128)} %modal_ref.1), custom_call_target="tpu_custom_call" | custom-call | flops 2147483648 | bytes 8192000 | tf_op jit(solution)/shard_map/sensor/pallas_call | solution.py:181
  6.3 3.8 %collective-permute-start = (f32[8,8,128]{2,1,0:T(8,128)}, f32[8,8,128]{2,1,0:T(8,128)S(1)}, u32[]{:S(2)}, u32[]{:S(2)}) collective-permute-start(f32[8,8,128]{2,1,0:T(8,128)} %get-tuple-element.42), channel_id=1, source_target_pairs={{0,1},{1,2},{2,3},{3,4},{4,5},{5,6},{6,7},{8,9},{9,10},{10,11},{11... | collective-permute-start | bytes 98312 | tf_op jit(solution)/shard_map/ppermute | solution.py:690
  10.1 1.9 collective-permute-start.1
  12.0 0.0 collective-permute-done.refs_7_
  12.1 3.5 %collective-permute-done.1.refs_8_ = f32[8,8,128]{2,1,0:T(8,128)S(1)} collective-permute-done((f32[8,8,128]{2,1,0:T(8,128)}, f32[8,8,128]{2,1,0:T(8,128)S(1)}, u32[]{:S(2)}, u32[]{:S(2)}) %collective-permute-start.1) | collective-permute-done | bytes 32800 | tf_op jit(solution)/shard_map/ppermute | solution.py:691
  15.6 0.8 copy-done.5
  16.4 7.6 %sweep_1.1 = (f32[8,752,128]{2,1,0:T(8,128)}, f32[1,256]{1,0:T(1,128)S(1)}, f32[1,256]{1,0:T(1,128)S(1)}) custom-call(s32[1]{0:T(128)} %bitcast.refs_0_.me_ref, f32[8,2000,128]{2,1,0:T(8,128)} %bitcast.8, f32[8,2000,128]{2,1,0:T(8,128)} %bitcast.13, f32[125,125]{1,0:T(8,128)S(1)} %copy-done.4, f32[125,64,125]{2,1,0:T(8,128)} %bitcast.15, ...), custom_call_target="tpu_custom_call" | custom-call | flops 2415919104 | bytes 12320768 | tf_op jit(solution)/shard_map/sweep_1/pallas_call | solution.py:374
  24.0 4.4 %all-to-all-start = ((f32[8,752,128]{2,1,0:T(8,128)}), f32[8,752,128]{2,1,0:T(8,128)}, u32[]{:S(2)}, u32[]{:S(2)}) async-start(f32[8,752,128]{2,1,0:T(8,128)} %get-tuple-element.44.refs_0_.refs_11_), calls=%async_computation | async-start | bytes 6160384 | tf_op jit(solution)/shard_map/all_to_all | solution.py:696
  28.4 1.3 collective-permute-start.2
  29.7 1.2 collective-permute-start.3
  30.9 8.2 %maps.1 = (f32[8,128,128]{2,1,0:T(8,128)}, f32[8,128,128]{2,1,0:T(8,128)}, f32[8,128,128]{2,1,0:T(8,128)}, f32[8,128,128]{2,1,0:T(8,128)}, f32[8,128,128]{2,1,0:T(8,128)}, /*index=5*/f32[128,128]{1,0:T(8,128)}) custom-call(s32[1]{0:T(128)} %bitcast.refs_0_.me_ref, f32[125,64,125]{2,1,0:T(8,128)} %bitcast.11, f32[8,752,128]{2,1,0:T(8,128)} %get-tuple-element.44.refs_0_.refs_11_), custom_call_target="tpu_custom_call" | custom-call | flops 1207959552 | bytes 4194304 | tf_op jit(solution)/shard_map/maps/pallas_call | solution.py:421
  39.1 0.0 collective-permute-done.3.refs_10_
  39.2 0.8 copy-done.7
  40.0 15.8 %sweep_4.1 = (f32[4,752,128]{2,1,0:T(8,128)}, f32[4,752,128]{2,1,0:T(8,128)}, f32[4,256,128]{2,1,0:T(8,128)S(1)}, f32[4,256,128]{2,1,0:T(8,128)S(1)}, f32[8,128,256]{2,1,0:T(8,128)}, /*index=5*/f32[8,128,256]{2,1,0:T(8,128)}) custom-call(s32[1]{0:T(128)} %bitcast.refs_0_.me_ref, f32[8,2000,128]{2,1,0:T(8,128)} %bitcast.9, f32[8,2000,128]{2,1,0:T(8,128)} %bitcast.14, ...), custom_call_target="tpu_custom_call" | custom-call | flops 4026531840 | bytes 16384000 | tf_op jit(solution)/shard_map/sweep_4/pallas_call | solution.py:374
  55.8 0.8 copy-done.2
  56.6 0.4 collective-permute-start.12
  57.0 4.5 %chain.1 = (f32[8,128,256]{2,1,0:T(8,128)}, f32[128,384]{1,0:T(8,128)}) custom-call(f32[8,128,256]{2,1,0:T(8,128)} %get-tuple-element.49.start_ref.refs_8_, f32[8,128,256]{2,1,0:T(8,128)} %get-tuple-element.50.end_ref, f32[8,128,128]{2,1,0:T(8,128)} %get-tuple-element.51.tail_ref, f32[8,128,128]{2,1,0:T(8,128)} %get-tuple-element.52.whole_ref, ...), custom_call_target="tpu_custom_call" | custom-call | flops 536870912 | bytes 4194304 | tf_op jit(solution)/shard_map/chain/pallas_call | solution.py:451
  61.5 1.3 collective-permute-start.6
  62.8 0.2 collective-permute-start.5
  63.0 1.2 collective-permute-start.4
  64.2 0.6 pad_add_fusion.refs_0_
  64.8 3.5 %collective-permute-done.6.refs_4_ = f32[128,384]{1,0:T(8,128)S(1)} collective-permute-done((f32[128,384]{1,0:T(8,128)}, f32[128,384]{1,0:T(8,128)S(1)}, u32[]{:S(2)}, u32[]{:S(2)}) %collective-permute-start.6) | collective-permute-done | bytes 196640 | tf_op jit(solution)/shard_map/ppermute | solution.py:685
  68.3 1.0 collective-permute-done.5.refs_3_
  69.3 4.3 %collective-permute-done.4.refs_2_ = f32[128,384]{1,0:T(8,128)S(1)} collective-permute-done((f32[128,384]{1,0:T(8,128)}, f32[128,384]{1,0:T(8,128)S(1)}, u32[]{:S(2)}, u32[]{:S(2)}) %collective-permute-start.4) | collective-permute-done | bytes 196640 | tf_op jit(solution)/shard_map/ppermute | solution.py:685
  73.6 0.7 copy-done.19
  74.2 5.4 %first.1 = (f32[4,256,128]{2,1,0:T(8,128)}, f32[4,256,128]{2,1,0:T(8,128)}) custom-call(s32[2]{0:T(128)} %pad_add_fusion.refs_0_, f32[128,384]{1,0:T(8,128)} %get-tuple-element.53.refs_1_, f32[128,384]{1,0:T(8,128)} %copy-done.19, f32[128,384]{1,0:T(8,128)} %copy-done.18, f32[128,384]{1,0:T(8,128)} %copy-done.17, f32[8,128,256]{2,1,0:T(8,128)} %get-tuple-element.54.refs_5_, ...), custom_call_target="tpu_custom_call" | custom-call | flops 805306368 | bytes 4194304 | tf_op jit(solution)/shard_map/first/pallas_call | solution.py:492
  79.6 1.1 collective-permute-start.7
  80.7 1.7 collective-permute-done.7.refs_1_
  82.5 0.8 copy-done.15
  83.3 2.1 couple.3
  85.3 1.2 collective-permute-start.8
  86.6 0.3 collective-permute-start.10
  86.8 2.1 collective-permute-start.9
  88.9 0.0 collective-permute-done.12.refs_1_
  88.9 1.2 copy-done.9
  90.1 2.9 %couple.5 = (f32[2,752,128]{2,1,0:T(8,128)}, f32[2,752,128]{2,1,0:T(8,128)}, f32[2,752,128]{2,1,0:T(8,128)}, f32[2,752,128]{2,1,0:T(8,128)}) custom-call(f32[4,752,128]{2,1,0:T(8,128)} %get-tuple-element.68.refs_0_, f32[4,752,128]{2,1,0:T(8,128)} %copy-done.9), custom_call_target="tpu_custom_call" | custom-call | bytes 6160384 | tf_op jit(solution)/shard_map/couple/pallas_call | solution.py:527
  93.0 18.8 %collective-permute-done.8.refs_1_ = f32[2,256,128]{2,1,0:T(8,128)S(1)} collective-permute-done((f32[2,256,128]{2,1,0:T(8,128)}, f32[2,256,128]{2,1,0:T(8,128)S(1)}, u32[]{:S(2)}, u32[]{:S(2)}) %collective-permute-start.8) | collective-permute-done | bytes 262176 | tf_op jit(solution)/shard_map/ppermute | solution.py:685
  111.7 0.7 copy-done.10
  112.5 2.1 collective-permute-start.13
  114.5 15.8 %collective-permute-done.10.refs_3_.refs_1_ = f32[2,256,128]{2,1,0:T(8,128)S(1)} collective-permute-done((f32[2,256,128]{2,1,0:T(8,128)}, f32[2,256,128]{2,1,0:T(8,128)S(1)}, u32[]{:S(2)}, u32[]{:S(2)}) %collective-permute-start.10) | collective-permute-done | bytes 262176 | tf_op jit(solution)/shard_map/ppermute | solution.py:685
  130.3 0.7 copy-done.11
  131.1 0.0 collective-permute-start.18
  131.1 0.0 collective-permute-done.9.refs_2_.refs_1_
  131.1 0.7 copy-done.12
  131.8 0.5 collective-permute-start.17
  132.3 1.2 collective-permute-start.11
  133.6 1.5 collective-permute-done.11.refs_1_
  135.1 0.8 copy-done.16
  135.9 2.1 couple.4
  137.9 29.0 %collective-permute-done.13.refs_1_ = f32[2,752,128]{2,1,0:T(8,128)S(1)} collective-permute-done((f32[2,752,128]{2,1,0:T(8,128)}, f32[2,752,128]{2,1,0:T(8,128)S(1)}, u32[]{:S(2)}, u32[]{:S(2)}) %collective-permute-start.13) | collective-permute-done | bytes 770080 | tf_op jit(solution)/shard_map/ppermute | solution.py:685
  166.9 0.9 copy-done.8
  167.8 2.1 collective-permute-start.14
  169.9 0.0 collective-permute-start.15
  169.9 1.2 collective-permute-start.16
  171.1 0.0 all-to-all-done.one_ref
  171.1 6.2 %finish_0.1 = (f32[8,2000,128]{2,1,0:T(8,128)}, bf16[8,256,256]{2,1,0:T(8,128)(2,1)}) custom-call(s32[1]{0:T(128)} %bitcast.refs_0_.me_ref, f32[8,128,128]{2,1,0:T(8,128)} %get-tuple-element.45.own_ref, f32[8,752,128]{2,1,0:T(8,128)} %all-to-all-done.one_ref, f32[2,256,128]{2,1,0:T(8,128)} %get-tuple-element.59.refs_0_, f32[2,256,128]{2,1,0:T(8,128)} %copy-done.10, ...), custom_call_target="tpu_custom_call" | custom-call | flops 805306368 | bytes 8192000 | tf_op jit(solution)/shard_map/finish_0/pallas_call | solution.py:604
  177.3 2.6 %collective-permute-done.18.refs_3_ = f32[2,752,128]{2,1,0:T(8,128)S(1)} collective-permute-done((f32[2,752,128]{2,1,0:T(8,128)}, f32[2,752,128]{2,1,0:T(8,128)S(1)}, u32[]{:S(2)}, u32[]{:S(2)}) %collective-permute-start.18) | collective-permute-done | bytes 770080 | tf_op jit(solution)/shard_map/ppermute | solution.py:685
  179.9 14.7 %collective-permute-done.17.refs_2_ = f32[2,752,128]{2,1,0:T(8,128)S(1)} collective-permute-done((f32[2,752,128]{2,1,0:T(8,128)}, f32[2,752,128]{2,1,0:T(8,128)S(1)}, u32[]{:S(2)}, u32[]{:S(2)}) %collective-permute-start.17) | collective-permute-done | bytes 770080 | tf_op jit(solution)/shard_map/ppermute | solution.py:685
  194.7 0.9 copy-done.14
  195.6 4.8 %finish_4.1.refs_4_ = f32[8,2000,128]{2,1,0:T(8,128)} custom-call(s32[1]{0:T(128)} %bitcast.refs_0_.me_ref, f32[8,128,128]{2,1,0:T(8,128)} %get-tuple-element.45.own_ref, bf16[8,256,256]{2,1,0:T(8,128)(2,1)} %get-tuple-element.63.operand_ref, f32[2,752,128]{2,1,0:T(8,128)} %get-tuple-element.73.refs_0_, ...), custom_call_target="tpu_custom_call", output_to_operand_aliasing={{}: (7, {})} | custom-call | flops 805306368 | bytes 6144000 | tf_op jit(solution)/shard_map/finish_4/pallas_call | solution.py:661
  200.4 0.0 collective-permute-done.14.refs_1_
  200.5 5.5 %collective-permute-done.15.refs_2_ = f32[2,256,128]{2,1,0:T(8,128)S(1)} collective-permute-done((f32[2,256,128]{2,1,0:T(8,128)}, f32[2,256,128]{2,1,0:T(8,128)S(1)}, u32[]{:S(2)}, u32[]{:S(2)}) %collective-permute-start.15) | collective-permute-done | bytes 262176 | tf_op jit(solution)/shard_map/ppermute | solution.py:685
  205.9 2.1 collective-permute-done.16.refs_3_
  208.0 3.1 %finish_7.1 = f32[8,2000,128]{2,1,0:T(8,128)} custom-call(s32[1]{0:T(128)} %bitcast.refs_0_.me_ref, f32[8,128,128]{2,1,0:T(8,128)S(1)} %copy-done, bf16[8,256,256]{2,1,0:T(8,128)(2,1)S(1)} %copy-done.1, f32[2,256,128]{2,1,0:T(8,128)S(1)} %copy-done.3, f32[2,256,128]{2,1,0:T(8,128)S(1)} %collective-permute-done.14.refs_1_, ...), custom_call_target="tpu_custom_call", output_to_operand_aliasing={{}: (7, {})} | custom-call | flops 268435456 | bytes 2048000 | tf_op jit(solution)/shard_map/finish_7/pallas_call | solution.py:661
  (35 shorter events, 0.1 us)
Async XLA Ops:
  0.0 15.6 %copy-start.4 = (f32[125,125]{1,0:T(8,128)S(1)}, f32[125,125]{1,0:T(8,128)}, u32[]{:S(2)}) copy-start(f32[125,125]{1,0:T(8,128)} %refs_3_.3) | copy-start | bytes 187504
  6.3 5.7 %collective-permute-start = (f32[8,8,128]{2,1,0:T(8,128)}, f32[8,8,128]{2,1,0:T(8,128)S(1)}, u32[]{:S(2)}, u32[]{:S(2)}) collective-permute-start(f32[8,8,128]{2,1,0:T(8,128)} %get-tuple-element.42), channel_id=1, source_target_pairs={{0,1},{1,2},{2,3},{3,4},{4,5},{5,6},{6,7},{8,9},{9,10},{10,11},{11... | collective-permute-start | bytes 98312 | tf_op jit(solution)/shard_map/ppermute | solution.py:690
  10.1 5.4 %collective-permute-start.1 = (f32[8,8,128]{2,1,0:T(8,128)}, f32[8,8,128]{2,1,0:T(8,128)S(1)}, u32[]{:S(2)}, u32[]{:S(2)}) collective-permute-start(f32[8,8,128]{2,1,0:T(8,128)} %get-tuple-element.43), channel_id=1, source_target_pairs={{1,0},{2,1},{3,2},{4,3},{5,4},{6,5},{7,6},{9,8},{10,9},{11,10},{12... | collective-permute-start | bytes 98312 | tf_op jit(solution)/shard_map/ppermute | solution.py:691
  15.6 0.8 copy-start.5
  24.0 147.1 %all-to-all-start = ((f32[8,752,128]{2,1,0:T(8,128)}), f32[8,752,128]{2,1,0:T(8,128)}, u32[]{:S(2)}, u32[]{:S(2)}) async-start(f32[8,752,128]{2,1,0:T(8,128)} %get-tuple-element.44.refs_0_.refs_11_), calls=%async_computation | async-start | bytes 6160384 | tf_op jit(solution)/shard_map/all_to_all | solution.py:696
  28.4 10.7 %copy-start.6 = (f32[8,8,256]{2,1,0:T(8,128)S(1)}, f32[8,8,256]{2,1,0:T(8,128)}, u32[]{:S(2)}) copy-start(f32[8,8,256]{2,1,0:T(8,128)} %get-tuple-element.41.refs_6_) | copy-start | bytes 196612
  28.4 10.7 %collective-permute-start.2 = (f32[1,256]{1,0:T(1,128)S(1)}, f32[1,256]{1,0:T(1,128)S(1)}, u32[]{:S(2)}, u32[]{:S(2)}) collective-permute-start(f32[1,256]{1,0:T(1,128)S(1)} %get-tuple-element.46), channel_id=1, source_target_pairs={{0,8},{8,16},{16,24},{24,0},{1,9},{9,17},{17,25},{25,1},{2,10},{10... | collective-permute-start | bytes 3080 | tf_op jit(solution)/shard_map/ppermute | solution.py:685
  29.7 9.5 %collective-permute-start.3 = (f32[1,256]{1,0:T(1,128)S(1)}, f32[1,256]{1,0:T(1,128)S(1)}, u32[]{:S(2)}, u32[]{:S(2)}) collective-permute-start(f32[1,256]{1,0:T(1,128)S(1)} %get-tuple-element.47), channel_id=1, source_target_pairs={{0,24},{8,0},{16,8},{24,16},{1,25},{9,1},{17,9},{25,17},{2,26},{10... | collective-permute-start | bytes 3080 | tf_op jit(solution)/shard_map/ppermute | solution.py:685
  39.2 0.8 copy-start.7
  55.8 0.8 copy-start.2
  56.6 32.3 %collective-permute-start.12 = (f32[4,752,128]{2,1,0:T(8,128)}, f32[4,752,128]{2,1,0:T(8,128)S(1)}, u32[]{:S(2)}, u32[]{:S(2)}) collective-permute-start(f32[4,752,128]{2,1,0:T(8,128)} %get-tuple-element.69), channel_id=1, source_target_pairs={{0,1},{1,0},{2,3},{3,2},{4,5},{5,4},{6,7},{7,6},{8,9},{9,8},{10,11... | collective-permute-start | bytes 4620296 | tf_op jit(solution)/shard_map/ppermute | solution.py:700
  61.5 6.8 %collective-permute-start.6 = (f32[128,384]{1,0:T(8,128)}, f32[128,384]{1,0:T(8,128)S(1)}, u32[]{:S(2)}, u32[]{:S(2)}) collective-permute-start(f32[128,384]{1,0:T(8,128)} %get-tuple-element.53.refs_1_), channel_id=1, source_target_pairs={{0,24},{8,0},{16,8},{24,16},{1,25},{9,1},{17,9},{25,17},{2,26},{10... | collective-permute-start | bytes 589832 | tf_op jit(solution)/shard_map/ppermute | solution.py:685
  62.8 6.5 %collective-permute-start.5 = (f32[128,384]{1,0:T(8,128)}, f32[128,384]{1,0:T(8,128)S(1)}, u32[]{:S(2)}, u32[]{:S(2)}) collective-permute-start(f32[128,384]{1,0:T(8,128)} %get-tuple-element.53.refs_1_), channel_id=1, source_target_pairs={{0,16},{8,24},{16,0},{24,8},{1,17},{9,25},{17,1},{25,9},{2,18},{10... | collective-permute-start | bytes 589832 | tf_op jit(solution)/shard_map/ppermute | solution.py:685
  63.0 10.6 %collective-permute-start.4 = (f32[128,384]{1,0:T(8,128)}, f32[128,384]{1,0:T(8,128)S(1)}, u32[]{:S(2)}, u32[]{:S(2)}) collective-permute-start(f32[128,384]{1,0:T(8,128)} %get-tuple-element.53.refs_1_), channel_id=1, source_target_pairs={{0,8},{8,16},{16,24},{24,0},{1,9},{9,17},{17,25},{25,1},{2,10},{10... | collective-permute-start | bytes 589832 | tf_op jit(solution)/shard_map/ppermute | solution.py:685
  68.3 5.3 %copy-start.17 = (f32[128,384]{1,0:T(8,128)}, f32[128,384]{1,0:T(8,128)S(1)}, u32[]{:S(2)}) copy-start(f32[128,384]{1,0:T(8,128)S(1)} %collective-permute-done.6.refs_4_) | copy-start | bytes 589828
  69.3 4.3 %copy-start.18 = (f32[128,384]{1,0:T(8,128)}, f32[128,384]{1,0:T(8,128)S(1)}, u32[]{:S(2)}) copy-start(f32[128,384]{1,0:T(8,128)S(1)} %collective-permute-done.5.refs_3_) | copy-start | bytes 589828
  73.6 0.7 copy-start.19
  79.6 2.8 %collective-permute-start.7 = (f32[4,256,128]{2,1,0:T(8,128)}, f32[4,256,128]{2,1,0:T(8,128)S(1)}, u32[]{:S(2)}, u32[]{:S(2)}) collective-permute-start(f32[4,256,128]{2,1,0:T(8,128)} %get-tuple-element.58), channel_id=1, source_target_pairs={{0,1},{1,0},{2,3},{3,2},{4,5},{5,4},{6,7},{7,6},{8,9},{9,8},{10,11... | collective-permute-start | bytes 1572872 | tf_op jit(solution)/shard_map/ppermute | solution.py:700
  82.5 0.8 copy-start.15
  85.3 26.4 %collective-permute-start.8 = (f32[2,256,128]{2,1,0:T(8,128)}, f32[2,256,128]{2,1,0:T(8,128)S(1)}, u32[]{:S(2)}, u32[]{:S(2)}) collective-permute-start(f32[2,256,128]{2,1,0:T(8,128)} %get-tuple-element.60), channel_id=1, source_target_pairs={{0,2},{1,3},{2,4},{3,5},{4,6},{5,7},{6,0},{7,1},{8,10},{9,11},{10,... | collective-permute-start | bytes 786440 | tf_op jit(solution)/shard_map/ppermute | solution.py:685
  86.6 43.8 %collective-permute-start.10 = (f32[2,256,128]{2,1,0:T(8,128)}, f32[2,256,128]{2,1,0:T(8,128)S(1)}, u32[]{:S(2)}, u32[]{:S(2)}) collective-permute-start(f32[2,256,128]{2,1,0:T(8,128)} %get-tuple-element.62), channel_id=1, source_target_pairs={{0,6},{1,7},{2,0},{3,1},{4,2},{5,3},{6,4},{7,5},{8,14},{9,15},{10,... | collective-permute-start | bytes 786440 | tf_op jit(solution)/shard_map/ppermute | solution.py:685
  86.8 44.2 %collective-permute-start.9 = (f32[2,256,128]{2,1,0:T(8,128)}, f32[2,256,128]{2,1,0:T(8,128)S(1)}, u32[]{:S(2)}, u32[]{:S(2)}) collective-permute-start(f32[2,256,128]{2,1,0:T(8,128)} %get-tuple-element.61), channel_id=1, source_target_pairs={{0,4},{1,5},{2,6},{3,7},{4,0},{5,1},{6,2},{7,3},{8,12},{9,13},{10,... | collective-permute-start | bytes 786440 | tf_op jit(solution)/shard_map/ppermute | solution.py:685
  88.9 1.2 copy-start.9
  111.7 0.7 copy-start.10
  112.5 54.5 %collective-permute-start.13 = (f32[2,752,128]{2,1,0:T(8,128)}, f32[2,752,128]{2,1,0:T(8,128)S(1)}, u32[]{:S(2)}, u32[]{:S(2)}) collective-permute-start(f32[2,752,128]{2,1,0:T(8,128)} %gate.6), channel_id=1, source_target_pairs={{0,2},{1,3},{2,4},{3,5},{4,6},{5,7},{6,0},{7,1},{8,10},{9,11},{10,... | collective-permute-start | bytes 2310152 | tf_op jit(solution)/shard_map/ppermute | solution.py:685
  130.3 0.7 copy-start.11
  131.1 48.9 %collective-permute-start.18 = (f32[2,752,128]{2,1,0:T(8,128)}, f32[2,752,128]{2,1,0:T(8,128)S(1)}, u32[]{:S(2)}, u32[]{:S(2)}) collective-permute-start(f32[2,752,128]{2,1,0:T(8,128)} %gate.11), channel_id=1, source_target_pairs={{0,6},{1,7},{2,0},{3,1},{4,2},{5,3},{6,4},{7,5},{8,14},{9,15},{10,... | collective-permute-start | bytes 2310152 | tf_op jit(solution)/shard_map/ppermute | solution.py:685
  131.1 0.7 copy-start.12
  131.8 62.9 %collective-permute-start.17 = (f32[2,752,128]{2,1,0:T(8,128)}, f32[2,752,128]{2,1,0:T(8,128)S(1)}, u32[]{:S(2)}, u32[]{:S(2)}) collective-permute-start(f32[2,752,128]{2,1,0:T(8,128)} %gate.10), channel_id=1, source_target_pairs={{0,4},{1,5},{2,6},{3,7},{4,0},{5,1},{6,2},{7,3},{8,12},{9,13},{10,... | collective-permute-start | bytes 2310152 | tf_op jit(solution)/shard_map/ppermute | solution.py:685
  132.3 2.8 %collective-permute-start.11 = (f32[4,256,128]{2,1,0:T(8,128)S(1)}, f32[4,256,128]{2,1,0:T(8,128)S(1)}, u32[]{:S(2)}, u32[]{:S(2)}) collective-permute-start(f32[4,256,128]{2,1,0:T(8,128)S(1)} %get-tuple-element.65), channel_id=1, source_target_pairs={{0,1},{1,0},{2,3},{3,2},{4,5},{5,4},{6,7},{7,6},{8,9},{9,8},{10,11... | collective-permute-start | bytes 1572872 | tf_op jit(solution)/shard_map/ppermute | solution.py:700
  135.1 0.8 copy-start.16
  166.9 0.9 copy-start.8
  167.8 32.6 %collective-permute-start.14 = (f32[2,256,128]{2,1,0:T(8,128)}, f32[2,256,128]{2,1,0:T(8,128)S(1)}, u32[]{:S(2)}, u32[]{:S(2)}) collective-permute-start(f32[2,256,128]{2,1,0:T(8,128)} %gate.7), channel_id=1, source_target_pairs={{0,2},{1,3},{2,4},{3,5},{4,6},{5,7},{6,0},{7,1},{8,10},{9,11},{10,... | collective-permute-start | bytes 786440 | tf_op jit(solution)/shard_map/ppermute | solution.py:685
  169.9 36.0 %collective-permute-start.15 = (f32[2,256,128]{2,1,0:T(8,128)}, f32[2,256,128]{2,1,0:T(8,128)S(1)}, u32[]{:S(2)}, u32[]{:S(2)}) collective-permute-start(f32[2,256,128]{2,1,0:T(8,128)} %gate.8), channel_id=1, source_target_pairs={{0,4},{1,5},{2,6},{3,7},{4,0},{5,1},{6,2},{7,3},{8,12},{9,13},{10,... | collective-permute-start | bytes 786440 | tf_op jit(solution)/shard_map/ppermute | solution.py:685
  169.9 38.1 %collective-permute-start.16 = (f32[2,256,128]{2,1,0:T(8,128)}, f32[2,256,128]{2,1,0:T(8,128)S(1)}, u32[]{:S(2)}, u32[]{:S(2)}) collective-permute-start(f32[2,256,128]{2,1,0:T(8,128)} %gate.9), channel_id=1, source_target_pairs={{0,6},{1,7},{2,0},{3,1},{4,2},{5,3},{6,4},{7,5},{8,14},{9,15},{10,... | collective-permute-start | bytes 786440 | tf_op jit(solution)/shard_map/ppermute | solution.py:685
  179.9 15.6 %copy-start.13 = (f32[2,752,128]{2,1,0:T(8,128)}, f32[2,752,128]{2,1,0:T(8,128)S(1)}, u32[]{:S(2)}) copy-start(f32[2,752,128]{2,1,0:T(8,128)S(1)} %collective-permute-done.18.refs_3_) | copy-start | bytes 2310148
  194.7 0.9 copy-start.14
  195.6 12.4 %copy-start = (f32[8,128,128]{2,1,0:T(8,128)S(1)}, f32[8,128,128]{2,1,0:T(8,128)}, u32[]{:S(2)}) copy-start(f32[8,128,128]{2,1,0:T(8,128)} %get-tuple-element.45.own_ref) | copy-start | bytes 1572868
  195.6 12.4 %copy-start.1 = (bf16[8,256,256]{2,1,0:T(8,128)(2,1)S(1)}, bf16[8,256,256]{2,1,0:T(8,128)(2,1)}, u32[]{:S(2)}) copy-start(bf16[8,256,256]{2,1,0:T(8,128)(2,1)} %get-tuple-element.63.operand_ref) | copy-start | bytes 3145732
  195.6 12.4 %copy-start.3 = (f32[2,256,128]{2,1,0:T(8,128)S(1)}, f32[2,256,128]{2,1,0:T(8,128)}, u32[]{:S(2)}) copy-start(f32[2,256,128]{2,1,0:T(8,128)} %get-tuple-element.66.refs_0_) | copy-start | bytes 786436

commit v8 on v7

--- a/solution.py
+++ b/solution.py
@@ -192,7 +192,7 @@
         ],
         z.flops * z.steps * z.segments,
         4 * z.segments * tall * z.ax,
-        limit=57,
+        limit=52,
     )(state, to_modal)
 
 
@@ -431,6 +431,7 @@
         ],
         z.flops * z.segments * (z.steps + 1) // 2,
         4 * z.segments * z.steps * z.pad * z.pad,
+        limit=52,
     )(me, gain, *after)
 
 
@@ -676,7 +677,44 @@
         z.flops * count * z.segments,
         4 * 2 * count * tall * z.ax,
         {len(inputs) - 1: 0},
-        limit=57 if count > 1 else 40,
+    )(*inputs)
+
+
+def close_call(z, step, me, own, messages, operands, out):
+    radial = z.segments * z.rows
+    tall = z.nodes * radial
+    pairs = z.segments // 2
+
+    def kernel(me_ref, own_ref, operand_ref, *refs):
+        message_refs = refs[:pairs]
+        _, out_ref, stage, out_sem = refs[pairs:]
+        matrix = operand_left(own_ref[step])
+        mine = me_ref[0]
+        side = lax.rem(mine, 2)
+        for d in range(pairs):
+            pair = lax.rem(mine // 2 - d + pairs, pairs) * 2
+            for n in range(2):
+                e = pair + (side if n == 0 else 1 - side)
+                value = product(matrix, operand_ref[e])[: z.nodes] + read_exact(z, message_refs[d], (n,), 0)
+                for j in range(z.rows):
+                    rows = pl.ds(e * z.rows + j, z.nodes, stride=radial)
+                    stage[rows, :] = value[:, j * z.ax : (j + 1) * z.ax]
+        copy = pltpu.make_async_copy(stage, out_ref.at[step], out_sem)
+        copy.start()
+        copy.wait()
+
+    inputs = [me, own, operands] + list(messages) + [out]
+    return call(
+        kernel,
+        f"finish_{step}",
+        f32(z.steps, tall, z.ax),
+        [spec_smem()] + [spec_vmem()] * (2 + pairs) + [spec_hbm()],
+        spec_hbm(),
+        [pltpu.VMEM((tall, z.ax), F32), pltpu.SemaphoreType.DMA],
+        z.flops * z.segments,
+        4 * 2 * tall * z.ax,
+        {len(inputs) - 1: 0},
+        limit=36,
     )(*inputs)
 
 
@@ -746,7 +784,10 @@
     after = received_first
     for n, part in enumerate(parts):
         received = spread_pairs(z, pairs[2 * n], pairs[2 * n + 1], after)
-        out = finish_call(z, part, me, own, received, operands, out)
+        if part == (z.steps - 1, z.steps):
+            out = close_call(z, part[0], me, own, received, operands, out)
+        else:
+            out = finish_call(z, part, me, own, received, operands, out)
         after = [received[1]] * len(received)
     return out.reshape(z.steps, z.nodes, segments * z.rows, z.ax)
 

time: 212 us -> 209 us (0.986)
  Pallas kernels: 68.9 us -> 66.1 us
    pallas_call x2 -> x1, Pallas kernels: 7.98 us -> 4.84 us  [finish_call(): call(kernel, f'finish_{low}', f32(z.steps, tall, z.ax), [spec_smem()] + [...]
    unnamed x40 -> x44, local copies, waits for them, and re-layouts: 9.86 us -> 11.5 us
where the time goes in v8:
time: 209 us; the launch traced here: 208 us
  waiting for transfers between devices  102 us (49%)
  Pallas kernels  66.1 us (32%)
  starting transfers between devices  27.6 us (13%)
  local copies, waits for them, and re-layouts  11.5 us (6%)
    ppermute x14, waiting for transfers between devices, shift_by(): lax.ppermute(array, axis, [(i, (i + by) % size) for i in range(size)])  95.6 us
    pallas_call x2, Pallas kernels, sweep_call(): call(kernel, f'sweep_{low}', outs + more, in_specs + extra_specs + [spec_...  23.4 us
    ppermute x14, starting transfers between devices, shift_by(): lax.ppermute(array, axis, [(i, (i + by) % size) for i in range(size)])  14.7 us
    unnamed x44, local copies, waits for them, and re-layouts  11.5 us
    pallas_call x1, Pallas kernels, maps_call(): call(kernel, 'maps', outs, [spec_smem(), spec_hbm()] + [spec_any()] * len...  8.27 us
    pallas_call x3, Pallas kernels, couple_call(): call(kernel, 'couple', [f32(2, message, z.ax)] * pairs, [spec_hbm()] * 2,...  7 us
    pallas_call x1, Pallas kernels, open_call(): call(kernel, 'finish_0', [f32(z.steps, tall, z.ax), jax.ShapeDtypeStruct(...  6.2 us
    pallas_call x1, Pallas kernels, first_call(): call(kernel, 'first', [f32(pairs, rows, z.ax)] * 2, [spec_smem()] + [spec...  5.34 us
  transfers between devices with their start and end apart: 20, of which 13 were waited for; matrix products, arithmetic and copies ran while one was open for 0% of the time, Pallas kernels for 25%

profile of v8, /device:TPU:9, one launch (start us, length us, event | category | flops | bytes accessed | tf_op | source)
XLA Modules:
  0.0 208.2 jit_solution(9336125387612466326)
XLA Ops:
  0.0 0.8 copy-done.9
  0.8 4.9 %sensor.1 = (f32[8,8,256]{2,1,0:T(8,128)S(1)}, f32[8,8,128]{2,1,0:T(8,128)S(1)}, f32[8,8,128]{2,1,0:T(8,128)S(1)}) custom-call(f32[8,2000,128]{2,1,0:T(8,128)} %bitcast.7, f32[125,125]{1,0:T(8,128)S(1)} %copy-done.9), custom_call_target="tpu_custom_call" | custom-call | flops 2147483648 | bytes 8192000 | tf_op jit(solution)/shard_map/sensor/pallas_call | solution.py:181
  5.7 3.8 %collective-permute-start = (f32[8,8,128]{2,1,0:T(8,128)S(1)}, f32[8,8,128]{2,1,0:T(8,128)S(1)}, u32[]{:S(2)}, u32[]{:S(2)}) collective-permute-start(f32[8,8,128]{2,1,0:T(8,128)S(1)} %get-tuple-element.42), channel_id=1, source_target_pairs={{0,1},{1,2},{2,3},{3,4},{4,5},{5,6},{6,7},{8,9},{9,10},{10,11},{11... | collective-permute-start | bytes 98312 | tf_op jit(solution)/shard_map/ppermute | solution.py:728
  9.5 1.9 collective-permute-start.1
  11.4 0.0 collective-permute-done.refs_7_
  11.4 3.3 %collective-permute-done.1.refs_8_ = f32[8,8,128]{2,1,0:T(8,128)S(1)} collective-permute-done((f32[8,8,128]{2,1,0:T(8,128)S(1)}, f32[8,8,128]{2,1,0:T(8,128)S(1)}, u32[]{:S(2)}, u32[]{:S(2)}) %collective-permute-start.1) | collective-permute-done | bytes 32800 | tf_op jit(solution)/shard_map/ppermute | solution.py:729
  14.7 7.6 %sweep_1.1 = (f32[8,752,128]{2,1,0:T(8,128)}, f32[1,256]{1,0:T(1,128)S(1)}, f32[1,256]{1,0:T(1,128)S(1)}) custom-call(s32[1]{0:T(128)} %bitcast.refs_0_.me_ref, f32[8,2000,128]{2,1,0:T(8,128)} %bitcast.8, f32[8,2000,128]{2,1,0:T(8,128)} %bitcast.13, f32[125,125]{1,0:T(8,128)S(1)} %copy-done.7, f32[125,64,125]{2,1,0:T(8,128)} %bitcast.15, ...), custom_call_target="tpu_custom_call" | custom-call | flops 2415919104 | bytes 12320768 | tf_op jit(solution)/shard_map/sweep_1/pallas_call | solution.py:374
  22.3 4.4 %all-to-all-start = ((f32[8,752,128]{2,1,0:T(8,128)}), f32[8,752,128]{2,1,0:T(8,128)}, u32[]{:S(2)}, u32[]{:S(2)}) async-start(f32[8,752,128]{2,1,0:T(8,128)} %get-tuple-element.44.refs_0_.refs_11_), calls=%async_computation | async-start | bytes 6160384 | tf_op jit(solution)/shard_map/all_to_all | solution.py:734
  26.8 1.3 collective-permute-start.2
  28.0 1.2 collective-permute-start.3
  29.2 8.3 %maps.1 = (f32[8,128,128]{2,1,0:T(8,128)S(1)}, f32[8,128,128]{2,1,0:T(8,128)S(1)}, f32[8,128,128]{2,1,0:T(8,128)S(1)}, f32[8,128,128]{2,1,0:T(8,128)}, f32[8,128,128]{2,1,0:T(8,128)}, /*index=5*/f32[128,128]{1,0:T(8,128)S(1)}) custom-call(s32[1]{0:T(128)} %bitcast.refs_0_.me_ref, f32[125,64,125]{2,1,0:T(8,128)} %bitcast.11, ...), custom_call_target="tpu_custom_call" | custom-call | flops 1207959552 | bytes 4194304 | tf_op jit(solution)/shard_map/maps/pallas_call | solution.py:421
  37.5 0.8 copy-done
  38.3 0.8 copy-done.3
  39.1 0.8 copy-done.4
  39.9 0.0 collective-permute-done.2.refs_9_
  39.9 0.0 collective-permute-done.3.refs_10_
  39.9 15.8 %sweep_4.1 = (f32[4,752,128]{2,1,0:T(8,128)}, f32[4,752,128]{2,1,0:T(8,128)}, f32[4,256,128]{2,1,0:T(8,128)S(1)}, f32[4,256,128]{2,1,0:T(8,128)S(1)}, f32[8,128,256]{2,1,0:T(8,128)}, /*index=5*/f32[8,128,256]{2,1,0:T(8,128)}) custom-call(s32[1]{0:T(128)} %bitcast.refs_0_.me_ref, f32[8,2000,128]{2,1,0:T(8,128)} %bitcast.9, f32[8,2000,128]{2,1,0:T(8,128)} %bitcast.14, ...), custom_call_target="tpu_custom_call" | custom-call | flops 4026531840 | bytes 16384000 | tf_op jit(solution)/shard_map/sweep_4/pallas_call | solution.py:374
  55.8 0.8 copy-done.5
  56.6 0.5 collective-permute-start.12
  57.0 4.5 %chain.1 = (f32[8,128,256]{2,1,0:T(8,128)}, f32[128,384]{1,0:T(8,128)}) custom-call(f32[8,128,256]{2,1,0:T(8,128)} %get-tuple-element.49.start_ref.refs_8_, f32[8,128,256]{2,1,0:T(8,128)} %get-tuple-element.50.end_ref, f32[8,128,128]{2,1,0:T(8,128)} %copy-done.4, f32[8,128,128]{2,1,0:T(8,128)} %get-tuple-element.52.whole_ref, f32[128,128]{1,0:T(8,128)} %copy-done.8), custom_call_target="tpu_custom_call" | custom-call | flops 536870912 | bytes 4194304 | tf_op jit(solution)/shard_map/chain/pallas_call | solution.py:452
  61.5 1.3 collective-permute-start.6
  62.8 0.2 collective-permute-start.5
  63.0 1.2 collective-permute-start.4
  64.2 0.6 pad_add_fusion.refs_0_
  64.8 3.5 %collective-permute-done.6.refs_4_ = f32[128,384]{1,0:T(8,128)S(1)} collective-permute-done((f32[128,384]{1,0:T(8,128)}, f32[128,384]{1,0:T(8,128)S(1)}, u32[]{:S(2)}, u32[]{:S(2)}) %collective-permute-start.6) | collective-permute-done | bytes 196640 | tf_op jit(solution)/shard_map/ppermute | solution.py:723
  68.3 1.0 collective-permute-done.5.refs_3_
  69.3 4.3 %collective-permute-done.4.refs_2_ = f32[128,384]{1,0:T(8,128)S(1)} collective-permute-done((f32[128,384]{1,0:T(8,128)}, f32[128,384]{1,0:T(8,128)S(1)}, u32[]{:S(2)}, u32[]{:S(2)}) %collective-permute-start.4) | collective-permute-done | bytes 196640 | tf_op jit(solution)/shard_map/ppermute | solution.py:723
  73.6 0.7 copy-done.21
  74.2 5.3 %first.1 = (f32[4,256,128]{2,1,0:T(8,128)}, f32[4,256,128]{2,1,0:T(8,128)}) custom-call(s32[2]{0:T(128)} %pad_add_fusion.refs_0_, f32[128,384]{1,0:T(8,128)} %get-tuple-element.53.refs_1_, f32[128,384]{1,0:T(8,128)} %copy-done.21, f32[128,384]{1,0:T(8,128)} %copy-done.20, f32[128,384]{1,0:T(8,128)} %copy-done.19, f32[8,128,256]{2,1,0:T(8,128)} %get-tuple-element.54.refs_5_, ...), custom_call_target="tpu_custom_call" | custom-call | flops 805306368 | bytes 4194304 | tf_op jit(solution)/shard_map/first/pallas_call | solution.py:493
  79.6 1.1 collective-permute-start.7
  80.6 1.7 collective-permute-done.7.refs_1_
  82.4 0.8 copy-done.17
  83.2 2.1 couple.3
  85.3 1.3 collective-permute-start.8
  86.5 0.2 collective-permute-start.10
  86.8 2.1 collective-permute-start.9
  88.9 0.0 collective-permute-done.12.refs_1_
  88.9 1.2 copy-done.11
  90.1 2.9 %couple.5 = (f32[2,752,128]{2,1,0:T(8,128)}, f32[2,752,128]{2,1,0:T(8,128)}, f32[2,752,128]{2,1,0:T(8,128)}, f32[2,752,128]{2,1,0:T(8,128)}) custom-call(f32[4,752,128]{2,1,0:T(8,128)} %get-tuple-element.68.refs_0_, f32[4,752,128]{2,1,0:T(8,128)} %copy-done.11), custom_call_target="tpu_custom_call" | custom-call | bytes 6160384 | tf_op jit(solution)/shard_map/couple/pallas_call | solution.py:528
  92.9 17.1 %collective-permute-done.8.refs_1_ = f32[2,256,128]{2,1,0:T(8,128)S(1)} collective-permute-done((f32[2,256,128]{2,1,0:T(8,128)}, f32[2,256,128]{2,1,0:T(8,128)S(1)}, u32[]{:S(2)}, u32[]{:S(2)}) %collective-permute-start.8) | collective-permute-done | bytes 262176 | tf_op jit(solution)/shard_map/ppermute | solution.py:723
  110.1 0.7 copy-done.12
  110.8 2.1 %collective-permute-start.13 = (f32[2,752,128]{2,1,0:T(8,128)}, f32[2,752,128]{2,1,0:T(8,128)S(1)}, u32[]{:S(2)}, u32[]{:S(2)}) collective-permute-start(f32[2,752,128]{2,1,0:T(8,128)} %gate.6), channel_id=1, source_target_pairs={{0,2},{1,3},{2,4},{3,5},{4,6},{5,7},{6,0},{7,1},{8,10},{9,11},{10,... | collective-permute-start | bytes 2310152 | tf_op jit(solution)/shard_map/ppermute | solution.py:723
  112.9 15.8 %collective-permute-done.10.refs_3_.refs_1_ = f32[2,256,128]{2,1,0:T(8,128)S(1)} collective-permute-done((f32[2,256,128]{2,1,0:T(8,128)}, f32[2,256,128]{2,1,0:T(8,128)S(1)}, u32[]{:S(2)}, u32[]{:S(2)}) %collective-permute-start.10) | collective-permute-done | bytes 262176 | tf_op jit(solution)/shard_map/ppermute | solution.py:723
  128.7 0.7 copy-done.13
  129.4 0.0 collective-permute-start.18
  129.4 0.7 copy-done.14
  130.1 0.5 collective-permute-start.17
  130.7 1.2 collective-permute-start.11
  131.9 1.5 collective-permute-done.11.refs_1_
  133.4 0.8 copy-done.18
  134.3 2.1 couple.4
  136.3 28.9 %collective-permute-done.13.refs_1_ = f32[2,752,128]{2,1,0:T(8,128)S(1)} collective-permute-done((f32[2,752,128]{2,1,0:T(8,128)}, f32[2,752,128]{2,1,0:T(8,128)S(1)}, u32[]{:S(2)}, u32[]{:S(2)}) %collective-permute-start.13) | collective-permute-done | bytes 770080 | tf_op jit(solution)/shard_map/ppermute | solution.py:723
  165.3 0.9 copy-done.10
  166.2 2.1 %collective-permute-start.14 = (f32[2,256,128]{2,1,0:T(8,128)}, f32[2,256,128]{2,1,0:T(8,128)S(1)}, u32[]{:S(2)}, u32[]{:S(2)}) collective-permute-start(f32[2,256,128]{2,1,0:T(8,128)} %gate.7), channel_id=1, source_target_pairs={{0,2},{1,3},{2,4},{3,5},{4,6},{5,7},{6,0},{7,1},{8,10},{9,11},{10,... | collective-permute-start | bytes 786440 | tf_op jit(solution)/shard_map/ppermute | solution.py:723
  168.3 1.2 collective-permute-start.16
  169.4 6.2 %finish_0.1 = (f32[8,2000,128]{2,1,0:T(8,128)}, bf16[8,256,256]{2,1,0:T(8,128)(2,1)}) custom-call(s32[1]{0:T(128)} %bitcast.refs_0_.me_ref, f32[8,128,128]{2,1,0:T(8,128)} %copy-done, f32[8,752,128]{2,1,0:T(8,128)} %all-to-all-done.one_ref, f32[2,256,128]{2,1,0:T(8,128)} %get-tuple-element.59.refs_0_, f32[2,256,128]{2,1,0:T(8,128)} %copy-done.12, ...), custom_call_target="tpu_custom_call" | custom-call | flops 805306368 | bytes 8192000 | tf_op jit(solution)/shard_map/finish_0/pallas_call | solution.py:605
  175.6 2.7 %collective-permute-done.18.refs_3_ = f32[2,752,128]{2,1,0:T(8,128)S(1)} collective-permute-done((f32[2,752,128]{2,1,0:T(8,128)}, f32[2,752,128]{2,1,0:T(8,128)S(1)}, u32[]{:S(2)}, u32[]{:S(2)}) %collective-permute-start.18) | collective-permute-done | bytes 770080 | tf_op jit(solution)/shard_map/ppermute | solution.py:723
  178.3 14.7 %collective-permute-done.17.refs_2_ = f32[2,752,128]{2,1,0:T(8,128)S(1)} collective-permute-done((f32[2,752,128]{2,1,0:T(8,128)}, f32[2,752,128]{2,1,0:T(8,128)S(1)}, u32[]{:S(2)}, u32[]{:S(2)}) %collective-permute-start.17) | collective-permute-done | bytes 770080 | tf_op jit(solution)/shard_map/ppermute | solution.py:723
  193.0 0.9 copy-done.16
  193.9 4.8 %finish_4.1.refs_4_ = f32[8,2000,128]{2,1,0:T(8,128)} custom-call(s32[1]{0:T(128)} %bitcast.refs_0_.me_ref, f32[8,128,128]{2,1,0:T(8,128)} %copy-done, bf16[8,256,256]{2,1,0:T(8,128)(2,1)} %get-tuple-element.63.operand_ref, f32[2,752,128]{2,1,0:T(8,128)} %get-tuple-element.73.refs_0_, f32[2,752,128]{2,1,0:T(8,128)} %copy-done.10, ...), custom_call_target="tpu_custom_call", output_to_operand_aliasing={{}: (7, {})} | custom-call | flops 805306368 | bytes 6144000 | tf_op jit(solution)/shard_map/finish_4/pallas_call | solution.py:662
  198.8 0.0 collective-permute-done.14.refs_1_
  198.8 5.5 %collective-permute-done.15.refs_2_ = f32[2,256,128]{2,1,0:T(8,128)S(1)} collective-permute-done((f32[2,256,128]{2,1,0:T(8,128)}, f32[2,256,128]{2,1,0:T(8,128)S(1)}, u32[]{:S(2)}, u32[]{:S(2)}) %collective-permute-start.15) | collective-permute-done | bytes 262176 | tf_op jit(solution)/shard_map/ppermute | solution.py:723
  204.3 2.1 collective-permute-done.16.refs_3_
  206.3 1.7 finish_7.1
  (39 shorter events, 0.1 us)
Async XLA Ops:
  0.0 0.8 copy-start.9
  0.8 13.9 %copy-start.7 = (f32[125,125]{1,0:T(8,128)S(1)}, f32[125,125]{1,0:T(8,128)}, u32[]{:S(2)}) copy-start(f32[125,125]{1,0:T(8,128)} %refs_3_.3) | copy-start | bytes 187504
  5.7 5.7 %collective-permute-start = (f32[8,8,128]{2,1,0:T(8,128)S(1)}, f32[8,8,128]{2,1,0:T(8,128)S(1)}, u32[]{:S(2)}, u32[]{:S(2)}) collective-permute-start(f32[8,8,128]{2,1,0:T(8,128)S(1)} %get-tuple-element.42), channel_id=1, source_target_pairs={{0,1},{1,2},{2,3},{3,4},{4,5},{5,6},{6,7},{8,9},{9,10},{10,11},{11... | collective-permute-start | bytes 98312 | tf_op jit(solution)/shard_map/ppermute | solution.py:728
  9.5 5.2 %collective-permute-start.1 = (f32[8,8,128]{2,1,0:T(8,128)S(1)}, f32[8,8,128]{2,1,0:T(8,128)S(1)}, u32[]{:S(2)}, u32[]{:S(2)}) collective-permute-start(f32[8,8,128]{2,1,0:T(8,128)S(1)} %get-tuple-element.43), channel_id=1, source_target_pairs={{1,0},{2,1},{3,2},{4,3},{5,4},{6,5},{7,6},{9,8},{10,9},{11,10},{12... | collective-permute-start | bytes 98312 | tf_op jit(solution)/shard_map/ppermute | solution.py:729
  22.3 147.1 %all-to-all-start = ((f32[8,752,128]{2,1,0:T(8,128)}), f32[8,752,128]{2,1,0:T(8,128)}, u32[]{:S(2)}, u32[]{:S(2)}) async-start(f32[8,752,128]{2,1,0:T(8,128)} %get-tuple-element.44.refs_0_.refs_11_), calls=%async_computation | async-start | bytes 6160384 | tf_op jit(solution)/shard_map/all_to_all | solution.py:734
  26.8 13.2 %collective-permute-start.2 = (f32[1,256]{1,0:T(1,128)S(1)}, f32[1,256]{1,0:T(1,128)S(1)}, u32[]{:S(2)}, u32[]{:S(2)}) collective-permute-start(f32[1,256]{1,0:T(1,128)S(1)} %get-tuple-element.46), channel_id=1, source_target_pairs={{0,8},{8,16},{16,24},{24,0},{1,9},{9,17},{17,25},{25,1},{2,10},{10... | collective-permute-start | bytes 3080 | tf_op jit(solution)/shard_map/ppermute | solution.py:723
  28.0 11.9 %collective-permute-start.3 = (f32[1,256]{1,0:T(1,128)S(1)}, f32[1,256]{1,0:T(1,128)S(1)}, u32[]{:S(2)}, u32[]{:S(2)}) collective-permute-start(f32[1,256]{1,0:T(1,128)S(1)} %get-tuple-element.47), channel_id=1, source_target_pairs={{0,24},{8,0},{16,8},{24,16},{1,25},{9,1},{17,9},{25,17},{2,26},{10... | collective-permute-start | bytes 3080 | tf_op jit(solution)/shard_map/ppermute | solution.py:723
  37.5 0.8 copy-start
  38.3 0.8 copy-start.3
  39.1 0.8 copy-start.4
  39.9 15.8 %copy-start.8 = (f32[128,128]{1,0:T(8,128)}, f32[128,128]{1,0:T(8,128)S(1)}, u32[]{:S(2)}) copy-start(f32[128,128]{1,0:T(8,128)S(1)} %get-tuple-element.48.refs_12_.group_ref) | copy-start | bytes 196612
  55.8 0.8 copy-start.5
  56.6 32.3 %collective-permute-start.12 = (f32[4,752,128]{2,1,0:T(8,128)}, f32[4,752,128]{2,1,0:T(8,128)S(1)}, u32[]{:S(2)}, u32[]{:S(2)}) collective-permute-start(f32[4,752,128]{2,1,0:T(8,128)} %get-tuple-element.69), channel_id=1, source_target_pairs={{0,1},{1,0},{2,3},{3,2},{4,5},{5,4},{6,7},{7,6},{8,9},{9,8},{10,11... | collective-permute-start | bytes 4620296 | tf_op jit(solution)/shard_map/ppermute | solution.py:738
  61.5 6.8 %collective-permute-start.6 = (f32[128,384]{1,0:T(8,128)}, f32[128,384]{1,0:T(8,128)S(1)}, u32[]{:S(2)}, u32[]{:S(2)}) collective-permute-start(f32[128,384]{1,0:T(8,128)} %get-tuple-element.53.refs_1_), channel_id=1, source_target_pairs={{0,24},{8,0},{16,8},{24,16},{1,25},{9,1},{17,9},{25,17},{2,26},{10... | collective-permute-start | bytes 589832 | tf_op jit(solution)/shard_map/ppermute | solution.py:723
  62.8 6.5 %collective-permute-start.5 = (f32[128,384]{1,0:T(8,128)}, f32[128,384]{1,0:T(8,128)S(1)}, u32[]{:S(2)}, u32[]{:S(2)}) collective-permute-start(f32[128,384]{1,0:T(8,128)} %get-tuple-element.53.refs_1_), channel_id=1, source_target_pairs={{0,16},{8,24},{16,0},{24,8},{1,17},{9,25},{17,1},{25,9},{2,18},{10... | collective-permute-start | bytes 589832 | tf_op jit(solution)/shard_map/ppermute | solution.py:723
  63.0 10.6 %collective-permute-start.4 = (f32[128,384]{1,0:T(8,128)}, f32[128,384]{1,0:T(8,128)S(1)}, u32[]{:S(2)}, u32[]{:S(2)}) collective-permute-start(f32[128,384]{1,0:T(8,128)} %get-tuple-element.53.refs_1_), channel_id=1, source_target_pairs={{0,8},{8,16},{16,24},{24,0},{1,9},{9,17},{17,25},{25,1},{2,10},{10... | collective-permute-start | bytes 589832 | tf_op jit(solution)/shard_map/ppermute | solution.py:723
  68.3 5.3 %copy-start.19 = (f32[128,384]{1,0:T(8,128)}, f32[128,384]{1,0:T(8,128)S(1)}, u32[]{:S(2)}) copy-start(f32[128,384]{1,0:T(8,128)S(1)} %collective-permute-done.6.refs_4_) | copy-start | bytes 589828
  69.3 4.3 %copy-start.20 = (f32[128,384]{1,0:T(8,128)}, f32[128,384]{1,0:T(8,128)S(1)}, u32[]{:S(2)}) copy-start(f32[128,384]{1,0:T(8,128)S(1)} %collective-permute-done.5.refs_3_) | copy-start | bytes 589828
  73.5 0.7 copy-start.21
  79.6 2.8 %collective-permute-start.7 = (f32[4,256,128]{2,1,0:T(8,128)}, f32[4,256,128]{2,1,0:T(8,128)S(1)}, u32[]{:S(2)}, u32[]{:S(2)}) collective-permute-start(f32[4,256,128]{2,1,0:T(8,128)} %get-tuple-element.58), channel_id=1, source_target_pairs={{0,1},{1,0},{2,3},{3,2},{4,5},{5,4},{6,7},{7,6},{8,9},{9,8},{10,11... | collective-permute-start | bytes 1572872 | tf_op jit(solution)/shard_map/ppermute | solution.py:738
  82.4 0.8 copy-start.17
  85.3 24.8 %collective-permute-start.8 = (f32[2,256,128]{2,1,0:T(8,128)}, f32[2,256,128]{2,1,0:T(8,128)S(1)}, u32[]{:S(2)}, u32[]{:S(2)}) collective-permute-start(f32[2,256,128]{2,1,0:T(8,128)} %get-tuple-element.60), channel_id=1, source_target_pairs={{0,2},{1,3},{2,4},{3,5},{4,6},{5,7},{6,0},{7,1},{8,10},{9,11},{10,... | collective-permute-start | bytes 786440 | tf_op jit(solution)/shard_map/ppermute | solution.py:723
  86.5 42.2 %collective-permute-start.10 = (f32[2,256,128]{2,1,0:T(8,128)}, f32[2,256,128]{2,1,0:T(8,128)S(1)}, u32[]{:S(2)}, u32[]{:S(2)}) collective-permute-start(f32[2,256,128]{2,1,0:T(8,128)} %get-tuple-element.62), channel_id=1, source_target_pairs={{0,6},{1,7},{2,0},{3,1},{4,2},{5,3},{6,4},{7,5},{8,14},{9,15},{10,... | collective-permute-start | bytes 786440 | tf_op jit(solution)/shard_map/ppermute | solution.py:723
  86.8 42.6 %collective-permute-start.9 = (f32[2,256,128]{2,1,0:T(8,128)}, f32[2,256,128]{2,1,0:T(8,128)S(1)}, u32[]{:S(2)}, u32[]{:S(2)}) collective-permute-start(f32[2,256,128]{2,1,0:T(8,128)} %get-tuple-element.61), channel_id=1, source_target_pairs={{0,4},{1,5},{2,6},{3,7},{4,0},{5,1},{6,2},{7,3},{8,12},{9,13},{10,... | collective-permute-start | bytes 786440 | tf_op jit(solution)/shard_map/ppermute | solution.py:723
  88.9 1.2 copy-start.11
  110.1 0.7 copy-start.12
  110.8 54.5 %collective-permute-start.13 = (f32[2,752,128]{2,1,0:T(8,128)}, f32[2,752,128]{2,1,0:T(8,128)S(1)}, u32[]{:S(2)}, u32[]{:S(2)}) collective-permute-start(f32[2,752,128]{2,1,0:T(8,128)} %gate.6), channel_id=1, source_target_pairs={{0,2},{1,3},{2,4},{3,5},{4,6},{5,7},{6,0},{7,1},{8,10},{9,11},{10,... | collective-permute-start | bytes 2310152 | tf_op jit(solution)/shard_map/ppermute | solution.py:723
  128.7 0.7 copy-start.13
  129.4 48.9 %collective-permute-start.18 = (f32[2,752,128]{2,1,0:T(8,128)}, f32[2,752,128]{2,1,0:T(8,128)S(1)}, u32[]{:S(2)}, u32[]{:S(2)}) collective-permute-start(f32[2,752,128]{2,1,0:T(8,128)} %gate.11), channel_id=1, source_target_pairs={{0,6},{1,7},{2,0},{3,1},{4,2},{5,3},{6,4},{7,5},{8,14},{9,15},{10,... | collective-permute-start | bytes 2310152 | tf_op jit(solution)/shard_map/ppermute | solution.py:723
  129.4 0.7 copy-start.14
  130.1 62.9 %collective-permute-start.17 = (f32[2,752,128]{2,1,0:T(8,128)}, f32[2,752,128]{2,1,0:T(8,128)S(1)}, u32[]{:S(2)}, u32[]{:S(2)}) collective-permute-start(f32[2,752,128]{2,1,0:T(8,128)} %gate.10), channel_id=1, source_target_pairs={{0,4},{1,5},{2,6},{3,7},{4,0},{5,1},{6,2},{7,3},{8,12},{9,13},{10,... | collective-permute-start | bytes 2310152 | tf_op jit(solution)/shard_map/ppermute | solution.py:723
  130.7 2.8 %collective-permute-start.11 = (f32[4,256,128]{2,1,0:T(8,128)S(1)}, f32[4,256,128]{2,1,0:T(8,128)S(1)}, u32[]{:S(2)}, u32[]{:S(2)}) collective-permute-start(f32[4,256,128]{2,1,0:T(8,128)S(1)} %get-tuple-element.65), channel_id=1, source_target_pairs={{0,1},{1,0},{2,3},{3,2},{4,5},{5,4},{6,7},{7,6},{8,9},{9,8},{10,11... | collective-permute-start | bytes 1572872 | tf_op jit(solution)/shard_map/ppermute | solution.py:738
  133.4 0.8 copy-start.18
  165.3 0.9 copy-start.10
  166.2 32.6 %collective-permute-start.14 = (f32[2,256,128]{2,1,0:T(8,128)}, f32[2,256,128]{2,1,0:T(8,128)S(1)}, u32[]{:S(2)}, u32[]{:S(2)}) collective-permute-start(f32[2,256,128]{2,1,0:T(8,128)} %gate.7), channel_id=1, source_target_pairs={{0,2},{1,3},{2,4},{3,5},{4,6},{5,7},{6,0},{7,1},{8,10},{9,11},{10,... | collective-permute-start | bytes 786440 | tf_op jit(solution)/shard_map/ppermute | solution.py:723
  168.3 36.0 %collective-permute-start.15 = (f32[2,256,128]{2,1,0:T(8,128)}, f32[2,256,128]{2,1,0:T(8,128)S(1)}, u32[]{:S(2)}, u32[]{:S(2)}) collective-permute-start(f32[2,256,128]{2,1,0:T(8,128)} %gate.8), channel_id=1, source_target_pairs={{0,4},{1,5},{2,6},{3,7},{4,0},{5,1},{6,2},{7,3},{8,12},{9,13},{10,... | collective-permute-start | bytes 786440 | tf_op jit(solution)/shard_map/ppermute | solution.py:723
  168.3 38.1 %collective-permute-start.16 = (f32[2,256,128]{2,1,0:T(8,128)}, f32[2,256,128]{2,1,0:T(8,128)S(1)}, u32[]{:S(2)}, u32[]{:S(2)}) collective-permute-start(f32[2,256,128]{2,1,0:T(8,128)} %gate.9), channel_id=1, source_target_pairs={{0,6},{1,7},{2,0},{3,1},{4,2},{5,3},{6,4},{7,5},{8,14},{9,15},{10,... | collective-permute-start | bytes 786440 | tf_op jit(solution)/shard_map/ppermute | solution.py:723
  178.3 15.6 %copy-start.15 = (f32[2,752,128]{2,1,0:T(8,128)}, f32[2,752,128]{2,1,0:T(8,128)S(1)}, u32[]{:S(2)}) copy-start(f32[2,752,128]{2,1,0:T(8,128)S(1)} %collective-permute-done.18.refs_3_) | copy-start | bytes 2310148
  193.0 0.9 copy-start.16
  193.9 12.4 %copy-start.1 = (f32[8,128,128]{2,1,0:T(8,128)S(1)}, f32[8,128,128]{2,1,0:T(8,128)}, u32[]{:S(2)}) copy-start(f32[8,128,128]{2,1,0:T(8,128)} %copy-done) | copy-start | bytes 1572868
  193.9 12.4 %copy-start.2 = (bf16[8,256,256]{2,1,0:T(8,128)(2,1)S(1)}, bf16[8,256,256]{2,1,0:T(8,128)(2,1)}, u32[]{:S(2)}) copy-start(bf16[8,256,256]{2,1,0:T(8,128)(2,1)} %get-tuple-element.63.operand_ref) | copy-start | bytes 3145732
  193.9 12.4 %copy-start.6 = (f32[2,256,128]{2,1,0:T(8,128)S(1)}, f32[2,256,128]{2,1,0:T(8,128)}, u32[]{:S(2)}) copy-start(f32[2,256,128]{2,1,0:T(8,128)} %get-tuple-element.66.refs_0_) | copy-start | bytes 786436

commit v9 on v8

--- a/solution.py
+++ b/solution.py
@@ -81,6 +81,7 @@
         self.height = self.nodes * self.rows
         self.pad = up(self.nodes, LANES)
         self.spill = up((self.pad - self.nodes) * self.rows, TILE)
+        self.tail = up((self.pad - self.nodes) * segments * self.rows, TILE)
         self.flops = 2 * 4 * self.pad * self.pad * self.cols
 
     def window(self, low, high):
@@ -118,23 +119,25 @@
 
 
 def read_matrix(z, ref, k):
-    return z.square(ref[:, k, :])
+    x = z.rows_masked(ref[:, k, :])
+    return jnp.concatenate([x, jnp.zeros((z.pad, z.pad - z.nodes), F32)], axis=1)
 
 
 def send_pair(z, mine, e, stage, keep_ref, give_ref, sem):
     pairs = z.segments // 2
     place = lax.rem(e // 2 - mine // 2 + pairs, pairs)
     own = lax.rem(mine, 2) == e % 2
+    source = stage.at[e, pl.ds(0, keep_ref.shape[1])]
 
     @pl.when(own)
     def _():
-        pltpu.make_async_copy(stage.at[e], keep_ref.at[place], sem.at[e]).start()
+        pltpu.make_async_copy(source, keep_ref.at[place], sem.at[e]).start()
 
     @pl.when(jnp.logical_not(own))
     def _():
-        pltpu.make_async_copy(stage.at[e], give_ref.at[place], sem.at[e]).start()
-
-    return pltpu.make_async_copy(stage.at[e], keep_ref.at[place], sem.at[e])
+        pltpu.make_async_copy(source, give_ref.at[place], sem.at[e]).start()
+
+    return pltpu.make_async_copy(source, keep_ref.at[place], sem.at[e])
 
 
 def load_pairs(z, mine, sources, buf, sem):
@@ -145,7 +148,8 @@
         pair = lax.rem(mine // 2 - d + pairs, pairs) * 2
         for n in range(2):
             e = pair + (side if n == 0 else 1 - side)
-            copies.append(pltpu.make_async_copy(sources[d].at[n], buf.at[e], sem.at[2 * d + n]))
+            target = buf.at[e, pl.ds(0, sources[d].shape[1])]
+            copies.append(pltpu.make_async_copy(sources[d].at[n], target, sem.at[2 * d + n]))
     return copies
 
 
@@ -266,13 +270,15 @@
                     for source, target, needed in ((inverse_ref, inverse_buf, steps), (gain_ref, gain_buf, gains)):
                         if needed:
                             part = pl.ds(s * z.steps + needed[0], len(needed))
-                            moves.append((source.at[:, part], target.at[:, part]))
+                            moves.append((source.at[:, part], target.at[pl.ds(0, z.nodes), part]))
                 for n, (source, target) in enumerate(moves):
                     copies[s].append(pltpu.make_async_copy(source, target, sem.at[s, n]))
             if not narrow:
                 part = pl.ds(s0 * z.steps, (s1 - s0) * z.steps)
                 for n, (source, target) in enumerate(((inverse_ref, inverse_buf), (gain_ref, gain_buf))):
-                    copy = pltpu.make_async_copy(source.at[:, part], target.at[:, part], matrix_sem.at[s0, n])
+                    copy = pltpu.make_async_copy(
+                        source.at[:, part], target.at[pl.ds(0, z.nodes), part], matrix_sem.at[s0, n]
+                    )
                     copies[s0].append(copy)
             for s in range(s0, s1):
                 for copy in copies[s]:
@@ -335,7 +341,9 @@
                 if opened:
                     end_ref[s] = value
                 if not parts:
-                    copy = pltpu.make_async_copy(stages[0].at[s], out_refs[0].at[s], out_sem.at[0, s])
+                    copy = pltpu.make_async_copy(
+                        stages[0].at[s, pl.ds(0, messages[0])], out_refs[0].at[s], out_sem.at[0, s]
+                    )
                     copy.start()
                     sends.append(copy)
             for p, stage in enumerate(stages if parts else []):
@@ -358,15 +366,15 @@
     scratch = [
         pltpu.VMEM((z.segments, size + z.spill, z.ax), F32),
         pltpu.VMEM((z.segments, size + z.spill, z.ax), F32),
-        pltpu.VMEM(inverse.shape, F32),
-        pltpu.VMEM(gain.shape, F32),
+        pltpu.VMEM((z.pad,) + inverse.shape[1:], F32),
+        pltpu.VMEM((z.pad,) + gain.shape[1:], F32),
         pltpu.VMEM(viscous.shape, F32),
         pltpu.VMEM((len(steps), z.segments, z.cols), F32),
         pltpu.SemaphoreType.DMA((z.segments, 7)),
         pltpu.SemaphoreType.DMA((z.segments, 2)),
         pltpu.SemaphoreType.DMA((len(messages), z.segments)),
     ]
-    scratch += [pltpu.VMEM((z.segments, message, z.ax), F32) for message in messages]
+    scratch += [pltpu.VMEM((z.segments, message + z.spill, z.ax), F32) for message in messages]
     if opened:
         scratch += [pltpu.VMEM((z.segments, size0 + z.spill, z.ax), F32)] * 2
     if has_carry:
@@ -387,7 +395,7 @@
 def maps_call(z, me, gain, after):
     def kernel(me_ref, gain_ref, *refs):
         own_ref, head_ref, tail_ref, whole_ref, prefix_ref, group_ref, gain_buf, kept, sem = refs[len(after) :]
-        copy = pltpu.make_async_copy(gain_ref, gain_buf, sem)
+        copy = pltpu.make_async_copy(gain_ref, gain_buf.at[pl.ds(0, z.nodes)], sem)
         copy.start()
         copy.wait()
 
@@ -425,7 +433,7 @@
         [spec_smem(), spec_hbm()] + [spec_any()] * len(after),
         [spec_vmem()] * 6,
         [
-            pltpu.VMEM(gain.shape, F32),
+            pltpu.VMEM((z.pad,) + gain.shape[1:], F32),
             pltpu.VMEM((z.segments, z.steps) + square, F32),
             pltpu.SemaphoreType.DMA,
         ],
@@ -496,7 +504,7 @@
         [f32(pairs, rows, z.ax)] * 2,
         [spec_smem()] + [spec_vmem()] * (z.groups + 4),
         [spec_hbm()] * 2,
-        [pltpu.VMEM((z.segments, rows, z.ax), F32), pltpu.SemaphoreType.DMA((z.segments,))],
+        [pltpu.VMEM((z.segments, rows + z.spill, z.ax), F32), pltpu.SemaphoreType.DMA((z.segments,))],
         z.flops * (z.segments * 2 + 2 * z.groups),
         4 * z.segments * z.pad * z.cols * 4,
     )(places, *packs, before, prefix, heads, starts)
@@ -566,7 +574,10 @@
         first_refs, refs = refs[:pairs], refs[pairs:]
         out_ref, operand_ref, own_buf, one_buf, first_buf, stage, one_sem, first_sem, own_sem, out_sem = refs
         first_copies = load_pairs(z, me_ref[0], first_refs, first_buf, first_sem)
-        one_copies = [pltpu.make_async_copy(one_ref.at[e], one_buf.at[e], one_sem.at[e]) for e in range(z.segments)]
+        one_copies = [
+            pltpu.make_async_copy(one_ref.at[e], one_buf.at[e, pl.ds(0, one_ref.shape[1])], one_sem.at[e])
+            for e in range(z.segments)
+        ]
         own_copy = pltpu.make_async_copy(own_ref, own_buf, own_sem)
         for copy in first_copies + [own_copy] + one_copies:
             copy.start()
@@ -580,7 +591,7 @@
                 stage[i, rows, :] = value[: z.nodes, j * z.ax : (j + 1) * z.ax]
 
         def send(i):
-            copy = pltpu.make_async_copy(stage.at[i], out_ref.at[i], out_sem.at[i])
+            copy = pltpu.make_async_copy(stage.at[i, pl.ds(0, tall)], out_ref.at[i], out_sem.at[i])
             copy.start()
             sends.append(copy)
 
@@ -610,9 +621,9 @@
         [spec_hbm(), spec_vmem()],
         [
             pltpu.VMEM((z.steps, z.pad, z.pad), F32),
-            pltpu.VMEM(received_one.shape, F32),
-            pltpu.VMEM((z.segments, message, z.ax), F32),
-            pltpu.VMEM((high, tall, z.ax), F32),
+            pltpu.VMEM((z.segments, received_one.shape[1] + z.spill, z.ax), F32),
+            pltpu.VMEM((z.segments, message + z.spill, z.ax), F32),
+            pltpu.VMEM((high, tall + z.tail, z.ax), F32),
             pltpu.SemaphoreType.DMA((z.segments,)),
             pltpu.SemaphoreType.DMA((z.segments,)),
             pltpu.SemaphoreType.DMA,
@@ -652,7 +663,7 @@
                 for j in range(z.rows):
                     rows = pl.ds(e * z.rows + j, z.nodes, stride=radial)
                     stage[n, rows, :] = value[:, j * z.ax : (j + 1) * z.ax]
-            copy = pltpu.make_async_copy(stage.at[n], out_ref.at[low + n], out_sem.at[n])
+            copy = pltpu.make_async_copy(stage.at[n, pl.ds(0, tall)], out_ref.at[low + n], out_sem.at[n])
             copy.start()
             sends.append(copy)
         for copy in sends:
@@ -666,10 +677,10 @@
         [spec_smem()] + [spec_hbm()] * (len(inputs) - 1),
         spec_hbm(),
         [
-            pltpu.VMEM((z.segments, message, z.ax), F32),
+            pltpu.VMEM((z.segments, message + z.spill, z.ax), F32),
             pltpu.VMEM((count, z.pad, z.pad), F32),
             pltpu.VMEM(operands.shape, BF16),
-            pltpu.VMEM((count, tall, z.ax), F32),
+            pltpu.VMEM((count, tall + z.tail, z.ax), F32),
             pltpu.SemaphoreType.DMA((z.segments,)),
             pltpu.SemaphoreType.DMA((2,)),
             pltpu.SemaphoreType.DMA((count,)),
@@ -699,7 +710,7 @@
                 for j in range(z.rows):
                     rows = pl.ds(e * z.rows + j, z.nodes, stride=radial)
                     stage[rows, :] = value[:, j * z.ax : (j + 1) * z.ax]
-        copy = pltpu.make_async_copy(stage, out_ref.at[step], out_sem)
+        copy = pltpu.make_async_copy(stage.at[pl.ds(0, tall)], out_ref.at[step], out_sem)
         copy.start()
         copy.wait()
 
@@ -710,7 +721,7 @@
         f32(z.steps, tall, z.ax),
         [spec_smem()] + [spec_vmem()] * (2 + pairs) + [spec_hbm()],
         spec_hbm(),
-        [pltpu.VMEM((tall, z.ax), F32), pltpu.SemaphoreType.DMA],
+        [pltpu.VMEM((tall + z.tail, z.ax), F32), pltpu.SemaphoreType.DMA],
         z.flops * z.segments,
         4 * 2 * tall * z.ax,
         {len(inputs) - 1: 0},

time: 209 us -> 209 us (level)
  no operation moved by 1% of the time
where the time goes in v9:
time: 209 us; the launch traced here: 208 us
  waiting for transfers between devices  102 us (49%)
  Pallas kernels  66.4 us (32%)
  starting transfers between devices  27.6 us (13%)
  local copies, waits for them, and re-layouts  11.5 us (6%)
    ppermute x14, waiting for transfers between devices, shift_by(): lax.ppermute(array, axis, [(i, (i + by) % size) for i in range(size)])  95.3 us
    pallas_call x2, Pallas kernels, sweep_call(): call(kernel, f'sweep_{low}', outs + more, in_specs + extra_specs + [spec_...  23.5 us
    ppermute x14, starting transfers between devices, shift_by(): lax.ppermute(array, axis, [(i, (i + by) % size) for i in range(size)])  14.7 us
    unnamed x44, local copies, waits for them, and re-layouts  11.5 us
    pallas_call x1, Pallas kernels, maps_call(): call(kernel, 'maps', outs, [spec_smem(), spec_hbm()] + [spec_any()] * len...  8.42 us
    pallas_call x3, Pallas kernels, couple_call(): call(kernel, 'couple', [f32(2, message, z.ax)] * pairs, [spec_hbm()] * 2,...  7 us
    pallas_call x1, Pallas kernels, open_call(): call(kernel, 'finish_0', [f32(z.steps, tall, z.ax), jax.ShapeDtypeStruct(...  6.21 us
    pallas_call x1, Pallas kernels, first_call(): call(kernel, 'first', [f32(pairs, rows, z.ax)] * 2, [spec_smem()] + [spec...  5.33 us
  transfers between devices with their start and end apart: 20, of which 13 were waited for; matrix products, arithmetic and copies ran while one was open for 0% of the time, Pallas kernels for 25%

profile of v9, /device:TPU:9, one launch (start us, length us, event | category | flops | bytes accessed | tf_op | source)
XLA Modules:
  0.0 208.3 jit_solution(1170413042026074201)
XLA Ops:
  0.0 0.8 copy-done.9
  0.8 4.9 %sensor.1 = (f32[8,8,256]{2,1,0:T(8,128)S(1)}, f32[8,8,128]{2,1,0:T(8,128)S(1)}, f32[8,8,128]{2,1,0:T(8,128)S(1)}) custom-call(f32[8,2000,128]{2,1,0:T(8,128)} %bitcast.7, f32[125,125]{1,0:T(8,128)S(1)} %copy-done.9), custom_call_target="tpu_custom_call" | custom-call | flops 2147483648 | bytes 8192000 | tf_op jit(solution)/shard_map/sensor/pallas_call | solution.py:185
  5.7 3.8 %collective-permute-start = (f32[8,8,128]{2,1,0:T(8,128)S(1)}, f32[8,8,128]{2,1,0:T(8,128)S(1)}, u32[]{:S(2)}, u32[]{:S(2)}) collective-permute-start(f32[8,8,128]{2,1,0:T(8,128)S(1)} %get-tuple-element.42), channel_id=1, source_target_pairs={{0,1},{1,2},{2,3},{3,4},{4,5},{5,6},{6,7},{8,9},{9,10},{10,11},{11... | collective-permute-start | bytes 98312 | tf_op jit(solution)/shard_map/ppermute | solution.py:739
  9.5 1.9 collective-permute-start.1
  11.4 3.3 %collective-permute-done.1.refs_8_ = f32[8,8,128]{2,1,0:T(8,128)S(1)} collective-permute-done((f32[8,8,128]{2,1,0:T(8,128)S(1)}, f32[8,8,128]{2,1,0:T(8,128)S(1)}, u32[]{:S(2)}, u32[]{:S(2)}) %collective-permute-start.1) | collective-permute-done | bytes 32800 | tf_op jit(solution)/shard_map/ppermute | solution.py:740
  14.7 7.6 %sweep_1.1 = (f32[8,752,128]{2,1,0:T(8,128)}, f32[1,256]{1,0:T(1,128)S(1)}, f32[1,256]{1,0:T(1,128)S(1)}) custom-call(s32[1]{0:T(128)} %bitcast.refs_0_.me_ref, f32[8,2000,128]{2,1,0:T(8,128)} %bitcast.8, f32[8,2000,128]{2,1,0:T(8,128)} %bitcast.13, f32[125,125]{1,0:T(8,128)S(1)} %copy-done.7, f32[125,64,125]{2,1,0:T(8,128)} %bitcast.15, ...), custom_call_target="tpu_custom_call" | custom-call | flops 2415919104 | bytes 12320768 | tf_op jit(solution)/shard_map/sweep_1/pallas_call | solution.py:382
  22.4 4.4 %all-to-all-start = ((f32[8,752,128]{2,1,0:T(8,128)}), f32[8,752,128]{2,1,0:T(8,128)}, u32[]{:S(2)}, u32[]{:S(2)}) async-start(f32[8,752,128]{2,1,0:T(8,128)} %get-tuple-element.44.refs_0_.refs_11_), calls=%async_computation | async-start | bytes 6160384 | tf_op jit(solution)/shard_map/all_to_all | solution.py:745
  26.8 1.3 collective-permute-start.2
  28.1 1.2 collective-permute-start.3
  29.3 8.4 %maps.1 = (f32[8,128,128]{2,1,0:T(8,128)S(1)}, f32[8,128,128]{2,1,0:T(8,128)S(1)}, f32[8,128,128]{2,1,0:T(8,128)S(1)}, f32[8,128,128]{2,1,0:T(8,128)}, f32[8,128,128]{2,1,0:T(8,128)}, /*index=5*/f32[128,128]{1,0:T(8,128)S(1)}) custom-call(s32[1]{0:T(128)} %bitcast.refs_0_.me_ref, f32[125,64,125]{2,1,0:T(8,128)} %bitcast.11, ...), custom_call_target="tpu_custom_call" | custom-call | flops 1207959552 | bytes 4194304 | tf_op jit(solution)/shard_map/maps/pallas_call | solution.py:429
  37.7 0.8 copy-done
  38.5 0.8 copy-done.3
  39.3 0.8 copy-done.4
  40.1 0.0 collective-permute-done.2.refs_9_
  40.1 0.0 collective-permute-done.3.refs_10_
  40.1 15.9 %sweep_4.1 = (f32[4,752,128]{2,1,0:T(8,128)}, f32[4,752,128]{2,1,0:T(8,128)}, f32[4,256,128]{2,1,0:T(8,128)S(1)}, f32[4,256,128]{2,1,0:T(8,128)S(1)}, f32[8,128,256]{2,1,0:T(8,128)}, /*index=5*/f32[8,128,256]{2,1,0:T(8,128)}) custom-call(s32[1]{0:T(128)} %bitcast.refs_0_.me_ref, f32[8,2000,128]{2,1,0:T(8,128)} %bitcast.9, f32[8,2000,128]{2,1,0:T(8,128)} %bitcast.14, ...), custom_call_target="tpu_custom_call" | custom-call | flops 4026531840 | bytes 16384000 | tf_op jit(solution)/shard_map/sweep_4/pallas_call | solution.py:382
  56.1 0.8 copy-done.5
  56.9 0.5 collective-permute-start.12
  57.4 4.5 %chain.1 = (f32[8,128,256]{2,1,0:T(8,128)}, f32[128,384]{1,0:T(8,128)}) custom-call(f32[8,128,256]{2,1,0:T(8,128)} %get-tuple-element.49.start_ref.refs_8_, f32[8,128,256]{2,1,0:T(8,128)} %get-tuple-element.50.end_ref, f32[8,128,128]{2,1,0:T(8,128)} %copy-done.4, f32[8,128,128]{2,1,0:T(8,128)} %get-tuple-element.52.whole_ref, f32[128,128]{1,0:T(8,128)} %copy-done.8), custom_call_target="tpu_custom_call" | custom-call | flops 536870912 | bytes 4194304 | tf_op jit(solution)/shard_map/chain/pallas_call | solution.py:460
  61.8 1.3 collective-permute-start.6
  63.1 0.2 collective-permute-start.5
  63.3 1.2 collective-permute-start.4
  64.5 0.6 pad_add_fusion.refs_0_
  65.1 3.5 %collective-permute-done.6.refs_4_ = f32[128,384]{1,0:T(8,128)S(1)} collective-permute-done((f32[128,384]{1,0:T(8,128)}, f32[128,384]{1,0:T(8,128)S(1)}, u32[]{:S(2)}, u32[]{:S(2)}) %collective-permute-start.6) | collective-permute-done | bytes 196640 | tf_op jit(solution)/shard_map/ppermute | solution.py:734
  68.6 1.0 collective-permute-done.5.refs_3_
  69.6 4.3 %collective-permute-done.4.refs_2_ = f32[128,384]{1,0:T(8,128)S(1)} collective-permute-done((f32[128,384]{1,0:T(8,128)}, f32[128,384]{1,0:T(8,128)S(1)}, u32[]{:S(2)}, u32[]{:S(2)}) %collective-permute-start.4) | collective-permute-done | bytes 196640 | tf_op jit(solution)/shard_map/ppermute | solution.py:734
  73.9 0.7 copy-done.21
  74.5 5.3 %first.1 = (f32[4,256,128]{2,1,0:T(8,128)}, f32[4,256,128]{2,1,0:T(8,128)}) custom-call(s32[2]{0:T(128)} %pad_add_fusion.refs_0_, f32[128,384]{1,0:T(8,128)} %get-tuple-element.53.refs_1_, f32[128,384]{1,0:T(8,128)} %copy-done.21, f32[128,384]{1,0:T(8,128)} %copy-done.20, f32[128,384]{1,0:T(8,128)} %copy-done.19, f32[8,128,256]{2,1,0:T(8,128)} %get-tuple-element.54.refs_5_, ...), custom_call_target="tpu_custom_call" | custom-call | flops 805306368 | bytes 4194304 | tf_op jit(solution)/shard_map/first/pallas_call | solution.py:501
  79.9 1.1 collective-permute-start.7
  81.0 1.7 collective-permute-done.7.refs_1_
  82.7 0.8 copy-done.17
  83.5 2.1 couple.3
  85.6 1.3 collective-permute-start.8
  86.9 0.2 collective-permute-start.10
  87.1 2.1 collective-permute-start.9
  89.2 0.0 collective-permute-done.12.refs_1_
  89.2 1.2 copy-done.11
  90.4 2.9 %couple.5 = (f32[2,752,128]{2,1,0:T(8,128)}, f32[2,752,128]{2,1,0:T(8,128)}, f32[2,752,128]{2,1,0:T(8,128)}, f32[2,752,128]{2,1,0:T(8,128)}) custom-call(f32[4,752,128]{2,1,0:T(8,128)} %get-tuple-element.68.refs_0_, f32[4,752,128]{2,1,0:T(8,128)} %copy-done.11), custom_call_target="tpu_custom_call" | custom-call | bytes 6160384 | tf_op jit(solution)/shard_map/couple/pallas_call | solution.py:536
  93.3 16.9 %collective-permute-done.8.refs_1_ = f32[2,256,128]{2,1,0:T(8,128)S(1)} collective-permute-done((f32[2,256,128]{2,1,0:T(8,128)}, f32[2,256,128]{2,1,0:T(8,128)S(1)}, u32[]{:S(2)}, u32[]{:S(2)}) %collective-permute-start.8) | collective-permute-done | bytes 262176 | tf_op jit(solution)/shard_map/ppermute | solution.py:734
  110.2 0.7 copy-done.12
  110.9 2.1 %collective-permute-start.13 = (f32[2,752,128]{2,1,0:T(8,128)}, f32[2,752,128]{2,1,0:T(8,128)S(1)}, u32[]{:S(2)}, u32[]{:S(2)}) collective-permute-start(f32[2,752,128]{2,1,0:T(8,128)} %gate.6), channel_id=1, source_target_pairs={{0,2},{1,3},{2,4},{3,5},{4,6},{5,7},{6,0},{7,1},{8,10},{9,11},{10,... | collective-permute-start | bytes 2310152 | tf_op jit(solution)/shard_map/ppermute | solution.py:734
  113.0 15.8 %collective-permute-done.10.refs_3_.refs_1_ = f32[2,256,128]{2,1,0:T(8,128)S(1)} collective-permute-done((f32[2,256,128]{2,1,0:T(8,128)}, f32[2,256,128]{2,1,0:T(8,128)S(1)}, u32[]{:S(2)}, u32[]{:S(2)}) %collective-permute-start.10) | collective-permute-done | bytes 262176 | tf_op jit(solution)/shard_map/ppermute | solution.py:734
  128.8 0.7 copy-done.13
  129.5 0.0 collective-permute-start.18
  129.5 0.0 collective-permute-done.9.refs_2_.refs_1_
  129.5 0.7 copy-done.14
  130.2 0.5 collective-permute-start.17
  130.7 1.2 collective-permute-start.11
  132.0 1.5 collective-permute-done.11.refs_1_
  133.5 0.8 copy-done.18
  134.3 2.1 couple.4
  136.4 28.9 %collective-permute-done.13.refs_1_ = f32[2,752,128]{2,1,0:T(8,128)S(1)} collective-permute-done((f32[2,752,128]{2,1,0:T(8,128)}, f32[2,752,128]{2,1,0:T(8,128)S(1)}, u32[]{:S(2)}, u32[]{:S(2)}) %collective-permute-start.13) | collective-permute-done | bytes 770080 | tf_op jit(solution)/shard_map/ppermute | solution.py:734
  165.3 0.9 copy-done.10
  166.2 2.1 %collective-permute-start.14 = (f32[2,256,128]{2,1,0:T(8,128)}, f32[2,256,128]{2,1,0:T(8,128)S(1)}, u32[]{:S(2)}, u32[]{:S(2)}) collective-permute-start(f32[2,256,128]{2,1,0:T(8,128)} %gate.7), channel_id=1, source_target_pairs={{0,2},{1,3},{2,4},{3,5},{4,6},{5,7},{6,0},{7,1},{8,10},{9,11},{10,... | collective-permute-start | bytes 786440 | tf_op jit(solution)/shard_map/ppermute | solution.py:734
  168.3 0.0 collective-permute-start.15
  168.3 1.2 collective-permute-start.16
  169.5 6.2 %finish_0.1 = (f32[8,2000,128]{2,1,0:T(8,128)}, bf16[8,256,256]{2,1,0:T(8,128)(2,1)}) custom-call(s32[1]{0:T(128)} %bitcast.refs_0_.me_ref, f32[8,128,128]{2,1,0:T(8,128)} %copy-done, f32[8,752,128]{2,1,0:T(8,128)} %all-to-all-done.one_ref, f32[2,256,128]{2,1,0:T(8,128)} %get-tuple-element.59.refs_0_, f32[2,256,128]{2,1,0:T(8,128)} %copy-done.12, ...), custom_call_target="tpu_custom_call" | custom-call | flops 805306368 | bytes 8192000 | tf_op jit(solution)/shard_map/finish_0/pallas_call | solution.py:616
  175.7 2.7 %collective-permute-done.18.refs_3_ = f32[2,752,128]{2,1,0:T(8,128)S(1)} collective-permute-done((f32[2,752,128]{2,1,0:T(8,128)}, f32[2,752,128]{2,1,0:T(8,128)S(1)}, u32[]{:S(2)}, u32[]{:S(2)}) %collective-permute-start.18) | collective-permute-done | bytes 770080 | tf_op jit(solution)/shard_map/ppermute | solution.py:734
  178.4 14.7 %collective-permute-done.17.refs_2_ = f32[2,752,128]{2,1,0:T(8,128)S(1)} collective-permute-done((f32[2,752,128]{2,1,0:T(8,128)}, f32[2,752,128]{2,1,0:T(8,128)S(1)}, u32[]{:S(2)}, u32[]{:S(2)}) %collective-permute-start.17) | collective-permute-done | bytes 770080 | tf_op jit(solution)/shard_map/ppermute | solution.py:734
  193.1 0.9 copy-done.16
  194.0 4.8 %finish_4.1.refs_4_ = f32[8,2000,128]{2,1,0:T(8,128)} custom-call(s32[1]{0:T(128)} %bitcast.refs_0_.me_ref, f32[8,128,128]{2,1,0:T(8,128)} %copy-done, bf16[8,256,256]{2,1,0:T(8,128)(2,1)} %get-tuple-element.63.operand_ref, f32[2,752,128]{2,1,0:T(8,128)} %get-tuple-element.73.refs_0_, f32[2,752,128]{2,1,0:T(8,128)} %copy-done.10, ...), custom_call_target="tpu_custom_call", output_to_operand_aliasing={{}: (7, {})} | custom-call | flops 805306368 | bytes 6144000 | tf_op jit(solution)/shard_map/finish_4/pallas_call | solution.py:673
  198.9 5.5 %collective-permute-done.15.refs_2_ = f32[2,256,128]{2,1,0:T(8,128)S(1)} collective-permute-done((f32[2,256,128]{2,1,0:T(8,128)}, f32[2,256,128]{2,1,0:T(8,128)S(1)}, u32[]{:S(2)}, u32[]{:S(2)}) %collective-permute-start.15) | collective-permute-done | bytes 262176 | tf_op jit(solution)/shard_map/ppermute | solution.py:734
  204.3 2.1 collective-permute-done.16.refs_3_
  206.4 1.7 finish_7.1
  (39 shorter events, 0.1 us)
Async XLA Ops:
  0.0 0.8 copy-start.9
  0.8 13.9 %copy-start.7 = (f32[125,125]{1,0:T(8,128)S(1)}, f32[125,125]{1,0:T(8,128)}, u32[]{:S(2)}) copy-start(f32[125,125]{1,0:T(8,128)} %refs_3_.3) | copy-start | bytes 187504
  5.7 5.7 %collective-permute-start = (f32[8,8,128]{2,1,0:T(8,128)S(1)}, f32[8,8,128]{2,1,0:T(8,128)S(1)}, u32[]{:S(2)}, u32[]{:S(2)}) collective-permute-start(f32[8,8,128]{2,1,0:T(8,128)S(1)} %get-tuple-element.42), channel_id=1, source_target_pairs={{0,1},{1,2},{2,3},{3,4},{4,5},{5,6},{6,7},{8,9},{9,10},{10,11},{11... | collective-permute-start | bytes 98312 | tf_op jit(solution)/shard_map/ppermute | solution.py:739
  9.5 5.2 %collective-permute-start.1 = (f32[8,8,128]{2,1,0:T(8,128)S(1)}, f32[8,8,128]{2,1,0:T(8,128)S(1)}, u32[]{:S(2)}, u32[]{:S(2)}) collective-permute-start(f32[8,8,128]{2,1,0:T(8,128)S(1)} %get-tuple-element.43), channel_id=1, source_target_pairs={{1,0},{2,1},{3,2},{4,3},{5,4},{6,5},{7,6},{9,8},{10,9},{11,10},{12... | collective-permute-start | bytes 98312 | tf_op jit(solution)/shard_map/ppermute | solution.py:740
  22.4 147.1 %all-to-all-start = ((f32[8,752,128]{2,1,0:T(8,128)}), f32[8,752,128]{2,1,0:T(8,128)}, u32[]{:S(2)}, u32[]{:S(2)}) async-start(f32[8,752,128]{2,1,0:T(8,128)} %get-tuple-element.44.refs_0_.refs_11_), calls=%async_computation | async-start | bytes 6160384 | tf_op jit(solution)/shard_map/all_to_all | solution.py:745
  26.8 13.3 %collective-permute-start.2 = (f32[1,256]{1,0:T(1,128)S(1)}, f32[1,256]{1,0:T(1,128)S(1)}, u32[]{:S(2)}, u32[]{:S(2)}) collective-permute-start(f32[1,256]{1,0:T(1,128)S(1)} %get-tuple-element.46), channel_id=1, source_target_pairs={{0,8},{8,16},{16,24},{24,0},{1,9},{9,17},{17,25},{25,1},{2,10},{10... | collective-permute-start | bytes 3080 | tf_op jit(solution)/shard_map/ppermute | solution.py:734
  28.1 12.1 %collective-permute-start.3 = (f32[1,256]{1,0:T(1,128)S(1)}, f32[1,256]{1,0:T(1,128)S(1)}, u32[]{:S(2)}, u32[]{:S(2)}) collective-permute-start(f32[1,256]{1,0:T(1,128)S(1)} %get-tuple-element.47), channel_id=1, source_target_pairs={{0,24},{8,0},{16,8},{24,16},{1,25},{9,1},{17,9},{25,17},{2,26},{10... | collective-permute-start | bytes 3080 | tf_op jit(solution)/shard_map/ppermute | solution.py:734
  37.7 0.8 copy-start
  38.5 0.8 copy-start.3
  39.3 0.8 copy-start.4
  40.1 15.9 %copy-start.8 = (f32[128,128]{1,0:T(8,128)}, f32[128,128]{1,0:T(8,128)S(1)}, u32[]{:S(2)}) copy-start(f32[128,128]{1,0:T(8,128)S(1)} %get-tuple-element.48.refs_12_.group_ref) | copy-start | bytes 196612
  56.1 0.8 copy-start.5
  56.9 32.3 %collective-permute-start.12 = (f32[4,752,128]{2,1,0:T(8,128)}, f32[4,752,128]{2,1,0:T(8,128)S(1)}, u32[]{:S(2)}, u32[]{:S(2)}) collective-permute-start(f32[4,752,128]{2,1,0:T(8,128)} %get-tuple-element.69), channel_id=1, source_target_pairs={{0,1},{1,0},{2,3},{3,2},{4,5},{5,4},{6,7},{7,6},{8,9},{9,8},{10,11... | collective-permute-start | bytes 4620296 | tf_op jit(solution)/shard_map/ppermute | solution.py:749
  61.8 6.8 %collective-permute-start.6 = (f32[128,384]{1,0:T(8,128)}, f32[128,384]{1,0:T(8,128)S(1)}, u32[]{:S(2)}, u32[]{:S(2)}) collective-permute-start(f32[128,384]{1,0:T(8,128)} %get-tuple-element.53.refs_1_), channel_id=1, source_target_pairs={{0,24},{8,0},{16,8},{24,16},{1,25},{9,1},{17,9},{25,17},{2,26},{10... | collective-permute-start | bytes 589832 | tf_op jit(solution)/shard_map/ppermute | solution.py:734
  63.1 6.5 %collective-permute-start.5 = (f32[128,384]{1,0:T(8,128)}, f32[128,384]{1,0:T(8,128)S(1)}, u32[]{:S(2)}, u32[]{:S(2)}) collective-permute-start(f32[128,384]{1,0:T(8,128)} %get-tuple-element.53.refs_1_), channel_id=1, source_target_pairs={{0,16},{8,24},{16,0},{24,8},{1,17},{9,25},{17,1},{25,9},{2,18},{10... | collective-permute-start | bytes 589832 | tf_op jit(solution)/shard_map/ppermute | solution.py:734
  63.3 10.6 %collective-permute-start.4 = (f32[128,384]{1,0:T(8,128)}, f32[128,384]{1,0:T(8,128)S(1)}, u32[]{:S(2)}, u32[]{:S(2)}) collective-permute-start(f32[128,384]{1,0:T(8,128)} %get-tuple-element.53.refs_1_), channel_id=1, source_target_pairs={{0,8},{8,16},{16,24},{24,0},{1,9},{9,17},{17,25},{25,1},{2,10},{10... | collective-permute-start | bytes 589832 | tf_op jit(solution)/shard_map/ppermute | solution.py:734
  68.6 5.2 %copy-start.19 = (f32[128,384]{1,0:T(8,128)}, f32[128,384]{1,0:T(8,128)S(1)}, u32[]{:S(2)}) copy-start(f32[128,384]{1,0:T(8,128)S(1)} %collective-permute-done.6.refs_4_) | copy-start | bytes 589828
  69.6 4.3 %copy-start.20 = (f32[128,384]{1,0:T(8,128)}, f32[128,384]{1,0:T(8,128)S(1)}, u32[]{:S(2)}) copy-start(f32[128,384]{1,0:T(8,128)S(1)} %collective-permute-done.5.refs_3_) | copy-start | bytes 589828
  73.9 0.7 copy-start.21
  79.9 2.8 %collective-permute-start.7 = (f32[4,256,128]{2,1,0:T(8,128)}, f32[4,256,128]{2,1,0:T(8,128)S(1)}, u32[]{:S(2)}, u32[]{:S(2)}) collective-permute-start(f32[4,256,128]{2,1,0:T(8,128)} %get-tuple-element.58), channel_id=1, source_target_pairs={{0,1},{1,0},{2,3},{3,2},{4,5},{5,4},{6,7},{7,6},{8,9},{9,8},{10,11... | collective-permute-start | bytes 1572872 | tf_op jit(solution)/shard_map/ppermute | solution.py:749
  82.7 0.8 copy-start.17
  85.6 24.6 %collective-permute-start.8 = (f32[2,256,128]{2,1,0:T(8,128)}, f32[2,256,128]{2,1,0:T(8,128)S(1)}, u32[]{:S(2)}, u32[]{:S(2)}) collective-permute-start(f32[2,256,128]{2,1,0:T(8,128)} %get-tuple-element.60), channel_id=1, source_target_pairs={{0,2},{1,3},{2,4},{3,5},{4,6},{5,7},{6,0},{7,1},{8,10},{9,11},{10,... | collective-permute-start | bytes 786440 | tf_op jit(solution)/shard_map/ppermute | solution.py:734
  86.9 41.9 %collective-permute-start.10 = (f32[2,256,128]{2,1,0:T(8,128)}, f32[2,256,128]{2,1,0:T(8,128)S(1)}, u32[]{:S(2)}, u32[]{:S(2)}) collective-permute-start(f32[2,256,128]{2,1,0:T(8,128)} %get-tuple-element.62), channel_id=1, source_target_pairs={{0,6},{1,7},{2,0},{3,1},{4,2},{5,3},{6,4},{7,5},{8,14},{9,15},{10,... | collective-permute-start | bytes 786440 | tf_op jit(solution)/shard_map/ppermute | solution.py:734
  87.1 42.4 %collective-permute-start.9 = (f32[2,256,128]{2,1,0:T(8,128)}, f32[2,256,128]{2,1,0:T(8,128)S(1)}, u32[]{:S(2)}, u32[]{:S(2)}) collective-permute-start(f32[2,256,128]{2,1,0:T(8,128)} %get-tuple-element.61), channel_id=1, source_target_pairs={{0,4},{1,5},{2,6},{3,7},{4,0},{5,1},{6,2},{7,3},{8,12},{9,13},{10,... | collective-permute-start | bytes 786440 | tf_op jit(solution)/shard_map/ppermute | solution.py:734
  89.2 1.2 copy-start.11
  110.1 0.7 copy-start.12
  110.9 54.5 %collective-permute-start.13 = (f32[2,752,128]{2,1,0:T(8,128)}, f32[2,752,128]{2,1,0:T(8,128)S(1)}, u32[]{:S(2)}, u32[]{:S(2)}) collective-permute-start(f32[2,752,128]{2,1,0:T(8,128)} %gate.6), channel_id=1, source_target_pairs={{0,2},{1,3},{2,4},{3,5},{4,6},{5,7},{6,0},{7,1},{8,10},{9,11},{10,... | collective-permute-start | bytes 2310152 | tf_op jit(solution)/shard_map/ppermute | solution.py:734
  128.8 0.7 copy-start.13
  129.5 48.9 %collective-permute-start.18 = (f32[2,752,128]{2,1,0:T(8,128)}, f32[2,752,128]{2,1,0:T(8,128)S(1)}, u32[]{:S(2)}, u32[]{:S(2)}) collective-permute-start(f32[2,752,128]{2,1,0:T(8,128)} %gate.11), channel_id=1, source_target_pairs={{0,6},{1,7},{2,0},{3,1},{4,2},{5,3},{6,4},{7,5},{8,14},{9,15},{10,... | collective-permute-start | bytes 2310152 | tf_op jit(solution)/shard_map/ppermute | solution.py:734
  129.5 0.7 copy-start.14
  130.2 62.9 %collective-permute-start.17 = (f32[2,752,128]{2,1,0:T(8,128)}, f32[2,752,128]{2,1,0:T(8,128)S(1)}, u32[]{:S(2)}, u32[]{:S(2)}) collective-permute-start(f32[2,752,128]{2,1,0:T(8,128)} %gate.10), channel_id=1, source_target_pairs={{0,4},{1,5},{2,6},{3,7},{4,0},{5,1},{6,2},{7,3},{8,12},{9,13},{10,... | collective-permute-start | bytes 2310152 | tf_op jit(solution)/shard_map/ppermute | solution.py:734
  130.7 2.8 %collective-permute-start.11 = (f32[4,256,128]{2,1,0:T(8,128)S(1)}, f32[4,256,128]{2,1,0:T(8,128)S(1)}, u32[]{:S(2)}, u32[]{:S(2)}) collective-permute-start(f32[4,256,128]{2,1,0:T(8,128)S(1)} %get-tuple-element.65), channel_id=1, source_target_pairs={{0,1},{1,0},{2,3},{3,2},{4,5},{5,4},{6,7},{7,6},{8,9},{9,8},{10,11... | collective-permute-start | bytes 1572872 | tf_op jit(solution)/shard_map/ppermute | solution.py:749
  133.5 0.8 copy-start.18
  165.3 0.9 copy-start.10
  166.2 32.6 %collective-permute-start.14 = (f32[2,256,128]{2,1,0:T(8,128)}, f32[2,256,128]{2,1,0:T(8,128)S(1)}, u32[]{:S(2)}, u32[]{:S(2)}) collective-permute-start(f32[2,256,128]{2,1,0:T(8,128)} %gate.7), channel_id=1, source_target_pairs={{0,2},{1,3},{2,4},{3,5},{4,6},{5,7},{6,0},{7,1},{8,10},{9,11},{10,... | collective-permute-start | bytes 786440 | tf_op jit(solution)/shard_map/ppermute | solution.py:734
  168.3 36.0 %collective-permute-start.15 = (f32[2,256,128]{2,1,0:T(8,128)}, f32[2,256,128]{2,1,0:T(8,128)S(1)}, u32[]{:S(2)}, u32[]{:S(2)}) collective-permute-start(f32[2,256,128]{2,1,0:T(8,128)} %gate.8), channel_id=1, source_target_pairs={{0,4},{1,5},{2,6},{3,7},{4,0},{5,1},{6,2},{7,3},{8,12},{9,13},{10,... | collective-permute-start | bytes 786440 | tf_op jit(solution)/shard_map/ppermute | solution.py:734
  168.3 38.1 %collective-permute-start.16 = (f32[2,256,128]{2,1,0:T(8,128)}, f32[2,256,128]{2,1,0:T(8,128)S(1)}, u32[]{:S(2)}, u32[]{:S(2)}) collective-permute-start(f32[2,256,128]{2,1,0:T(8,128)} %gate.9), channel_id=1, source_target_pairs={{0,6},{1,7},{2,0},{3,1},{4,2},{5,3},{6,4},{7,5},{8,14},{9,15},{10,... | collective-permute-start | bytes 786440 | tf_op jit(solution)/shard_map/ppermute | solution.py:734
  178.4 15.6 %copy-start.15 = (f32[2,752,128]{2,1,0:T(8,128)}, f32[2,752,128]{2,1,0:T(8,128)S(1)}, u32[]{:S(2)}) copy-start(f32[2,752,128]{2,1,0:T(8,128)S(1)} %collective-permute-done.18.refs_3_) | copy-start | bytes 2310148
  193.1 0.9 copy-start.16
  194.0 12.4 %copy-start.1 = (f32[8,128,128]{2,1,0:T(8,128)S(1)}, f32[8,128,128]{2,1,0:T(8,128)}, u32[]{:S(2)}) copy-start(f32[8,128,128]{2,1,0:T(8,128)} %copy-done) | copy-start | bytes 1572868
  194.0 12.4 %copy-start.2 = (bf16[8,256,256]{2,1,0:T(8,128)(2,1)S(1)}, bf16[8,256,256]{2,1,0:T(8,128)(2,1)}, u32[]{:S(2)}) copy-start(bf16[8,256,256]{2,1,0:T(8,128)(2,1)} %get-tuple-element.63.operand_ref) | copy-start | bytes 3145732
  194.0 12.4 %copy-start.6 = (f32[2,256,128]{2,1,0:T(8,128)S(1)}, f32[2,256,128]{2,1,0:T(8,128)}, u32[]{:S(2)}) copy-start(f32[2,256,128]{2,1,0:T(8,128)} %get-tuple-element.66.refs_0_) | copy-start | bytes 786436

commit v10 on v9

--- a/solution.py
+++ b/solution.py
@@ -196,7 +196,7 @@
         ],
         z.flops * z.steps * z.segments,
         4 * z.segments * tall * z.ax,
-        limit=52,
+        limit=53,
     )(state, to_modal)
 
 

time: 209 us -> 209 us (level)
  no operation moved by 1% of the time
where the time goes in v10:
time: 209 us; the launch traced here: 208 us
  waiting for transfers between devices  102 us (49%)
  Pallas kernels  66.4 us (32%)
  starting transfers between devices  27.6 us (13%)
  local copies, waits for them, and re-layouts  11.5 us (6%)
    ppermute x14, waiting for transfers between devices, shift_by(): lax.ppermute(array, axis, [(i, (i + by) % size) for i in range(size)])  95.3 us
    pallas_call x2, Pallas kernels, sweep_call(): call(kernel, f'sweep_{low}', outs + more, in_specs + extra_specs + [spec_...  23.5 us
    ppermute x14, starting transfers between devices, shift_by(): lax.ppermute(array, axis, [(i, (i + by) % size) for i in range(size)])  14.7 us
    unnamed x44, local copies, waits for them, and re-layouts  11.5 us
    pallas_call x1, Pallas kernels, maps_call(): call(kernel, 'maps', outs, [spec_smem(), spec_hbm()] + [spec_any()] * len...  8.42 us
    pallas_call x3, Pallas kernels, couple_call(): call(kernel, 'couple', [f32(2, message, z.ax)] * pairs, [spec_hbm()] * 2,...  7 us
    pallas_call x1, Pallas kernels, open_call(): call(kernel, 'finish_0', [f32(z.steps, tall, z.ax), jax.ShapeDtypeStruct(...  6.21 us
    pallas_call x1, Pallas kernels, first_call(): call(kernel, 'first', [f32(pairs, rows, z.ax)] * 2, [spec_smem()] + [spec...  5.33 us
  transfers between devices with their start and end apart: 20, of which 13 were waited for; matrix products, arithmetic and copies ran while one was open for 0% of the time, Pallas kernels for 25%

profile of v10, /device:TPU:9, one launch (start us, length us, event | category | flops | bytes accessed | tf_op | source)
XLA Modules:
  0.0 208.3 jit_solution(1170413042026074201)
XLA Ops:
  0.0 0.8 copy-done.9
  0.8 4.9 %sensor.1 = (f32[8,8,256]{2,1,0:T(8,128)S(1)}, f32[8,8,128]{2,1,0:T(8,128)S(1)}, f32[8,8,128]{2,1,0:T(8,128)S(1)}) custom-call(f32[8,2000,128]{2,1,0:T(8,128)} %bitcast.7, f32[125,125]{1,0:T(8,128)S(1)} %copy-done.9), custom_call_target="tpu_custom_call" | custom-call | flops 2147483648 | bytes 8192000 | tf_op jit(solution)/shard_map/sensor/pallas_call | solution.py:185
  5.7 3.8 %collective-permute-start = (f32[8,8,128]{2,1,0:T(8,128)S(1)}, f32[8,8,128]{2,1,0:T(8,128)S(1)}, u32[]{:S(2)}, u32[]{:S(2)}) collective-permute-start(f32[8,8,128]{2,1,0:T(8,128)S(1)} %get-tuple-element.42), channel_id=1, source_target_pairs={{0,1},{1,2},{2,3},{3,4},{4,5},{5,6},{6,7},{8,9},{9,10},{10,11},{11... | collective-permute-start | bytes 98312 | tf_op jit(solution)/shard_map/ppermute | solution.py:739
  9.5 1.9 collective-permute-start.1
  11.4 3.3 %collective-permute-done.1.refs_8_ = f32[8,8,128]{2,1,0:T(8,128)S(1)} collective-permute-done((f32[8,8,128]{2,1,0:T(8,128)S(1)}, f32[8,8,128]{2,1,0:T(8,128)S(1)}, u32[]{:S(2)}, u32[]{:S(2)}) %collective-permute-start.1) | collective-permute-done | bytes 32800 | tf_op jit(solution)/shard_map/ppermute | solution.py:740
  14.7 7.6 %sweep_1.1 = (f32[8,752,128]{2,1,0:T(8,128)}, f32[1,256]{1,0:T(1,128)S(1)}, f32[1,256]{1,0:T(1,128)S(1)}) custom-call(s32[1]{0:T(128)} %bitcast.refs_0_.me_ref, f32[8,2000,128]{2,1,0:T(8,128)} %bitcast.8, f32[8,2000,128]{2,1,0:T(8,128)} %bitcast.13, f32[125,125]{1,0:T(8,128)S(1)} %copy-done.7, f32[125,64,125]{2,1,0:T(8,128)} %bitcast.15, ...), custom_call_target="tpu_custom_call" | custom-call | flops 2415919104 | bytes 12320768 | tf_op jit(solution)/shard_map/sweep_1/pallas_call | solution.py:382
  22.4 4.4 %all-to-all-start = ((f32[8,752,128]{2,1,0:T(8,128)}), f32[8,752,128]{2,1,0:T(8,128)}, u32[]{:S(2)}, u32[]{:S(2)}) async-start(f32[8,752,128]{2,1,0:T(8,128)} %get-tuple-element.44.refs_0_.refs_11_), calls=%async_computation | async-start | bytes 6160384 | tf_op jit(solution)/shard_map/all_to_all | solution.py:745
  26.8 1.3 collective-permute-start.2
  28.1 1.2 collective-permute-start.3
  29.3 8.4 %maps.1 = (f32[8,128,128]{2,1,0:T(8,128)S(1)}, f32[8,128,128]{2,1,0:T(8,128)S(1)}, f32[8,128,128]{2,1,0:T(8,128)S(1)}, f32[8,128,128]{2,1,0:T(8,128)}, f32[8,128,128]{2,1,0:T(8,128)}, /*index=5*/f32[128,128]{1,0:T(8,128)S(1)}) custom-call(s32[1]{0:T(128)} %bitcast.refs_0_.me_ref, f32[125,64,125]{2,1,0:T(8,128)} %bitcast.11, ...), custom_call_target="tpu_custom_call" | custom-call | flops 1207959552 | bytes 4194304 | tf_op jit(solution)/shard_map/maps/pallas_call | solution.py:429
  37.7 0.8 copy-done
  38.5 0.8 copy-done.3
  39.3 0.8 copy-done.4
  40.1 0.0 collective-permute-done.2.refs_9_
  40.1 0.0 collective-permute-done.3.refs_10_
  40.1 15.9 %sweep_4.1 = (f32[4,752,128]{2,1,0:T(8,128)}, f32[4,752,128]{2,1,0:T(8,128)}, f32[4,256,128]{2,1,0:T(8,128)S(1)}, f32[4,256,128]{2,1,0:T(8,128)S(1)}, f32[8,128,256]{2,1,0:T(8,128)}, /*index=5*/f32[8,128,256]{2,1,0:T(8,128)}) custom-call(s32[1]{0:T(128)} %bitcast.refs_0_.me_ref, f32[8,2000,128]{2,1,0:T(8,128)} %bitcast.9, f32[8,2000,128]{2,1,0:T(8,128)} %bitcast.14, ...), custom_call_target="tpu_custom_call" | custom-call | flops 4026531840 | bytes 16384000 | tf_op jit(solution)/shard_map/sweep_4/pallas_call | solution.py:382
  56.1 0.8 copy-done.5
  56.9 0.5 collective-permute-start.12
  57.4 4.5 %chain.1 = (f32[8,128,256]{2,1,0:T(8,128)}, f32[128,384]{1,0:T(8,128)}) custom-call(f32[8,128,256]{2,1,0:T(8,128)} %get-tuple-element.49.start_ref.refs_8_, f32[8,128,256]{2,1,0:T(8,128)} %get-tuple-element.50.end_ref, f32[8,128,128]{2,1,0:T(8,128)} %copy-done.4, f32[8,128,128]{2,1,0:T(8,128)} %get-tuple-element.52.whole_ref, f32[128,128]{1,0:T(8,128)} %copy-done.8), custom_call_target="tpu_custom_call" | custom-call | flops 536870912 | bytes 4194304 | tf_op jit(solution)/shard_map/chain/pallas_call | solution.py:460
  61.8 1.3 collective-permute-start.6
  63.1 0.2 collective-permute-start.5
  63.3 1.2 collective-permute-start.4
  64.5 0.6 pad_add_fusion.refs_0_
  65.1 3.5 %collective-permute-done.6.refs_4_ = f32[128,384]{1,0:T(8,128)S(1)} collective-permute-done((f32[128,384]{1,0:T(8,128)}, f32[128,384]{1,0:T(8,128)S(1)}, u32[]{:S(2)}, u32[]{:S(2)}) %collective-permute-start.6) | collective-permute-done | bytes 196640 | tf_op jit(solution)/shard_map/ppermute | solution.py:734
  68.6 1.0 collective-permute-done.5.refs_3_
  69.6 4.3 %collective-permute-done.4.refs_2_ = f32[128,384]{1,0:T(8,128)S(1)} collective-permute-done((f32[128,384]{1,0:T(8,128)}, f32[128,384]{1,0:T(8,128)S(1)}, u32[]{:S(2)}, u32[]{:S(2)}) %collective-permute-start.4) | collective-permute-done | bytes 196640 | tf_op jit(solution)/shard_map/ppermute | solution.py:734
  73.9 0.7 copy-done.21
  74.5 5.3 %first.1 = (f32[4,256,128]{2,1,0:T(8,128)}, f32[4,256,128]{2,1,0:T(8,128)}) custom-call(s32[2]{0:T(128)} %pad_add_fusion.refs_0_, f32[128,384]{1,0:T(8,128)} %get-tuple-element.53.refs_1_, f32[128,384]{1,0:T(8,128)} %copy-done.21, f32[128,384]{1,0:T(8,128)} %copy-done.20, f32[128,384]{1,0:T(8,128)} %copy-done.19, f32[8,128,256]{2,1,0:T(8,128)} %get-tuple-element.54.refs_5_, ...), custom_call_target="tpu_custom_call" | custom-call | flops 805306368 | bytes 4194304 | tf_op jit(solution)/shard_map/first/pallas_call | solution.py:501
  79.9 1.1 collective-permute-start.7
  81.0 1.7 collective-permute-done.7.refs_1_
  82.7 0.8 copy-done.17
  83.5 2.1 couple.3
  85.6 1.3 collective-permute-start.8
  86.9 0.2 collective-permute-start.10
  87.1 2.1 collective-permute-start.9
  89.2 0.0 collective-permute-done.12.refs_1_
  89.2 1.2 copy-done.11
  90.4 2.9 %couple.5 = (f32[2,752,128]{2,1,0:T(8,128)}, f32[2,752,128]{2,1,0:T(8,128)}, f32[2,752,128]{2,1,0:T(8,128)}, f32[2,752,128]{2,1,0:T(8,128)}) custom-call(f32[4,752,128]{2,1,0:T(8,128)} %get-tuple-element.68.refs_0_, f32[4,752,128]{2,1,0:T(8,128)} %copy-done.11), custom_call_target="tpu_custom_call" | custom-call | bytes 6160384 | tf_op jit(solution)/shard_map/couple/pallas_call | solution.py:536
  93.3 16.9 %collective-permute-done.8.refs_1_ = f32[2,256,128]{2,1,0:T(8,128)S(1)} collective-permute-done((f32[2,256,128]{2,1,0:T(8,128)}, f32[2,256,128]{2,1,0:T(8,128)S(1)}, u32[]{:S(2)}, u32[]{:S(2)}) %collective-permute-start.8) | collective-permute-done | bytes 262176 | tf_op jit(solution)/shard_map/ppermute | solution.py:734
  110.2 0.7 copy-done.12
  110.9 2.1 %collective-permute-start.13 = (f32[2,752,128]{2,1,0:T(8,128)}, f32[2,752,128]{2,1,0:T(8,128)S(1)}, u32[]{:S(2)}, u32[]{:S(2)}) collective-permute-start(f32[2,752,128]{2,1,0:T(8,128)} %gate.6), channel_id=1, source_target_pairs={{0,2},{1,3},{2,4},{3,5},{4,6},{5,7},{6,0},{7,1},{8,10},{9,11},{10,... | collective-permute-start | bytes 2310152 | tf_op jit(solution)/shard_map/ppermute | solution.py:734
  113.0 15.8 %collective-permute-done.10.refs_3_.refs_1_ = f32[2,256,128]{2,1,0:T(8,128)S(1)} collective-permute-done((f32[2,256,128]{2,1,0:T(8,128)}, f32[2,256,128]{2,1,0:T(8,128)S(1)}, u32[]{:S(2)}, u32[]{:S(2)}) %collective-permute-start.10) | collective-permute-done | bytes 262176 | tf_op jit(solution)/shard_map/ppermute | solution.py:734
  128.8 0.7 copy-done.13
  129.5 0.0 collective-permute-start.18
  129.5 0.0 collective-permute-done.9.refs_2_.refs_1_
  129.5 0.7 copy-done.14
  130.2 0.5 collective-permute-start.17
  130.7 1.2 collective-permute-start.11
  132.0 1.5 collective-permute-done.11.refs_1_
  133.5 0.8 copy-done.18
  134.3 2.1 couple.4
  136.4 28.9 %collective-permute-done.13.refs_1_ = f32[2,752,128]{2,1,0:T(8,128)S(1)} collective-permute-done((f32[2,752,128]{2,1,0:T(8,128)}, f32[2,752,128]{2,1,0:T(8,128)S(1)}, u32[]{:S(2)}, u32[]{:S(2)}) %collective-permute-start.13) | collective-permute-done | bytes 770080 | tf_op jit(solution)/shard_map/ppermute | solution.py:734
  165.3 0.9 copy-done.10
  166.2 2.1 %collective-permute-start.14 = (f32[2,256,128]{2,1,0:T(8,128)}, f32[2,256,128]{2,1,0:T(8,128)S(1)}, u32[]{:S(2)}, u32[]{:S(2)}) collective-permute-start(f32[2,256,128]{2,1,0:T(8,128)} %gate.7), channel_id=1, source_target_pairs={{0,2},{1,3},{2,4},{3,5},{4,6},{5,7},{6,0},{7,1},{8,10},{9,11},{10,... | collective-permute-start | bytes 786440 | tf_op jit(solution)/shard_map/ppermute | solution.py:734
  168.3 0.0 collective-permute-start.15
  168.3 1.2 collective-permute-start.16
  169.5 6.2 %finish_0.1 = (f32[8,2000,128]{2,1,0:T(8,128)}, bf16[8,256,256]{2,1,0:T(8,128)(2,1)}) custom-call(s32[1]{0:T(128)} %bitcast.refs_0_.me_ref, f32[8,128,128]{2,1,0:T(8,128)} %copy-done, f32[8,752,128]{2,1,0:T(8,128)} %all-to-all-done.one_ref, f32[2,256,128]{2,1,0:T(8,128)} %get-tuple-element.59.refs_0_, f32[2,256,128]{2,1,0:T(8,128)} %copy-done.12, ...), custom_call_target="tpu_custom_call" | custom-call | flops 805306368 | bytes 8192000 | tf_op jit(solution)/shard_map/finish_0/pallas_call | solution.py:616
  175.7 2.7 %collective-permute-done.18.refs_3_ = f32[2,752,128]{2,1,0:T(8,128)S(1)} collective-permute-done((f32[2,752,128]{2,1,0:T(8,128)}, f32[2,752,128]{2,1,0:T(8,128)S(1)}, u32[]{:S(2)}, u32[]{:S(2)}) %collective-permute-start.18) | collective-permute-done | bytes 770080 | tf_op jit(solution)/shard_map/ppermute | solution.py:734
  178.4 14.7 %collective-permute-done.17.refs_2_ = f32[2,752,128]{2,1,0:T(8,128)S(1)} collective-permute-done((f32[2,752,128]{2,1,0:T(8,128)}, f32[2,752,128]{2,1,0:T(8,128)S(1)}, u32[]{:S(2)}, u32[]{:S(2)}) %collective-permute-start.17) | collective-permute-done | bytes 770080 | tf_op jit(solution)/shard_map/ppermute | solution.py:734
  193.1 0.9 copy-done.16
  194.0 4.8 %finish_4.1.refs_4_ = f32[8,2000,128]{2,1,0:T(8,128)} custom-call(s32[1]{0:T(128)} %bitcast.refs_0_.me_ref, f32[8,128,128]{2,1,0:T(8,128)} %copy-done, bf16[8,256,256]{2,1,0:T(8,128)(2,1)} %get-tuple-element.63.operand_ref, f32[2,752,128]{2,1,0:T(8,128)} %get-tuple-element.73.refs_0_, f32[2,752,128]{2,1,0:T(8,128)} %copy-done.10, ...), custom_call_target="tpu_custom_call", output_to_operand_aliasing={{}: (7, {})} | custom-call | flops 805306368 | bytes 6144000 | tf_op jit(solution)/shard_map/finish_4/pallas_call | solution.py:673
  198.9 5.5 %collective-permute-done.15.refs_2_ = f32[2,256,128]{2,1,0:T(8,128)S(1)} collective-permute-done((f32[2,256,128]{2,1,0:T(8,128)}, f32[2,256,128]{2,1,0:T(8,128)S(1)}, u32[]{:S(2)}, u32[]{:S(2)}) %collective-permute-start.15) | collective-permute-done | bytes 262176 | tf_op jit(solution)/shard_map/ppermute | solution.py:734
  204.3 2.1 collective-permute-done.16.refs_3_
  206.4 1.7 finish_7.1
  (39 shorter events, 0.1 us)
Async XLA Ops:
  0.0 0.8 copy-start.9
  0.8 13.9 %copy-start.7 = (f32[125,125]{1,0:T(8,128)S(1)}, f32[125,125]{1,0:T(8,128)}, u32[]{:S(2)}) copy-start(f32[125,125]{1,0:T(8,128)} %refs_3_.3) | copy-start | bytes 187504
  5.7 5.7 %collective-permute-start = (f32[8,8,128]{2,1,0:T(8,128)S(1)}, f32[8,8,128]{2,1,0:T(8,128)S(1)}, u32[]{:S(2)}, u32[]{:S(2)}) collective-permute-start(f32[8,8,128]{2,1,0:T(8,128)S(1)} %get-tuple-element.42), channel_id=1, source_target_pairs={{0,1},{1,2},{2,3},{3,4},{4,5},{5,6},{6,7},{8,9},{9,10},{10,11},{11... | collective-permute-start | bytes 98312 | tf_op jit(solution)/shard_map/ppermute | solution.py:739
  9.5 5.2 %collective-permute-start.1 = (f32[8,8,128]{2,1,0:T(8,128)S(1)}, f32[8,8,128]{2,1,0:T(8,128)S(1)}, u32[]{:S(2)}, u32[]{:S(2)}) collective-permute-start(f32[8,8,128]{2,1,0:T(8,128)S(1)} %get-tuple-element.43), channel_id=1, source_target_pairs={{1,0},{2,1},{3,2},{4,3},{5,4},{6,5},{7,6},{9,8},{10,9},{11,10},{12... | collective-permute-start | bytes 98312 | tf_op jit(solution)/shard_map/ppermute | solution.py:740
  22.4 147.1 %all-to-all-start = ((f32[8,752,128]{2,1,0:T(8,128)}), f32[8,752,128]{2,1,0:T(8,128)}, u32[]{:S(2)}, u32[]{:S(2)}) async-start(f32[8,752,128]{2,1,0:T(8,128)} %get-tuple-element.44.refs_0_.refs_11_), calls=%async_computation | async-start | bytes 6160384 | tf_op jit(solution)/shard_map/all_to_all | solution.py:745
  26.8 13.3 %collective-permute-start.2 = (f32[1,256]{1,0:T(1,128)S(1)}, f32[1,256]{1,0:T(1,128)S(1)}, u32[]{:S(2)}, u32[]{:S(2)}) collective-permute-start(f32[1,256]{1,0:T(1,128)S(1)} %get-tuple-element.46), channel_id=1, source_target_pairs={{0,8},{8,16},{16,24},{24,0},{1,9},{9,17},{17,25},{25,1},{2,10},{10... | collective-permute-start | bytes 3080 | tf_op jit(solution)/shard_map/ppermute | solution.py:734
  28.1 12.1 %collective-permute-start.3 = (f32[1,256]{1,0:T(1,128)S(1)}, f32[1,256]{1,0:T(1,128)S(1)}, u32[]{:S(2)}, u32[]{:S(2)}) collective-permute-start(f32[1,256]{1,0:T(1,128)S(1)} %get-tuple-element.47), channel_id=1, source_target_pairs={{0,24},{8,0},{16,8},{24,16},{1,25},{9,1},{17,9},{25,17},{2,26},{10... | collective-permute-start | bytes 3080 | tf_op jit(solution)/shard_map/ppermute | solution.py:734
  37.7 0.8 copy-start
  38.5 0.8 copy-start.3
  39.3 0.8 copy-start.4
  40.1 15.9 %copy-start.8 = (f32[128,128]{1,0:T(8,128)}, f32[128,128]{1,0:T(8,128)S(1)}, u32[]{:S(2)}) copy-start(f32[128,128]{1,0:T(8,128)S(1)} %get-tuple-element.48.refs_12_.group_ref) | copy-start | bytes 196612
  56.1 0.8 copy-start.5
  56.9 32.3 %collective-permute-start.12 = (f32[4,752,128]{2,1,0:T(8,128)}, f32[4,752,128]{2,1,0:T(8,128)S(1)}, u32[]{:S(2)}, u32[]{:S(2)}) collective-permute-start(f32[4,752,128]{2,1,0:T(8,128)} %get-tuple-element.69), channel_id=1, source_target_pairs={{0,1},{1,0},{2,3},{3,2},{4,5},{5,4},{6,7},{7,6},{8,9},{9,8},{10,11... | collective-permute-start | bytes 4620296 | tf_op jit(solution)/shard_map/ppermute | solution.py:749
  61.8 6.8 %collective-permute-start.6 = (f32[128,384]{1,0:T(8,128)}, f32[128,384]{1,0:T(8,128)S(1)}, u32[]{:S(2)}, u32[]{:S(2)}) collective-permute-start(f32[128,384]{1,0:T(8,128)} %get-tuple-element.53.refs_1_), channel_id=1, source_target_pairs={{0,24},{8,0},{16,8},{24,16},{1,25},{9,1},{17,9},{25,17},{2,26},{10... | collective-permute-start | bytes 589832 | tf_op jit(solution)/shard_map/ppermute | solution.py:734
  63.1 6.5 %collective-permute-start.5 = (f32[128,384]{1,0:T(8,128)}, f32[128,384]{1,0:T(8,128)S(1)}, u32[]{:S(2)}, u32[]{:S(2)}) collective-permute-start(f32[128,384]{1,0:T(8,128)} %get-tuple-element.53.refs_1_), channel_id=1, source_target_pairs={{0,16},{8,24},{16,0},{24,8},{1,17},{9,25},{17,1},{25,9},{2,18},{10... | collective-permute-start | bytes 589832 | tf_op jit(solution)/shard_map/ppermute | solution.py:734
  63.3 10.6 %collective-permute-start.4 = (f32[128,384]{1,0:T(8,128)}, f32[128,384]{1,0:T(8,128)S(1)}, u32[]{:S(2)}, u32[]{:S(2)}) collective-permute-start(f32[128,384]{1,0:T(8,128)} %get-tuple-element.53.refs_1_), channel_id=1, source_target_pairs={{0,8},{8,16},{16,24},{24,0},{1,9},{9,17},{17,25},{25,1},{2,10},{10... | collective-permute-start | bytes 589832 | tf_op jit(solution)/shard_map/ppermute | solution.py:734
  68.6 5.2 %copy-start.19 = (f32[128,384]{1,0:T(8,128)}, f32[128,384]{1,0:T(8,128)S(1)}, u32[]{:S(2)}) copy-start(f32[128,384]{1,0:T(8,128)S(1)} %collective-permute-done.6.refs_4_) | copy-start | bytes 589828
  69.6 4.3 %copy-start.20 = (f32[128,384]{1,0:T(8,128)}, f32[128,384]{1,0:T(8,128)S(1)}, u32[]{:S(2)}) copy-start(f32[128,384]{1,0:T(8,128)S(1)} %collective-permute-done.5.refs_3_) | copy-start | bytes 589828
  73.9 0.7 copy-start.21
  79.9 2.8 %collective-permute-start.7 = (f32[4,256,128]{2,1,0:T(8,128)}, f32[4,256,128]{2,1,0:T(8,128)S(1)}, u32[]{:S(2)}, u32[]{:S(2)}) collective-permute-start(f32[4,256,128]{2,1,0:T(8,128)} %get-tuple-element.58), channel_id=1, source_target_pairs={{0,1},{1,0},{2,3},{3,2},{4,5},{5,4},{6,7},{7,6},{8,9},{9,8},{10,11... | collective-permute-start | bytes 1572872 | tf_op jit(solution)/shard_map/ppermute | solution.py:749
  82.7 0.8 copy-start.17
  85.6 24.6 %collective-permute-start.8 = (f32[2,256,128]{2,1,0:T(8,128)}, f32[2,256,128]{2,1,0:T(8,128)S(1)}, u32[]{:S(2)}, u32[]{:S(2)}) collective-permute-start(f32[2,256,128]{2,1,0:T(8,128)} %get-tuple-element.60), channel_id=1, source_target_pairs={{0,2},{1,3},{2,4},{3,5},{4,6},{5,7},{6,0},{7,1},{8,10},{9,11},{10,... | collective-permute-start | bytes 786440 | tf_op jit(solution)/shard_map/ppermute | solution.py:734
  86.9 41.9 %collective-permute-start.10 = (f32[2,256,128]{2,1,0:T(8,128)}, f32[2,256,128]{2,1,0:T(8,128)S(1)}, u32[]{:S(2)}, u32[]{:S(2)}) collective-permute-start(f32[2,256,128]{2,1,0:T(8,128)} %get-tuple-element.62), channel_id=1, source_target_pairs={{0,6},{1,7},{2,0},{3,1},{4,2},{5,3},{6,4},{7,5},{8,14},{9,15},{10,... | collective-permute-start | bytes 786440 | tf_op jit(solution)/shard_map/ppermute | solution.py:734
  87.1 42.4 %collective-permute-start.9 = (f32[2,256,128]{2,1,0:T(8,128)}, f32[2,256,128]{2,1,0:T(8,128)S(1)}, u32[]{:S(2)}, u32[]{:S(2)}) collective-permute-start(f32[2,256,128]{2,1,0:T(8,128)} %get-tuple-element.61), channel_id=1, source_target_pairs={{0,4},{1,5},{2,6},{3,7},{4,0},{5,1},{6,2},{7,3},{8,12},{9,13},{10,... | collective-permute-start | bytes 786440 | tf_op jit(solution)/shard_map/ppermute | solution.py:734
  89.2 1.2 copy-start.11
  110.1 0.7 copy-start.12
  110.9 54.5 %collective-permute-start.13 = (f32[2,752,128]{2,1,0:T(8,128)}, f32[2,752,128]{2,1,0:T(8,128)S(1)}, u32[]{:S(2)}, u32[]{:S(2)}) collective-permute-start(f32[2,752,128]{2,1,0:T(8,128)} %gate.6), channel_id=1, source_target_pairs={{0,2},{1,3},{2,4},{3,5},{4,6},{5,7},{6,0},{7,1},{8,10},{9,11},{10,... | collective-permute-start | bytes 2310152 | tf_op jit(solution)/shard_map/ppermute | solution.py:734
  128.8 0.7 copy-start.13
  129.5 48.9 %collective-permute-start.18 = (f32[2,752,128]{2,1,0:T(8,128)}, f32[2,752,128]{2,1,0:T(8,128)S(1)}, u32[]{:S(2)}, u32[]{:S(2)}) collective-permute-start(f32[2,752,128]{2,1,0:T(8,128)} %gate.11), channel_id=1, source_target_pairs={{0,6},{1,7},{2,0},{3,1},{4,2},{5,3},{6,4},{7,5},{8,14},{9,15},{10,... | collective-permute-start | bytes 2310152 | tf_op jit(solution)/shard_map/ppermute | solution.py:734
  129.5 0.7 copy-start.14
  130.2 62.9 %collective-permute-start.17 = (f32[2,752,128]{2,1,0:T(8,128)}, f32[2,752,128]{2,1,0:T(8,128)S(1)}, u32[]{:S(2)}, u32[]{:S(2)}) collective-permute-start(f32[2,752,128]{2,1,0:T(8,128)} %gate.10), channel_id=1, source_target_pairs={{0,4},{1,5},{2,6},{3,7},{4,0},{5,1},{6,2},{7,3},{8,12},{9,13},{10,... | collective-permute-start | bytes 2310152 | tf_op jit(solution)/shard_map/ppermute | solution.py:734
  130.7 2.8 %collective-permute-start.11 = (f32[4,256,128]{2,1,0:T(8,128)S(1)}, f32[4,256,128]{2,1,0:T(8,128)S(1)}, u32[]{:S(2)}, u32[]{:S(2)}) collective-permute-start(f32[4,256,128]{2,1,0:T(8,128)S(1)} %get-tuple-element.65), channel_id=1, source_target_pairs={{0,1},{1,0},{2,3},{3,2},{4,5},{5,4},{6,7},{7,6},{8,9},{9,8},{10,11... | collective-permute-start | bytes 1572872 | tf_op jit(solution)/shard_map/ppermute | solution.py:749
  133.5 0.8 copy-start.18
  165.3 0.9 copy-start.10
  166.2 32.6 %collective-permute-start.14 = (f32[2,256,128]{2,1,0:T(8,128)}, f32[2,256,128]{2,1,0:T(8,128)S(1)}, u32[]{:S(2)}, u32[]{:S(2)}) collective-permute-start(f32[2,256,128]{2,1,0:T(8,128)} %gate.7), channel_id=1, source_target_pairs={{0,2},{1,3},{2,4},{3,5},{4,6},{5,7},{6,0},{7,1},{8,10},{9,11},{10,... | collective-permute-start | bytes 786440 | tf_op jit(solution)/shard_map/ppermute | solution.py:734
  168.3 36.0 %collective-permute-start.15 = (f32[2,256,128]{2,1,0:T(8,128)}, f32[2,256,128]{2,1,0:T(8,128)S(1)}, u32[]{:S(2)}, u32[]{:S(2)}) collective-permute-start(f32[2,256,128]{2,1,0:T(8,128)} %gate.8), channel_id=1, source_target_pairs={{0,4},{1,5},{2,6},{3,7},{4,0},{5,1},{6,2},{7,3},{8,12},{9,13},{10,... | collective-permute-start | bytes 786440 | tf_op jit(solution)/shard_map/ppermute | solution.py:734
  168.3 38.1 %collective-permute-start.16 = (f32[2,256,128]{2,1,0:T(8,128)}, f32[2,256,128]{2,1,0:T(8,128)S(1)}, u32[]{:S(2)}, u32[]{:S(2)}) collective-permute-start(f32[2,256,128]{2,1,0:T(8,128)} %gate.9), channel_id=1, source_target_pairs={{0,6},{1,7},{2,0},{3,1},{4,2},{5,3},{6,4},{7,5},{8,14},{9,15},{10,... | collective-permute-start | bytes 786440 | tf_op jit(solution)/shard_map/ppermute | solution.py:734
  178.4 15.6 %copy-start.15 = (f32[2,752,128]{2,1,0:T(8,128)}, f32[2,752,128]{2,1,0:T(8,128)S(1)}, u32[]{:S(2)}) copy-start(f32[2,752,128]{2,1,0:T(8,128)S(1)} %collective-permute-done.18.refs_3_) | copy-start | bytes 2310148
  193.1 0.9 copy-start.16
  194.0 12.4 %copy-start.1 = (f32[8,128,128]{2,1,0:T(8,128)S(1)}, f32[8,128,128]{2,1,0:T(8,128)}, u32[]{:S(2)}) copy-start(f32[8,128,128]{2,1,0:T(8,128)} %copy-done) | copy-start | bytes 1572868
  194.0 12.4 %copy-start.2 = (bf16[8,256,256]{2,1,0:T(8,128)(2,1)S(1)}, bf16[8,256,256]{2,1,0:T(8,128)(2,1)}, u32[]{:S(2)}) copy-start(bf16[8,256,256]{2,1,0:T(8,128)(2,1)} %get-tuple-element.63.operand_ref) | copy-start | bytes 3145732
  194.0 12.4 %copy-start.6 = (f32[2,256,128]{2,1,0:T(8,128)S(1)}, f32[2,256,128]{2,1,0:T(8,128)}, u32[]{:S(2)}) copy-start(f32[2,256,128]{2,1,0:T(8,128)} %get-tuple-element.66.refs_0_) | copy-start | bytes 786436
